TPU v7x, 32 devices: a whole 2x2x4 slice. The times are simulated.
32 devices in a mesh: dp: 8 (over y, x, core), blk: 4 (over z).
Axes of the slice: x: 2, y: 2, z: 4, core: 2. Of those that a mesh axis runs over, the one named last changes fastest.
Arguments:
- tokens: bfloat16 [8, 768, 768], P('dp', 'blk'), may hold values from -6 to 6
- lengths: int32 [8, 4], P('dp'), may hold values from 1 to 765, as said below
- distance_bucket: int32 [2049], replicated, may hold values from 0 to 512, as said below
- w_qkv: bfloat16 [768, 2304], P(('dp', 'blk')), may hold values from -0.21875 to 0.21875
- w_out: bfloat16 [768, 768], P(('dp', 'blk')), may hold values from -0.21875 to 0.21875
- w_fc1: bfloat16 [768, 3072], P(('dp', 'blk')), may hold values from -0.21875 to 0.21875
- w_fc2: bfloat16 [3072, 768], P(('dp', 'blk')), may hold values from -0.109375 to 0.109375
- gain_in: float32 [768], replicated, may hold values from 0.25 to 1.75
- gain_attn: float32 [768], replicated, may hold values from 0.25 to 1.75
- gain_ffn_in: float32 [768], replicated, may hold values from 0.25 to 1.75
- gain_hidden: float32 [3072], replicated, may hold values from 0.25 to 1.75
- head_scale: float32 [12], replicated, may hold values from 0.25 to 1.75
- bias_table: float32 [513, 12], replicated, may hold values from -5 to 5
- cotangent: bfloat16 [8, 768, 768], P('dp', 'blk'), may hold values from -6 to 6
Outputs:
- mixed: bfloat16 [8, 768, 768], P('dp', 'blk')
- grad_tokens: bfloat16 [8, 768, 768], P('dp', 'blk')
- grad_qkv: float32 [768, 2304], P(('dp', 'blk'))
- grad_out: float32 [768, 768], P(('dp', 'blk'))
- grad_fc1: float32 [768, 3072], P(('dp', 'blk'))
- grad_fc2: float32 [3072, 768], P(('dp', 'blk'))
- grad_gain_in: float32 [768], replicated
- grad_gain_attn: float32 [768], replicated
- grad_gain_ffn_in: float32 [768], replicated
- grad_gain_hidden: float32 [3072], replicated
- grad_head_scale: float32 [12], replicated
- grad_bias_table: float32 [513, 12], replicated
Inputs may be any that keep to these rules, and one draw needn't show every extreme that they name: In every row the 4 lengths sum to 768; one document, at an index that varies, starts within the first 192 positions of the row and ends within the last 192. `distance_bucket`: entry 1024 + r is the bucket of the clipped relative distance r; it never falls as r rises and equals 256 at r = 0.
All inputs are finite; a program needn't handle non-finite values.
Results may differ from a plain program's by a relative error of at most 0.02.
Values may be sent and summed in bfloat16 or wider, within the bound.
No kernel may reach another device: no remote copies, remote signals or barrier semaphores. Data moves between devices by JAX's collectives and lax.ppermute only.
A program may use at most 320 MiB of HBM per device.

v0:
```python
import math

import jax
import jax.numpy as jnp
from jax import lax
from jax.sharding import PartitionSpec as P

epsilon = 1e-05
masked_score = -1e30
query_scale = 0.125
highest = lax.Precision.HIGHEST


def layer_norm(value, gain):
    center = value - jnp.mean(value, axis=-1, keepdims=True)
    spread = jnp.mean(center * center, axis=-1, keepdims=True)
    return center * lax.rsqrt(spread + epsilon) * gain


def hidden_norm(value, gain):
    return layer_norm(jax.nn.gelu(value, approximate=False), gain)


def column_product(left, right):
    return lax.dot_general(
        left, right, (((0,), (0,)), ((), ())), preferred_element_type=jnp.float32
    )


def times_transpose(left, matrix):
    return lax.dot_general(
        left, matrix, (((1,), (1,)), ((), ())), preferred_element_type=jnp.float32
    )


def toeplitz(diagonals, rows, cols):
    heads = diagonals.shape[0]
    padded = jnp.pad(diagonals, ((0, 0), (0, 1)))
    stride = rows + cols - 1
    tiled = jnp.tile(padded, (1, rows))[:, : rows * stride].reshape(heads, rows, stride)
    return tiled[:, :, rows - 1 : rows - 1 + cols]


def diagonal_sums(grid):
    heads, rows, cols = grid.shape
    flipped = grid[:, ::-1, :]
    padded = jnp.pad(flipped, ((0, 0), (0, 0), (0, rows)))
    skewed = padded.reshape(heads, -1)[:, : rows * (rows + cols - 1)].reshape(
        heads, rows, rows + cols - 1
    )
    return jnp.sum(skewed, axis=1)


def on_device(
    tokens,
    lengths,
    distance_bucket,
    w_qkv,
    w_out,
    w_fc1,
    w_fc2,
    gain_in,
    gain_attn,
    gain_ffn_in,
    gain_hidden,
    head_scale,
    bias_table,
    cotangent,
):
    rows_here = tokens.shape[1]
    width = tokens.shape[2]
    heads = head_scale.shape[0]
    head_size = width // heads
    reach = distance_bucket.shape[0] // 2
    bucket_count = bias_table.shape[0]
    row_len = rows_here * lax.axis_size("blk")
    key_block = math.gcd(row_len, 512)
    block_count = row_len // key_block
    query_anchor = lax.axis_index("blk") * rows_here
    positions = query_anchor + jnp.arange(rows_here, dtype=jnp.int32)
    ends = jnp.cumsum(lengths[0])
    bucket_ids = jnp.arange(bucket_count, dtype=jnp.int32)

    def document_of(where):
        return jnp.sum((where[:, None] >= ends[None, :]).astype(jnp.int32), axis=1)

    query_docs = document_of(positions)

    def bucket_index(query_start, rows, key_start, cols):
        steps = jnp.arange(rows + cols - 1, dtype=jnp.int32)
        relative = key_start - query_start - (rows - 1) + steps
        return jnp.take(distance_bucket, jnp.clip(relative, -reach, reach) + reach)

    def scores_for(query_heads, query_start, query_doc, key_heads, key_start, key_doc):
        rows = query_heads.shape[0]
        cols = key_heads.shape[0]
        raw = jnp.einsum("qhd,khd->hqk", query_heads, key_heads, preferred_element_type=jnp.float32)
        buckets = bucket_index(query_start, rows, key_start, cols)
        diagonals = jnp.take(bias_table, buckets, axis=0).T
        same = query_doc[:, None] == key_doc[None, :]
        full = raw + toeplitz(diagonals, rows, cols)
        return (jnp.where(same[None], full, masked_score), same, buckets)

    residual_in = tokens[0].astype(jnp.float32)
    wqkv_all, wout_all = (
        lax.all_gather(w_qkv, ("dp", "blk"), axis=0, tiled=True),
        lax.all_gather(w_out, ("dp", "blk"), axis=0, tiled=True),
    )
    normed_f, norm_in_back = jax.vjp(layer_norm, residual_in, gain_in)
    normed_in = normed_f.astype(jnp.bfloat16)
    projected = jnp.dot(normed_in, wqkv_all, preferred_element_type=jnp.float32)
    queries = (projected[:, :width] * query_scale).astype(jnp.bfloat16)
    keys_here = projected[:, width : 2 * width].astype(jnp.bfloat16)
    values_here = projected[:, 2 * width :].astype(jnp.bfloat16)
    query_heads = queries.reshape(rows_here, heads, head_size)
    best = jnp.full((heads, rows_here), masked_score, jnp.float32)
    key_piece = lax.all_gather(keys_here, "blk", axis=0, tiled=True)
    value_piece = lax.all_gather(values_here, "blk", axis=0, tiled=True)
    length = key_piece.shape[0]
    key_pos = jnp.arange(length, dtype=jnp.int32)
    scores, same, buckets = scores_for(
        query_heads,
        query_anchor,
        query_docs,
        key_piece.reshape(length, heads, head_size),
        jnp.int32(0),
        document_of(key_pos),
    )
    new_best = jnp.maximum(best, jnp.max(scores, axis=-1))
    weights = jnp.where(same[None], jnp.exp(scores - new_best[..., None]), 0.0)
    total = jnp.sum(weights, axis=-1)
    accum = jnp.einsum(
        "hqk,khd->hqd",
        weights.astype(jnp.bfloat16),
        value_piece.reshape(length, heads, head_size),
        preferred_element_type=jnp.float32,
    )
    best, total, accum = (new_best, total, accum)
    log_total = best + jnp.log(total)
    attention = jnp.transpose(accum / total[..., None], (1, 0, 2)).reshape(rows_here, width)
    scale_cols = jnp.repeat(head_scale, head_size)
    scaled = (attention * scale_cols).astype(jnp.bfloat16)
    attn_out = jnp.dot(scaled, wout_all, preferred_element_type=jnp.float32)
    normed_attn, norm_attn_back = jax.vjp(layer_norm, attn_out, gain_attn)
    middle = residual_in + normed_attn
    fc1_all, fc2_all = (
        lax.all_gather(w_fc1, ("dp", "blk"), axis=0, tiled=True),
        lax.all_gather(w_fc2, ("dp", "blk"), axis=0, tiled=True),
    )
    normed_mid_f, norm_mid_back = jax.vjp(layer_norm, middle, gain_ffn_in)
    normed_mid = normed_mid_f.astype(jnp.bfloat16)
    hidden = jnp.dot(normed_mid, fc1_all, preferred_element_type=jnp.float32)
    activated_f, hidden_back = jax.vjp(hidden_norm, hidden, gain_hidden)
    activated = activated_f.astype(jnp.bfloat16)
    mixed = (middle + jnp.dot(activated, fc2_all, preferred_element_type=jnp.float32)).astype(
        jnp.bfloat16
    )
    grad_in = cotangent[0]
    fc1_back, fc2_back = (
        lax.all_gather(w_fc1, ("dp", "blk"), axis=0, tiled=True),
        lax.all_gather(w_fc2, ("dp", "blk"), axis=0, tiled=True),
    )
    grad_fc2 = lax.psum_scatter(
        column_product(activated, grad_in), ("dp", "blk"), scatter_dimension=0, tiled=True
    )
    d_activated = times_transpose(grad_in, fc2_back)
    d_hidden_f, grad_gain_hidden = hidden_back(d_activated)
    d_hidden = d_hidden_f.astype(jnp.bfloat16)
    grad_fc1 = lax.psum_scatter(
        column_product(normed_mid, d_hidden), ("dp", "blk"), scatter_dimension=0, tiled=True
    )
    d_mid_part, grad_gain_ffn_in = norm_mid_back(times_transpose(d_hidden, fc1_back))
    d_middle = grad_in.astype(jnp.float32) + d_mid_part
    d_attn_f, grad_gain_attn = norm_attn_back(d_middle)
    d_attn_out = d_attn_f.astype(jnp.bfloat16)
    qkv_back, out_back = (
        lax.all_gather(w_qkv, ("dp", "blk"), axis=0, tiled=True),
        lax.all_gather(w_out, ("dp", "blk"), axis=0, tiled=True),
    )
    grad_out = lax.psum_scatter(
        column_product(scaled, d_attn_out), ("dp", "blk"), scatter_dimension=0, tiled=True
    )
    d_scaled = times_transpose(d_attn_out, out_back)
    grad_scale = jnp.sum((d_scaled * attention).reshape(rows_here, heads, head_size), axis=(0, 2))
    d_attention = (d_scaled * scale_cols).astype(jnp.bfloat16)
    grad_heads = d_attention.reshape(rows_here, heads, head_size)
    row_delta = jnp.sum(
        (d_attention.astype(jnp.float32) * attention).reshape(rows_here, heads, head_size), axis=2
    ).T
    keys_back, values_back = (
        lax.all_gather(keys_here, "blk", axis=0, tiled=True),
        lax.all_gather(values_here, "blk", axis=0, tiled=True),
    )

    def pair_grads(
        query_part,
        grad_part,
        total_part,
        delta_part,
        query_start,
        query_doc,
        key_part,
        value_part,
        key_start,
        key_doc,
    ):
        scores, same, buckets = scores_for(
            query_part, query_start, query_doc, key_part, key_start, key_doc
        )
        probs = jnp.where(same[None], jnp.exp(scores - total_part[..., None]), 0.0)
        d_probs = jnp.einsum(
            "qhd,khd->hqk", grad_part, value_part, preferred_element_type=jnp.float32
        )
        d_scores = probs * (d_probs - delta_part[..., None])
        return (probs.astype(jnp.bfloat16), d_scores, buckets)

    def bias_sum(d_scores, buckets):
        sums = diagonal_sums(d_scores)
        selector = (buckets[:, None] == bucket_ids[None, :]).astype(jnp.float32)
        return jnp.dot(sums, selector, precision=highest).T

    def key_slices(index):
        begin = index * key_block
        key_part = lax.dynamic_slice_in_dim(keys_back, begin, key_block, 0).reshape(
            key_block, heads, head_size
        )
        value_part = lax.dynamic_slice_in_dim(values_back, begin, key_block, 0).reshape(
            key_block, heads, head_size
        )
        return (key_part, value_part, begin)

    query_carry = (
        jnp.zeros((rows_here, heads, head_size), jnp.float32),
        jnp.zeros((bucket_count, heads), jnp.float32),
    )

    def key_step(carry, index):
        d_query, d_bias = carry
        key_part, value_part, begin = key_slices(index)
        key_doc = document_of(begin + jnp.arange(key_block, dtype=jnp.int32))
        probs_low, d_scores, buckets = pair_grads(
            query_heads,
            grad_heads,
            log_total,
            row_delta,
            query_anchor,
            query_docs,
            key_part,
            value_part,
            begin,
            key_doc,
        )
        scores_low = d_scores.astype(jnp.bfloat16)
        d_query = d_query + jnp.einsum(
            "hqk,khd->qhd", scores_low, key_part, preferred_element_type=jnp.float32
        )
        d_key = jnp.einsum(
            "hqk,qhd->khd", scores_low, query_heads, preferred_element_type=jnp.float32
        ).reshape(key_block, width)
        d_value = jnp.einsum(
            "hqk,qhd->khd", probs_low, grad_heads, preferred_element_type=jnp.float32
        ).reshape(key_block, width)
        return (
            (d_query, d_bias + bias_sum(d_scores, buckets)),
            jnp.concatenate([d_key, d_value], axis=1),
        )

    (d_query, d_bias), kv_terms = lax.scan(
        key_step, query_carry, jnp.arange(block_count, dtype=jnp.int32)
    )
    kv_grad = lax.psum_scatter(
        kv_terms.reshape(row_len, 2 * width).astype(jnp.bfloat16),
        "blk",
        scatter_dimension=0,
        tiled=True,
    )
    d_query_low = d_query.reshape(rows_here, width).astype(jnp.bfloat16)
    d_projected = jnp.concatenate(
        [d_query_low * jnp.asarray(query_scale, jnp.bfloat16), kv_grad], axis=1
    )
    grad_qkv = lax.psum_scatter(
        column_product(normed_in, d_projected), ("dp", "blk"), scatter_dimension=0, tiled=True
    )
    d_input_part, grad_gain_in = norm_in_back(times_transpose(d_projected, qkv_back))
    grad_tokens = (d_middle + d_input_part).astype(jnp.bfloat16)[None]
    small = lax.psum(
        (grad_gain_in, grad_gain_attn, grad_gain_ffn_in, grad_gain_hidden, grad_scale, d_bias),
        ("dp", "blk"),
    )
    return (
        mixed[None],
        grad_tokens,
        grad_qkv,
        grad_out,
        grad_fc1,
        grad_fc2,
        small[0],
        small[1],
        small[2],
        small[3],
        small[4],
        small[5],
    )


def solution(mesh):
    return jax.shard_map(
        on_device,
        mesh=mesh,
        in_specs=(
            P("dp", "blk", None),
            P("dp", None),
            P(),
            P(("dp", "blk"), None),
            P(("dp", "blk"), None),
            P(("dp", "blk"), None),
            P(("dp", "blk"), None),
            P(),
            P(),
            P(),
            P(),
            P(),
            P(),
            P("dp", "blk", None),
        ),
        out_specs=(
            P("dp", "blk", None),
            P("dp", "blk", None),
            P(("dp", "blk"), None),
            P(("dp", "blk"), None),
            P(("dp", "blk"), None),
            P(("dp", "blk"), None),
            P(),
            P(),
            P(),
            P(),
            P(),
            P(),
        ),
        check_vma=False,
    )
```

profile of v0, /device:TPU:18, one launch (start us, length us, event | category | flops | bytes accessed | tf_op | source)
XLA Modules:
  0.0 1164.0 jit_solution(1821494866603235414)
XLA Ops:
  10.3 60.4 %all-gather.7.cloned.1.call-done = bf16[768,2304]{1,0:T(8,128)(2,1)} async-done(((bf16[24,2304]{1,0:T(8,128)(2,1)}), bf16[768,2304]{1,0:T(8,128)(2,1)}) %all-gather.7.cloned.1.call-update) | async-done | bytes 3538960 | tf_op jit(solution)/shard_map/all_gather | solution.py:106
  70.7 3.0 fusion.84
  77.4 5.9 gather_fusion.2
  83.3 2.9 gather_fusion.3
  86.6 4.7 tile.21
  91.3 15.9 %tile.22 = f32[12,184320]{1,0:T(8,128)} reshape(f32[12,192,960]{2,1,0:T(8,128)} %tile.21) | data formatting | bytes 17694720 | tf_op jit(solution)/shard_map/tile | solution.py:40
  107.3 9.7 slice.56
  117.0 17.4 %reshape.443 = f32[12,192,959]{2,1,0:T(8,128)} reshape(f32[12,184128]{1,0:T(8,128)} %slice.56) | data formatting | bytes 17676288 | tf_op jit(solution)/shard_map/reshape | solution.py:40
  135.3 2.6 copy.78
  140.3 6.6 fusion.85
  148.9 3.0 fusion.35
  152.3 39.2 %all-gather.13.cloned.1.call-done = bf16[768,768]{1,0:T(8,128)(2,1)} async-done(((bf16[24,768]{1,0:T(8,128)(2,1)}), bf16[768,768]{1,0:T(8,128)(2,1)}) %all-gather.13.cloned.1.call-update) | async-done | bytes 1179664 | tf_op jit(solution)/shard_map/all_gather | solution.py:107
  194.7 63.1 %all-gather.15.cloned.1.call-done = bf16[768,3072]{1,0:T(8,128)(2,1)} async-done(((bf16[24,3072]{1,0:T(8,128)(2,1)}), bf16[768,3072]{1,0:T(8,128)(2,1)}) %all-gather.15.cloned.1.call-update) | async-done | bytes 4718608 | tf_op jit(solution)/shard_map/all_gather | solution.py:147
  257.8 9.1 fusion.79
  266.9 56.0 %all-gather.17.cloned.1.call-done = bf16[3072,768]{1,0:T(8,128)(2,1)} async-done(((bf16[96,768]{1,0:T(8,128)(2,1)}), bf16[3072,768]{1,0:T(8,128)(2,1)}) %all-gather.17.cloned.1.call-update) | async-done | bytes 4718608 | tf_op jit(solution)/shard_map/all_gather | solution.py:148
  322.9 4.2 multiply_reduce_fusion.1
  338.2 259.3 %while.17 = (s32[]{:T(128)}, f32[192,12,64]{0,2,1:T(8,128)}, f32[513,12]{0,1:T(8,128)S(1)}, bf16[3,256,1536]{2,1,0:T(8,128)(2,1)}, s32[3]{0:T(128)S(1)}, /*index...) while((s32[]{:T(128)}, f32[192,12,64]{0,2,1:T(8,128)}, ...), condition=%wide.region_23.24_spmd.clone, body=%wide.region_20.23_spmd.clone.sunk | while | flops 419025792 | bytes 109865672 | solution.py:268
  352.9 2.8 gather_fusion
  357.3 2.8 tile.27
  360.0 6.4 tile.28
  366.4 5.4 slice.84
  371.8 7.0 reshape.504
  379.0 3.3 fusion.135
  385.9 15.2 %rev.8 = f32[12,192,256]{2,1,0:T(8,128)} reverse(f32[12,192,256]{2,1,0:T(8,128)S(1)} %bitcast_multiply_fusion.2), dimensions={1} | reverse | bytes 4718592 | tf_op jit(solution)/shard_map/while/body/eval_jaxpr/rev | solution.py:46
  401.1 4.5 pad.54
  405.6 6.4 reshape.505
  412.0 5.4 slice.85
  417.4 7.0 reshape.506
  424.4 2.9 reduce_sum.361
  434.6 2.8 gather_fusion
  439.0 2.8 tile.27
  441.8 6.4 tile.28
  448.1 5.4 slice.84
  453.5 7.0 reshape.504
  460.7 3.3 fusion.135
  466.2 2.5 fusion.136
  468.7 15.2 %rev.8 = f32[12,192,256]{2,1,0:T(8,128)} reverse(f32[12,192,256]{2,1,0:T(8,128)S(1)} %bitcast_multiply_fusion.2), dimensions={1} | reverse | bytes 4718592 | tf_op jit(solution)/shard_map/while/body/eval_jaxpr/rev | solution.py:46
  484.0 4.5 pad.54
  488.5 6.4 reshape.505
  494.9 5.4 slice.85
  500.2 7.0 reshape.506
  507.2 2.9 reduce_sum.361
  517.6 2.8 gather_fusion
  521.9 2.8 tile.27
  524.7 6.4 tile.28
  531.1 5.4 slice.84
  536.5 7.0 reshape.504
  543.7 3.3 fusion.135
  551.7 15.2 %rev.8 = f32[12,192,256]{2,1,0:T(8,128)} reverse(f32[12,192,256]{2,1,0:T(8,128)S(1)} %bitcast_multiply_fusion.2), dimensions={1} | reverse | bytes 4718592 | tf_op jit(solution)/shard_map/while/body/eval_jaxpr/rev | solution.py:46
  566.9 4.5 pad.54
  571.4 6.4 reshape.505
  577.8 5.4 slice.85
  583.2 7.0 reshape.506
  590.2 2.9 reduce_sum.361
  600.9 5.2 fusion.75
  607.8 5.2 fusion.54
  616.1 28.4 %reduce-scatter.6.cloned.1.call-done = bf16[192,1536]{1,0:T(8,128)(2,1)} async-done(((bf16[768,1536]{1,0:T(8,128)(2,1)}), bf16[192,1536]{1,0:T(8,128)(2,1)}) %reduce-scatter.6.cloned.1.call-update) | async-done | bytes 589840 | tf_op jit(solution)/shard_map/reduce_scatter | solution.py:271
  644.5 5.3 fusion.51
  650.9 4.3 fusion.34
  657.2 41.5 %all-reduce.3 = (f32[768]{0:T(1024)}, f32[768]{0:T(1024)}, f32[768]{0:T(1024)}, f32[3072]{0:T(1024)}, f32[12]{0:T(128)}, /*index=5*/f32[513,12]{0,1:T(8,128)}) all-reduce(f32[768]{0:T(1024)S(1)} %get-tuple-element.353, f32[768]{0:T(1024)S(1)} %copy-done.61, f32[768]{0:T(1024)S(1)} %copy-done.67, ...), channel_id=1, replica_groups=mesh['dp'=8,'blk'=4] {'dp','blk'}, use_global_device_ids=true, to_apply=%region_32.33 | all-reduce | flops 11544 | bytes 92352 | tf_op jit(solution)/shard_map/psum | solution.py:286
  699.7 48.7 %reduce-scatter.10.cloned.1.call-done = f32[24,768]{1,0:T(8,128)} async-done(((f32[768,768]{1,0:T(8,128)}), f32[24,768]{1,0:T(8,128)}) %reduce-scatter.10.cloned.1.call-update) | async-done | bytes 73744 | tf_op jit(solution)/shard_map/reduce_scatter | solution.py:180
  748.4 142.1 %reduce-scatter.12.cloned.1.call-done = f32[24,3072]{1,0:T(8,128)} async-done(((f32[768,3072]{1,0:T(8,128)}), f32[24,3072]{1,0:T(8,128)}) %reduce-scatter.12.cloned.1.call-update) | async-done | bytes 294928 | tf_op jit(solution)/shard_map/reduce_scatter | solution.py:169
  890.6 140.9 %reduce-scatter.14.cloned.1.call-done = f32[96,768]{1,0:T(8,128)} async-done(((f32[3072,768]{1,0:T(8,128)}), f32[96,768]{1,0:T(8,128)}) %reduce-scatter.14.cloned.1.call-update) | async-done | bytes 294928 | tf_op jit(solution)/shard_map/reduce_scatter | solution.py:163
  1031.5 125.6 %reduce-scatter.8.cloned.1.call-done = f32[24,2304]{1,0:T(8,128)} async-done(((f32[768,2304]{1,0:T(8,128)}), f32[24,2304]{1,0:T(8,128)}) %reduce-scatter.8.cloned.1.call-update) | async-done | bytes 221200 | tf_op jit(solution)/shard_map/reduce_scatter | solution.py:281
  (317 shorter events, 73.9 us)
Async XLA Ops:
  7.2 63.5 %all-gather.7.cloned.1.call-start = ((), (), s32[]{:S(2)}) async-start(), calls=%async_computation.5 | async-start | bytes 3649536 | tf_op jit(solution)/shard_map/all_gather | solution.py:106
  7.9 127.4 %all-gather.11.cloned.1.call-start = ((), (), s32[]{:S(2)}) async-start(), calls=%async_computation.7 | async-start | bytes 1474560 | tf_op jit(solution)/shard_map/all_gather | solution.py:118
  9.1 61.6 %copy-start.42 = (f32[192]{0:T(256)}, f32[192]{0:T(256)S(1)}, u32[]{:S(2)}) copy-start(f32[192]{0:T(256)S(1)} %broadcast_multiply_fusion.3) | copy-start | bytes 2308
  10.3 60.4 %copy-start.65 = (f32[192]{0:T(256)}, f32[192]{0:T(256)S(1)}, u32[]{:S(2)}) copy-start(f32[192]{0:T(256)S(1)} %fusion.48) | copy-start | bytes 2308
  10.3 60.4 %copy-start.51 = (f32[192]{0:T(256)}, f32[192]{0:T(256)S(1)}, u32[]{:S(2)}) copy-start(f32[192]{0:T(256)S(1)} %fusion.63) | copy-start | bytes 2308
  10.3 66.9 %copy-start.47 = (f32[513,12]{0,1:T(8,128)S(1)}, f32[513,12]{0,1:T(8,128)}, u32[]{:S(2)}) copy-start(f32[513,12]{0,1:T(8,128)} %param.28) | copy-start | bytes 73876
  73.7 3.6 copy-start
  74.6 63.3 %all-gather.9.cloned.1.call-start = ((), (), s32[]{:S(2)}) async-start(), calls=%async_computation.6 | async-start | bytes 1474560 | tf_op jit(solution)/shard_map/all_gather | solution.py:117
  75.4 116.2 %all-gather.13.cloned.1.call-start = ((), (), s32[]{:S(2)}) async-start(), calls=%async_computation.8 | async-start | bytes 1216512 | tf_op jit(solution)/shard_map/all_gather | solution.py:107
  75.9 181.9 %all-gather.15.cloned.1.call-start = ((), (), s32[]{:S(2)}) async-start(), calls=%async_computation.9 | async-start | bytes 4866048 | tf_op jit(solution)/shard_map/all_gather | solution.py:147
  76.5 246.4 %all-gather.17.cloned.1.call-start = ((), (), s32[]{:S(2)}) async-start(), calls=%async_computation.10 | async-start | bytes 4866048 | tf_op jit(solution)/shard_map/all_gather | solution.py:148
  77.1 567.4 %reduce-scatter.6.cloned.1.call-start = ((), (), s32[]{:S(2)}) async-start(), calls=%async_computation.11 | async-start | bytes 2949120 | tf_op jit(solution)/shard_map/reduce_scatter | solution.py:271
  117.0 17.4 %copy-start.69 = (s32[1,4]{1,0:T(1,128)S(1)}, s32[1,4]{1,0:T(1,128)}, u32[]{:S(2)}) copy-start(s32[1,4]{1,0:T(1,128)} %param.17) | copy-start | bytes 52
  117.0 17.5 %copy-start.68 = (f32[12]{0:T(128)S(1)}, f32[12]{0:T(128)}, u32[]{:S(2)}) copy-start(f32[12]{0:T(128)} %param.27) | copy-start | bytes 148
  134.7 201.0 %copy-start.40 = (f32[768]{0:T(1024)}, f32[768]{0:T(1024)S(1)}, u32[]{:S(2)}) copy-start(f32[768]{0:T(1024)S(1)} %mul.305) | copy-start | bytes 9220
  152.0 41.5 %copy-start.8 = (bf16[1,192,768]{2,1,0:T(8,128)(2,1)S(1)}, bf16[1,192,768]{2,1,0:T(8,128)(2,1)}, u32[]{:S(2)}) copy-start(bf16[1,192,768]{2,1,0:T(8,128)(2,1)} %param.16) | copy-start | bytes 884740
  152.0 41.5 %copy-start.50 = (f32[768]{0:T(1024)S(1)}, f32[768]{0:T(1024)}, u32[]{:S(2)}) copy-start(f32[768]{0:T(1024)} %param.24) | copy-start | bytes 9220
  152.3 41.2 %copy-start.18 = (f32[192,768]{1,0:T(8,128)}, f32[192,768]{1,0:T(8,128)S(1)}, u32[]{:S(2)}) copy-start(f32[192,768]{1,0:T(8,128)S(1)} %copy.79) | copy-start | bytes 1769476
  152.3 105.5 %copy-start.38 = (f32[768]{0:T(1024)S(1)}, f32[768]{0:T(1024)}, u32[]{:S(2)}) copy-start(f32[768]{0:T(1024)} %param.25) | copy-start | bytes 9220
  193.9 140.0 %copy-start.55 = (f32[192]{0:T(256)}, f32[192]{0:T(256)S(1)}, u32[]{:S(2)}) copy-start(f32[192]{0:T(256)S(1)} %broadcast_multiply_fusion.1) | copy-start | bytes 2308
  194.1 139.8 %copy-start.59 = (f32[192]{0:T(256)}, f32[192]{0:T(256)S(1)}, u32[]{:S(2)}) copy-start(f32[192]{0:T(256)S(1)} %fusion.65) | copy-start | bytes 2308
  194.7 128.2 %copy-start.21 = (bf16[1,192,768]{2,1,0:T(8,128)(2,1)S(1)}, bf16[1,192,768]{2,1,0:T(8,128)(2,1)}, u32[]{:S(2)}) copy-start(bf16[1,192,768]{2,1,0:T(8,128)(2,1)} %param.29) | copy-start | bytes 884740
  194.7 128.2 %copy-start.35 = (f32[3072]{0:T(1024)S(1)}, f32[3072]{0:T(1024)}, u32[]{:S(2)}) copy-start(f32[3072]{0:T(1024)} %param.26) | copy-start | bytes 36868
  266.9 61.7 %copy-start.2 = (f32[192,3072]{1,0:T(8,128)}, f32[192,3072]{1,0:T(8,128)S(1)}, u32[]{:S(2)}) copy-start(f32[192,3072]{1,0:T(8,128)S(1)} %get-tuple-element.402) | copy-start | bytes 7077892
  266.9 61.7 %copy-start.44 = (f32[192]{0:T(256)}, f32[192]{0:T(256)S(1)}, u32[]{:S(2)}) copy-start(f32[192]{0:T(256)S(1)} %broadcast_multiply_fusion) | copy-start | bytes 2308
  327.1 2.4 copy-start.31
  327.1 4.2 slice-start
  331.4 2.5 copy-start.26
  331.4 2.9 copy-start.15
  334.2 2.7 copy-start.16
  334.2 2.7 copy-start.57
  335.7 2.4 copy-start.63
  379.0 4.7 copy-start.4
  379.0 4.7 copy-start.6
  424.4 3.5 copy-start.5
  460.7 4.7 copy-start.4
  460.7 4.7 copy-start.6
  507.2 3.5 copy-start.5
  543.6 4.7 copy-start.4
  543.6 4.7 copy-start.6
  590.1 3.5 copy-start.5
  597.5 3.2 copy-start.48
  597.6 3.2 copy-start.12
  597.6 3.2 copy-start.27
  597.6 3.2 copy-start.39
  597.7 3.2 copy-start.56
  597.7 3.2 copy-start.60
  597.7 150.8 %reduce-scatter.10.cloned.1.call-start = ((), (), s32[]{:S(2)}) async-start(), calls=%async_computation.13 | async-start | bytes 2433024 | tf_op jit(solution)/shard_map/reduce_scatter | solution.py:180
  600.8 289.8 %reduce-scatter.12.cloned.1.call-start = ((), (), s32[]{:S(2)}) async-start(), calls=%async_computation.14 | async-start | bytes 9732096 | tf_op jit(solution)/shard_map/reduce_scatter | solution.py:169
  606.1 425.3 %reduce-scatter.14.cloned.1.call-start = ((), (), s32[]{:S(2)}) async-start(), calls=%async_computation.15 | async-start | bytes 9732096 | tf_op jit(solution)/shard_map/reduce_scatter | solution.py:163
  613.0 31.5 %copy-start.37 = (f32[768]{0:T(1024)S(1)}, f32[768]{0:T(1024)}, u32[]{:S(2)}) copy-start(f32[768]{0:T(1024)} %param.23) | copy-start | bytes 9220
  613.0 31.5 %copy-start.43 = (f32[192]{0:T(256)S(1)}, f32[192]{0:T(256)}, u32[]{:S(2)}) copy-start(f32[192]{0:T(256)} %copy-done.42) | copy-start | bytes 2308
  613.0 31.5 %copy-start.52 = (f32[192]{0:T(256)S(1)}, f32[192]{0:T(256)}, u32[]{:S(2)}) copy-start(f32[192]{0:T(256)} %copy-done.51) | copy-start | bytes 2308
  613.0 544.0 %reduce-scatter.8.cloned.1.call-start = ((), (), s32[]{:S(2)}) async-start(), calls=%async_computation.12 | async-start | bytes 7299072 | tf_op jit(solution)/shard_map/reduce_scatter | solution.py:281
  616.1 33.7 %copy-start.32 = (bf16[192,768]{1,0:T(8,128)(2,1)}, bf16[192,768]{1,0:T(8,128)(2,1)S(1)}, u32[]{:S(2)}) copy-start(bf16[192,768]{1,0:T(8,128)(2,1)S(1)} %copy.87) | copy-start | bytes 884740
  650.9 4.4 copy-start.9
  650.9 4.4 copy-start.29
  650.9 4.4 copy-start.33
  650.9 4.4 copy-start.34
  655.3 1.9 copy-start.46
  655.3 1.9 copy-start.49
  655.3 43.4 %copy-start.17 = (f32[192,768]{1,0:T(8,128)S(1)}, f32[192,768]{1,0:T(8,128)}, u32[]{:S(2)}) copy-start(f32[192,768]{1,0:T(8,128)} %copy-done.16) | copy-start | bytes 1769476
  655.3 43.4 %copy-start.23 = (bf16[1,192,768]{2,1,0:T(8,128)(2,1)S(1)}, bf16[1,192,768]{2,1,0:T(8,128)(2,1)}, u32[]{:S(2)}) copy-start(bf16[1,192,768]{2,1,0:T(8,128)(2,1)} %param.29) | copy-start | bytes 884740
  655.3 43.4 %copy-start.58 = (f32[192]{0:T(256)S(1)}, f32[192]{0:T(256)}, u32[]{:S(2)}) copy-start(f32[192]{0:T(256)} %copy-done.57) | copy-start | bytes 2308
  (27 other events, 39.0 us)
Sparse Core Ops, SparseCore 0:
  10.8 59.8 all-gather.6
  74.7 29.6 all-gather.10
  106.6 29.5 all-gather.8
  138.9 52.5 all-gather.12
  194.2 63.6 all-gather.14
  260.5 62.3 all-gather.16
  597.7 46.6 reduce-scatter.5
  650.3 98.0 reduce-scatter.9
  755.9 134.5 reduce-scatter.11
  896.9 134.5 reduce-scatter.13
  1038.7 118.3 reduce-scatter.7
where the time goes:
time: 1180 us; the launch traced here: 1160 us
  waiting for transfers between devices  707 us (60%)
  local copies, waits for them, and re-layouts  280 us (24%)
  matrix products  82 us (7%)
  blocking collectives  41.5 us (4%)
  other arithmetic  23.4 us (2%)
  between operations  15.2 us (1%)
  loops' own time  14.1 us (1%)
    reduce_scatter x1, waiting for transfers between devices, on_device(): lax.psum_scatter(column_product(normed_mid, d_hidden), ('dp', 'blk'), sca...  142 us
    reduce_scatter x1, waiting for transfers between devices, on_device(): lax.psum_scatter(column_product(activated, grad_in), ('dp', 'blk'), scatt...  141 us
    reduce_scatter x1, waiting for transfers between devices, on_device(): lax.psum_scatter(column_product(normed_in, d_projected), ('dp', 'blk'), s...  126 us
    all_gather x1, waiting for transfers between devices, on_device(): lax.all_gather(w_fc1, ('dp', 'blk'), axis=0, tiled=True)  63.1 us
    all_gather x1, waiting for transfers between devices, on_device(): lax.all_gather(w_qkv, ('dp', 'blk'), axis=0, tiled=True)  60.4 us
    all_gather x1, waiting for transfers between devices, on_device(): lax.all_gather(w_fc2, ('dp', 'blk'), axis=0, tiled=True)  56 us
    reduce_scatter x1, waiting for transfers between devices, on_device(): lax.psum_scatter(column_product(scaled, d_attn_out), ('dp', 'blk'), scatt...  48.7 us
    another operation x8, local copies, waits for them, and re-layouts, toeplitz(): jnp.tile(padded, (1, rows))[:, :rows * stride].reshape(heads, rows, stride)  48.2 us
  transfers between devices with their start and end apart: 11, of which 9 were waited for; matrix products, arithmetic and copies ran while one was open for 10% of the time, Pallas kernels for 0%

commit v1 on v0

--- a/solution.py
+++ b/solution.py
@@ -1,8 +1,11 @@
+import functools
 import math
 
 import jax
 import jax.numpy as jnp
 from jax import lax
+from jax.experimental import pallas as pl
+from jax.experimental.pallas import tpu as pltpu
 from jax.sharding import PartitionSpec as P
 
 epsilon = 1e-05
@@ -51,7 +54,7 @@
     return jnp.sum(skewed, axis=1)
 
 
-def on_device(
+def by_sequence(
     tokens,
     lengths,
     distance_bucket,
@@ -303,9 +306,417 @@
     )
 
 
+lanes = 128
+core_bit, x_bit, y_bit = 1, 2, 4
+
+
+def swap(value, bit):
+    size = lax.axis_size("dp")
+    return lax.ppermute(value, "dp", [(i, i ^ bit) for i in range(size)])
+
+
+def turn(value, steps):
+    size = lax.axis_size("blk")
+    return lax.ppermute(value, "blk", [(i, (i + steps) % size) for i in range(size)])
+
+
+def swap_line(value, bit):
+    size = lax.axis_size("blk")
+    return lax.ppermute(value, "blk", [(i, i ^ bit) for i in range(size)])
+
+
+def pick(stack, index):
+    return lax.dynamic_index_in_dim(stack, index, 0, keepdims=False)
+
+
+def place(blocks):
+    shape = blocks[0][1].shape
+    out = jnp.zeros((len(blocks),) + shape, blocks[0][1].dtype)
+    for index, block in blocks:
+        out = lax.dynamic_update_index_in_dim(out, block, index, 0)
+    return out
+
+
+def gather_line(value):
+    here, size = lax.axis_index("blk"), lax.axis_size("blk")
+    blocks = [(here, value)]
+    for steps in range(1, size):
+        blocks.append((lax.rem(here - steps + size, size), turn(value, steps)))
+    out = place(blocks)
+    return out.reshape((size * value.shape[0],) + value.shape[1:])
+
+
+def deal_line(stack):
+    here, size = lax.axis_index("blk"), lax.axis_size("blk")
+    got = [pick(stack, here)]
+    for steps in range(1, size):
+        got.append(turn(pick(stack, lax.rem(here + steps, size)), steps))
+    return got
+
+
+def gather_planes(line):
+    me = lax.axis_index("dp")
+    half = line.shape[0] // 2
+    along_x, along_y = swap(line, x_bit), swap(line, y_bit)
+    across = jnp.concatenate([swap(along_y[:half], x_bit), swap(along_x[half:], y_bit)], axis=0)
+    blocks = []
+    for bits, block in ((0, line), (x_bit, along_x), (y_bit, along_y), (x_bit | y_bit, across)):
+        blocks.append((me ^ bits, block))
+        blocks.append((me ^ bits ^ core_bit, swap(block, core_bit)))
+    out = place(blocks)
+    return out.reshape((-1,) + line.shape[1:])
+
+
+def gather_weight(shard):
+    return gather_planes(gather_line(shard))
+
+
+def add_low(left, right):
+    return (left.astype(jnp.float32) + right.astype(jnp.float32)).astype(jnp.bfloat16)
+
+
+def scatter_planes(block_of):
+    me = lax.axis_index("dp")
+
+    def with_core(bits):
+        other = swap(block_of(me ^ bits ^ core_bit), core_bit)
+        return add_low(block_of(me ^ bits), other)
+
+    across = with_core(x_bit | y_bit)
+    half = across.shape[0] // 2
+    from_x, from_y = swap(across[:half], x_bit), swap(across[half:], y_bit)
+    to_x, to_y, own = with_core(x_bit), with_core(y_bit), with_core(0)
+    to_y = jnp.concatenate([add_low(to_y[:half], from_x), to_y[half:]], axis=0)
+    to_x = jnp.concatenate([to_x[:half], add_low(to_x[half:], from_y)], axis=0)
+    got_x, got_y = swap(to_x, x_bit), swap(to_y, y_bit)
+    total = own.astype(jnp.float32) + got_x.astype(jnp.float32) + got_y.astype(jnp.float32)
+    return total.astype(jnp.bfloat16)
+
+
+def sum_parts(parts):
+    total = parts[0].astype(jnp.float32)
+    for part in parts[1:]:
+        total = total + part.astype(jnp.float32)
+    return total
+
+
+def scatter_weight(block_of):
+    size = lax.axis_size("blk")
+    line = scatter_planes(block_of)
+    return sum_parts(deal_line(line.reshape((size, -1) + line.shape[1:])))
+
+
+def sum_everywhere(value):
+    for bit in (core_bit, x_bit, y_bit):
+        value = value + swap(value, bit)
+    bit = 1
+    while bit < lax.axis_size("blk"):
+        value = value + swap_line(value, bit)
+        bit *= 2
+    return value
+
+
+def contract(left, right, left_axis, right_axis):
+    return lax.dot_general(
+        left, right, (((left_axis,), (right_axis,)), ((), ())), preferred_element_type=jnp.float32
+    )
+
+
+def attend_kernel(
+    heads, head_size, qkv_ref, diagonal_ref, doc_col_ref, doc_row_ref, scale_ref, probs_ref, attention_ref, scaled_ref, bias
+):
+    length = qkv_ref.shape[0]
+    blocks = length // lanes
+    width = heads * head_size
+    for head in range(heads):
+        for step in range(2 * blocks - 1):
+            window = diagonal_ref[head : head + 1, step * lanes : (step + 2) * lanes]
+            window = jnp.broadcast_to(window, (lanes, 2 * lanes))
+            window = pltpu.roll(window, 0, 1, stride=1, stride_axis=0)
+            bias[:, step * lanes : (step + 1) * lanes] = window[:, lanes:]
+        low = head * head_size
+        keys = qkv_ref[:, width + low : width + low + head_size]
+        values = qkv_ref[:, 2 * width + low : 2 * width + low + head_size]
+        for block in range(blocks):
+            rows = slice(block * lanes, (block + 1) * lanes)
+            first = (blocks - 1 - block) * lanes
+            scores = contract(qkv_ref[rows, low : low + head_size], keys, 1, 1)
+            scores = scores + bias[:, first : first + length]
+            same = doc_col_ref[rows, :] == doc_row_ref[...]
+            scores = jnp.where(same, scores, masked_score)
+            weights = jnp.exp(scores - jnp.max(scores, axis=1, keepdims=True))
+            probs = weights * (1.0 / jnp.sum(weights, axis=1, keepdims=True))
+            probs = probs.astype(jnp.bfloat16)
+            probs_ref[head, rows, :] = probs
+            attention_ref[rows, low : low + head_size] = contract(probs, values, 1, 0)
+    scaled_ref[...] = (attention_ref[...] * scale_ref[...]).astype(jnp.bfloat16)
+
+
+def attend(qkv, diagonals, doc_col, doc_row, scale_cols, heads, head_size):
+    length, width = qkv.shape[0], heads * head_size
+    return pl.pallas_call(
+        functools.partial(attend_kernel, heads, head_size),
+        out_shape=(
+            jax.ShapeDtypeStruct((heads, length, length), jnp.bfloat16),
+            jax.ShapeDtypeStruct((length, width), jnp.float32),
+            jax.ShapeDtypeStruct((length, width), jnp.bfloat16),
+        ),
+        scratch_shapes=[pltpu.VMEM((lanes, 2 * length - lanes), jnp.float32)],
+        compiler_params=pltpu.CompilerParams(vmem_limit_bytes=40 * 2**20),
+        cost_estimate=pl.CostEstimate(
+            flops=4 * heads * length * length * head_size,
+            bytes_accessed=2 * heads * length * length,
+            transcendentals=heads * length * length,
+        ),
+        name="attend",
+    )(qkv, diagonals, doc_col, doc_row, scale_cols)
+
+
+def attend_back_kernel(
+    heads, head_size, qkv_ref, probs_ref, attention_ref, grad_ref, out_ref, diagonal_ref, delta_ref, sums
+):
+    length = qkv_ref.shape[0]
+    blocks = length // lanes
+    width = heads * head_size
+    diagonal_ref[...] = jnp.zeros_like(diagonal_ref)
+    for head in range(heads):
+        sums[...] = jnp.zeros_like(sums)
+        low = head * head_size
+        keys = qkv_ref[:, width + low : width + low + head_size]
+        values = qkv_ref[:, 2 * width + low : 2 * width + low + head_size]
+        d_keys = jnp.zeros((head_size, length), jnp.float32)
+        d_values = jnp.zeros((head_size, length), jnp.float32)
+        for block in range(blocks):
+            rows = slice(block * lanes, (block + 1) * lanes)
+            first = (blocks - 1 - block) * lanes
+            queries = qkv_ref[rows, low : low + head_size]
+            grad = grad_ref[rows, low : low + head_size]
+            probs = probs_ref[head, rows, :]
+            part = grad.astype(jnp.float32) * attention_ref[rows, low : low + head_size]
+            delta = jnp.sum(part, axis=1, keepdims=True)
+            delta_ref[rows, head : head + 1] = delta
+            d_scores = probs.astype(jnp.float32) * (contract(grad, values, 1, 1) - delta)
+            sums[:, first : first + length] += d_scores
+            d_scores = d_scores.astype(jnp.bfloat16)
+            d_query = contract(d_scores, keys, 1, 0).astype(jnp.bfloat16)
+            out_ref[rows, low : low + head_size] = d_query * jnp.asarray(query_scale, jnp.bfloat16)
+            d_keys = d_keys + contract(queries, d_scores, 0, 0)
+            d_values = d_values + contract(grad, probs, 0, 0)
+        out_ref[:, width + low : width + low + head_size] = d_keys.T.astype(jnp.bfloat16)
+        out_ref[:, 2 * width + low : 2 * width + low + head_size] = d_values.T.astype(jnp.bfloat16)
+        row_ids = lax.broadcasted_iota(jnp.int32, (lanes, lanes), 0)
+        col_ids = lax.broadcasted_iota(jnp.int32, (lanes, lanes), 1)
+        reverse = (row_ids + col_ids == lanes - 1).astype(jnp.float32)
+        flipped = jnp.dot(reverse, sums[...], precision=highest)
+        for step in range(2 * blocks - 1):
+            window = flipped[:, step * lanes : (step + 1) * lanes]
+            window = jnp.concatenate([window, jnp.zeros_like(window)], axis=1)
+            window = pltpu.roll(window, 1, 1, stride=1, stride_axis=0)
+            diagonal_ref[head : head + 1, step * lanes : (step + 2) * lanes] += jnp.sum(
+                window, axis=0, keepdims=True
+            )
+
+
+def attend_back(qkv, probs, attention, grad, heads, head_size):
+    length, width = qkv.shape[0], heads * head_size
+    return pl.pallas_call(
+        functools.partial(attend_back_kernel, heads, head_size),
+        out_shape=(
+            jax.ShapeDtypeStruct((length, 3 * width), jnp.bfloat16),
+            jax.ShapeDtypeStruct((heads, 2 * length), jnp.float32),
+            jax.ShapeDtypeStruct((length, heads), jnp.float32),
+        ),
+        scratch_shapes=[pltpu.VMEM((lanes, 2 * length - lanes), jnp.float32)],
+        compiler_params=pltpu.CompilerParams(vmem_limit_bytes=40 * 2**20),
+        cost_estimate=pl.CostEstimate(
+            flops=8 * heads * length * length * head_size,
+            bytes_accessed=2 * heads * length * length,
+            transcendentals=0,
+        ),
+        name="attend_back",
+    )(qkv, probs, attention, grad)
+
+
+def by_heads(
+    tokens,
+    lengths,
+    distance_bucket,
+    w_qkv,
+    w_out,
+    w_fc1,
+    w_fc2,
+    gain_in,
+    gain_attn,
+    gain_ffn_in,
+    gain_hidden,
+    head_scale,
+    bias_table,
+    cotangent,
+):
+    here, line_size = lax.axis_index("blk"), lax.axis_size("blk")
+    rows_here, width = tokens.shape[1], tokens.shape[2]
+    row_len = rows_here * line_size
+    all_heads = head_scale.shape[0]
+    head_size = width // all_heads
+    heads = all_heads // line_size
+    part = heads * head_size
+    reach = distance_bucket.shape[0] // 2
+    bucket_count = bias_table.shape[0]
+    shard_rows = w_qkv.shape[0]
+
+    row_tokens = gather_line(tokens[0])
+    by_head = w_qkv.reshape(shard_rows, 3, line_size, part).transpose(2, 0, 1, 3)
+    by_head = by_head.reshape(line_size, shard_rows, 3 * part)
+    dealt = deal_line(by_head)
+    qkv_line = place(
+        [(lax.rem(here - steps + line_size, line_size), block) for steps, block in enumerate(dealt)]
+    ).reshape(line_size * shard_rows, 3 * part)
+    wqkv_part = gather_planes(qkv_line)
+    wout_all = gather_weight(w_out)
+    fc1_all = gather_weight(w_fc1)
+    fc2_all = gather_weight(w_fc2)
+
+    ends = jnp.cumsum(lengths[0])
+    positions = jnp.arange(row_len, dtype=jnp.int32)
+    documents = jnp.sum((positions[:, None] >= ends[None, :]).astype(jnp.int32), axis=1)
+    relative = jnp.clip(jnp.arange(-row_len, row_len, dtype=jnp.int32), -reach, reach) + reach
+    buckets = jnp.take(distance_bucket, relative)
+    selector = (buckets[None, :] == jnp.arange(bucket_count, dtype=jnp.int32)[:, None]).astype(jnp.float32)
+    head_table = lax.dynamic_slice_in_dim(bias_table.T, here * heads, heads, 0)
+    diagonals = jnp.dot(head_table, selector, precision=highest)
+    scale_cols = jnp.repeat(head_scale, head_size)
+    head_cols = lax.dynamic_slice_in_dim(scale_cols, here * part, part, 0)[None, :]
+
+    row_in = row_tokens.astype(jnp.float32)
+    normed_row = layer_norm(row_in, gain_in).astype(jnp.bfloat16)
+    projected = jnp.dot(normed_row, wqkv_part, preferred_element_type=jnp.float32)
+    column_scale = jnp.where(jnp.arange(3 * part) < part, query_scale, 1.0)
+    qkv = (projected * column_scale).astype(jnp.bfloat16)
+    probs, attention, scaled_part = attend(
+        qkv, diagonals, documents[:, None], documents[None, :], head_cols, heads, head_size
+    )
+
+    def arrival(stack):
+        return jnp.concatenate(
+            [pick(stack, lax.rem(here - steps + line_size, line_size)) for steps in range(line_size)], axis=0
+        )
+
+    scaled = jnp.concatenate(deal_line(scaled_part.reshape(line_size, rows_here, part)), axis=1)
+    wout_here = arrival(wout_all.reshape(line_size, part, width))
+    residual_in = tokens[0].astype(jnp.float32)
+    attn_out = jnp.dot(scaled, wout_here, preferred_element_type=jnp.float32)
+    normed_attn, norm_attn_back = jax.vjp(layer_norm, attn_out, gain_attn)
+    middle = residual_in + normed_attn
+    normed_mid_f, norm_mid_back = jax.vjp(layer_norm, middle, gain_ffn_in)
+    normed_mid = normed_mid_f.astype(jnp.bfloat16)
+    hidden = jnp.dot(normed_mid, fc1_all, preferred_element_type=jnp.float32)
+    activated_f, hidden_back = jax.vjp(hidden_norm, hidden, gain_hidden)
+    activated = activated_f.astype(jnp.bfloat16)
+    mixed = (middle + jnp.dot(activated, fc2_all, preferred_element_type=jnp.float32)).astype(
+        jnp.bfloat16
+    )
+
+    def blocks_of(grad):
+        stack = grad.astype(jnp.bfloat16).reshape((lax.axis_size("dp"), -1) + grad.shape[1:])
+        return lambda index: pick(stack, index)
+
+    grad_in = cotangent[0]
+    grad_fc2 = scatter_weight(blocks_of(column_product(activated, grad_in)))
+    d_activated = times_transpose(grad_in, fc2_all)
+    d_hidden_f, grad_gain_hidden = hidden_back(d_activated)
+    d_hidden = d_hidden_f.astype(jnp.bfloat16)
+    grad_fc1 = scatter_weight(blocks_of(column_product(normed_mid, d_hidden)))
+    d_mid_part, grad_gain_ffn_in = norm_mid_back(times_transpose(d_hidden, fc1_all))
+    d_middle = grad_in.astype(jnp.float32) + d_mid_part
+    d_attn_f, grad_gain_attn = norm_attn_back(d_middle)
+    d_attn_out = d_attn_f.astype(jnp.bfloat16)
+
+    scale_here = arrival(scale_cols.reshape(line_size, part))
+    d_scaled = times_transpose(d_attn_out, wout_here)
+    d_attention = (d_scaled * scale_here).astype(jnp.bfloat16)
+    pieces = [(here, d_attention[:, :part])]
+    for steps in range(1, line_size):
+        piece = d_attention[:, steps * part : (steps + 1) * part]
+        pieces.append((lax.rem(here + steps, line_size), turn(piece, line_size - steps)))
+    grad_row = place(pieces).reshape(row_len, part)
+
+    out_grad = blocks_of(column_product(scaled, d_attn_out))
+    per_part = lax.axis_size("dp") // line_size
+
+    def out_block(index):
+        owner = lax.div(index, per_part)
+        steps = lax.rem(here - owner + line_size, line_size)
+        return out_grad(steps * per_part + lax.rem(index, per_part))
+
+    grad_out = scatter_weight(out_block)
+
+    d_projected, diagonal_sums_here, deltas = attend_back(qkv, probs, attention, grad_row, heads, head_size)
+    d_normed = times_transpose(d_projected, wqkv_part)
+    d_normed_low = d_normed.astype(jnp.bfloat16).reshape(line_size, rows_here, width)
+    d_normed_here = sum_parts(deal_line(d_normed_low))
+    qkv_line_grad = scatter_planes(blocks_of(column_product(normed_row, d_projected)))
+    qkv_dealt = deal_line(qkv_line_grad.reshape(line_size, shard_rows, 3 * part))
+    grad_qkv = place(
+        [
+            (lax.rem(here - steps + line_size, line_size), block.astype(jnp.float32))
+            for steps, block in enumerate(qkv_dealt)
+        ]
+    )
+    grad_qkv = grad_qkv.reshape(line_size, shard_rows, 3, part).transpose(1, 2, 0, 3)
+    grad_qkv = grad_qkv.reshape(shard_rows, 3 * width)
+
+    _, gain_in_back = jax.vjp(lambda gain: layer_norm(row_in, gain), gain_in)
+    (grad_gain_in,) = gain_in_back(d_normed)
+    _, norm_in_back = jax.vjp(lambda value: layer_norm(value, gain_in), residual_in)
+    (d_input_part,) = norm_in_back(d_normed_here)
+    grad_tokens = (d_middle + d_input_part).astype(jnp.bfloat16)[None]
+
+    d_table = lax.dot_general(
+        diagonal_sums_here, selector, (((1,), (1,)), ((), ())), precision=highest
+    )
+    d_bias = lax.dynamic_update_slice_in_dim(
+        jnp.zeros((all_heads, bucket_count), jnp.float32), d_table, here * heads, 0
+    )
+    scale_part = jnp.sum(deltas, axis=0)
+    grad_scale = lax.dynamic_update_slice_in_dim(
+        jnp.zeros((all_heads,), jnp.float32), scale_part, here * heads, 0
+    )
+    small = (grad_gain_in, grad_gain_attn, grad_gain_ffn_in, grad_gain_hidden, grad_scale, d_bias)
+    sizes = [math.prod(value.shape) for value in small]
+    flat = jnp.concatenate([value.reshape(-1) for value in small])
+    flat = jnp.pad(flat, (0, -flat.shape[0] % 1024)).reshape(-1, lanes)
+    flat = sum_everywhere(flat).reshape(-1)
+    sums, begin = [], 0
+    for value, size in zip(small, sizes):
+        sums.append(flat[begin : begin + size].reshape(value.shape))
+        begin += size
+    return (
+        mixed[None],
+        grad_tokens,
+        grad_qkv,
+        grad_out,
+        grad_fc1,
+        grad_fc2,
+        sums[0],
+        sums[1],
+        sums[2],
+        sums[3],
+        sums[4] / head_scale,
+        sums[5].T,
+    )
+
+
+def on_device(dp_size, line_size, tokens, *rest):
+    head_scale, row_len = rest[10], tokens.shape[1] * line_size
+    whole_heads = head_scale.shape[0] % line_size == 0 and dp_size % line_size == 0
+    if dp_size == 8 and line_size == 4 and whole_heads and row_len % lanes == 0:
+        return by_heads(tokens, *rest)
+    return by_sequence(tokens, *rest)
+
+
 def solution(mesh):
     return jax.shard_map(
-        on_device,
+        functools.partial(on_device, mesh.shape["dp"], mesh.shape["blk"]),
         mesh=mesh,
         in_specs=(
             P("dp", "blk", None),

time: 1180 us -> 378 us (0.32)
  the two profiles are of different devices: /device:TPU:18 before, /device:TPU:0 now
where the time goes in v1:
time: 378 us; the launch traced here: 372 us
  waiting for transfers between devices  159 us (42%)
  starting transfers between devices  98.5 us (26%)
  local copies, waits for them, and re-layouts  41.9 us (11%)
  other arithmetic  29.9 us (8%)
  matrix products  25.2 us (7%)
  Pallas kernels  15 us (4%)
    ppermute x67, waiting for transfers between devices, swap(): return lax.ppermute(value, 'dp', [(i, i ^ bit) for i in range(size)])  82.3 us
    ppermute x36, waiting for transfers between devices, turn(): lax.ppermute(value, 'blk', [(i, (i + steps) % size) for i in range(size)])  73.6 us
    ppermute x36, starting transfers between devices, turn(): lax.ppermute(value, 'blk', [(i, (i + steps) % size) for i in range(size)])  54.9 us
    ppermute x67, starting transfers between devices, swap(): return lax.ppermute(value, 'dp', [(i, i ^ bit) for i in range(size)])  41.6 us
    dynamic_update_slice x55, local copies, waits for them, and re-layouts, place(): out = lax.dynamic_update_index_in_dim(out, block, index, 0)  12.6 us
    gather x1, local copies, waits for them, and re-layouts, by_heads(): buckets = jnp.take(distance_bucket, relative)  8.39 us
    pallas_call x1, Pallas kernels, attend(): pl.pallas_call(functools.partial(attend_kernel, heads, head_size), out_sh...  7.97 us
  transfers between devices with their start and end apart: 105, of which 48 were waited for; matrix products, arithmetic and copies ran while one was open for 22% of the time, Pallas kernels for 4%

profile of v1, /device:TPU:0, one launch (start us, length us, event | category | flops | bytes accessed | tf_op | source)
XLA Modules:
  0.0 372.4 jit_solution(873261953652247855)
XLA Ops:
  0.7 3.1 collective-permute-start.17
  3.8 2.6 collective-permute-start.18
  12.1 8.4 %gather_fusion = s32[1536]{0:T(1024)S(1)} fusion(s32[2049]{0:T(1024)S(1)} %copy-done.2, s32[2048]{0:T(1024)S(1)} %pad_clamp_fusion), kind=kCustom, calls=%fused_computation | custom fusion | bytes 18432 | tf_op jit(solution)/shard_map/jit(_take)/gather | solution.py:583
  23.7 3.6 collective-permute-start.4
  28.1 1.6 collective-permute-done.4
  29.7 2.7 collective-permute-start.5
  32.5 1.9 collective-permute-done.5
  34.4 2.4 collective-permute-start.1
  42.4 3.0 collective-permute-done.9
  45.5 2.0 collective-permute-start.2
  48.1 2.1 collective-permute-start.28
  50.2 10.3 %collective-permute-done.28 = bf16[24,3072]{1,0:T(8,128)(2,1)S(1)} collective-permute-done((bf16[24,3072]{1,0:T(8,128)(2,1)S(1)}, bf16[24,3072]{1,0:T(8,128)(2,1)S(1)}, u32[]{:S(2)}, u32[]{:S(2)}) %collective-permute-start.28) | collective-permute-done | bytes 147488 | tf_op jit(solution)/shard_map/ppermute | solution.py:320
  60.5 2.5 collective-permute-start.29
  63.0 7.2 %collective-permute-done.29 = bf16[24,3072]{1,0:T(8,128)(2,1)S(1)} collective-permute-done((bf16[24,3072]{1,0:T(8,128)(2,1)S(1)}, bf16[24,3072]{1,0:T(8,128)(2,1)S(1)}, u32[]{:S(2)}, u32[]{:S(2)}) %collective-permute-start.29) | collective-permute-done | bytes 147488 | tf_op jit(solution)/shard_map/ppermute | solution.py:320
  70.2 2.9 collective-permute-start.30
  73.1 2.7 collective-permute-done.30
  77.7 3.2 collective-permute-start.41
  81.0 4.5 %collective-permute-done.40 = bf16[96,768]{1,0:T(8,128)(2,1)S(1)} collective-permute-done((bf16[96,768]{1,0:T(8,128)(2,1)S(1)}, bf16[96,768]{1,0:T(8,128)(2,1)S(1)}, u32[]{:S(2)}, u32[]{:S(2)}) %collective-permute-start.40) | collective-permute-done | bytes 147488 | tf_op jit(solution)/shard_map/ppermute | solution.py:320
  88.4 3.4 collective-permute-done.21
  94.3 1.8 collective-permute-done.11
  101.0 14.0 %collective-permute-done.25 = bf16[48,768]{1,0:T(8,128)(2,1)S(1)} collective-permute-done((bf16[48,768]{1,0:T(8,128)(2,1)S(1)}, bf16[48,768]{1,0:T(8,128)(2,1)S(1)}, u32[]{:S(2)}, u32[]{:S(2)}) %collective-permute-start.25) | collective-permute-done | bytes 73760 | tf_op jit(solution)/shard_map/ppermute | solution.py:315
  116.5 2.8 collective-permute-done.26
  128.4 2.6 multiply_convert_fusion.3.qkv_ref
  131.0 8.0 %attend.1 = (bf16[3,768,768]{2,1,0:T(8,128)(2,1)S(1)}, f32[768,192]{1,0:T(8,128)S(1)}, bf16[768,192]{1,0:T(8,128)(2,1)S(1)}) custom-call(bf16[768,576]{1,0:T(8,128)(2,1)S(1)} %multiply_convert_fusion.3.qkv_ref, f32[3,1536]{1,0:T(4,128)S(1)} %fusion.1.diagonal_ref, s32[768,1]{1,0:T(8,128)S(1)} %broadcast_in_dim.410.doc_col_ref, ...), custom_call_target="tpu_custom_call" | custom-call | flops 452984832 | bytes 3538944 | tf_op jit(solution)/shard_map/attend/pallas_call | solution.py:457
  139.0 4.2 %collective-permute-start.16 = (bf16[192,192]{1,0:T(8,128)(2,1)S(1)}, bf16[192,192]{1,0:T(8,128)(2,1)S(1)}, u32[]{:S(2)}, u32[]{:S(2)}) collective-permute-start(bf16[192,192]{1,0:T(8,128)(2,1)S(1)} %get-tuple-element.94), channel_id=1, source_target_pairs={{0,3},{1,0},{2,1},{3,2},{4,7},{5,4},{6,5},{7,6},{8,11},{9,8},{10,9... | collective-permute-start | bytes 221192 | tf_op jit(solution)/shard_map/ppermute | solution.py:320
  146.5 6.1 %collective-permute-done.15 = bf16[192,192]{1,0:T(8,128)(2,1)S(1)} collective-permute-done((bf16[192,192]{1,0:T(8,128)(2,1)S(1)}, bf16[192,192]{1,0:T(8,128)(2,1)S(1)}, u32[]{:S(2)}, u32[]{:S(2)}) %collective-permute-start.15) | collective-permute-done | bytes 73760 | tf_op jit(solution)/shard_map/ppermute | solution.py:320
  159.1 9.4 %collective-permute-done.34 = bf16[96,3072]{1,0:T(8,128)(2,1)S(1)} collective-permute-done((bf16[96,3072]{1,0:T(8,128)(2,1)S(1)}, bf16[96,3072]{1,0:T(8,128)(2,1)S(1)}, u32[]{:S(2)}, u32[]{:S(2)}) %collective-permute-start.34) | collective-permute-done | bytes 589856 | tf_op jit(solution)/shard_map/ppermute | solution.py:315
  172.8 2.3 collective-permute-done.47
  175.1 3.3 collective-permute-done.48
  178.5 1.6 collective-permute-done.36
  180.1 2.1 collective-permute-done.37
  185.2 6.0 %fusion.74 = (f32[192]{0:T(256)S(1)}, f32[192,3072]{1,0:T(8,128)S(1)}, f32[192,3072]{1,0:T(8,128)S(1)}, f32[192,3072]{1,0:T(8,128)S(1)}) fusion(bf16[768,3072]{1,0:T(8,128)(2,1)S(1)} %bitcast.386, f32[192,768]{1,0:T(8,128)S(1)} %get-tuple-element.44, f32[768]{0:T(1024)S(1)} %copy-done.20, f32[192]{0:T(256)S(1)} %fusion.63, f32[192]{0:T(256)S(1)} %broadcast_multiply_fusion.3), kind=kOutput, calls=%fused_computation.313 | convolution fusion | flops 944897856 | bytes 12391680 | tf_op jit(solution)/shard_map/dot_general | solution.py:612
  191.3 2.0 multiply_reduce_fusion.2
  193.3 2.0 fusion.22
  196.6 1.9 add_convert_fusion
  198.5 1.9 multiply_reduce_fusion.5
  205.6 2.1 collective-permute-start.50
  208.4 2.1 collective-permute-start.52
  215.6 2.1 collective-permute-done.51
  217.8 7.0 %attend_back.1 = (bf16[768,576]{1,0:T(8,128)(2,1)S(1)}, f32[3,1536]{1,0:T(4,128)S(1)}, f32[768,3]{1,0:T(8,128)S(1)}) custom-call(bf16[768,576]{1,0:T(8,128)(2,1)S(1)} %multiply_convert_fusion.3.qkv_ref, bf16[3,768,768]{2,1,0:T(8,128)(2,1)S(1)} %get-tuple-element.19.probs_ref, f32[768,192]{1,0:T(8,128)S(1)} %get-tuple-element.20.attention_ref, ...), custom_call_target="tpu_custom_call" | custom-call | flops 905969664 | bytes 3538944 | tf_op jit(solution)/shard_map/attend_back/pallas_call | solution.py:522
  227.6 1.9 convolution_convert_fusion.3
  229.5 1.7 copy.45
  242.7 2.3 collective-permute-done.73
  251.2 2.4 collective-permute-done.59
  254.7 1.9 collective-permute-start.104
  257.3 2.5 collective-permute-done.104
  265.8 1.7 collective-permute-start.53
  268.7 6.6 %collective-permute-done.55 = bf16[192,768]{1,0:T(8,128)(2,1)S(1)} collective-permute-done((bf16[192,768]{1,0:T(8,128)(2,1)}, bf16[192,768]{1,0:T(8,128)(2,1)S(1)}, u32[]{:S(2)}, u32[]{:S(2)}) %collective-permute-start.55) | collective-permute-done | bytes 294944 | tf_op jit(solution)/shard_map/ppermute | solution.py:320
  275.3 11.9 %collective-permute-done.54 = bf16[192,768]{1,0:T(8,128)(2,1)S(1)} collective-permute-done((bf16[192,768]{1,0:T(8,128)(2,1)}, bf16[192,768]{1,0:T(8,128)(2,1)S(1)}, u32[]{:S(2)}, u32[]{:S(2)}) %collective-permute-start.54) | collective-permute-done | bytes 294944 | tf_op jit(solution)/shard_map/ppermute | solution.py:320
  296.0 2.8 collective-permute-done.64
  299.4 2.1 collective-permute-start.77
  303.4 2.0 collective-permute-start.75
  307.5 1.8 collective-permute-done.75
  311.0 2.2 fusion.19
  315.5 1.8 fusion.15
  318.6 4.7 %collective-permute-done.84 = bf16[48,3072]{1,0:T(8,128)(2,1)S(1)} collective-permute-done((bf16[48,3072]{1,0:T(8,128)(2,1)S(1)}, bf16[48,3072]{1,0:T(8,128)(2,1)S(1)}, u32[]{:S(2)}, u32[]{:S(2)}) %collective-permute-start.84) | collective-permute-done | bytes 294944 | tf_op jit(solution)/shard_map/ppermute | solution.py:315
  325.7 3.1 collective-permute-done.95
  330.4 2.9 collective-permute-done.92
  335.5 10.4 %collective-permute-done.85 = bf16[96,3072]{1,0:T(8,128)(2,1)S(1)} collective-permute-done((bf16[96,3072]{1,0:T(8,128)(2,1)S(1)}, bf16[96,3072]{1,0:T(8,128)(2,1)S(1)}, u32[]{:S(2)}, u32[]{:S(2)}) %collective-permute-start.85) | collective-permute-done | bytes 589856 | tf_op jit(solution)/shard_map/ppermute | solution.py:315
  347.3 2.1 collective-permute-start.88
  350.0 5.8 %collective-permute-done.96 = bf16[384,768]{1,0:T(8,128)(2,1)S(1)} collective-permute-done((bf16[384,768]{1,0:T(8,128)(2,1)S(1)}, bf16[384,768]{1,0:T(8,128)(2,1)S(1)}, u32[]{:S(2)}, u32[]{:S(2)}) %collective-permute-start.96) | collective-permute-done | bytes 589856 | tf_op jit(solution)/shard_map/ppermute | solution.py:315
  357.3 2.1 collective-permute-start.99
  360.8 2.9 collective-permute-done.99
  363.6 7.7 %collective-permute-done.98 = bf16[96,768]{1,0:T(8,128)(2,1)S(1)} collective-permute-done((bf16[96,768]{1,0:T(8,128)(2,1)S(1)}, bf16[96,768]{1,0:T(8,128)(2,1)S(1)}, u32[]{:S(2)}, u32[]{:S(2)}) %collective-permute-start.98) | collective-permute-done | bytes 147488 | tf_op jit(solution)/shard_map/ppermute | solution.py:320
  (456 shorter events, 126.8 us)
Async XLA Ops:
  0.7 36.2 %collective-permute-start.17 = (bf16[24,768]{1,0:T(8,128)(2,1)}, bf16[24,768]{1,0:T(8,128)(2,1)}, u32[]{:S(2)}, u32[]{:S(2)}) collective-permute-start(bf16[24,768]{1,0:T(8,128)(2,1)} %param.18), channel_id=1, source_target_pairs={{0,1},{1,2},{2,3},{3,0},{4,5},{5,6},{6,7},{7,4},{8,9},{9,10},{10,1... | collective-permute-start | bytes 110600 | tf_op jit(solution)/shard_map/ppermute | solution.py:320
  3.8 34.0 %collective-permute-start.18 = (bf16[24,768]{1,0:T(8,128)(2,1)}, bf16[24,768]{1,0:T(8,128)(2,1)}, u32[]{:S(2)}, u32[]{:S(2)}) collective-permute-start(bf16[24,768]{1,0:T(8,128)(2,1)} %param.18), channel_id=1, source_target_pairs={{0,2},{1,3},{2,0},{3,1},{4,6},{5,7},{6,4},{7,5},{8,10},{9,11},{10,... | collective-permute-start | bytes 110600 | tf_op jit(solution)/shard_map/ppermute | solution.py:320
  6.3 33.7 %collective-permute-start.19 = (bf16[24,768]{1,0:T(8,128)(2,1)}, bf16[24,768]{1,0:T(8,128)(2,1)}, u32[]{:S(2)}, u32[]{:S(2)}) collective-permute-start(bf16[24,768]{1,0:T(8,128)(2,1)} %param.18), channel_id=1, source_target_pairs={{0,3},{1,0},{2,1},{3,2},{4,7},{5,4},{6,5},{7,6},{8,11},{9,8},{10,9... | collective-permute-start | bytes 110600 | tf_op jit(solution)/shard_map/ppermute | solution.py:320
  7.7 113.1 %collective-permute-start = (bf16[192,768]{1,0:T(8,128)(2,1)}, bf16[192,768]{1,0:T(8,128)(2,1)}, u32[]{:S(2)}, u32[]{:S(2)}) collective-permute-start(bf16[192,768]{1,0:T(8,128)(2,1)} %bitcast.388), channel_id=1, source_target_pairs={{0,1},{1,2},{2,3},{3,0},{4,5},{5,6},{6,7},{7,4},{8,9},{9,10},{10,1... | collective-permute-start | bytes 884744 | tf_op jit(solution)/shard_map/ppermute | solution.py:320
  10.4 13.3 %collective-permute-start.3 = (bf16[24,576]{1,0:T(8,128)(2,1)}, bf16[24,576]{1,0:T(8,128)(2,1)}, u32[]{:S(2)}, u32[]{:S(2)}) collective-permute-start(bf16[24,576]{1,0:T(8,128)(2,1)} %get-tuple-element.113), channel_id=1, source_target_pairs={{0,1},{1,2},{2,3},{3,0},{4,5},{5,6},{6,7},{7,4},{8,9},{9,10},{10,1... | collective-permute-start | bytes 82952 | tf_op jit(solution)/shard_map/ppermute | solution.py:320
  34.4 87.5 %collective-permute-start.1 = (bf16[192,768]{1,0:T(8,128)(2,1)S(1)}, bf16[192,768]{1,0:T(8,128)(2,1)S(1)}, u32[]{:S(2)}, u32[]{:S(2)}) collective-permute-start(bf16[192,768]{1,0:T(8,128)(2,1)S(1)} %bitcast.389), channel_id=1, source_target_pairs={{0,2},{1,3},{2,0},{3,1},{4,6},{5,7},{6,4},{7,5},{8,10},{9,11},{10,... | collective-permute-start | bytes 884744 | tf_op jit(solution)/shard_map/ppermute | solution.py:320
  36.9 11.2 %collective-permute-start.6 = (bf16[96,576]{1,0:T(8,128)(2,1)S(1)}, bf16[96,576]{1,0:T(8,128)(2,1)S(1)}, u32[]{:S(2)}, u32[]{:S(2)}) collective-permute-start(bf16[96,576]{1,0:T(8,128)(2,1)S(1)} %bitcast.427), channel_id=1, source_target_pairs={{0,4},{4,0},{8,12},{12,8},{16,20},{20,16},{24,28},{28,24},{1,5},{5... | collective-permute-start | bytes 331784 | tf_op jit(solution)/shard_map/ppermute | solution.py:315
  37.8 9.7 %collective-permute-start.7 = (bf16[96,576]{1,0:T(8,128)(2,1)S(1)}, bf16[96,576]{1,0:T(8,128)(2,1)S(1)}, u32[]{:S(2)}, u32[]{:S(2)}) collective-permute-start(bf16[96,576]{1,0:T(8,128)(2,1)S(1)} %bitcast.428), channel_id=1, source_target_pairs={{0,8},{4,12},{8,0},{12,4},{16,24},{20,28},{24,16},{28,20},{1,9},{5... | collective-permute-start | bytes 331784 | tf_op jit(solution)/shard_map/ppermute | solution.py:315
  45.5 77.0 %collective-permute-start.2 = (bf16[192,768]{1,0:T(8,128)(2,1)S(1)}, bf16[192,768]{1,0:T(8,128)(2,1)S(1)}, u32[]{:S(2)}, u32[]{:S(2)}) collective-permute-start(bf16[192,768]{1,0:T(8,128)(2,1)S(1)} %bitcast.390), channel_id=1, source_target_pairs={{0,3},{1,0},{2,1},{3,2},{4,7},{5,4},{6,5},{7,6},{8,11},{9,8},{10,9... | collective-permute-start | bytes 884744 | tf_op jit(solution)/shard_map/ppermute | solution.py:320
  47.5 30.2 %collective-permute-start.39 = (bf16[96,768]{1,0:T(8,128)(2,1)S(1)}, bf16[96,768]{1,0:T(8,128)(2,1)S(1)}, u32[]{:S(2)}, u32[]{:S(2)}) collective-permute-start(bf16[96,768]{1,0:T(8,128)(2,1)S(1)} %copy-done.18), channel_id=1, source_target_pairs={{0,1},{1,2},{2,3},{3,0},{4,5},{5,6},{6,7},{7,4},{8,9},{9,10},{10,1... | collective-permute-start | bytes 442376 | tf_op jit(solution)/shard_map/ppermute | solution.py:320
  48.1 12.4 %collective-permute-start.28 = (bf16[24,3072]{1,0:T(8,128)(2,1)S(1)}, bf16[24,3072]{1,0:T(8,128)(2,1)S(1)}, u32[]{:S(2)}, u32[]{:S(2)}) collective-permute-start(bf16[24,3072]{1,0:T(8,128)(2,1)S(1)} %copy-done.16), channel_id=1, source_target_pairs={{0,1},{1,2},{2,3},{3,0},{4,5},{5,6},{6,7},{7,4},{8,9},{9,10},{10,1... | collective-permute-start | bytes 442376 | tf_op jit(solution)/shard_map/ppermute | solution.py:320
  60.5 9.7 %collective-permute-start.29 = (bf16[24,3072]{1,0:T(8,128)(2,1)S(1)}, bf16[24,3072]{1,0:T(8,128)(2,1)S(1)}, u32[]{:S(2)}, u32[]{:S(2)}) collective-permute-start(bf16[24,3072]{1,0:T(8,128)(2,1)S(1)} %copy-done.16), channel_id=1, source_target_pairs={{0,2},{1,3},{2,0},{3,1},{4,6},{5,7},{6,4},{7,5},{8,10},{9,11},{10,... | collective-permute-start | bytes 442376 | tf_op jit(solution)/shard_map/ppermute | solution.py:320
  75.8 9.7 %collective-permute-start.40 = (bf16[96,768]{1,0:T(8,128)(2,1)S(1)}, bf16[96,768]{1,0:T(8,128)(2,1)S(1)}, u32[]{:S(2)}, u32[]{:S(2)}) collective-permute-start(bf16[96,768]{1,0:T(8,128)(2,1)S(1)} %copy-done.18), channel_id=1, source_target_pairs={{0,2},{1,3},{2,0},{3,1},{4,6},{5,7},{6,4},{7,5},{8,10},{9,11},{10,... | collective-permute-start | bytes 442376 | tf_op jit(solution)/shard_map/ppermute | solution.py:320
  77.7 7.8 %collective-permute-start.41 = (bf16[96,768]{1,0:T(8,128)(2,1)S(1)}, bf16[96,768]{1,0:T(8,128)(2,1)S(1)}, u32[]{:S(2)}, u32[]{:S(2)}) collective-permute-start(bf16[96,768]{1,0:T(8,128)(2,1)S(1)} %copy-done.18), channel_id=1, source_target_pairs={{0,3},{1,0},{2,1},{3,2},{4,7},{5,4},{6,5},{7,6},{8,11},{9,8},{10,9... | collective-permute-start | bytes 442376 | tf_op jit(solution)/shard_map/ppermute | solution.py:320
  97.8 59.5 %collective-permute-start.43 = (bf16[384,768]{1,0:T(8,128)(2,1)S(1)}, bf16[384,768]{1,0:T(8,128)(2,1)}, u32[]{:S(2)}, u32[]{:S(2)}) collective-permute-start(bf16[384,768]{1,0:T(8,128)(2,1)S(1)} %bitcast.396), channel_id=1, source_target_pairs={{0,8},{4,12},{8,0},{12,4},{16,24},{20,28},{24,16},{28,20},{1,9},{5... | collective-permute-start | bytes 1769480 | tf_op jit(solution)/shard_map/ppermute | solution.py:315
  99.0 15.9 %collective-permute-start.25 = (bf16[48,768]{1,0:T(8,128)(2,1)S(1)}, bf16[48,768]{1,0:T(8,128)(2,1)S(1)}, u32[]{:S(2)}, u32[]{:S(2)}) collective-permute-start(bf16[48,768]{1,0:T(8,128)(2,1)S(1)} %slice.188), channel_id=1, source_target_pairs={{0,8},{4,12},{8,0},{12,4},{16,24},{20,28},{24,16},{28,20},{1,9},{5... | collective-permute-start | bytes 221192 | tf_op jit(solution)/shard_map/ppermute | solution.py:315
  119.3 37.0 %collective-permute-start.45 = (bf16[384,768]{1,0:T(8,128)(2,1)S(1)}, bf16[384,768]{1,0:T(8,128)(2,1)}, u32[]{:S(2)}, u32[]{:S(2)}) collective-permute-start(bf16[384,768]{1,0:T(8,128)(2,1)S(1)} %bitcast.397), channel_id=1, source_target_pairs={{0,16},{4,20},{8,24},{12,28},{16,0},{20,4},{24,8},{28,12},{1,17},{... | collective-permute-start | bytes 1769480 | tf_op jit(solution)/shard_map/ppermute | solution.py:315
  120.8 18.2 %collective-permute-start.22 = (bf16[96,768]{1,0:T(8,128)(2,1)S(1)}, bf16[96,768]{1,0:T(8,128)(2,1)}, u32[]{:S(2)}, u32[]{:S(2)}) collective-permute-start(bf16[96,768]{1,0:T(8,128)(2,1)S(1)} %collective-permute-done.21), channel_id=1, source_target_pairs={{0,4},{4,0},{8,12},{12,8},{16,20},{20,16},{24,28},{28,24},{1,5},{5... | collective-permute-start | bytes 442376 | tf_op jit(solution)/shard_map/ppermute | solution.py:315
  121.9 22.3 %collective-permute-start.24 = (bf16[96,768]{1,0:T(8,128)(2,1)S(1)}, bf16[96,768]{1,0:T(8,128)(2,1)}, u32[]{:S(2)}, u32[]{:S(2)}) collective-permute-start(bf16[96,768]{1,0:T(8,128)(2,1)S(1)} %collective-permute-done.23), channel_id=1, source_target_pairs={{0,4},{4,0},{8,12},{12,8},{16,20},{20,16},{24,28},{28,24},{1,5},{5... | collective-permute-start | bytes 442376 | tf_op jit(solution)/shard_map/ppermute | solution.py:315
  126.3 19.0 %collective-permute-start.27 = (bf16[96,768]{1,0:T(8,128)(2,1)S(1)}, bf16[96,768]{1,0:T(8,128)(2,1)S(1)}, u32[]{:S(2)}, u32[]{:S(2)}) collective-permute-start(bf16[96,768]{1,0:T(8,128)(2,1)S(1)} %constant_dynamic-update-slice_fusion.7), channel_id=1, source_target_pairs={{0,4},{4,0},{8,12},{12,8},{16,20},{20,16},{24,28},{28,24},{1,5},{5... | collective-permute-start | bytes 442376 | tf_op jit(solution)/shard_map/ppermute | solution.py:315
  139.0 7.4 %collective-permute-start.16 = (bf16[192,192]{1,0:T(8,128)(2,1)S(1)}, bf16[192,192]{1,0:T(8,128)(2,1)S(1)}, u32[]{:S(2)}, u32[]{:S(2)}) collective-permute-start(bf16[192,192]{1,0:T(8,128)(2,1)S(1)} %get-tuple-element.94), channel_id=1, source_target_pairs={{0,3},{1,0},{2,1},{3,2},{4,7},{5,4},{6,5},{7,6},{8,11},{9,8},{10,9... | collective-permute-start | bytes 221192 | tf_op jit(solution)/shard_map/ppermute | solution.py:320
  144.2 8.3 %collective-permute-start.15 = (bf16[192,192]{1,0:T(8,128)(2,1)S(1)}, bf16[192,192]{1,0:T(8,128)(2,1)S(1)}, u32[]{:S(2)}, u32[]{:S(2)}) collective-permute-start(bf16[192,192]{1,0:T(8,128)(2,1)S(1)} %get-tuple-element.95), channel_id=1, source_target_pairs={{0,2},{1,3},{2,0},{3,1},{4,6},{5,7},{6,4},{7,5},{8,10},{9,11},{10,... | collective-permute-start | bytes 221192 | tf_op jit(solution)/shard_map/ppermute | solution.py:320
  145.3 8.6 %collective-permute-start.14 = (bf16[192,192]{1,0:T(8,128)(2,1)S(1)}, bf16[192,192]{1,0:T(8,128)(2,1)S(1)}, u32[]{:S(2)}, u32[]{:S(2)}) collective-permute-start(bf16[192,192]{1,0:T(8,128)(2,1)S(1)} %get-tuple-element.96), channel_id=1, source_target_pairs={{0,1},{1,2},{2,3},{3,0},{4,5},{5,6},{6,7},{7,4},{8,9},{9,10},{10,1... | collective-permute-start | bytes 221192 | tf_op jit(solution)/shard_map/ppermute | solution.py:320
  146.5 23.7 %collective-permute-start.31 = (bf16[96,3072]{1,0:T(8,128)(2,1)S(1)}, bf16[96,3072]{1,0:T(8,128)(2,1)S(1)}, u32[]{:S(2)}, u32[]{:S(2)}) collective-permute-start(bf16[96,3072]{1,0:T(8,128)(2,1)S(1)} %bitcast.400), channel_id=1, source_target_pairs={{0,4},{4,0},{8,12},{12,8},{16,20},{20,16},{24,28},{28,24},{1,5},{5... | collective-permute-start | bytes 1769480 | tf_op jit(solution)/shard_map/ppermute | solution.py:315
  152.6 16.5 %collective-permute-start.32 = (bf16[96,3072]{1,0:T(8,128)(2,1)S(1)}, bf16[96,3072]{1,0:T(8,128)(2,1)S(1)}, u32[]{:S(2)}, u32[]{:S(2)}) collective-permute-start(bf16[96,3072]{1,0:T(8,128)(2,1)S(1)} %bitcast.401), channel_id=1, source_target_pairs={{0,8},{4,12},{8,0},{12,4},{16,24},{20,28},{24,16},{28,20},{1,9},{5... | collective-permute-start | bytes 1769480 | tf_op jit(solution)/shard_map/ppermute | solution.py:315
  153.9 14.6 %collective-permute-start.34 = (bf16[96,3072]{1,0:T(8,128)(2,1)S(1)}, bf16[96,3072]{1,0:T(8,128)(2,1)S(1)}, u32[]{:S(2)}, u32[]{:S(2)}) collective-permute-start(bf16[96,3072]{1,0:T(8,128)(2,1)S(1)} %bitcast.402), channel_id=1, source_target_pairs={{0,16},{4,20},{8,24},{12,28},{16,0},{20,4},{24,8},{28,12},{1,17},{... | collective-permute-start | bytes 1769480 | tf_op jit(solution)/shard_map/ppermute | solution.py:315
  156.3 15.2 %collective-permute-start.42 = (bf16[384,768]{1,0:T(8,128)(2,1)S(1)}, bf16[384,768]{1,0:T(8,128)(2,1)S(1)}, u32[]{:S(2)}, u32[]{:S(2)}) collective-permute-start(bf16[384,768]{1,0:T(8,128)(2,1)S(1)} %bitcast.398), channel_id=1, source_target_pairs={{0,4},{4,0},{8,12},{12,8},{16,20},{20,16},{24,28},{28,24},{1,5},{5... | collective-permute-start | bytes 1769480 | tf_op jit(solution)/shard_map/ppermute | solution.py:315
  157.3 17.8 %collective-permute-start.47 = (bf16[192,768]{1,0:T(8,128)(2,1)S(1)}, bf16[192,768]{1,0:T(8,128)(2,1)S(1)}, u32[]{:S(2)}, u32[]{:S(2)}) collective-permute-start(bf16[192,768]{1,0:T(8,128)(2,1)S(1)} %slice.192), channel_id=1, source_target_pairs={{0,8},{4,12},{8,0},{12,4},{16,24},{20,28},{24,16},{28,20},{1,9},{5... | collective-permute-start | bytes 884744 | tf_op jit(solution)/shard_map/ppermute | solution.py:315
  168.5 9.9 %collective-permute-start.48 = (bf16[192,768]{1,0:T(8,128)(2,1)S(1)}, bf16[192,768]{1,0:T(8,128)(2,1)S(1)}, u32[]{:S(2)}, u32[]{:S(2)}) collective-permute-start(bf16[192,768]{1,0:T(8,128)(2,1)S(1)} %slice.193), channel_id=1, source_target_pairs={{0,16},{4,20},{8,24},{12,28},{16,0},{20,4},{24,8},{28,12},{1,17},{... | collective-permute-start | bytes 884744 | tf_op jit(solution)/shard_map/ppermute | solution.py:315
  169.1 11.0 %collective-permute-start.36 = (bf16[48,3072]{1,0:T(8,128)(2,1)S(1)}, bf16[48,3072]{1,0:T(8,128)(2,1)S(1)}, u32[]{:S(2)}, u32[]{:S(2)}) collective-permute-start(bf16[48,3072]{1,0:T(8,128)(2,1)S(1)} %slice.190), channel_id=1, source_target_pairs={{0,8},{4,12},{8,0},{12,4},{16,24},{20,28},{24,16},{28,20},{1,9},{5... | collective-permute-start | bytes 884744 | tf_op jit(solution)/shard_map/ppermute | solution.py:315
  170.1 12.1 %collective-permute-start.37 = (bf16[48,3072]{1,0:T(8,128)(2,1)S(1)}, bf16[48,3072]{1,0:T(8,128)(2,1)S(1)}, u32[]{:S(2)}, u32[]{:S(2)}) collective-permute-start(bf16[48,3072]{1,0:T(8,128)(2,1)S(1)} %slice.191), channel_id=1, source_target_pairs={{0,16},{4,20},{8,24},{12,28},{16,0},{20,4},{24,8},{28,12},{1,17},{... | collective-permute-start | bytes 884744 | tf_op jit(solution)/shard_map/ppermute | solution.py:315
  171.6 10.7 %collective-permute-start.44 = (bf16[384,768]{1,0:T(8,128)(2,1)}, bf16[384,768]{1,0:T(8,128)(2,1)S(1)}, u32[]{:S(2)}, u32[]{:S(2)}) collective-permute-start(bf16[384,768]{1,0:T(8,128)(2,1)} %collective-permute-done.43), channel_id=1, source_target_pairs={{0,4},{4,0},{8,12},{12,8},{16,20},{20,16},{24,28},{28,24},{1,5},{5... | collective-permute-start | bytes 1769480 | tf_op jit(solution)/shard_map/ppermute | solution.py:315
  175.1 8.9 %collective-permute-start.46 = (bf16[384,768]{1,0:T(8,128)(2,1)}, bf16[384,768]{1,0:T(8,128)(2,1)S(1)}, u32[]{:S(2)}, u32[]{:S(2)}) collective-permute-start(bf16[384,768]{1,0:T(8,128)(2,1)} %collective-permute-done.45), channel_id=1, source_target_pairs={{0,4},{4,0},{8,12},{12,8},{16,20},{20,16},{24,28},{28,24},{1,5},{5... | collective-permute-start | bytes 1769480 | tf_op jit(solution)/shard_map/ppermute | solution.py:315
  182.3 9.0 %collective-permute-start.49 = (bf16[384,768]{1,0:T(8,128)(2,1)S(1)}, bf16[384,768]{1,0:T(8,128)(2,1)S(1)}, u32[]{:S(2)}, u32[]{:S(2)}) collective-permute-start(bf16[384,768]{1,0:T(8,128)(2,1)S(1)} %constant_dynamic-update-slice_fusion.11), channel_id=1, source_target_pairs={{0,4},{4,0},{8,12},{12,8},{16,20},{20,16},{24,28},{28,24},{1,5},{5... | collective-permute-start | bytes 1769480 | tf_op jit(solution)/shard_map/ppermute | solution.py:315
  205.6 10.0 %collective-permute-start.50 = (bf16[192,192]{1,0:T(8,128)(2,1)S(1)}, bf16[192,192]{1,0:T(8,128)(2,1)S(1)}, u32[]{:S(2)}, u32[]{:S(2)}) collective-permute-start(bf16[192,192]{1,0:T(8,128)(2,1)S(1)} %get-tuple-element.99), channel_id=1, source_target_pairs={{0,3},{1,0},{2,1},{3,2},{4,7},{5,4},{6,5},{7,6},{8,11},{9,8},{10,9... | collective-permute-start | bytes 221192 | tf_op jit(solution)/shard_map/ppermute | solution.py:320
  207.8 10.0 %collective-permute-start.51 = (bf16[192,192]{1,0:T(8,128)(2,1)S(1)}, bf16[192,192]{1,0:T(8,128)(2,1)S(1)}, u32[]{:S(2)}, u32[]{:S(2)}) collective-permute-start(bf16[192,192]{1,0:T(8,128)(2,1)S(1)} %get-tuple-element.98), channel_id=1, source_target_pairs={{0,2},{1,3},{2,0},{3,1},{4,6},{5,7},{6,4},{7,5},{8,10},{9,11},{10,... | collective-permute-start | bytes 221192 | tf_op jit(solution)/shard_map/ppermute | solution.py:320
  208.4 9.4 %collective-permute-start.52 = (bf16[192,192]{1,0:T(8,128)(2,1)S(1)}, bf16[192,192]{1,0:T(8,128)(2,1)S(1)}, u32[]{:S(2)}, u32[]{:S(2)}) collective-permute-start(bf16[192,192]{1,0:T(8,128)(2,1)S(1)} %get-tuple-element.97), channel_id=1, source_target_pairs={{0,1},{1,2},{2,3},{3,0},{4,5},{5,6},{6,7},{7,4},{8,9},{9,10},{10,1... | collective-permute-start | bytes 221192 | tf_op jit(solution)/shard_map/ppermute | solution.py:320
  212.1 23.3 %collective-permute-start.68 = (bf16[96,768]{1,0:T(8,128)(2,1)}, bf16[96,768]{1,0:T(8,128)(2,1)}, u32[]{:S(2)}, u32[]{:S(2)}) collective-permute-start(bf16[96,768]{1,0:T(8,128)(2,1)} %get-tuple-element.65), channel_id=1, source_target_pairs={{0,4},{4,0},{8,12},{12,8},{16,20},{20,16},{24,28},{28,24},{1,5},{5... | collective-permute-start | bytes 442376 | tf_op jit(solution)/shard_map/ppermute | solution.py:315
  212.1 23.5 %collective-permute-start.72 = (bf16[96,768]{1,0:T(8,128)(2,1)}, bf16[96,768]{1,0:T(8,128)(2,1)}, u32[]{:S(2)}, u32[]{:S(2)}) collective-permute-start(bf16[96,768]{1,0:T(8,128)(2,1)} %get-tuple-element.63), channel_id=1, source_target_pairs={{0,4},{4,0},{8,12},{12,8},{16,20},{20,16},{24,28},{28,24},{1,5},{5... | collective-permute-start | bytes 442376 | tf_op jit(solution)/shard_map/ppermute | solution.py:315
  215.6 20.4 %collective-permute-start.69 = (bf16[96,768]{1,0:T(8,128)(2,1)}, bf16[96,768]{1,0:T(8,128)(2,1)}, u32[]{:S(2)}, u32[]{:S(2)}) collective-permute-start(bf16[96,768]{1,0:T(8,128)(2,1)} %get-tuple-element.64), channel_id=1, source_target_pairs={{0,4},{4,0},{8,12},{12,8},{16,20},{20,16},{24,28},{28,24},{1,5},{5... | collective-permute-start | bytes 442376 | tf_op jit(solution)/shard_map/ppermute | solution.py:315
  217.8 75.1 %collective-permute-start.67 = (bf16[96,768]{1,0:T(8,128)(2,1)S(1)}, bf16[96,768]{1,0:T(8,128)(2,1)}, u32[]{:S(2)}, u32[]{:S(2)}) collective-permute-start(bf16[96,768]{1,0:T(8,128)(2,1)S(1)} %get-tuple-element.62), channel_id=1, source_target_pairs={{0,4},{4,0},{8,12},{12,8},{16,20},{20,16},{24,28},{28,24},{1,5},{5... | collective-permute-start | bytes 442376 | tf_op jit(solution)/shard_map/ppermute | solution.py:315
  235.0 75.0 %collective-permute-start.79 = (bf16[96,3072]{1,0:T(8,128)(2,1)}, bf16[96,3072]{1,0:T(8,128)(2,1)S(1)}, u32[]{:S(2)}, u32[]{:S(2)}) collective-permute-start(bf16[96,3072]{1,0:T(8,128)(2,1)} %get-tuple-element.55), channel_id=1, source_target_pairs={{0,4},{4,0},{8,12},{12,8},{16,20},{20,16},{24,28},{28,24},{1,5},{5... | collective-permute-start | bytes 1769480 | tf_op jit(solution)/shard_map/ppermute | solution.py:315
  240.1 23.5 %collective-permute-start.56 = (bf16[96,576]{1,0:T(8,128)(2,1)S(1)}, bf16[96,576]{1,0:T(8,128)(2,1)}, u32[]{:S(2)}, u32[]{:S(2)}) collective-permute-start(bf16[96,576]{1,0:T(8,128)(2,1)S(1)} %get-tuple-element.76), channel_id=1, source_target_pairs={{0,4},{4,0},{8,12},{12,8},{16,20},{20,16},{24,28},{28,24},{1,5},{5... | collective-permute-start | bytes 331784 | tf_op jit(solution)/shard_map/ppermute | solution.py:315
  253.7 10.5 %collective-permute-start.63 = (bf16[96,576]{1,0:T(8,128)(2,1)}, bf16[96,576]{1,0:T(8,128)(2,1)}, u32[]{:S(2)}, u32[]{:S(2)}) collective-permute-start(bf16[96,576]{1,0:T(8,128)(2,1)} %pad_maximum_fusion.11), channel_id=1, source_target_pairs={{0,16},{4,20},{8,24},{12,28},{16,0},{20,4},{24,8},{28,12},{1,17},{... | collective-permute-start | bytes 331784 | tf_op jit(solution)/shard_map/ppermute | solution.py:315
  263.6 11.7 %collective-permute-start.55 = (bf16[192,768]{1,0:T(8,128)(2,1)}, bf16[192,768]{1,0:T(8,128)(2,1)S(1)}, u32[]{:S(2)}, u32[]{:S(2)}) collective-permute-start(bf16[192,768]{1,0:T(8,128)(2,1)} %get-tuple-element.70), channel_id=1, source_target_pairs={{0,3},{1,0},{2,1},{3,2},{4,7},{5,4},{6,5},{7,6},{8,11},{9,8},{10,9... | collective-permute-start | bytes 884744 | tf_op jit(solution)/shard_map/ppermute | solution.py:320
  264.1 23.0 %collective-permute-start.54 = (bf16[192,768]{1,0:T(8,128)(2,1)}, bf16[192,768]{1,0:T(8,128)(2,1)S(1)}, u32[]{:S(2)}, u32[]{:S(2)}) collective-permute-start(bf16[192,768]{1,0:T(8,128)(2,1)} %get-tuple-element.71), channel_id=1, source_target_pairs={{0,2},{1,3},{2,0},{3,1},{4,6},{5,7},{6,4},{7,5},{8,10},{9,11},{10,... | collective-permute-start | bytes 884744 | tf_op jit(solution)/shard_map/ppermute | solution.py:320
  265.8 22.9 %collective-permute-start.53 = (bf16[192,768]{1,0:T(8,128)(2,1)S(1)}, bf16[192,768]{1,0:T(8,128)(2,1)S(1)}, u32[]{:S(2)}, u32[]{:S(2)}) collective-permute-start(bf16[192,768]{1,0:T(8,128)(2,1)S(1)} %get-tuple-element.69), channel_id=1, source_target_pairs={{0,1},{1,2},{2,3},{3,0},{4,5},{5,6},{6,7},{7,4},{8,9},{9,10},{10,1... | collective-permute-start | bytes 884744 | tf_op jit(solution)/shard_map/ppermute | solution.py:320
  275.3 35.2 %collective-permute-start.83 = (bf16[96,3072]{1,0:T(8,128)(2,1)}, bf16[96,3072]{1,0:T(8,128)(2,1)}, u32[]{:S(2)}, u32[]{:S(2)}) collective-permute-start(bf16[96,3072]{1,0:T(8,128)(2,1)} %get-tuple-element.53), channel_id=1, source_target_pairs={{0,4},{4,0},{8,12},{12,8},{16,20},{20,16},{24,28},{28,24},{1,5},{5... | collective-permute-start | bytes 1769480 | tf_op jit(solution)/shard_map/ppermute | solution.py:315
  292.9 17.7 %collective-permute-start.80 = (bf16[96,3072]{1,0:T(8,128)(2,1)}, bf16[96,3072]{1,0:T(8,128)(2,1)S(1)}, u32[]{:S(2)}, u32[]{:S(2)}) collective-permute-start(bf16[96,3072]{1,0:T(8,128)(2,1)} %get-tuple-element.54), channel_id=1, source_target_pairs={{0,4},{4,0},{8,12},{12,8},{16,20},{20,16},{24,28},{28,24},{1,5},{5... | collective-permute-start | bytes 1769480 | tf_op jit(solution)/shard_map/ppermute | solution.py:315
  307.5 26.9 %collective-permute-start.78 = (bf16[96,3072]{1,0:T(8,128)(2,1)}, bf16[96,3072]{1,0:T(8,128)(2,1)S(1)}, u32[]{:S(2)}, u32[]{:S(2)}) collective-permute-start(bf16[96,3072]{1,0:T(8,128)(2,1)} %get-tuple-element.52), channel_id=1, source_target_pairs={{0,4},{4,0},{8,12},{12,8},{16,20},{20,16},{24,28},{28,24},{1,5},{5... | collective-permute-start | bytes 1769480 | tf_op jit(solution)/shard_map/ppermute | solution.py:315
  310.6 38.8 %collective-permute-start.89 = (bf16[384,768]{1,0:T(8,128)(2,1)}, bf16[384,768]{1,0:T(8,128)(2,1)S(1)}, u32[]{:S(2)}, u32[]{:S(2)}) collective-permute-start(bf16[384,768]{1,0:T(8,128)(2,1)} %get-tuple-element.45), channel_id=1, source_target_pairs={{0,4},{4,0},{8,12},{12,8},{16,20},{20,16},{24,28},{28,24},{1,5},{5... | collective-permute-start | bytes 1769480 | tf_op jit(solution)/shard_map/ppermute | solution.py:315
  313.4 9.9 %collective-permute-start.84 = (bf16[48,3072]{1,0:T(8,128)(2,1)S(1)}, bf16[48,3072]{1,0:T(8,128)(2,1)S(1)}, u32[]{:S(2)}, u32[]{:S(2)}) collective-permute-start(bf16[48,3072]{1,0:T(8,128)(2,1)S(1)} %get-tuple-element.92), channel_id=1, source_target_pairs={{0,8},{4,12},{8,0},{12,4},{16,24},{20,28},{24,16},{28,20},{1,9},{5... | collective-permute-start | bytes 884744 | tf_op jit(solution)/shard_map/ppermute | solution.py:315
  315.0 9.5 %collective-permute-start.81 = (bf16[48,3072]{1,0:T(8,128)(2,1)S(1)}, bf16[48,3072]{1,0:T(8,128)(2,1)S(1)}, u32[]{:S(2)}, u32[]{:S(2)}) collective-permute-start(bf16[48,3072]{1,0:T(8,128)(2,1)S(1)} %get-tuple-element.91), channel_id=1, source_target_pairs={{0,16},{4,20},{8,24},{12,28},{16,0},{20,4},{24,8},{28,12},{1,17},{... | collective-permute-start | bytes 884744 | tf_op jit(solution)/shard_map/ppermute | solution.py:315
  317.4 11.3 %collective-permute-start.95 = (bf16[192,768]{1,0:T(8,128)(2,1)S(1)}, bf16[192,768]{1,0:T(8,128)(2,1)S(1)}, u32[]{:S(2)}, u32[]{:S(2)}) collective-permute-start(bf16[192,768]{1,0:T(8,128)(2,1)S(1)} %get-tuple-element.87), channel_id=1, source_target_pairs={{0,8},{4,12},{8,0},{12,4},{16,24},{20,28},{24,16},{28,20},{1,9},{5... | collective-permute-start | bytes 884744 | tf_op jit(solution)/shard_map/ppermute | solution.py:315
  323.3 9.9 %collective-permute-start.92 = (bf16[192,768]{1,0:T(8,128)(2,1)S(1)}, bf16[192,768]{1,0:T(8,128)(2,1)S(1)}, u32[]{:S(2)}, u32[]{:S(2)}) collective-permute-start(bf16[192,768]{1,0:T(8,128)(2,1)S(1)} %get-tuple-element.86), channel_id=1, source_target_pairs={{0,16},{4,20},{8,24},{12,28},{16,0},{20,4},{24,8},{28,12},{1,17},{... | collective-permute-start | bytes 884744 | tf_op jit(solution)/shard_map/ppermute | solution.py:315
  324.5 21.4 %collective-permute-start.85 = (bf16[96,3072]{1,0:T(8,128)(2,1)S(1)}, bf16[96,3072]{1,0:T(8,128)(2,1)S(1)}, u32[]{:S(2)}, u32[]{:S(2)}) collective-permute-start(bf16[96,3072]{1,0:T(8,128)(2,1)S(1)} %pad_maximum_fusion.2), channel_id=1, source_target_pairs={{0,16},{4,20},{8,24},{12,28},{16,0},{20,4},{24,8},{28,12},{1,17},{... | collective-permute-start | bytes 1769480 | tf_op jit(solution)/shard_map/ppermute | solution.py:315
  328.7 17.2 %collective-permute-start.82 = (bf16[96,3072]{1,0:T(8,128)(2,1)S(1)}, bf16[96,3072]{1,0:T(8,128)(2,1)S(1)}, u32[]{:S(2)}, u32[]{:S(2)}) collective-permute-start(bf16[96,3072]{1,0:T(8,128)(2,1)S(1)} %pad_maximum_fusion.1), channel_id=1, source_target_pairs={{0,8},{4,12},{8,0},{12,4},{16,24},{20,28},{24,16},{28,20},{1,9},{5... | collective-permute-start | bytes 1769480 | tf_op jit(solution)/shard_map/ppermute | solution.py:315
  333.3 22.6 %collective-permute-start.96 = (bf16[384,768]{1,0:T(8,128)(2,1)S(1)}, bf16[384,768]{1,0:T(8,128)(2,1)S(1)}, u32[]{:S(2)}, u32[]{:S(2)}) collective-permute-start(bf16[384,768]{1,0:T(8,128)(2,1)S(1)} %pad_maximum_fusion.4), channel_id=1, source_target_pairs={{0,16},{4,20},{8,24},{12,28},{16,0},{20,4},{24,8},{28,12},{1,17},{... | collective-permute-start | bytes 1769480 | tf_op jit(solution)/shard_map/ppermute | solution.py:315
  334.5 21.4 %collective-permute-start.93 = (bf16[384,768]{1,0:T(8,128)(2,1)S(1)}, bf16[384,768]{1,0:T(8,128)(2,1)S(1)}, u32[]{:S(2)}, u32[]{:S(2)}) collective-permute-start(bf16[384,768]{1,0:T(8,128)(2,1)S(1)} %pad_maximum_fusion.3), channel_id=1, source_target_pairs={{0,8},{4,12},{8,0},{12,4},{16,24},{20,28},{24,16},{28,20},{1,9},{5... | collective-permute-start | bytes 1769480 | tf_op jit(solution)/shard_map/ppermute | solution.py:315
  347.3 12.0 %collective-permute-start.88 = (bf16[24,3072]{1,0:T(8,128)(2,1)S(1)}, bf16[24,3072]{1,0:T(8,128)(2,1)S(1)}, u32[]{:S(2)}, u32[]{:S(2)}) collective-permute-start(bf16[24,3072]{1,0:T(8,128)(2,1)S(1)} %get-tuple-element.89), channel_id=1, source_target_pairs={{0,3},{1,0},{2,1},{3,2},{4,7},{5,4},{6,5},{7,6},{8,11},{9,8},{10,9... | collective-permute-start | bytes 442376 | tf_op jit(solution)/shard_map/ppermute | solution.py:320
  349.4 10.6 %collective-permute-start.87 = (bf16[24,3072]{1,0:T(8,128)(2,1)S(1)}, bf16[24,3072]{1,0:T(8,128)(2,1)S(1)}, u32[]{:S(2)}, u32[]{:S(2)}) collective-permute-start(bf16[24,3072]{1,0:T(8,128)(2,1)S(1)} %get-tuple-element.90), channel_id=1, source_target_pairs={{0,2},{1,3},{2,0},{3,1},{4,6},{5,7},{6,4},{7,5},{8,10},{9,11},{10,... | collective-permute-start | bytes 442376 | tf_op jit(solution)/shard_map/ppermute | solution.py:320
  349.4 10.6 %collective-permute-start.86 = (bf16[24,3072]{1,0:T(8,128)(2,1)S(1)}, bf16[24,3072]{1,0:T(8,128)(2,1)S(1)}, u32[]{:S(2)}, u32[]{:S(2)}) collective-permute-start(bf16[24,3072]{1,0:T(8,128)(2,1)S(1)} %get-tuple-element.88), channel_id=1, source_target_pairs={{0,1},{1,2},{2,3},{3,0},{4,5},{5,6},{6,7},{7,4},{8,9},{9,10},{10,1... | collective-permute-start | bytes 442376 | tf_op jit(solution)/shard_map/ppermute | solution.py:320
  359.3 12.0 %collective-permute-start.98 = (bf16[96,768]{1,0:T(8,128)(2,1)S(1)}, bf16[96,768]{1,0:T(8,128)(2,1)S(1)}, u32[]{:S(2)}, u32[]{:S(2)}) collective-permute-start(bf16[96,768]{1,0:T(8,128)(2,1)S(1)} %get-tuple-element.85), channel_id=1, source_target_pairs={{0,2},{1,3},{2,0},{3,1},{4,6},{5,7},{6,4},{7,5},{8,10},{9,11},{10,... | collective-permute-start | bytes 442376 | tf_op jit(solution)/shard_map/ppermute | solution.py:320
  359.3 12.0 %collective-permute-start.97 = (bf16[96,768]{1,0:T(8,128)(2,1)S(1)}, bf16[96,768]{1,0:T(8,128)(2,1)S(1)}, u32[]{:S(2)}, u32[]{:S(2)}) collective-permute-start(bf16[96,768]{1,0:T(8,128)(2,1)S(1)} %get-tuple-element.83), channel_id=1, source_target_pairs={{0,1},{1,2},{2,3},{3,0},{4,5},{5,6},{6,7},{7,4},{8,9},{9,10},{10,1... | collective-permute-start | bytes 442376 | tf_op jit(solution)/shard_map/ppermute | solution.py:320
  (81 other events, 747.3 us)

commit v2 on v1

--- a/solution.py
+++ b/solution.py
@@ -337,13 +337,23 @@
     return out
 
 
-def gather_line(value):
+def after(value, *others):
+    return lax.optimization_barrier((value, *others))[0]
+
+
+def all_after(values, *others):
+    return list(lax.optimization_barrier((*values, *others))[: len(values)])
+
+
+def turns(value):
+    size = lax.axis_size("blk")
+    return [value] + [turn(value, steps) for steps in range(1, size)]
+
+
+def in_line(pieces):
     here, size = lax.axis_index("blk"), lax.axis_size("blk")
-    blocks = [(here, value)]
-    for steps in range(1, size):
-        blocks.append((lax.rem(here - steps + size, size), turn(value, steps)))
-    out = place(blocks)
-    return out.reshape((size * value.shape[0],) + value.shape[1:])
+    ordered = [lax.select_n(lax.rem(here - owner + size, size), *pieces) for owner in range(size)]
+    return jnp.concatenate(ordered, axis=0)
 
 
 def deal_line(stack):
@@ -354,40 +364,57 @@
     return got
 
 
-def gather_planes(line):
+def swap_cores(blocks):
+    return [swap(block, core_bit) for block in blocks]
+
+
+def in_planes(blocks, others, cut):
     me = lax.axis_index("dp")
+    bits = (0, x_bit, y_bit, x_bit | y_bit)
+    both = [(me ^ bit, block) for bit, block in zip(bits, blocks)]
+    both += [(me ^ bit ^ core_bit, block) for bit, block in zip(bits, others)]
+    outs = []
+    for begin, end in cut:
+        out = place([(index, block[:, begin:end]) for index, block in both])
+        outs.append(out.reshape((-1, end - begin)))
+    return outs
+
+
+def beside(line):
+    return [line, swap(line, x_bit), swap(line, y_bit)]
+
+
+def across_plane(near):
+    line, along_x, along_y = near
     half = line.shape[0] // 2
-    along_x, along_y = swap(line, x_bit), swap(line, y_bit)
-    across = jnp.concatenate([swap(along_y[:half], x_bit), swap(along_x[half:], y_bit)], axis=0)
-    blocks = []
-    for bits, block in ((0, line), (x_bit, along_x), (y_bit, along_y), (x_bit | y_bit, across)):
-        blocks.append((me ^ bits, block))
-        blocks.append((me ^ bits ^ core_bit, swap(block, core_bit)))
-    out = place(blocks)
-    return out.reshape((-1,) + line.shape[1:])
-
-
-def gather_weight(shard):
-    return gather_planes(gather_line(shard))
+    across = [swap(along_y[:half], x_bit), swap(along_x[half:], y_bit)]
+    return [line, along_x, along_y, jnp.concatenate(across, axis=0)]
+
+
+def near_planes(line):
+    return beside(line) + [swap(line, x_bit | y_bit)]
 
 
 def add_low(left, right):
     return (left.astype(jnp.float32) + right.astype(jnp.float32)).astype(jnp.bfloat16)
 
 
-def scatter_planes(block_of):
+def add_cores(block_of):
     me = lax.axis_index("dp")
-
-    def with_core(bits):
-        other = swap(block_of(me ^ bits ^ core_bit), core_bit)
-        return add_low(block_of(me ^ bits), other)
-
-    across = with_core(x_bit | y_bit)
+    order = (x_bit | y_bit, x_bit, y_bit, 0)
+    got = swap_cores([block_of(me ^ bits ^ core_bit) for bits in order])
+    return [add_low(block_of(me ^ bits), term) for bits, term in zip(order, got)]
+
+
+def add_across(across, to_x, to_y):
     half = across.shape[0] // 2
     from_x, from_y = swap(across[:half], x_bit), swap(across[half:], y_bit)
-    to_x, to_y, own = with_core(x_bit), with_core(y_bit), with_core(0)
     to_y = jnp.concatenate([add_low(to_y[:half], from_x), to_y[half:]], axis=0)
     to_x = jnp.concatenate([to_x[:half], add_low(to_x[half:], from_y)], axis=0)
+    return to_x, to_y
+
+
+def add_planes(to_x, to_y, own):
     got_x, got_y = swap(to_x, x_bit), swap(to_y, y_bit)
     total = own.astype(jnp.float32) + got_x.astype(jnp.float32) + got_y.astype(jnp.float32)
     return total.astype(jnp.bfloat16)
@@ -400,9 +427,8 @@
     return total
 
 
-def scatter_weight(block_of):
+def add_line(line):
     size = lax.axis_size("blk")
-    line = scatter_planes(block_of)
     return sum_parts(deal_line(line.reshape((size, -1) + line.shape[1:])))
 
 
@@ -564,23 +590,31 @@
     bucket_count = bias_table.shape[0]
     shard_rows = w_qkv.shape[0]
 
-    row_tokens = gather_line(tokens[0])
+    hidden_width = w_fc1.shape[1]
+    summed = hidden_width + width
     by_head = w_qkv.reshape(shard_rows, 3, line_size, part).transpose(2, 0, 1, 3)
     by_head = by_head.reshape(line_size, shard_rows, 3 * part)
-    dealt = deal_line(by_head)
-    qkv_line = place(
-        [(lax.rem(here - steps + line_size, line_size), block) for steps, block in enumerate(dealt)]
-    ).reshape(line_size * shard_rows, 3 * part)
-    wqkv_part = gather_planes(qkv_line)
-    wout_all = gather_weight(w_out)
-    fc1_all = gather_weight(w_fc1)
-    fc2_all = gather_weight(w_fc2)
+    shared = jnp.broadcast_to(
+        jnp.concatenate([w_fc1, w_out], axis=1)[None], (line_size, shard_rows, summed)
+    )
+    first_pieces = deal_line(jnp.concatenate([shared, by_head], axis=2))
+    first_line = in_line(first_pieces)
+    row_tokens = lax.all_gather(after(tokens[0], *first_pieces[1:]), "blk", axis=0, tiled=True)
+    second_pieces = turns(after(w_fc2, first_line))
+    first_planes = across_plane(beside(first_line))
+    first_others = swap_cores(first_planes)
+    fc1_all, wout_all, wqkv_part = in_planes(
+        first_planes, first_others, [(0, hidden_width), (hidden_width, summed), (summed, summed + 3 * part)]
+    )
+    second_near = beside(after(in_line(second_pieces), *first_planes))
 
     ends = jnp.cumsum(lengths[0])
     positions = jnp.arange(row_len, dtype=jnp.int32)
     documents = jnp.sum((positions[:, None] >= ends[None, :]).astype(jnp.int32), axis=1)
-    relative = jnp.clip(jnp.arange(-row_len, row_len, dtype=jnp.int32), -reach, reach) + reach
-    buckets = jnp.take(distance_bucket, relative)
+    if row_len <= reach:
+        buckets = distance_bucket[reach - row_len : reach + row_len]
+    else:
+        buckets = jnp.pad(distance_bucket, row_len - reach, mode="edge")[: 2 * row_len]
     selector = (buckets[None, :] == jnp.arange(bucket_count, dtype=jnp.int32)[:, None]).astype(jnp.float32)
     head_table = lax.dynamic_slice_in_dim(bias_table.T, here * heads, heads, 0)
     diagonals = jnp.dot(head_table, selector, precision=highest)
@@ -601,7 +635,8 @@
             [pick(stack, lax.rem(here - steps + line_size, line_size)) for steps in range(line_size)], axis=0
         )
 
-    scaled = jnp.concatenate(deal_line(scaled_part.reshape(line_size, rows_here, part)), axis=1)
+    dealt = deal_line(scaled_part.reshape(line_size, rows_here, part))
+    scaled = jnp.concatenate(dealt, axis=1)
     wout_here = arrival(wout_all.reshape(line_size, part, width))
     residual_in = tokens[0].astype(jnp.float32)
     attn_out = jnp.dot(scaled, wout_here, preferred_element_type=jnp.float32)
@@ -610,6 +645,8 @@
     normed_mid_f, norm_mid_back = jax.vjp(layer_norm, middle, gain_ffn_in)
     normed_mid = normed_mid_f.astype(jnp.bfloat16)
     hidden = jnp.dot(normed_mid, fc1_all, preferred_element_type=jnp.float32)
+    second_planes = across_plane(all_after(second_near, *first_others))
+    (fc2_all,) = in_planes(second_planes, swap_cores(second_planes), [(0, width)])
     activated_f, hidden_back = jax.vjp(hidden_norm, hidden, gain_hidden)
     activated = activated_f.astype(jnp.bfloat16)
     mixed = (middle + jnp.dot(activated, fc2_all, preferred_element_type=jnp.float32)).astype(
@@ -621,11 +658,11 @@
         return lambda index: pick(stack, index)
 
     grad_in = cotangent[0]
-    grad_fc2 = scatter_weight(blocks_of(column_product(activated, grad_in)))
+    second = add_cores(blocks_of(column_product(activated, grad_in)))
     d_activated = times_transpose(grad_in, fc2_all)
     d_hidden_f, grad_gain_hidden = hidden_back(d_activated)
-    d_hidden = d_hidden_f.astype(jnp.bfloat16)
-    grad_fc1 = scatter_weight(blocks_of(column_product(normed_mid, d_hidden)))
+    d_hidden = after(d_hidden_f.astype(jnp.bfloat16), *second)
+    third = add_cores(blocks_of(column_product(normed_mid, d_hidden)))
     d_mid_part, grad_gain_ffn_in = norm_mid_back(times_transpose(d_hidden, fc1_all))
     d_middle = grad_in.astype(jnp.float32) + d_mid_part
     d_attn_f, grad_gain_attn = norm_attn_back(d_middle)
@@ -633,6 +670,7 @@
 
     scale_here = arrival(scale_cols.reshape(line_size, part))
     d_scaled = times_transpose(d_attn_out, wout_here)
+    second_x, second_y = add_across(*second[:3])
     d_attention = (d_scaled * scale_here).astype(jnp.bfloat16)
     pieces = [(here, d_attention[:, :part])]
     for steps in range(1, line_size):
@@ -648,20 +686,31 @@
         steps = lax.rem(here - owner + line_size, line_size)
         return out_grad(steps * per_part + lax.rem(index, per_part))
 
-    grad_out = scatter_weight(out_block)
-
+    second_x, second_y = all_after([second_x, second_y], d_attention)
+    second_line = add_planes(second_x, second_y, second[3])
     d_projected, diagonal_sums_here, deltas = attend_back(qkv, probs, attention, grad_row, heads, head_size)
     d_normed = times_transpose(d_projected, wqkv_part)
-    d_normed_low = d_normed.astype(jnp.bfloat16).reshape(line_size, rows_here, width)
-    d_normed_here = sum_parts(deal_line(d_normed_low))
-    qkv_line_grad = scatter_planes(blocks_of(column_product(normed_row, d_projected)))
-    qkv_dealt = deal_line(qkv_line_grad.reshape(line_size, shard_rows, 3 * part))
-    grad_qkv = place(
-        [
-            (lax.rem(here - steps + line_size, line_size), block.astype(jnp.float32))
-            for steps, block in enumerate(qkv_dealt)
-        ]
-    )
+    d_normed_low = lax.psum_scatter(
+        d_normed.astype(jnp.bfloat16), "blk", scatter_dimension=0, tiled=True
+    )
+    d_normed_here = d_normed_low.astype(jnp.float32)
+
+    qkv_grad = blocks_of(column_product(normed_row, d_projected))
+
+    def small_block(index):
+        return jnp.concatenate([out_block(index), qkv_grad(index)], axis=1)
+
+    fourth = add_cores(small_block)
+    first = [jnp.concatenate(pair, axis=1) for pair in zip(third, fourth)]
+    first[0] = after(first[0], second_line)
+    first_x, first_y = add_across(*first[:3])
+    grad_fc2 = add_line(after(second_line, d_projected))
+    first_x, first_y = all_after([first_x, first_y], d_normed_low)
+    first_line = add_planes(first_x, first_y, first[3])
+    dealt = deal_line(first_line.reshape((line_size, shard_rows) + first_line.shape[1:]))
+    first_grad = sum_parts([piece[:, :summed] for piece in dealt])
+    grad_fc1, grad_out = first_grad[:, :hidden_width], first_grad[:, hidden_width:]
+    grad_qkv = in_line([piece[:, summed:].astype(jnp.float32) for piece in dealt])
     grad_qkv = grad_qkv.reshape(line_size, shard_rows, 3, part).transpose(1, 2, 0, 3)
     grad_qkv = grad_qkv.reshape(shard_rows, 3 * width)
 
@@ -685,6 +734,7 @@
     sizes = [math.prod(value.shape) for value in small]
     flat = jnp.concatenate([value.reshape(-1) for value in small])
     flat = jnp.pad(flat, (0, -flat.shape[0] % 1024)).reshape(-1, lanes)
+    flat = after(flat, grad_fc2, first_x, first_y)
     flat = sum_everywhere(flat).reshape(-1)
     sums, begin = [], 0
     for value, size in zip(small, sizes):

time: 378 us -> 307 us (0.81)
  the two profiles are of different devices: /device:TPU:0 before, /device:TPU:18 now
where the time goes in v2:
time: 307 us; the launch traced here: 301 us
  waiting for transfers between devices  104 us (34%)
  local copies, waits for them, and re-layouts  53.8 us (18%)
  starting transfers between devices  45 us (15%)
  other arithmetic  34.2 us (11%)
  matrix products  33.1 us (11%)
  between operations  15.9 us (5%)
  Pallas kernels  15 us (5%)
    ppermute x18, waiting for transfers between devices, turn(): lax.ppermute(value, 'blk', [(i, (i + steps) % size) for i in range(size)])  48.5 us
    ppermute x39, waiting for transfers between devices, swap(): return lax.ppermute(value, 'dp', [(i, i ^ bit) for i in range(size)])  48.4 us
    dynamic_update_slice x36, local copies, waits for them, and re-layouts, place(): out = lax.dynamic_update_index_in_dim(out, block, index, 0)  26.4 us
    ppermute x39, starting transfers between devices, swap(): return lax.ppermute(value, 'dp', [(i, i ^ bit) for i in range(size)])  25.6 us
    ppermute x18, starting transfers between devices, turn(): lax.ppermute(value, 'blk', [(i, (i + steps) % size) for i in range(size)])  19 us
    dot_general x4, matrix products, times_transpose(): lax.dot_general(left, matrix, (((1,), (1,)), ((), ())), preferred_element...  10.5 us
    convert_element_type x10, other arithmetic, add_low(): (left.astype(jnp.float32) + right.astype(jnp.float32)).astype(jnp.bfloat16)  8.5 us
    pallas_call x1, Pallas kernels, attend(): pl.pallas_call(functools.partial(attend_kernel, heads, head_size), out_sh...  7.94 us
  transfers between devices with their start and end apart: 61, of which 26 were waited for; matrix products, arithmetic and copies ran while one was open for 31% of the time, Pallas kernels for 5%

profile of v2, /device:TPU:18, one launch (start us, length us, event | category | flops | bytes accessed | tf_op | source)
XLA Modules:
  0.0 301.0 jit_solution(15091923004340210704)
XLA Ops:
  10.1 2.7 collective-permute-start.2
  15.3 5.9 %collective-permute-done.1 = bf16[24,4416]{1,0:T(8,128)(2,1)S(1)} collective-permute-done((bf16[24,4416]{1,0:T(8,128)(2,1)S(1)}, bf16[24,4416]{1,0:T(8,128)(2,1)S(1)}, u32[]{:S(2)}, u32[]{:S(2)}) %collective-permute-start.1) | collective-permute-done | bytes 212000 | tf_op jit(solution)/shard_map/ppermute | solution.py:320
  21.2 7.4 %collective-permute-done.2 = bf16[24,4416]{1,0:T(8,128)(2,1)S(1)} collective-permute-done((bf16[24,4416]{1,0:T(8,128)(2,1)S(1)}, bf16[24,4416]{1,0:T(8,128)(2,1)S(1)}, u32[]{:S(2)}, u32[]{:S(2)}) %collective-permute-start.2) | collective-permute-done | bytes 212000 | tf_op jit(solution)/shard_map/ppermute | solution.py:320
  28.5 3.0 %collective-permute-done = bf16[24,4416]{1,0:T(8,128)(2,1)S(1)} collective-permute-done((bf16[24,4416]{1,0:T(8,128)(2,1)S(1)}, bf16[24,4416]{1,0:T(8,128)(2,1)S(1)}, u32[]{:S(2)}, u32[]{:S(2)}) %collective-permute-start) | collective-permute-done | bytes 212000 | tf_op jit(solution)/shard_map/ppermute | solution.py:320
  32.6 1.5 collective-permute-start.4
  34.1 2.0 collective-permute-start.14
  36.5 2.8 broadcast_in_dim.241
  42.0 5.1 %collective-permute-done.16 = bf16[96,768]{1,0:T(8,128)(2,1)S(1)} collective-permute-done((bf16[96,768]{1,0:T(8,128)(2,1)S(1)}, bf16[96,768]{1,0:T(8,128)(2,1)S(1)}, u32[]{:S(2)}, u32[]{:S(2)}) %collective-permute-start.16) | collective-permute-done | bytes 147488 | tf_op jit(solution)/shard_map/ppermute | solution.py:320
  47.3 6.2 %collective-permute-done.4 = bf16[96,4416]{1,0:T(8,128)(2,1)} collective-permute-done((bf16[96,4416]{1,0:T(8,128)(2,1)S(1)}, bf16[96,4416]{1,0:T(8,128)(2,1)}, u32[]{:S(2)}, u32[]{:S(2)}) %collective-permute-start.4) | collective-permute-done | bytes 847904 | tf_op jit(solution)/shard_map/ppermute | solution.py:315
  54.5 1.5 collective-permute-start.5
  57.1 1.6 collective-permute-start.6
  60.1 1.6 fusion.77
  61.7 1.9 fusion.44
  63.6 1.9 fusion.43
  65.6 1.6 fusion.76
  71.1 1.6 fusion.75
  72.7 1.9 fusion.42
  79.9 1.6 convert_reduce_fusion
  81.5 1.8 fusion.8
  83.3 2.3 collective-permute-done.17
  85.5 4.7 %collective-permute-done.18 = bf16[384,768]{1,0:T(8,128)(2,1)} collective-permute-done((bf16[384,768]{1,0:T(8,128)(2,1)S(1)}, bf16[384,768]{1,0:T(8,128)(2,1)}, u32[]{:S(2)}, u32[]{:S(2)}) %collective-permute-start.18) | collective-permute-done | bytes 589856 | tf_op jit(solution)/shard_map/ppermute | solution.py:315
  91.2 1.6 fusion.71
  92.8 2.4 multiply_convert_fusion.1.qkv_ref
  95.3 7.9 %attend.1 = (bf16[3,768,768]{2,1,0:T(8,128)(2,1)S(1)}, f32[768,192]{1,0:T(8,128)S(1)}, bf16[768,192]{1,0:T(8,128)(2,1)S(1)}) custom-call(bf16[768,576]{1,0:T(8,128)(2,1)S(1)} %multiply_convert_fusion.1.qkv_ref, f32[3,1536]{1,0:T(4,128)S(1)} %fusion.1.diagonal_ref, s32[768,1]{1,0:T(8,128)S(1)} %broadcast_in_dim.278.doc_col_ref, ...), custom_call_target="tpu_custom_call" | custom-call | flops 452984832 | bytes 3538944 | tf_op jit(solution)/shard_map/attend/pallas_call | solution.py:483
  103.4 2.4 collective-permute-start.11
  110.3 1.9 fusion.38
  112.9 1.6 collective-permute-start.19
  116.5 7.8 %fusion.97 = (f32[192]{0:T(256)S(1)}, f32[192,3072]{1,0:T(8,128)S(1)}, f32[192,3072]{1,0:T(8,128)S(1)}, f32[192,3072]{1,0:T(8,128)S(1)}) fusion(bf16[768,3072]{1,0:T(8,128)(2,1)} %bitcast.44, f32[192,768]{1,0:T(8,128)S(1)} %get-tuple-element.70, f32[768]{0:T(1024)S(1)} %copy-done.33, f32[192]{0:T(256)S(1)} %fusion.86, f32[192]{0:T(256)S(1)} %broadcast_multiply_fusion.3), kind=kOutput, calls=%fused_computation.316 | convolution fusion | flops 944897856 | bytes 12391680 | tf_op jit(solution)/shard_map/dot_general | solution.py:647
  124.8 1.7 collective-permute-done.24
  126.6 2.0 multiply_reduce_fusion.1
  128.6 1.6 convolution_convert_fusion.1
  133.4 1.9 add_convert_fusion
  135.3 1.9 fusion.30
  138.1 2.8 fusion.25
  140.9 4.4 %multiply_reduce_fusion.3 = (f32[768]{0:T(1024)S(1)}, f32[192]{0:T(256)S(1)}, f32[192,768]{1,0:T(8,128)S(1)}) fusion(f32[192,768]{1,0:T(8,128)S(1)} %get-tuple-element.70, f32[192]{0:T(256)S(1)} %fusion.86, f32[192]{0:T(256)S(1)} %broadcast_multiply_fusion.3, f32[768]{0:T(1024)S(1)} %copy-done.33, bf16[192,3072]{1,0:T(8,128)(2,1)S(1)} %add_convert_fusion, ...), kind=kOutput, calls=%fused_computation.127 | convolution fusion | flops 907000896 | bytes 7086336 | tf_op jit(solution)/shard_map/dot_general | solution.py:34
  145.3 1.5 convolution_convert_fusion
  151.2 1.6 collective-permute-start.29
  152.8 3.3 %collective-permute-start.30 = (bf16[192,192]{1,0:T(8,128)(2,1)S(1)}, bf16[192,192]{1,0:T(8,128)(2,1)S(1)}, u32[]{:S(2)}, u32[]{:S(2)}) collective-permute-start(bf16[192,192]{1,0:T(8,128)(2,1)S(1)} %get-tuple-element.140), channel_id=1, source_target_pairs={{0,2},{1,3},{2,0},{3,1},{4,6},{5,7},{6,4},{7,5},{8,10},{9,11},{10,... | collective-permute-start | bytes 221192 | tf_op jit(solution)/shard_map/ppermute | solution.py:320
  160.2 2.0 collective-permute-done.30
  165.0 7.0 %attend_back.1 = (bf16[768,576]{1,0:T(8,128)(2,1)S(1)}, f32[3,1536]{1,0:T(4,128)S(1)}, f32[768,3]{1,0:T(8,128)S(1)}) custom-call(bf16[768,576]{1,0:T(8,128)(2,1)S(1)} %multiply_convert_fusion.1.qkv_ref, bf16[3,768,768]{2,1,0:T(8,128)(2,1)S(1)} %get-tuple-element.40.probs_ref, f32[768,192]{1,0:T(8,128)S(1)} %get-tuple-element.41.attention_ref, ...), custom_call_target="tpu_custom_call" | custom-call | flops 905969664 | bytes 3538944 | tf_op jit(solution)/shard_map/attend_back/pallas_call | solution.py:548
  172.0 3.4 %fusion.7 = (f32[768]{0:T(1024)S(1)}, bf16[768,768]{1,0:T(8,128)(2,1)}) fusion(bf16[768,768]{1,0:T(8,128)(2,1)S(1)} %copy-done.5, f32[768]{0:T(1024)S(1)} %add_rsqrt_fusion, f32[768]{0:T(1024)S(1)} %broadcast_multiply_fusion, bf16[768,576]{1,0:T(8,128)(2,1)S(1)} %get-tuple-element.42, bf16[768,576]{1,0:T(8,128)(2,1)} %bitcast.14), kind=kOutput, calls=%fused_computation.15 | convolution fusion | flops 683015424 | bytes 4137984 | tf_op jit(solution)/shard_map/dot_general | solution.py:34
  175.5 3.4 %convolution_convert_fusion.3 = bf16[768,576]{0,1:T(8,128)(2,1)} fusion(bf16[768,576]{1,0:T(8,128)(2,1)S(1)} %get-tuple-element.42, bf16[768,768]{1,0:T(8,128)(2,1)} %all-gather.2.cloned.1.call-done, f32[768]{0:T(1024)S(1)} %copy-done.35, f32[768]{0:T(1024)S(1)} %add_rsqrt_fusion, f32[768]{0:T(1024)S(1)} %broadcast_multiply_fusion), kind=kOutput, calls=%fused_computation.53 | convolution fusion | flops 682868736 | bytes 2958336 | tf_op jit(solution)/shard_map/dot_general | solution.py:28
  178.9 1.7 copy.48
  183.6 1.7 pad_maximum_fusion.11
  185.3 1.7 pad_maximum_fusion.10
  187.0 1.7 pad_maximum_fusion.12
  199.4 1.6 collective-permute-start.40
  201.0 3.0 fusion.24
  204.1 9.4 %collective-permute-done.41 = bf16[384,768]{1,0:T(8,128)(2,1)S(1)} collective-permute-done((bf16[384,768]{1,0:T(8,128)(2,1)S(1)}, bf16[384,768]{1,0:T(8,128)(2,1)S(1)}, u32[]{:S(2)}, u32[]{:S(2)}) %collective-permute-start.41) | collective-permute-done | bytes 589856 | tf_op jit(solution)/shard_map/ppermute | solution.py:315
  215.1 1.6 collective-permute-start.45
  216.8 3.1 %collective-permute-start.52 = (bf16[96,768]{1,0:T(8,128)(2,1)S(1)}, bf16[96,768]{1,0:T(8,128)(2,1)S(1)}, u32[]{:S(2)}, u32[]{:S(2)}) collective-permute-start(bf16[96,768]{1,0:T(8,128)(2,1)S(1)} %get-tuple-element.127), channel_id=1, source_target_pairs={{0,2},{1,3},{2,0},{3,1},{4,6},{5,7},{6,4},{7,5},{8,10},{9,11},{10,... | collective-permute-start | bytes 442376 | tf_op jit(solution)/shard_map/ppermute | solution.py:320
  223.6 5.4 %collective-permute-done.52 = bf16[96,768]{1,0:T(8,128)(2,1)S(1)} collective-permute-done((bf16[96,768]{1,0:T(8,128)(2,1)S(1)}, bf16[96,768]{1,0:T(8,128)(2,1)S(1)}, u32[]{:S(2)}, u32[]{:S(2)}) %collective-permute-start.52) | collective-permute-done | bytes 147488 | tf_op jit(solution)/shard_map/ppermute | solution.py:320
  228.9 3.1 %collective-permute-done.51 = bf16[96,768]{1,0:T(8,128)(2,1)S(1)} collective-permute-done((bf16[96,768]{1,0:T(8,128)(2,1)S(1)}, bf16[96,768]{1,0:T(8,128)(2,1)S(1)}, u32[]{:S(2)}, u32[]{:S(2)}) %collective-permute-start.51) | collective-permute-done | bytes 147488 | tf_op jit(solution)/shard_map/ppermute | solution.py:320
  236.7 1.6 collective-permute-start.55
  238.3 18.3 %collective-permute-done.55 = f32[96,128]{1,0:T(8,128)S(1)} collective-permute-done((f32[96,128]{1,0:T(8,128)S(1)}, f32[96,128]{1,0:T(8,128)S(1)}, u32[]{:S(2)}, u32[]{:S(2)}) %collective-permute-start.55) | collective-permute-done | bytes 49184 | tf_op jit(solution)/shard_map/ppermute | solution.py:315
  256.5 1.8 collective-permute-start.56
  260.8 4.1 %collective-permute-done.57 = f32[96,128]{1,0:T(8,128)S(1)} collective-permute-done((f32[96,128]{1,0:T(8,128)S(1)}, f32[96,128]{1,0:T(8,128)S(1)}, u32[]{:S(2)}, u32[]{:S(2)}) %collective-permute-start.57) | collective-permute-done | bytes 49184 | tf_op jit(solution)/shard_map/ppermute | solution.py:325
  264.9 2.0 fusion.49
  266.9 3.0 collective-permute-done.58
  271.9 1.8 add_convert_fusion.1
  273.9 2.3 collective-permute-start.49
  276.7 9.2 %collective-permute-done.50 = bf16[24,4416]{1,0:T(8,128)(2,1)S(1)} collective-permute-done((bf16[24,4416]{1,0:T(8,128)(2,1)S(1)}, bf16[24,4416]{1,0:T(8,128)(2,1)S(1)}, u32[]{:S(2)}, u32[]{:S(2)}) %collective-permute-start.50) | collective-permute-done | bytes 212000 | tf_op jit(solution)/shard_map/ppermute | solution.py:320
  286.0 2.3 collective-permute-done.49
  288.3 2.8 collective-permute-done.48
  (333 shorter events, 77.1 us)
Async XLA Ops:
  7.2 72.7 %all-gather.2.cloned.1.call-start = ((), (), s32[]{:S(2)}) async-start(), calls=%async_computation.1 | async-start | bytes 1474560 | tf_op jit(solution)/shard_map/all_gather | solution.py:602
  9.7 11.5 %collective-permute-start.1 = (bf16[24,4416]{1,0:T(8,128)(2,1)S(1)}, bf16[24,4416]{1,0:T(8,128)(2,1)S(1)}, u32[]{:S(2)}, u32[]{:S(2)}) collective-permute-start(bf16[24,4416]{1,0:T(8,128)(2,1)S(1)} %get-tuple-element.123), channel_id=1, source_target_pairs={{0,2},{1,3},{2,0},{3,1},{4,6},{5,7},{6,4},{7,5},{8,10},{9,11},{10,... | collective-permute-start | bytes 635912 | tf_op jit(solution)/shard_map/ppermute | solution.py:320
  10.1 18.4 %collective-permute-start.2 = (bf16[24,4416]{1,0:T(8,128)(2,1)S(1)}, bf16[24,4416]{1,0:T(8,128)(2,1)S(1)}, u32[]{:S(2)}, u32[]{:S(2)}) collective-permute-start(bf16[24,4416]{1,0:T(8,128)(2,1)S(1)} %get-tuple-element.124), channel_id=1, source_target_pairs={{0,3},{1,0},{2,1},{3,2},{4,7},{5,4},{6,5},{7,6},{8,11},{9,8},{10,9... | collective-permute-start | bytes 635912 | tf_op jit(solution)/shard_map/ppermute | solution.py:320
  12.8 18.8 %collective-permute-start = (bf16[24,4416]{1,0:T(8,128)(2,1)S(1)}, bf16[24,4416]{1,0:T(8,128)(2,1)S(1)}, u32[]{:S(2)}, u32[]{:S(2)}) collective-permute-start(bf16[24,4416]{1,0:T(8,128)(2,1)S(1)} %get-tuple-element.122), channel_id=1, source_target_pairs={{0,1},{1,2},{2,3},{3,0},{4,5},{5,6},{6,7},{7,4},{8,9},{9,10},{10,1... | collective-permute-start | bytes 635912 | tf_op jit(solution)/shard_map/ppermute | solution.py:320
  32.0 24.1 %collective-permute-start.3 = (bf16[96,4416]{1,0:T(8,128)(2,1)S(1)}, bf16[96,4416]{1,0:T(8,128)(2,1)}, u32[]{:S(2)}, u32[]{:S(2)}) collective-permute-start(bf16[96,4416]{1,0:T(8,128)(2,1)S(1)} %pad_maximum_fusion.1), channel_id=1, source_target_pairs={{0,8},{4,12},{8,0},{12,4},{16,24},{20,28},{24,16},{28,20},{1,9},{5... | collective-permute-start | bytes 2543624 | tf_op jit(solution)/shard_map/ppermute | solution.py:315
  32.6 20.9 %collective-permute-start.4 = (bf16[96,4416]{1,0:T(8,128)(2,1)S(1)}, bf16[96,4416]{1,0:T(8,128)(2,1)}, u32[]{:S(2)}, u32[]{:S(2)}) collective-permute-start(bf16[96,4416]{1,0:T(8,128)(2,1)S(1)} %pad_maximum_fusion.1), channel_id=1, source_target_pairs={{0,16},{4,20},{8,24},{12,28},{16,0},{20,4},{24,8},{28,12},{1,17},{... | collective-permute-start | bytes 2543624 | tf_op jit(solution)/shard_map/ppermute | solution.py:315
  34.1 7.8 %collective-permute-start.15 = (bf16[96,768]{1,0:T(8,128)(2,1)S(1)}, bf16[96,768]{1,0:T(8,128)(2,1)S(1)}, u32[]{:S(2)}, u32[]{:S(2)}) collective-permute-start(bf16[96,768]{1,0:T(8,128)(2,1)S(1)} %copy-done.32), channel_id=1, source_target_pairs={{0,2},{1,3},{2,0},{3,1},{4,6},{5,7},{6,4},{7,5},{8,10},{9,11},{10,... | collective-permute-start | bytes 442376 | tf_op jit(solution)/shard_map/ppermute | solution.py:320
  34.1 13.0 %collective-permute-start.16 = (bf16[96,768]{1,0:T(8,128)(2,1)S(1)}, bf16[96,768]{1,0:T(8,128)(2,1)S(1)}, u32[]{:S(2)}, u32[]{:S(2)}) collective-permute-start(bf16[96,768]{1,0:T(8,128)(2,1)S(1)} %copy-done.32), channel_id=1, source_target_pairs={{0,3},{1,0},{2,1},{3,2},{4,7},{5,4},{6,5},{7,6},{8,11},{9,8},{10,9... | collective-permute-start | bytes 442376 | tf_op jit(solution)/shard_map/ppermute | solution.py:320
  34.1 13.0 %collective-permute-start.14 = (bf16[96,768]{1,0:T(8,128)(2,1)S(1)}, bf16[96,768]{1,0:T(8,128)(2,1)S(1)}, u32[]{:S(2)}, u32[]{:S(2)}) collective-permute-start(bf16[96,768]{1,0:T(8,128)(2,1)S(1)} %copy-done.32), channel_id=1, source_target_pairs={{0,1},{1,2},{2,3},{3,0},{4,5},{5,6},{6,7},{7,4},{8,9},{9,10},{10,1... | collective-permute-start | bytes 442376 | tf_op jit(solution)/shard_map/ppermute | solution.py:320
  36.2 198.0 %reduce-scatter.2.cloned.1.call-start = ((), (), s32[]{:S(2)}) async-start(), calls=%async_computation.2 | async-start | bytes 1474560 | tf_op jit(solution)/shard_map/reduce_scatter | solution.py:693
  42.0 32.6 %collective-permute-start.7 = (bf16[96,4416]{1,0:T(8,128)(2,1)S(1)}, bf16[96,4416]{1,0:T(8,128)(2,1)S(1)}, u32[]{:S(2)}, u32[]{:S(2)}) collective-permute-start(bf16[96,4416]{1,0:T(8,128)(2,1)S(1)} %pad_maximum_fusion.1), channel_id=1, source_target_pairs={{0,4},{4,0},{8,12},{12,8},{16,20},{20,16},{24,28},{28,24},{1,5},{5... | collective-permute-start | bytes 2543624 | tf_op jit(solution)/shard_map/ppermute | solution.py:315
  47.2 27.4 %copy-start.6 = (bf16[384,768]{1,0:T(8,128)(2,1)}, bf16[384,768]{1,0:T(8,128)(2,1)S(1)}, u32[]{:S(2)}) copy-start(bf16[384,768]{1,0:T(8,128)(2,1)S(1)} %pad_maximum_fusion.4) | copy-start | bytes 1769476
  54.5 13.5 %collective-permute-start.5 = (bf16[48,4416]{1,0:T(8,128)(2,1)S(1)}, bf16[48,4416]{1,0:T(8,128)(2,1)S(1)}, u32[]{:S(2)}, u32[]{:S(2)}) collective-permute-start(bf16[48,4416]{1,0:T(8,128)(2,1)S(1)} %slice.263), channel_id=1, source_target_pairs={{0,8},{4,12},{8,0},{12,4},{16,24},{20,28},{24,16},{28,20},{1,9},{5... | collective-permute-start | bytes 1271816 | tf_op jit(solution)/shard_map/ppermute | solution.py:315
  57.1 11.8 %collective-permute-start.6 = (bf16[48,4416]{1,0:T(8,128)(2,1)S(1)}, bf16[48,4416]{1,0:T(8,128)(2,1)S(1)}, u32[]{:S(2)}, u32[]{:S(2)}) collective-permute-start(bf16[48,4416]{1,0:T(8,128)(2,1)S(1)} %slice.264), channel_id=1, source_target_pairs={{0,16},{4,20},{8,24},{12,28},{16,0},{20,4},{24,8},{28,12},{1,17},{... | collective-permute-start | bytes 1271816 | tf_op jit(solution)/shard_map/ppermute | solution.py:315
  58.7 18.0 %collective-permute-start.8 = (bf16[96,4416]{1,0:T(8,128)(2,1)}, bf16[96,4416]{1,0:T(8,128)(2,1)S(1)}, u32[]{:S(2)}, u32[]{:S(2)}) collective-permute-start(bf16[96,4416]{1,0:T(8,128)(2,1)} %collective-permute-done.3), channel_id=1, source_target_pairs={{0,4},{4,0},{8,12},{12,8},{16,20},{20,16},{24,28},{28,24},{1,5},{5... | collective-permute-start | bytes 2543624 | tf_op jit(solution)/shard_map/ppermute | solution.py:315
  58.7 18.0 %collective-permute-start.9 = (bf16[96,4416]{1,0:T(8,128)(2,1)}, bf16[96,4416]{1,0:T(8,128)(2,1)S(1)}, u32[]{:S(2)}, u32[]{:S(2)}) collective-permute-start(bf16[96,4416]{1,0:T(8,128)(2,1)} %collective-permute-done.4), channel_id=1, source_target_pairs={{0,4},{4,0},{8,12},{12,8},{16,20},{20,16},{24,28},{28,24},{1,5},{5... | collective-permute-start | bytes 2543624 | tf_op jit(solution)/shard_map/ppermute | solution.py:315
  69.7 20.5 %collective-permute-start.10 = (bf16[96,4416]{1,0:T(8,128)(2,1)}, bf16[96,4416]{1,0:T(8,128)(2,1)}, u32[]{:S(2)}, u32[]{:S(2)}) collective-permute-start(bf16[96,4416]{1,0:T(8,128)(2,1)} %constant_dynamic-update-slice_fusion), channel_id=1, source_target_pairs={{0,4},{4,0},{8,12},{12,8},{16,20},{20,16},{24,28},{28,24},{1,5},{5... | collective-permute-start | bytes 2543624 | tf_op jit(solution)/shard_map/ppermute | solution.py:315
  69.7 15.8 %collective-permute-start.17 = (bf16[384,768]{1,0:T(8,128)(2,1)S(1)}, bf16[384,768]{1,0:T(8,128)(2,1)}, u32[]{:S(2)}, u32[]{:S(2)}) collective-permute-start(bf16[384,768]{1,0:T(8,128)(2,1)S(1)} %pad_maximum_fusion.4), channel_id=1, source_target_pairs={{0,8},{4,12},{8,0},{12,4},{16,24},{20,28},{24,16},{28,20},{1,9},{5... | collective-permute-start | bytes 1769480 | tf_op jit(solution)/shard_map/ppermute | solution.py:315
  74.6 15.6 %collective-permute-start.18 = (bf16[384,768]{1,0:T(8,128)(2,1)S(1)}, bf16[384,768]{1,0:T(8,128)(2,1)}, u32[]{:S(2)}, u32[]{:S(2)}) collective-permute-start(bf16[384,768]{1,0:T(8,128)(2,1)S(1)} %pad_maximum_fusion.4), channel_id=1, source_target_pairs={{0,16},{4,20},{8,24},{12,28},{16,0},{20,4},{24,8},{28,12},{1,17},{... | collective-permute-start | bytes 1769480 | tf_op jit(solution)/shard_map/ppermute | solution.py:315
  91.2 33.5 %collective-permute-start.22 = (bf16[384,768]{1,0:T(8,128)(2,1)}, bf16[384,768]{1,0:T(8,128)(2,1)S(1)}, u32[]{:S(2)}, u32[]{:S(2)}) collective-permute-start(bf16[384,768]{1,0:T(8,128)(2,1)} %collective-permute-done.17), channel_id=1, source_target_pairs={{0,4},{4,0},{8,12},{12,8},{16,20},{20,16},{24,28},{28,24},{1,5},{5... | collective-permute-start | bytes 1769480 | tf_op jit(solution)/shard_map/ppermute | solution.py:315
  103.2 9.1 %collective-permute-start.13 = (bf16[192,192]{1,0:T(8,128)(2,1)S(1)}, bf16[192,192]{1,0:T(8,128)(2,1)S(1)}, u32[]{:S(2)}, u32[]{:S(2)}) collective-permute-start(bf16[192,192]{1,0:T(8,128)(2,1)S(1)} %get-tuple-element.135), channel_id=1, source_target_pairs={{0,3},{1,0},{2,1},{3,2},{4,7},{5,4},{6,5},{7,6},{8,11},{9,8},{10,9... | collective-permute-start | bytes 221192 | tf_op jit(solution)/shard_map/ppermute | solution.py:320
  103.3 9.6 %collective-permute-start.12 = (bf16[192,192]{1,0:T(8,128)(2,1)S(1)}, bf16[192,192]{1,0:T(8,128)(2,1)S(1)}, u32[]{:S(2)}, u32[]{:S(2)}) collective-permute-start(bf16[192,192]{1,0:T(8,128)(2,1)S(1)} %get-tuple-element.136), channel_id=1, source_target_pairs={{0,2},{1,3},{2,0},{3,1},{4,6},{5,7},{6,4},{7,5},{8,10},{9,11},{10,... | collective-permute-start | bytes 221192 | tf_op jit(solution)/shard_map/ppermute | solution.py:320
  103.4 11.1 %collective-permute-start.11 = (bf16[192,192]{1,0:T(8,128)(2,1)S(1)}, bf16[192,192]{1,0:T(8,128)(2,1)S(1)}, u32[]{:S(2)}, u32[]{:S(2)}) collective-permute-start(bf16[192,192]{1,0:T(8,128)(2,1)S(1)} %get-tuple-element.137), channel_id=1, source_target_pairs={{0,1},{1,2},{2,3},{3,0},{4,5},{5,6},{6,7},{7,4},{8,9},{9,10},{10,1... | collective-permute-start | bytes 221192 | tf_op jit(solution)/shard_map/ppermute | solution.py:320
  105.8 18.8 %collective-permute-start.21 = (bf16[384,768]{1,0:T(8,128)(2,1)S(1)}, bf16[384,768]{1,0:T(8,128)(2,1)S(1)}, u32[]{:S(2)}, u32[]{:S(2)}) collective-permute-start(bf16[384,768]{1,0:T(8,128)(2,1)S(1)} %copy-done.7), channel_id=1, source_target_pairs={{0,4},{4,0},{8,12},{12,8},{16,20},{20,16},{24,28},{28,24},{1,5},{5... | collective-permute-start | bytes 1769480 | tf_op jit(solution)/shard_map/ppermute | solution.py:315
  112.4 12.4 %collective-permute-start.23 = (bf16[384,768]{1,0:T(8,128)(2,1)}, bf16[384,768]{1,0:T(8,128)(2,1)S(1)}, u32[]{:S(2)}, u32[]{:S(2)}) collective-permute-start(bf16[384,768]{1,0:T(8,128)(2,1)} %collective-permute-done.18), channel_id=1, source_target_pairs={{0,4},{4,0},{8,12},{12,8},{16,20},{20,16},{24,28},{28,24},{1,5},{5... | collective-permute-start | bytes 1769480 | tf_op jit(solution)/shard_map/ppermute | solution.py:315
  112.9 11.4 %collective-permute-start.19 = (bf16[192,768]{1,0:T(8,128)(2,1)S(1)}, bf16[192,768]{1,0:T(8,128)(2,1)S(1)}, u32[]{:S(2)}, u32[]{:S(2)}) collective-permute-start(bf16[192,768]{1,0:T(8,128)(2,1)S(1)} %slice.222), channel_id=1, source_target_pairs={{0,8},{4,12},{8,0},{12,4},{16,24},{20,28},{24,16},{28,20},{1,9},{5... | collective-permute-start | bytes 884744 | tf_op jit(solution)/shard_map/ppermute | solution.py:315
  114.5 9.9 %collective-permute-start.20 = (bf16[192,768]{1,0:T(8,128)(2,1)S(1)}, bf16[192,768]{1,0:T(8,128)(2,1)S(1)}, u32[]{:S(2)}, u32[]{:S(2)}) collective-permute-start(bf16[192,768]{1,0:T(8,128)(2,1)S(1)} %slice.223), channel_id=1, source_target_pairs={{0,16},{4,20},{8,24},{12,28},{16,0},{20,4},{24,8},{28,12},{1,17},{... | collective-permute-start | bytes 884744 | tf_op jit(solution)/shard_map/ppermute | solution.py:315
  124.4 2.1 collective-permute-start.24
  132.4 4.8 %collective-permute-start.28 = (bf16[384,768]{1,0:T(8,128)(2,1)}, bf16[384,768]{1,0:T(8,128)(2,1)S(1)}, u32[]{:S(2)}, u32[]{:S(2)}) collective-permute-start(bf16[384,768]{1,0:T(8,128)(2,1)} %get-tuple-element.83), channel_id=1, source_target_pairs={{0,4},{4,0},{8,12},{12,8},{16,20},{20,16},{24,28},{28,24},{1,5},{5... | collective-permute-start | bytes 1769480 | tf_op jit(solution)/shard_map/ppermute | solution.py:315
  132.5 4.7 %collective-permute-start.27 = (bf16[384,768]{1,0:T(8,128)(2,1)}, bf16[384,768]{1,0:T(8,128)(2,1)S(1)}, u32[]{:S(2)}, u32[]{:S(2)}) collective-permute-start(bf16[384,768]{1,0:T(8,128)(2,1)} %get-tuple-element.84), channel_id=1, source_target_pairs={{0,4},{4,0},{8,12},{12,8},{16,20},{20,16},{24,28},{28,24},{1,5},{5... | collective-permute-start | bytes 1769480 | tf_op jit(solution)/shard_map/ppermute | solution.py:315
  132.9 4.3 %collective-permute-start.26 = (bf16[384,768]{1,0:T(8,128)(2,1)}, bf16[384,768]{1,0:T(8,128)(2,1)S(1)}, u32[]{:S(2)}, u32[]{:S(2)}) collective-permute-start(bf16[384,768]{1,0:T(8,128)(2,1)} %get-tuple-element.85), channel_id=1, source_target_pairs={{0,4},{4,0},{8,12},{12,8},{16,20},{20,16},{24,28},{28,24},{1,5},{5... | collective-permute-start | bytes 1769480 | tf_op jit(solution)/shard_map/ppermute | solution.py:315
  133.0 5.1 %collective-permute-start.25 = (bf16[384,768]{1,0:T(8,128)(2,1)S(1)}, bf16[384,768]{1,0:T(8,128)(2,1)}, u32[]{:S(2)}, u32[]{:S(2)}) collective-permute-start(bf16[384,768]{1,0:T(8,128)(2,1)S(1)} %get-tuple-element.86), channel_id=1, source_target_pairs={{0,4},{4,0},{8,12},{12,8},{16,20},{20,16},{24,28},{28,24},{1,5},{5... | collective-permute-start | bytes 1769480 | tf_op jit(solution)/shard_map/ppermute | solution.py:315
  151.2 8.9 %collective-permute-start.29 = (bf16[192,192]{1,0:T(8,128)(2,1)S(1)}, bf16[192,192]{1,0:T(8,128)(2,1)S(1)}, u32[]{:S(2)}, u32[]{:S(2)}) collective-permute-start(bf16[192,192]{1,0:T(8,128)(2,1)S(1)} %get-tuple-element.141), channel_id=1, source_target_pairs={{0,3},{1,0},{2,1},{3,2},{4,7},{5,4},{6,5},{7,6},{8,11},{9,8},{10,9... | collective-permute-start | bytes 221192 | tf_op jit(solution)/shard_map/ppermute | solution.py:320
  152.8 9.4 %collective-permute-start.30 = (bf16[192,192]{1,0:T(8,128)(2,1)S(1)}, bf16[192,192]{1,0:T(8,128)(2,1)S(1)}, u32[]{:S(2)}, u32[]{:S(2)}) collective-permute-start(bf16[192,192]{1,0:T(8,128)(2,1)S(1)} %get-tuple-element.140), channel_id=1, source_target_pairs={{0,2},{1,3},{2,0},{3,1},{4,6},{5,7},{6,4},{7,5},{8,10},{9,11},{10,... | collective-permute-start | bytes 221192 | tf_op jit(solution)/shard_map/ppermute | solution.py:320
  156.2 8.3 %collective-permute-start.31 = (bf16[192,192]{1,0:T(8,128)(2,1)S(1)}, bf16[192,192]{1,0:T(8,128)(2,1)S(1)}, u32[]{:S(2)}, u32[]{:S(2)}) collective-permute-start(bf16[192,192]{1,0:T(8,128)(2,1)S(1)} %get-tuple-element.139), channel_id=1, source_target_pairs={{0,1},{1,2},{2,3},{3,0},{4,5},{5,6},{6,7},{7,4},{8,9},{9,10},{10,1... | collective-permute-start | bytes 221192 | tf_op jit(solution)/shard_map/ppermute | solution.py:320
  157.9 41.5 %collective-permute-start.32 = (bf16[96,3072]{1,0:T(8,128)(2,1)}, bf16[96,3072]{1,0:T(8,128)(2,1)}, u32[]{:S(2)}, u32[]{:S(2)}) collective-permute-start(bf16[96,3072]{1,0:T(8,128)(2,1)} %get-tuple-element.75), channel_id=1, source_target_pairs={{0,4},{4,0},{8,12},{12,8},{16,20},{20,16},{24,28},{28,24},{1,5},{5... | collective-permute-start | bytes 1769480 | tf_op jit(solution)/shard_map/ppermute | solution.py:315
  157.9 43.2 %collective-permute-start.43 = (bf16[96,3072]{1,0:T(8,128)(2,1)}, bf16[96,3072]{1,0:T(8,128)(2,1)}, u32[]{:S(2)}, u32[]{:S(2)}) collective-permute-start(bf16[96,3072]{1,0:T(8,128)(2,1)} %get-tuple-element.76), channel_id=1, source_target_pairs={{0,4},{4,0},{8,12},{12,8},{16,20},{20,16},{24,28},{28,24},{1,5},{5... | collective-permute-start | bytes 1769480 | tf_op jit(solution)/shard_map/ppermute | solution.py:315
  160.2 40.9 %collective-permute-start.36 = (bf16[96,3072]{1,0:T(8,128)(2,1)}, bf16[96,3072]{1,0:T(8,128)(2,1)}, u32[]{:S(2)}, u32[]{:S(2)}) collective-permute-start(bf16[96,3072]{1,0:T(8,128)(2,1)} %get-tuple-element.77), channel_id=1, source_target_pairs={{0,4},{4,0},{8,12},{12,8},{16,20},{20,16},{24,28},{28,24},{1,5},{5... | collective-permute-start | bytes 1769480 | tf_op jit(solution)/shard_map/ppermute | solution.py:315
  162.2 27.8 %collective-permute-start.38 = (bf16[192,768]{1,0:T(8,128)(2,1)}, bf16[192,768]{1,0:T(8,128)(2,1)}, u32[]{:S(2)}, u32[]{:S(2)}) collective-permute-start(bf16[192,768]{1,0:T(8,128)(2,1)} %get-tuple-element.129), channel_id=1, source_target_pairs={{0,16},{4,20},{8,24},{12,28},{16,0},{20,4},{24,8},{28,12},{1,17},{... | collective-permute-start | bytes 884744 | tf_op jit(solution)/shard_map/ppermute | solution.py:315
  164.5 26.8 %collective-permute-start.39 = (bf16[192,768]{1,0:T(8,128)(2,1)}, bf16[192,768]{1,0:T(8,128)(2,1)}, u32[]{:S(2)}, u32[]{:S(2)}) collective-permute-start(bf16[192,768]{1,0:T(8,128)(2,1)} %get-tuple-element.128), channel_id=1, source_target_pairs={{0,8},{4,12},{8,0},{12,4},{16,24},{20,28},{24,16},{28,20},{1,9},{5... | collective-permute-start | bytes 884744 | tf_op jit(solution)/shard_map/ppermute | solution.py:315
  190.1 11.0 %collective-permute-start.34 = (bf16[96,3072]{1,0:T(8,128)(2,1)}, bf16[96,3072]{1,0:T(8,128)(2,1)S(1)}, u32[]{:S(2)}, u32[]{:S(2)}) collective-permute-start(bf16[96,3072]{1,0:T(8,128)(2,1)} %get-tuple-element.78), channel_id=1, source_target_pairs={{0,4},{4,0},{8,12},{12,8},{16,20},{20,16},{24,28},{28,24},{1,5},{5... | collective-permute-start | bytes 1769480 | tf_op jit(solution)/shard_map/ppermute | solution.py:315
  191.3 1.9 collective-permute-start.37
  193.2 1.5 collective-permute-start.35
  194.7 1.5 collective-permute-start.44
  196.3 1.5 collective-permute-start.33
  197.8 15.6 %collective-permute-start.41 = (bf16[384,768]{1,0:T(8,128)(2,1)S(1)}, bf16[384,768]{1,0:T(8,128)(2,1)S(1)}, u32[]{:S(2)}, u32[]{:S(2)}) collective-permute-start(bf16[384,768]{1,0:T(8,128)(2,1)S(1)} %pad_maximum_fusion.6), channel_id=1, source_target_pairs={{0,16},{4,20},{8,24},{12,28},{16,0},{20,4},{24,8},{28,12},{1,17},{... | collective-permute-start | bytes 1769480 | tf_op jit(solution)/shard_map/ppermute | solution.py:315
  199.4 15.4 %copy-start.10 = (bf16[384,768]{1,0:T(8,128)(2,1)S(1)}, bf16[384,768]{1,0:T(8,128)(2,1)}, u32[]{:S(2)}) copy-start(bf16[384,768]{1,0:T(8,128)(2,1)} %get-tuple-element.79) | copy-start | bytes 1769476
  199.4 15.4 %collective-permute-start.40 = (bf16[384,768]{1,0:T(8,128)(2,1)S(1)}, bf16[384,768]{1,0:T(8,128)(2,1)S(1)}, u32[]{:S(2)}, u32[]{:S(2)}) collective-permute-start(bf16[384,768]{1,0:T(8,128)(2,1)S(1)} %pad_maximum_fusion.5), channel_id=1, source_target_pairs={{0,8},{4,12},{8,0},{12,4},{16,24},{20,28},{24,16},{28,20},{1,9},{5... | collective-permute-start | bytes 1769480 | tf_op jit(solution)/shard_map/ppermute | solution.py:315
  215.1 17.8 %collective-permute-start.45 = (bf16[48,4416]{1,0:T(8,128)(2,1)S(1)}, bf16[48,4416]{1,0:T(8,128)(2,1)S(1)}, u32[]{:S(2)}, u32[]{:S(2)}) collective-permute-start(bf16[48,4416]{1,0:T(8,128)(2,1)S(1)} %get-tuple-element.120), channel_id=1, source_target_pairs={{0,8},{4,12},{8,0},{12,4},{16,24},{20,28},{24,16},{28,20},{1,9},{5... | collective-permute-start | bytes 1271816 | tf_op jit(solution)/shard_map/ppermute | solution.py:315
  216.7 6.8 %collective-permute-start.53 = (bf16[96,768]{1,0:T(8,128)(2,1)S(1)}, bf16[96,768]{1,0:T(8,128)(2,1)S(1)}, u32[]{:S(2)}, u32[]{:S(2)}) collective-permute-start(bf16[96,768]{1,0:T(8,128)(2,1)S(1)} %get-tuple-element.126), channel_id=1, source_target_pairs={{0,3},{1,0},{2,1},{3,2},{4,7},{5,4},{6,5},{7,6},{8,11},{9,8},{10,9... | collective-permute-start | bytes 442376 | tf_op jit(solution)/shard_map/ppermute | solution.py:320
  216.8 12.1 %collective-permute-start.52 = (bf16[96,768]{1,0:T(8,128)(2,1)S(1)}, bf16[96,768]{1,0:T(8,128)(2,1)S(1)}, u32[]{:S(2)}, u32[]{:S(2)}) collective-permute-start(bf16[96,768]{1,0:T(8,128)(2,1)S(1)} %get-tuple-element.127), channel_id=1, source_target_pairs={{0,2},{1,3},{2,0},{3,1},{4,6},{5,7},{6,4},{7,5},{8,10},{9,11},{10,... | collective-permute-start | bytes 442376 | tf_op jit(solution)/shard_map/ppermute | solution.py:320
  219.9 12.2 %collective-permute-start.51 = (bf16[96,768]{1,0:T(8,128)(2,1)S(1)}, bf16[96,768]{1,0:T(8,128)(2,1)S(1)}, u32[]{:S(2)}, u32[]{:S(2)}) collective-permute-start(bf16[96,768]{1,0:T(8,128)(2,1)S(1)} %get-tuple-element.125), channel_id=1, source_target_pairs={{0,1},{1,2},{2,3},{3,0},{4,5},{5,6},{6,7},{7,4},{8,9},{9,10},{10,1... | collective-permute-start | bytes 442376 | tf_op jit(solution)/shard_map/ppermute | solution.py:320
  220.6 12.4 %collective-permute-start.42 = (bf16[48,4416]{1,0:T(8,128)(2,1)S(1)}, bf16[48,4416]{1,0:T(8,128)(2,1)S(1)}, u32[]{:S(2)}, u32[]{:S(2)}) collective-permute-start(bf16[48,4416]{1,0:T(8,128)(2,1)S(1)} %get-tuple-element.121), channel_id=1, source_target_pairs={{0,16},{4,20},{8,24},{12,28},{16,0},{20,4},{24,8},{28,12},{1,17},{... | collective-permute-start | bytes 1271816 | tf_op jit(solution)/shard_map/ppermute | solution.py:315
  234.2 37.7 %collective-permute-start.47 = (bf16[96,4416]{1,0:T(8,128)(2,1)S(1)}, bf16[96,4416]{1,0:T(8,128)(2,1)}, u32[]{:S(2)}, u32[]{:S(2)}) collective-permute-start(bf16[96,4416]{1,0:T(8,128)(2,1)S(1)} %fusion.32), channel_id=1, source_target_pairs={{0,16},{4,20},{8,24},{12,28},{16,0},{20,4},{24,8},{28,12},{1,17},{... | collective-permute-start | bytes 2543624 | tf_op jit(solution)/shard_map/ppermute | solution.py:315
  234.9 37.0 %collective-permute-start.46 = (bf16[96,4416]{1,0:T(8,128)(2,1)}, bf16[96,4416]{1,0:T(8,128)(2,1)}, u32[]{:S(2)}, u32[]{:S(2)}) collective-permute-start(bf16[96,4416]{1,0:T(8,128)(2,1)} %pad_maximum_fusion.3), channel_id=1, source_target_pairs={{0,8},{4,12},{8,0},{12,4},{16,24},{20,28},{24,16},{28,20},{1,9},{5... | collective-permute-start | bytes 2543624 | tf_op jit(solution)/shard_map/ppermute | solution.py:315
  235.4 1.3 collective-permute-start.54
  236.7 19.9 %collective-permute-start.55 = (f32[96,128]{1,0:T(8,128)S(1)}, f32[96,128]{1,0:T(8,128)S(1)}, u32[]{:S(2)}, u32[]{:S(2)}) collective-permute-start(f32[96,128]{1,0:T(8,128)S(1)} %add.489), channel_id=1, source_target_pairs={{0,8},{4,12},{8,0},{12,4},{16,24},{20,28},{24,16},{28,20},{1,9},{5... | collective-permute-start | bytes 147464 | tf_op jit(solution)/shard_map/ppermute | solution.py:315
  256.5 4.1 %collective-permute-start.56 = (f32[96,128]{1,0:T(8,128)S(1)}, f32[96,128]{1,0:T(8,128)S(1)}, u32[]{:S(2)}, u32[]{:S(2)}) collective-permute-start(f32[96,128]{1,0:T(8,128)S(1)} %add.490), channel_id=1, source_target_pairs={{0,16},{4,20},{8,24},{12,28},{16,0},{20,4},{24,8},{28,12},{1,17},{... | collective-permute-start | bytes 147464 | tf_op jit(solution)/shard_map/ppermute | solution.py:315
  260.7 4.2 %collective-permute-start.57 = (f32[96,128]{1,0:T(8,128)S(1)}, f32[96,128]{1,0:T(8,128)S(1)}, u32[]{:S(2)}, u32[]{:S(2)}) collective-permute-start(f32[96,128]{1,0:T(8,128)S(1)} %add.491), channel_id=1, source_target_pairs={{0,1},{1,0},{2,3},{3,2},{4,5},{5,4},{6,7},{7,6},{8,9},{9,8},{10,11... | collective-permute-start | bytes 147464 | tf_op jit(solution)/shard_map/ppermute | solution.py:325
  264.9 5.0 %collective-permute-start.58 = (f32[96,128]{1,0:T(8,128)S(1)}, f32[96,128]{1,0:T(8,128)S(1)}, u32[]{:S(2)}, u32[]{:S(2)}) collective-permute-start(f32[96,128]{1,0:T(8,128)S(1)} %add.492), channel_id=1, source_target_pairs={{0,2},{1,3},{2,0},{3,1},{4,6},{5,7},{6,4},{7,5},{8,10},{9,11},{10,... | collective-permute-start | bytes 147464 | tf_op jit(solution)/shard_map/ppermute | solution.py:325
  273.7 20.2 %copy-start.1 = (f32[513,12]{0,1:T(8,128)S(1)}, f32[513,12]{0,1:T(8,128)}, u32[]{:S(2)}) copy-start(f32[513,12]{0,1:T(8,128)} %param.26) | copy-start | bytes 73876
  273.8 12.1 %collective-permute-start.50 = (bf16[24,4416]{1,0:T(8,128)(2,1)S(1)}, bf16[24,4416]{1,0:T(8,128)(2,1)S(1)}, u32[]{:S(2)}, u32[]{:S(2)}) collective-permute-start(bf16[24,4416]{1,0:T(8,128)(2,1)S(1)} %get-tuple-element.117), channel_id=1, source_target_pairs={{0,3},{1,0},{2,1},{3,2},{4,7},{5,4},{6,5},{7,6},{8,11},{9,8},{10,9... | collective-permute-start | bytes 635912 | tf_op jit(solution)/shard_map/ppermute | solution.py:320
  273.9 14.4 %collective-permute-start.49 = (bf16[24,4416]{1,0:T(8,128)(2,1)S(1)}, bf16[24,4416]{1,0:T(8,128)(2,1)S(1)}, u32[]{:S(2)}, u32[]{:S(2)}) collective-permute-start(bf16[24,4416]{1,0:T(8,128)(2,1)S(1)} %get-tuple-element.118), channel_id=1, source_target_pairs={{0,2},{1,3},{2,0},{3,1},{4,6},{5,7},{6,4},{7,5},{8,10},{9,11},{10,... | collective-permute-start | bytes 635912 | tf_op jit(solution)/shard_map/ppermute | solution.py:320
  276.2 14.9 %collective-permute-start.48 = (bf16[24,4416]{1,0:T(8,128)(2,1)S(1)}, bf16[24,4416]{1,0:T(8,128)(2,1)S(1)}, u32[]{:S(2)}, u32[]{:S(2)}) collective-permute-start(bf16[24,4416]{1,0:T(8,128)(2,1)S(1)} %get-tuple-element.119), channel_id=1, source_target_pairs={{0,1},{1,2},{2,3},{3,0},{4,5},{5,6},{6,7},{7,4},{8,9},{9,10},{10,1... | collective-permute-start | bytes 635912 | tf_op jit(solution)/shard_map/ppermute | solution.py:320
  (42 other events, 190.8 us)
Sparse Core Ops, SparseCore 0:
  36.3 30.9 all-gather.1
  175.6 28.1 reduce-scatter.1

commit v3 on v2

--- a/solution.py
+++ b/solution.py
@@ -329,14 +329,6 @@
     return lax.dynamic_index_in_dim(stack, index, 0, keepdims=False)
 
 
-def place(blocks):
-    shape = blocks[0][1].shape
-    out = jnp.zeros((len(blocks),) + shape, blocks[0][1].dtype)
-    for index, block in blocks:
-        out = lax.dynamic_update_index_in_dim(out, block, index, 0)
-    return out
-
-
 def after(value, *others):
     return lax.optimization_barrier((value, *others))[0]
 
@@ -368,47 +360,32 @@
     return [swap(block, core_bit) for block in blocks]
 
 
-def in_planes(blocks, others, cut):
-    me = lax.axis_index("dp")
-    bits = (0, x_bit, y_bit, x_bit | y_bit)
-    both = [(me ^ bit, block) for bit, block in zip(bits, blocks)]
-    both += [(me ^ bit ^ core_bit, block) for bit, block in zip(bits, others)]
-    outs = []
-    for begin, end in cut:
-        out = place([(index, block[:, begin:end]) for index, block in both])
-        outs.append(out.reshape((-1, end - begin)))
-    return outs
-
-
 def beside(line):
     return [line, swap(line, x_bit), swap(line, y_bit)]
 
 
+def across_halves(near):
+    _, along_x, along_y = near
+    half = along_x.shape[0] // 2
+    return [swap(along_y[:half], x_bit), swap(along_x[half:], y_bit)]
+
+
 def across_plane(near):
-    line, along_x, along_y = near
-    half = line.shape[0] // 2
-    across = [swap(along_y[:half], x_bit), swap(along_x[half:], y_bit)]
-    return [line, along_x, along_y, jnp.concatenate(across, axis=0)]
-
-
-def near_planes(line):
-    return beside(line) + [swap(line, x_bit | y_bit)]
+    return near + [jnp.concatenate(across_halves(near), axis=0)]
 
 
 def add_low(left, right):
     return (left.astype(jnp.float32) + right.astype(jnp.float32)).astype(jnp.bfloat16)
 
 
-def add_cores(block_of):
-    me = lax.axis_index("dp")
-    order = (x_bit | y_bit, x_bit, y_bit, 0)
-    got = swap_cores([block_of(me ^ bits ^ core_bit) for bits in order])
-    return [add_low(block_of(me ^ bits), term) for bits, term in zip(order, got)]
-
-
-def add_across(across, to_x, to_y):
+def halves_across(across):
     half = across.shape[0] // 2
-    from_x, from_y = swap(across[:half], x_bit), swap(across[half:], y_bit)
+    return [swap(across[:half], x_bit), swap(across[half:], y_bit)]
+
+
+def add_across(halves, to_x, to_y):
+    from_x, from_y = halves
+    half = from_x.shape[0]
     to_y = jnp.concatenate([add_low(to_y[:half], from_x), to_y[half:]], axis=0)
     to_x = jnp.concatenate([to_x[:half], add_low(to_x[half:], from_y)], axis=0)
     return to_x, to_y
@@ -432,28 +409,105 @@
     return sum_parts(deal_line(line.reshape((size, -1) + line.shape[1:])))
 
 
-def sum_everywhere(value):
-    for bit in (core_bit, x_bit, y_bit):
-        value = value + swap(value, bit)
-    bit = 1
-    while bit < lax.axis_size("blk"):
-        value = value + swap_line(value, bit)
-        bit *= 2
-    return value
-
-
 def contract(left, right, left_axis, right_axis):
     return lax.dot_general(
         left, right, (((left_axis,), (right_axis,)), ((), ())), preferred_element_type=jnp.float32
     )
 
 
+tile_cols = 512
+far_first = (x_bit | y_bit, x_bit, y_bit, 0)
+
+
+def run_kernel(kernel, name, micros, place_here, operands, far, outputs, far_outputs, scratch=(), copies=1):
+    near_spec, far_spec = pl.BlockSpec(memory_space=pltpu.VMEM), pl.BlockSpec(memory_space=pl.ANY)
+    return pl.pallas_call(
+        kernel,
+        out_shape=[jax.ShapeDtypeStruct(shape, dtype) for shape, dtype in (*outputs, *far_outputs)],
+        in_specs=[pl.BlockSpec(memory_space=pltpu.SMEM)] + [near_spec] * len(operands) + [far_spec] * len(far),
+        out_specs=[near_spec] * len(outputs) + [far_spec] * len(far_outputs),
+        scratch_shapes=[pltpu.VMEM(shape, dtype) for shape, dtype in scratch]
+        + [pltpu.SemaphoreType.DMA((copies,))],
+        compiler_params=pltpu.CompilerParams(vmem_limit_bytes=52 * 2**20),
+        cost_estimate=pl.CostEstimate(
+            flops=int(micros * 1.1e9), bytes_accessed=int(micros * 3.6e6), transcendentals=0
+        ),
+        name=name,
+    )(place_here, *operands, *far)
+
+
+class Copies:
+    def __init__(self, semaphores):
+        self.semaphores, self.used = semaphores, 0
+
+    def start(self, source, target):
+        copy = pltpu.make_async_copy(source, target, self.semaphores.at[self.used])
+        self.used += 1
+        copy.start()
+        return copy
+
+
+def wait_all(copies):
+    for copy in copies:
+        copy.wait()
+
+
+def normalize(value):
+    center = value - jnp.mean(value, axis=-1, keepdims=True)
+    spread = jnp.mean(center * center, axis=-1, keepdims=True)
+    scale = lax.rsqrt(spread + epsilon)
+    return center * scale, scale
+
+
+def normalize_back(normed, scale, grad, gain):
+    inner = grad * gain
+    middle = jnp.mean(inner, axis=-1, keepdims=True)
+    along = jnp.mean(inner * normed, axis=-1, keepdims=True)
+    return scale * (inner - middle - normed * along), jnp.sum(grad * normed, axis=0, keepdims=True)
+
+
+def block_indices(place_ref):
+    me = place_ref[0]
+    return [me ^ bits ^ core_bit for bits in far_first], [me ^ bits for bits in far_first]
+
+
+near_first = (0, x_bit, y_bit, x_bit | y_bit)
+
+
+def fill_planes(copies, place_ref, blocks, cols, out_ref):
+    bits = near_first + tuple(bit | core_bit for bit in near_first)
+    started = []
+    for bit, block in zip(bits, blocks):
+        rows = block.shape[0]
+        begin = pl.multiple_of((place_ref[0] ^ bit) * rows, rows)
+        started.append(copies.start(block.at[:, cols], out_ref.at[pl.ds(begin, rows), :]))
+    return started
+
+
+def before(place_ref, steps, size):
+    return lax.rem(place_ref[1] - steps + size, size)
+
+
 def attend_kernel(
-    heads, head_size, qkv_ref, diagonal_ref, doc_col_ref, doc_row_ref, scale_ref, probs_ref, attention_ref, scaled_ref, bias
+    heads, head_size, place_ref, gain_ref, diagonal_ref, doc_col_ref, doc_row_ref, scale_ref, tokens_ref, *refs
 ):
-    length = qkv_ref.shape[0]
+    parts, refs = refs[:8], refs[8:]
+    w_ref, qkv_ref, normed_ref, attention_ref, scaled_ref, probs_out, bias, probs_ref, semaphores = refs
+    copies = Copies(semaphores)
+    last = parts[0].shape[1]
+    arriving = fill_planes(copies, place_ref, parts, slice(last - w_ref.shape[1], last), w_ref)
+    leaving = []
+    length = tokens_ref.shape[0]
     blocks = length // lanes
     width = heads * head_size
+    for block in range(blocks):
+        rows = slice(block * lanes, (block + 1) * lanes)
+        normed, _ = normalize(tokens_ref[rows, :].astype(jnp.float32))
+        normed_ref[rows, :] = (normed * gain_ref[...]).astype(jnp.bfloat16)
+    wait_all(arriving)
+    projected = contract(normed_ref[...], w_ref[...], 1, 0)
+    qkv_ref[:, :width] = (projected[:, :width] * query_scale).astype(jnp.bfloat16)
+    qkv_ref[:, width:] = projected[:, width:].astype(jnp.bfloat16)
     for head in range(heads):
         for step in range(2 * blocks - 1):
             window = diagonal_ref[head : head + 1, step * lanes : (step + 2) * lanes]
@@ -463,50 +517,175 @@
         low = head * head_size
         keys = qkv_ref[:, width + low : width + low + head_size]
         values = qkv_ref[:, 2 * width + low : 2 * width + low + head_size]
+        all_scores = contract(qkv_ref[:, low : low + head_size], keys, 1, 1)
         for block in range(blocks):
             rows = slice(block * lanes, (block + 1) * lanes)
             first = (blocks - 1 - block) * lanes
-            scores = contract(qkv_ref[rows, low : low + head_size], keys, 1, 1)
-            scores = scores + bias[:, first : first + length]
+            scores = all_scores[rows, :] + bias[:, first : first + length]
             same = doc_col_ref[rows, :] == doc_row_ref[...]
             scores = jnp.where(same, scores, masked_score)
             weights = jnp.exp(scores - jnp.max(scores, axis=1, keepdims=True))
             probs = weights * (1.0 / jnp.sum(weights, axis=1, keepdims=True))
             probs = probs.astype(jnp.bfloat16)
             probs_ref[head, rows, :] = probs
-            attention_ref[rows, low : low + head_size] = contract(probs, values, 1, 0)
+        leaving.append(copies.start(probs_ref.at[head], probs_out.at[head]))
+        attention_ref[:, low : low + head_size] = contract(probs_ref[head], values, 1, 0)
     scaled_ref[...] = (attention_ref[...] * scale_ref[...]).astype(jnp.bfloat16)
-
-
-def attend(qkv, diagonals, doc_col, doc_row, scale_cols, heads, head_size):
-    length, width = qkv.shape[0], heads * head_size
-    return pl.pallas_call(
-        functools.partial(attend_kernel, heads, head_size),
-        out_shape=(
-            jax.ShapeDtypeStruct((heads, length, length), jnp.bfloat16),
-            jax.ShapeDtypeStruct((length, width), jnp.float32),
-            jax.ShapeDtypeStruct((length, width), jnp.bfloat16),
-        ),
-        scratch_shapes=[pltpu.VMEM((lanes, 2 * length - lanes), jnp.float32)],
-        compiler_params=pltpu.CompilerParams(vmem_limit_bytes=40 * 2**20),
-        cost_estimate=pl.CostEstimate(
-            flops=4 * heads * length * length * head_size,
-            bytes_accessed=2 * heads * length * length,
-            transcendentals=heads * length * length,
-        ),
-        name="attend",
-    )(qkv, diagonals, doc_col, doc_row, scale_cols)
-
-
-def attend_back_kernel(
-    heads, head_size, qkv_ref, probs_ref, attention_ref, grad_ref, out_ref, diagonal_ref, delta_ref, sums
-):
+    wait_all(leaving)
+
+
+def forward_kernel(line, place_ref, *refs):
+    pieces, refs = refs[:line], refs[line:]
+    tokens_ref, gain_attn_ref, gain_mid_ref, gain_hidden_ref, cotangent_ref, *refs = refs
+    blocks, refs = refs[:8], refs[8:]
+    (attn_ref, middle_ref, normed_ref, mean_ref, scale_ref, activated_ref,
+     hidden_out, below_out, across_out, send_out, keep_out,
+     wout_ref, fc1_ref, hidden_ref, below_ref, grads_ref, semaphores) = refs
+    copies = Copies(semaphores)
+    part = pieces[0].shape[1]
+    hidden_width, width = fc1_ref.shape[1], wout_ref.shape[1]
+    wout_here = fill_planes(copies, place_ref, blocks, slice(hidden_width, hidden_width + width), wout_ref)
+    fc1_here = fill_planes(copies, place_ref, blocks, slice(0, hidden_width), fc1_ref)
+    leaving = []
+    wait_all(wout_here)
+    attn = jnp.zeros(attn_ref.shape, jnp.float32)
+    for steps in range(line):
+        rows = pl.ds(pl.multiple_of(before(place_ref, steps, line) * part, part), part)
+        attn = attn + contract(pieces[steps][...], wout_ref[rows, :], 1, 0)
+    attn_ref[...] = attn
+    normed, _ = normalize(attn)
+    middle = tokens_ref[...].astype(jnp.float32) + normed * gain_attn_ref[...]
+    middle_ref[...] = middle
+    normed, _ = normalize(middle)
+    normed = (normed * gain_mid_ref[...]).astype(jnp.bfloat16)
+    normed_ref[...] = normed
+    tiles = [slice(begin, begin + tile_cols) for begin in range(0, hidden_width, tile_cols)]
+    total = jnp.zeros(mean_ref.shape, jnp.float32)
+    wait_all(fc1_here)
+    for cols in tiles:
+        hidden = contract(normed, fc1_ref[:, cols], 1, 0)
+        below = 0.5 * (1.0 + lax.erf(hidden * (0.5**0.5)))
+        hidden_ref[:, cols] = hidden
+        below_ref[:, cols] = below
+        leaving.append(copies.start(hidden_ref.at[:, cols], hidden_out.at[:, cols]))
+        leaving.append(copies.start(below_ref.at[:, cols], below_out.at[:, cols]))
+        total = total + jnp.sum(hidden * below, axis=1, keepdims=True)
+    mean = total / hidden_width
+    total = jnp.zeros(mean_ref.shape, jnp.float32)
+    for cols in tiles:
+        center = hidden_ref[:, cols] * below_ref[:, cols] - mean
+        total = total + jnp.sum(center * center, axis=1, keepdims=True)
+    scale = lax.rsqrt(total / hidden_width + epsilon)
+    mean_ref[...] = mean
+    scale_ref[...] = scale
+    for cols in tiles:
+        center = hidden_ref[:, cols] * below_ref[:, cols] - mean
+        activated_ref[:, cols] = (center * scale * gain_hidden_ref[:, cols]).astype(jnp.bfloat16)
+    size = grads_ref.shape[1]
+    sent, kept = block_indices(place_ref)
+    outs = [across_out] + [send_out.at[slot] for slot in range(3)] + [keep_out.at[slot] for slot in range(4)]
+    for slot, (index, out) in enumerate(zip(sent + kept, outs)):
+        cols = pl.ds(pl.multiple_of(index * size, lanes), size)
+        grads_ref[slot] = contract(activated_ref[:, cols], cotangent_ref[...], 0, 0).astype(jnp.bfloat16)
+        leaving.append(copies.start(grads_ref.at[slot], out))
+    wait_all(leaving)
+
+
+def backward_kernel(line, place_ref, *refs):
+    pieces, refs = refs[:line], refs[line:]
+    (cotangent_ref, attn_ref, middle_ref, normed_ref, mean_ref, scale_ref, gain_attn_ref, gain_mid_ref,
+     gain_hidden_ref, head_scale_ref, *refs) = refs
+    first_blocks, second_blocks, refs = refs[:8], refs[8:16], refs[16:]
+    hidden_in, below_in, activated_in, *refs = refs
+    mixed_ref, d_middle_ref, d_hidden_gain_ref, d_mid_gain_ref, d_attn_gain_ref, *refs = refs
+    grads, refs = refs[:line], refs[line:]
+    (send_out, keep_out, wout_ref, fc1_ref, fc2_ref, hidden_ref, below_ref, activated_ref, inner_ref, fc1_grad,
+     out_grad, semaphores) = refs
+    copies = Copies(semaphores)
+    part = pieces[0].shape[1]
+    hidden_width, width = fc1_ref.shape[1], wout_ref.shape[1]
+    hidden_here = [copies.start(hidden_in, hidden_ref), copies.start(below_in, below_ref)]
+    fc2_here = fill_planes(copies, place_ref, second_blocks, slice(0, width), fc2_ref)
+    fc1_here = fill_planes(copies, place_ref, first_blocks, slice(0, hidden_width), fc1_ref)
+    activated_here = copies.start(activated_in, activated_ref)
+    wout_here = fill_planes(
+        copies, place_ref, first_blocks, slice(hidden_width, hidden_width + width), wout_ref
+    )
+    grad_in = cotangent_ref[...]
+    mean, scale = mean_ref[...], scale_ref[...]
+    tiles = [slice(begin, begin + tile_cols) for begin in range(0, hidden_width, tile_cols)]
+    wait_all(hidden_here + fc2_here)
+    total = jnp.zeros(mean.shape, jnp.float32)
+    along = jnp.zeros(mean.shape, jnp.float32)
+    for cols in tiles:
+        d_activated = contract(grad_in, fc2_ref[cols, :], 1, 1)
+        normed = (hidden_ref[:, cols] * below_ref[:, cols] - mean) * scale
+        d_hidden_gain_ref[:, cols] = jnp.sum(d_activated * normed, axis=0, keepdims=True)
+        inner = d_activated * gain_hidden_ref[:, cols]
+        inner_ref[:, cols] = inner
+        total = total + jnp.sum(inner, axis=1, keepdims=True)
+        along = along + jnp.sum(inner * normed, axis=1, keepdims=True)
+    total, along = total / hidden_width, along / hidden_width
+    d_normed = jnp.zeros(middle_ref.shape, jnp.float32)
+    normed_mid = normed_ref[...].T
+    wait_all(fc1_here)
+    for cols in tiles:
+        hidden, below = hidden_ref[:, cols], below_ref[:, cols]
+        normed = (hidden * below - mean) * scale
+        slope = below + hidden * jnp.exp(-0.5 * hidden * hidden) * (1.0 / math.sqrt(2.0 * math.pi))
+        d_hidden = scale * (inner_ref[:, cols] - total - normed * along) * slope
+        d_hidden = d_hidden.astype(jnp.bfloat16)
+        fc1_grad[:, cols] = contract(normed_mid, d_hidden, 1, 0).astype(jnp.bfloat16)
+        d_normed = d_normed + contract(d_hidden, fc1_ref[:, cols], 1, 1)
+    size = send_out.shape[1]
+    sent, kept = block_indices(place_ref)
+    outs = [send_out.at[slot] for slot in range(4)] + [keep_out.at[slot] for slot in range(4)]
+    places = [pl.ds(pl.multiple_of(index * size, size), size) for index in sent + kept]
+    leaving = [
+        copies.start(fc1_grad.at[rows, :], out.at[:, :hidden_width]) for rows, out in zip(places, outs)
+    ]
+    normed, scale = normalize(middle_ref[...])
+    d_value, d_mid_gain_ref[...] = normalize_back(normed, scale, d_normed, gain_mid_ref[...])
+    d_middle = grad_in.astype(jnp.float32) + d_value
+    d_middle_ref[...] = d_middle
+    normed, scale = normalize(attn_ref[...])
+    d_value, d_attn_gain_ref[...] = normalize_back(normed, scale, d_middle, gain_attn_ref[...])
+    d_attn = d_value.astype(jnp.bfloat16)
+    wait_all(wout_here)
+    for steps in range(line):
+        owner = before(place_ref, steps, line)
+        rows = pl.ds(pl.multiple_of(owner * part, part), part)
+        d_scaled = contract(d_attn, wout_ref[rows, :], 1, 1)
+        grads[steps][...] = (d_scaled * head_scale_ref[pl.ds(owner, 1), :]).astype(jnp.bfloat16)
+        out_grad[rows, :] = contract(pieces[steps][...], d_attn, 0, 0).astype(jnp.bfloat16)
+    leaving += [
+        copies.start(out_grad.at[rows, :], out.at[:, hidden_width:]) for rows, out in zip(places, outs)
+    ]
+    activated_here.wait()
+    mixed = middle_ref[...] + contract(activated_ref[...], fc2_ref[...], 1, 0)
+    mixed_ref[...] = mixed.astype(jnp.bfloat16)
+    wait_all(leaving)
+
+
+def attend_back_kernel(heads, head_size, line, place_ref, *refs):
+    pieces, refs = refs[:line], refs[line:]
+    (qkv_ref, attention_ref, probs_in, normed_in, w_in,
+     send_ref, keep_ref, diagonal_ref, delta_ref, gain_ref, d_normed_out,
+     grad_ref, out_ref, w_grad, sums, probs_ref, normed_ref, w_ref, d_normed_ref, semaphores) = refs
+    copies = Copies(semaphores)
+    probs_here = [copies.start(probs_in.at[head], probs_ref.at[head]) for head in range(heads)]
+    rest_here = [copies.start(w_in, w_ref), copies.start(normed_in, normed_ref)]
     length = qkv_ref.shape[0]
     blocks = length // lanes
     width = heads * head_size
+    rows_here = pieces[0].shape[0]
+    for steps in range(line):
+        owner = lax.rem(place_ref[1] + steps, line)
+        grad_ref[pl.ds(pl.multiple_of(owner * rows_here, rows_here), rows_here), :] = pieces[steps][...]
     diagonal_ref[...] = jnp.zeros_like(diagonal_ref)
     for head in range(heads):
         sums[...] = jnp.zeros_like(sums)
+        probs_here[head].wait()
         low = head * head_size
         keys = qkv_ref[:, width + low : width + low + head_size]
         values = qkv_ref[:, 2 * width + low : 2 * width + low + head_size]
@@ -518,8 +697,8 @@
             queries = qkv_ref[rows, low : low + head_size]
             grad = grad_ref[rows, low : low + head_size]
             probs = probs_ref[head, rows, :]
-            part = grad.astype(jnp.float32) * attention_ref[rows, low : low + head_size]
-            delta = jnp.sum(part, axis=1, keepdims=True)
+            product = grad.astype(jnp.float32) * attention_ref[rows, low : low + head_size]
+            delta = jnp.sum(product, axis=1, keepdims=True)
             delta_ref[rows, head : head + 1] = delta
             d_scores = probs.astype(jnp.float32) * (contract(grad, values, 1, 1) - delta)
             sums[:, first : first + length] += d_scores
@@ -541,26 +720,19 @@
             diagonal_ref[head : head + 1, step * lanes : (step + 2) * lanes] += jnp.sum(
                 window, axis=0, keepdims=True
             )
-
-
-def attend_back(qkv, probs, attention, grad, heads, head_size):
-    length, width = qkv.shape[0], heads * head_size
-    return pl.pallas_call(
-        functools.partial(attend_back_kernel, heads, head_size),
-        out_shape=(
-            jax.ShapeDtypeStruct((length, 3 * width), jnp.bfloat16),
-            jax.ShapeDtypeStruct((heads, 2 * length), jnp.float32),
-            jax.ShapeDtypeStruct((length, heads), jnp.float32),
-        ),
-        scratch_shapes=[pltpu.VMEM((lanes, 2 * length - lanes), jnp.float32)],
-        compiler_params=pltpu.CompilerParams(vmem_limit_bytes=40 * 2**20),
-        cost_estimate=pl.CostEstimate(
-            flops=8 * heads * length * length * head_size,
-            bytes_accessed=2 * heads * length * length,
-            transcendentals=0,
-        ),
-        name="attend_back",
-    )(qkv, probs, attention, grad)
+    wait_all(rest_here)
+    d_normed_ref[...] = contract(out_ref[...], w_ref[...], 1, 1).astype(jnp.bfloat16)
+    leaving = copies.start(d_normed_ref, d_normed_out)
+    for block in range(normed_ref.shape[1] // lanes):
+        cols = slice(block * lanes, (block + 1) * lanes)
+        grad = contract(normed_ref[:, cols], out_ref[...], 0, 0)
+        gain_ref[cols, :] = jnp.sum(grad * w_ref[cols, :].astype(jnp.float32), axis=1, keepdims=True)
+        w_grad[cols, :] = grad.astype(jnp.bfloat16)
+    size = send_ref.shape[1]
+    for indices, to_ref in zip(block_indices(place_ref), (send_ref, keep_ref)):
+        for slot, index in enumerate(indices):
+            to_ref[slot] = w_grad[pl.ds(pl.multiple_of(index * size, size), size), :]
+    leaving.wait()
 
 
 def by_heads(
@@ -599,13 +771,10 @@
     )
     first_pieces = deal_line(jnp.concatenate([shared, by_head], axis=2))
     first_line = in_line(first_pieces)
-    row_tokens = lax.all_gather(after(tokens[0], *first_pieces[1:]), "blk", axis=0, tiled=True)
+    row_tokens = lax.all_gather(after(tokens[0], first_line), "blk", axis=0, tiled=True)
     second_pieces = turns(after(w_fc2, first_line))
-    first_planes = across_plane(beside(first_line))
-    first_others = swap_cores(first_planes)
-    fc1_all, wout_all, wqkv_part = in_planes(
-        first_planes, first_others, [(0, hidden_width), (hidden_width, summed), (summed, summed + 3 * part)]
-    )
+    first_planes = across_plane(all_after(beside(first_line), *second_pieces[1:]))
+    first_others = swap_cores(first_planes[:3] + [after(first_planes[3], row_tokens)])
     second_near = beside(after(in_line(second_pieces), *first_planes))
 
     ends = jnp.cumsum(lengths[0])
@@ -621,124 +790,215 @@
     scale_cols = jnp.repeat(head_scale, head_size)
     head_cols = lax.dynamic_slice_in_dim(scale_cols, here * part, part, 0)[None, :]
 
-    row_in = row_tokens.astype(jnp.float32)
-    normed_row = layer_norm(row_in, gain_in).astype(jnp.bfloat16)
-    projected = jnp.dot(normed_row, wqkv_part, preferred_element_type=jnp.float32)
-    column_scale = jnp.where(jnp.arange(3 * part) < part, query_scale, 1.0)
-    qkv = (projected * column_scale).astype(jnp.bfloat16)
-    probs, attention, scaled_part = attend(
-        qkv, diagonals, documents[:, None], documents[None, :], head_cols, heads, head_size
-    )
-
-    def arrival(stack):
-        return jnp.concatenate(
-            [pick(stack, lax.rem(here - steps + line_size, line_size)) for steps in range(line_size)], axis=0
-        )
+    low, wide = jnp.bfloat16, jnp.float32
+    planes = lax.axis_size("dp")
+    place_here = jnp.stack([lax.axis_index("dp"), here]).astype(jnp.int32)
+    wqkv_part, qkv, normed_row, attention, scaled_part, probs = run_kernel(
+        functools.partial(attend_kernel, heads, head_size),
+        "attend",
+        13,
+        place_here,
+        (gain_in[None], diagonals, documents[:, None], documents[None, :], head_cols, row_tokens),
+        (*first_planes, *first_others),
+        [
+            ((width, 3 * part), low),
+            ((row_len, 3 * part), low),
+            ((row_len, width), low),
+            ((row_len, part), wide),
+            ((row_len, part), low),
+        ],
+        [((heads, row_len, row_len), low)],
+        [((lanes, 2 * row_len - lanes), wide), ((heads, row_len, row_len), low)],
+        8 + heads,
+    )
 
     dealt = deal_line(scaled_part.reshape(line_size, rows_here, part))
-    scaled = jnp.concatenate(dealt, axis=1)
-    wout_here = arrival(wout_all.reshape(line_size, part, width))
-    residual_in = tokens[0].astype(jnp.float32)
-    attn_out = jnp.dot(scaled, wout_here, preferred_element_type=jnp.float32)
-    normed_attn, norm_attn_back = jax.vjp(layer_norm, attn_out, gain_attn)
-    middle = residual_in + normed_attn
-    normed_mid_f, norm_mid_back = jax.vjp(layer_norm, middle, gain_ffn_in)
-    normed_mid = normed_mid_f.astype(jnp.bfloat16)
-    hidden = jnp.dot(normed_mid, fc1_all, preferred_element_type=jnp.float32)
-    second_planes = across_plane(all_after(second_near, *first_others))
-    (fc2_all,) = in_planes(second_planes, swap_cores(second_planes), [(0, width)])
-    activated_f, hidden_back = jax.vjp(hidden_norm, hidden, gain_hidden)
-    activated = activated_f.astype(jnp.bfloat16)
-    mixed = (middle + jnp.dot(activated, fc2_all, preferred_element_type=jnp.float32)).astype(
-        jnp.bfloat16
-    )
-
-    def blocks_of(grad):
-        stack = grad.astype(jnp.bfloat16).reshape((lax.axis_size("dp"), -1) + grad.shape[1:])
-        return lambda index: pick(stack, index)
-
+    second_halves = across_halves(all_after(second_near, scaled_part))
+    dealt[0] = after(dealt[0], *second_halves)
+    second_planes = second_near + [jnp.concatenate(second_halves, axis=0)]
+    second_others = swap_cores(all_after(second_planes, *dealt[1:]))
     grad_in = cotangent[0]
-    second = add_cores(blocks_of(column_product(activated, grad_in)))
-    d_activated = times_transpose(grad_in, fc2_all)
-    d_hidden_f, grad_gain_hidden = hidden_back(d_activated)
-    d_hidden = after(d_hidden_f.astype(jnp.bfloat16), *second)
-    third = add_cores(blocks_of(column_product(normed_mid, d_hidden)))
-    d_mid_part, grad_gain_ffn_in = norm_mid_back(times_transpose(d_hidden, fc1_all))
-    d_middle = grad_in.astype(jnp.float32) + d_mid_part
-    d_attn_f, grad_gain_attn = norm_attn_back(d_middle)
-    d_attn_out = d_attn_f.astype(jnp.bfloat16)
-
-    scale_here = arrival(scale_cols.reshape(line_size, part))
-    d_scaled = times_transpose(d_attn_out, wout_here)
-    second_x, second_y = add_across(*second[:3])
-    d_attention = (d_scaled * scale_here).astype(jnp.bfloat16)
-    pieces = [(here, d_attention[:, :part])]
-    for steps in range(1, line_size):
-        piece = d_attention[:, steps * part : (steps + 1) * part]
-        pieces.append((lax.rem(here + steps, line_size), turn(piece, line_size - steps)))
-    grad_row = place(pieces).reshape(row_len, part)
-
-    out_grad = blocks_of(column_product(scaled, d_attn_out))
-    per_part = lax.axis_size("dp") // line_size
-
-    def out_block(index):
-        owner = lax.div(index, per_part)
-        steps = lax.rem(here - owner + line_size, line_size)
-        return out_grad(steps * per_part + lax.rem(index, per_part))
-
-    second_x, second_y = all_after([second_x, second_y], d_attention)
-    second_line = add_planes(second_x, second_y, second[3])
-    d_projected, diagonal_sums_here, deltas = attend_back(qkv, probs, attention, grad_row, heads, head_size)
-    d_normed = times_transpose(d_projected, wqkv_part)
-    d_normed_low = lax.psum_scatter(
-        d_normed.astype(jnp.bfloat16), "blk", scatter_dimension=0, tiled=True
-    )
+    gains = (gain_attn[None], gain_ffn_in[None], gain_hidden[None])
+    block_rows, hidden_rows = width // planes, hidden_width // planes
+    *kept, activated, hidden, below, across_fc2, send_fc2, keep_fc2 = run_kernel(
+        functools.partial(forward_kernel, line_size),
+        "feed_forward",
+        9,
+        place_here,
+        (*dealt, tokens[0], *gains, grad_in),
+        (*first_planes, *first_others),
+        [
+            ((rows_here, width), wide),
+            ((rows_here, width), wide),
+            ((rows_here, width), low),
+            ((rows_here, 1), wide),
+            ((rows_here, 1), wide),
+            ((rows_here, hidden_width), low),
+        ],
+        [
+            ((rows_here, hidden_width), wide),
+            ((rows_here, hidden_width), wide),
+            ((hidden_rows, width), low),
+            ((3, hidden_rows, width), low),
+            ((4, hidden_rows, width), low),
+        ],
+        [
+            ((width, width), low),
+            ((width, hidden_width), low),
+            ((rows_here, hidden_width), wide),
+            ((rows_here, hidden_width), wide),
+            ((8, hidden_rows, width), low),
+        ],
+        24 + 2 * (hidden_width // tile_cols),
+    )
+    across_fc2, send_fc2 = all_after([across_fc2, send_fc2], *second_others)
+    second_across = add_low(keep_fc2[0], swap(across_fc2, core_bit))
+    halves = halves_across(second_across)
+    second_rest = add_low(keep_fc2[1:], swap(send_fc2, core_bit))
+    (
+        mixed,
+        d_middle,
+        grad_gain_hidden,
+        grad_gain_ffn_in,
+        grad_gain_attn,
+        *grad_pieces,
+        send_first,
+        keep_first,
+    ) = run_kernel(
+        functools.partial(backward_kernel, line_size),
+        "feed_forward_back",
+        13,
+        place_here,
+        (
+            *dealt,
+            after(grad_in, second_across),
+            *kept,
+            *gains,
+            scale_cols.reshape(line_size, part),
+        ),
+        (*first_planes, *first_others, *second_planes, *second_others, hidden, below, activated),
+        [
+            ((rows_here, width), low),
+            ((rows_here, width), wide),
+            ((1, hidden_width), wide),
+            ((1, width), wide),
+            ((1, width), wide),
+            *[((rows_here, part), low)] * line_size,
+        ],
+        [((4, block_rows, summed), low), ((4, block_rows, summed), low)],
+        [
+            ((width, width), low),
+            ((width, hidden_width), low),
+            ((hidden_width, width), low),
+            ((rows_here, hidden_width), wide),
+            ((rows_here, hidden_width), wide),
+            ((rows_here, hidden_width), low),
+            ((rows_here, hidden_width), wide),
+            ((width, hidden_width), low),
+            ((width, width), low),
+        ],
+        3 + 24 + 16,
+    )
+
+    grad_pieces = all_after(grad_pieces, *halves)
+    grad_pieces = grad_pieces[:1] + [
+        turn(piece, line_size - steps) for steps, piece in enumerate(grad_pieces[1:], 1)
+    ]
+    got_first = swap(after(send_first, *halves), core_bit)
+    first = add_low(keep_first, got_first)
+    grad_pieces[0] = after(grad_pieces[0], got_first)
+    second_x, second_y = add_across(halves, second_rest[0], second_rest[1])
+    second_got = [swap(second_x, x_bit), swap(second_y, y_bit)]
+    send_qkv, keep_qkv, diagonal_sums_here, deltas, gain_sums, d_normed = run_kernel(
+        functools.partial(attend_back_kernel, heads, head_size, line_size),
+        "attend_back",
+        12,
+        place_here,
+        (*grad_pieces, qkv, attention),
+        (probs, normed_row, wqkv_part),
+        [
+            ((4, block_rows, 3 * part), low),
+            ((4, block_rows, 3 * part), low),
+            ((heads, 2 * row_len), wide),
+            ((row_len, heads), wide),
+            ((width, 1), wide),
+        ],
+        [((row_len, width), low)],
+        [
+            ((row_len, part), low),
+            ((row_len, 3 * part), low),
+            ((width, 3 * part), low),
+            ((lanes, 2 * row_len - lanes), wide),
+            ((heads, row_len, row_len), low),
+            ((row_len, width), low),
+            ((width, 3 * part), low),
+            ((row_len, width), low),
+        ],
+        heads + 3,
+    )
+    d_normed_low = lax.psum_scatter(d_normed, "blk", scatter_dimension=0, tiled=True)
     d_normed_here = d_normed_low.astype(jnp.float32)
 
-    qkv_grad = blocks_of(column_product(normed_row, d_projected))
-
-    def small_block(index):
-        return jnp.concatenate([out_block(index), qkv_grad(index)], axis=1)
-
-    fourth = add_cores(small_block)
-    first = [jnp.concatenate(pair, axis=1) for pair in zip(third, fourth)]
-    first[0] = after(first[0], second_line)
-    first_x, first_y = add_across(*first[:3])
-    grad_fc2 = add_line(after(second_line, d_projected))
-    first_x, first_y = all_after([first_x, first_y], d_normed_low)
-    first_line = add_planes(first_x, first_y, first[3])
-    dealt = deal_line(first_line.reshape((line_size, shard_rows) + first_line.shape[1:]))
-    first_grad = sum_parts([piece[:, :summed] for piece in dealt])
-    grad_fc1, grad_out = first_grad[:, :hidden_width], first_grad[:, hidden_width:]
-    grad_qkv = in_line([piece[:, summed:].astype(jnp.float32) for piece in dealt])
+    second_got = all_after(second_got, d_normed)
+    second_line = sum_parts([second_rest[2], *second_got]).astype(low)
+    grad_gain_in = gain_sums[:, 0] / gain_in
+    d_table = lax.dot_general(
+        diagonal_sums_here, selector, (((1,), (1,)), ((), ())), precision=highest
+    )
+    small = (gain_sums[:, 0], grad_gain_attn[0], grad_gain_ffn_in[0], grad_gain_hidden[0])
+    own_small = (jnp.sum(deltas, axis=0), d_table)
+    sizes = [math.prod(value.shape) for value in small]
+    flat = jnp.concatenate([value.reshape(-1) for value in small + own_small])
+    tail_cols, pack_cols = 3 * part, summed + 3 * part
+    flat = jnp.pad(flat, (0, -flat.shape[0] % tail_cols)).reshape(-1, tail_cols)
+    terms = flat.astype(low)
+    got = swap(send_qkv, core_bit)
+    halves = halves_across(after(first[0], second_line, got))
+    first_x, first_y = add_across(halves, first[1], first[2])
+    last = add_low(keep_qkv, got)
+    terms = add_low(terms, swap(terms, core_bit))
+    last_got = [
+        swap(jnp.concatenate([last[slot], terms], axis=0), bits) for slot, bits in enumerate(far_first[:3])
+    ]
+    last_line = sum_parts([last[3]] + [piece[:block_rows] for piece in last_got]).astype(low)
+    plane_sums = [piece[block_rows:].astype(wide) for piece in last_got]
+    flat = (terms.astype(wide) + plane_sums[1]) + (plane_sums[2] + plane_sums[0])
+    flat = flat.reshape(-1)
+    flat = jnp.pad(flat, (0, -flat.shape[0] % (2 * pack_cols))).reshape(-1, pack_cols).astype(low)
+    first_x, first_y = all_after([first_x, first_y], *last_got)
+    first_got = [swap(first_x, x_bit), swap(first_y, y_bit)]
+    first_line = sum_parts([first[3], *first_got]).astype(low)
+    second_line = after(second_line, *last_got, *halves)
+    second_dealt = deal_line(second_line.reshape((line_size, -1, width)))
+    grad_fc2 = sum_parts(second_dealt)
+    both_lines = after(jnp.concatenate([first_line, last_line], axis=1), d_normed_low, *second_dealt[1:])
+    both_lines = both_lines.reshape(line_size, shard_rows, pack_cols)
+    spread = jnp.broadcast_to(flat[None], (line_size,) + flat.shape)
+    dealt_back = deal_line(jnp.concatenate([both_lines, spread], axis=1))
+    flats = [piece[shard_rows:].astype(wide).reshape(-1) for piece in dealt_back]
+    common = sum(sizes)
+    totals = [flat[:common] for flat in flats]
+    while len(totals) > 1:
+        half = len(totals) // 2
+        totals = [totals[step] + totals[step + half] for step in range(half)]
+    owned = common + heads + heads * bucket_count
+    by_owner = in_line([flat[None, common:owned] for flat in flats])
+    grad_scale = by_owner[:, :heads].reshape(-1)
+    d_bias = by_owner[:, heads:].reshape(all_heads, bucket_count)
+    dealt_back = [piece[:shard_rows] for piece in dealt_back]
+    grad_fc1 = sum_parts([piece[:, :hidden_width] for piece in dealt_back])
+    grad_out = sum_parts([piece[:, hidden_width:summed] for piece in dealt_back])
+    grad_qkv = in_line([piece[:, summed:].astype(jnp.float32) for piece in dealt_back])
     grad_qkv = grad_qkv.reshape(line_size, shard_rows, 3, part).transpose(1, 2, 0, 3)
     grad_qkv = grad_qkv.reshape(shard_rows, 3 * width)
 
-    _, gain_in_back = jax.vjp(lambda gain: layer_norm(row_in, gain), gain_in)
-    (grad_gain_in,) = gain_in_back(d_normed)
-    _, norm_in_back = jax.vjp(lambda value: layer_norm(value, gain_in), residual_in)
+    _, norm_in_back = jax.vjp(lambda value: layer_norm(value, gain_in), tokens[0].astype(jnp.float32))
     (d_input_part,) = norm_in_back(d_normed_here)
     grad_tokens = (d_middle + d_input_part).astype(jnp.bfloat16)[None]
 
-    d_table = lax.dot_general(
-        diagonal_sums_here, selector, (((1,), (1,)), ((), ())), precision=highest
-    )
-    d_bias = lax.dynamic_update_slice_in_dim(
-        jnp.zeros((all_heads, bucket_count), jnp.float32), d_table, here * heads, 0
-    )
-    scale_part = jnp.sum(deltas, axis=0)
-    grad_scale = lax.dynamic_update_slice_in_dim(
-        jnp.zeros((all_heads,), jnp.float32), scale_part, here * heads, 0
-    )
-    small = (grad_gain_in, grad_gain_attn, grad_gain_ffn_in, grad_gain_hidden, grad_scale, d_bias)
-    sizes = [math.prod(value.shape) for value in small]
-    flat = jnp.concatenate([value.reshape(-1) for value in small])
-    flat = jnp.pad(flat, (0, -flat.shape[0] % 1024)).reshape(-1, lanes)
-    flat = after(flat, grad_fc2, first_x, first_y)
-    flat = sum_everywhere(flat).reshape(-1)
     sums, begin = [], 0
-    for value, size in zip(small, sizes):
-        sums.append(flat[begin : begin + size].reshape(value.shape))
+    for size in sizes:
+        sums.append(totals[0][begin : begin + size])
         begin += size
     return (
         mixed[None],
@@ -747,12 +1007,12 @@
         grad_out,
         grad_fc1,
         grad_fc2,
-        sums[0],
+        sums[0] / gain_in,
         sums[1],
         sums[2],
         sums[3],
-        sums[4] / head_scale,
-        sums[5].T,
+        grad_scale / head_scale,
+        d_bias.T,
     )
 
 

time: 307 us -> 272 us (0.89)
  Pallas kernels: 15 us -> 61.4 us
  local copies, waits for them, and re-layouts: 53.8 us -> 20.9 us
  matrix products: 33.1 us -> 2.63 us
  other arithmetic: 34.2 us -> 21.3 us
  waiting for transfers between devices: 104 us -> 95.4 us
  starting transfers between devices: 45 us -> 49.5 us
    pallas_call x2 -> x4, Pallas kernels: 15 us -> 61.4 us  [run_kernel(): pl.pallas_call(kernel, out_shape=[jax.ShapeDtypeStruct(shape, dtype) for...]
    dot_general x12 -> x0, matrix products: 30.5 us -> none  [the longest x4 10.5 us: times_transpose(): lax.dot_general(left, matrix, (((1,), (1,)), ((), ())), preferred_element...]
    dynamic_update_slice x38 -> x0, local copies, waits for them, and re-layouts: 26.9 us -> none  [the longest x36 26.4 us: place(): out = lax.dynamic_update_index_in_dim(out, block, index, 0)]
    ppermute x39 -> x32, waiting for transfers between devices: 48.4 us -> 26.1 us  [swap(): return lax.ppermute(value, 'dp', [(i, i ^ bit) for i in range(size)])]
    ppermute x18, waiting for transfers between devices: 48.5 us -> 69.2 us  [turn(): lax.ppermute(value, 'blk', [(i, (i + steps) % size) for i in range(size)])]
    ppermute x2 -> x0, waiting for transfers between devices: 7.03 us -> none  [swap_line(): return lax.ppermute(value, 'blk', [(i, i ^ bit) for i in range(size)])]
    ppermute x18, starting transfers between devices: 19 us -> 25.7 us  [turn(): lax.ppermute(value, 'blk', [(i, (i + steps) % size) for i in range(size)])]
    slice x13 -> x8, local copies, waits for them, and re-layouts: 9.05 us -> 2.83 us  [the longest x4 2.12 us: across_halves(): return [swap(along_y[:half], x_bit), swap(along_x[half:], y_bit)]]
  transfers between devices with their start and end apart: 61 -> 52, of which waited for: 26 -> 25; matrix products, arithmetic and copies ran while one was open for 31% -> 12% of each run, Pallas kernels for 5% -> 23%
where the time goes in v3:
time: 272 us; the launch traced here: 266 us
  waiting for transfers between devices  95.4 us (35%)
  Pallas kernels  61.4 us (23%)
  starting transfers between devices  49.5 us (18%)
  other arithmetic  21.3 us (8%)
  local copies, waits for them, and re-layouts  20.9 us (8%)
  between operations  15.2 us (6%)
    ppermute x18, waiting for transfers between devices, turn(): lax.ppermute(value, 'blk', [(i, (i + steps) % size) for i in range(size)])  69.2 us
    pallas_call x4, Pallas kernels, run_kernel(): pl.pallas_call(kernel, out_shape=[jax.ShapeDtypeStruct(shape, dtype) for...  61.4 us
    ppermute x32, waiting for transfers between devices, swap(): return lax.ppermute(value, 'dp', [(i, i ^ bit) for i in range(size)])  26.1 us
    ppermute x18, starting transfers between devices, turn(): lax.ppermute(value, 'blk', [(i, (i + steps) % size) for i in range(size)])  25.7 us
    ppermute x32, starting transfers between devices, swap(): return lax.ppermute(value, 'dp', [(i, i ^ bit) for i in range(size)])  23.7 us
  transfers between devices with their start and end apart: 52, of which 25 were waited for; matrix products, arithmetic and copies ran while one was open for 12% of the time, Pallas kernels for 23%

profile of v3, /device:TPU:18, one launch (start us, length us, event | category | flops | bytes accessed | tf_op | source)
XLA Modules:
  0.0 266.2 jit_solution(14935487613277479671)
XLA Ops:
  7.3 1.1 reshape.189
  8.6 0.9 pad_maximum_fusion.11
  9.7 1.6 collective-permute-start
  11.6 1.3 collective-permute-start.2
  13.0 14.1 %collective-permute-done = bf16[24,4416]{1,0:T(8,128)(2,1)S(1)} collective-permute-done((bf16[24,4416]{1,0:T(8,128)(2,1)S(1)}, bf16[24,4416]{1,0:T(8,128)(2,1)S(1)}, u32[]{:S(2)}, u32[]{:S(2)}) %collective-permute-start) | collective-permute-done | bytes 212000 | tf_op jit(solution)/shard_map/ppermute | solution.py:320
  27.1 2.3 collective-permute-done.2
  30.5 1.5 collective-permute-start.4
  32.1 2.7 %collective-permute-start.5 = (bf16[96,768]{1,0:T(8,128)(2,1)S(1)}, bf16[96,768]{1,0:T(8,128)(2,1)S(1)}, u32[]{:S(2)}, u32[]{:S(2)}) collective-permute-start(bf16[96,768]{1,0:T(8,128)(2,1)S(1)} %copy-done.21), channel_id=1, source_target_pairs={{0,1},{1,2},{2,3},{3,0},{4,5},{5,6},{6,7},{7,4},{8,9},{9,10},{10,1... | collective-permute-start | bytes 442376 | tf_op jit(solution)/shard_map/ppermute | solution.py:320
  34.8 1.3 collective-permute-start.6
  36.3 4.6 %collective-permute-done.5 = bf16[96,768]{1,0:T(8,128)(2,1)S(1)} collective-permute-done((bf16[96,768]{1,0:T(8,128)(2,1)S(1)}, bf16[96,768]{1,0:T(8,128)(2,1)S(1)}, u32[]{:S(2)}, u32[]{:S(2)}) %collective-permute-start.5) | collective-permute-done | bytes 147488 | tf_op jit(solution)/shard_map/ppermute | solution.py:320
  41.0 4.5 %collective-permute-done.6 = bf16[96,768]{1,0:T(8,128)(2,1)S(1)} collective-permute-done((bf16[96,768]{1,0:T(8,128)(2,1)S(1)}, bf16[96,768]{1,0:T(8,128)(2,1)S(1)}, u32[]{:S(2)}, u32[]{:S(2)}) %collective-permute-start.6) | collective-permute-done | bytes 147488 | tf_op jit(solution)/shard_map/ppermute | solution.py:320
  45.4 10.6 %collective-permute-done.7 = bf16[96,768]{1,0:T(8,128)(2,1)S(1)} collective-permute-done((bf16[96,768]{1,0:T(8,128)(2,1)S(1)}, bf16[96,768]{1,0:T(8,128)(2,1)S(1)}, u32[]{:S(2)}, u32[]{:S(2)}) %collective-permute-start.7) | collective-permute-done | bytes 147488 | tf_op jit(solution)/shard_map/ppermute | solution.py:320
  56.0 1.0 slice.234
  57.1 2.9 %collective-permute-start.8 = (bf16[48,4416]{1,0:T(8,128)(2,1)S(1)}, bf16[48,4416]{1,0:T(8,128)(2,1)S(1)}, u32[]{:S(2)}, u32[]{:S(2)}) collective-permute-start(bf16[48,4416]{1,0:T(8,128)(2,1)S(1)} %slice.234), channel_id=1, source_target_pairs={{0,8},{4,12},{8,0},{12,4},{16,24},{20,28},{24,16},{28,20},{1,9},{5... | collective-permute-start | bytes 1271816 | tf_op jit(solution)/shard_map/ppermute | solution.py:315
  59.9 1.0 slice.235
  61.6 7.2 %collective-permute-done.8 = bf16[48,4416]{1,0:T(8,128)(2,1)S(1)} collective-permute-done((bf16[48,4416]{1,0:T(8,128)(2,1)S(1)}, bf16[48,4416]{1,0:T(8,128)(2,1)S(1)}, u32[]{:S(2)}, u32[]{:S(2)}) %collective-permute-start.8) | collective-permute-done | bytes 423968 | tf_op jit(solution)/shard_map/ppermute | solution.py:315
  69.6 3.8 %collective-permute-done.9 = bf16[48,4416]{1,0:T(8,128)(2,1)S(1)} collective-permute-done((bf16[48,4416]{1,0:T(8,128)(2,1)S(1)}, bf16[48,4416]{1,0:T(8,128)(2,1)S(1)}, u32[]{:S(2)}, u32[]{:S(2)}) %collective-permute-start.9) | collective-permute-done | bytes 423968 | tf_op jit(solution)/shard_map/ppermute | solution.py:315
  75.0 1.1 fusion.1.diagonal_ref
  77.0 13.1 %attend.1 = (bf16[768,576]{1,0:T(8,128)(2,1)}, bf16[768,576]{1,0:T(8,128)(2,1)}, bf16[768,768]{1,0:T(8,128)(2,1)}, f32[768,192]{1,0:T(8,128)S(1)}, bf16[768,192]...) custom-call(s32[2]{0:T(128)S(1)} %pad_add_fusion.place_ref, f32[1,768]{1,0:T(1,128)S(1)} %broadcast_in_dim.65.gain_ref, ...), custom_call_target="tpu_custom_call" | custom-call | flops 14300000256 | bytes 46800000 | tf_op jit(solution)/shard_map/attend/pallas_call | solution.py:424
  90.9 1.1 collective-permute-done.14.refs_23_
  92.2 1.7 collective-permute-start.16
  95.1 3.8 %collective-permute-start.19 = (bf16[192,192]{1,0:T(8,128)(2,1)S(1)}, bf16[192,192]{1,0:T(8,128)(2,1)S(1)}, u32[]{:S(2)}, u32[]{:S(2)}) collective-permute-start(bf16[192,192]{1,0:T(8,128)(2,1)S(1)} %get-tuple-element.179), channel_id=1, source_target_pairs={{0,2},{1,3},{2,0},{3,1},{4,6},{5,7},{6,4},{7,5},{8,10},{9,11},{10,... | collective-permute-start | bytes 221192 | tf_op jit(solution)/shard_map/ppermute | solution.py:320
  99.2 1.7 collective-permute-done.16
  100.9 1.1 collective-permute-done.17
  102.4 1.8 collective-permute-done.19.refs_2_
  105.3 10.3 %feed_forward.1 = (f32[192,768]{1,0:T(8,128)}, f32[192,768]{1,0:T(8,128)}, bf16[192,768]{1,0:T(8,128)(2,1)S(1)}, f32[192,1]{1,0:T(8,128)S(1)}, f32[192,1]{1,0:T(...) custom-call(s32[2]{0:T(128)S(1)} %pad_add_fusion.place_ref, ...), custom_call_target="tpu_custom_call" | custom-call | flops 9900000256 | bytes 32400000 | tf_op jit(solution)/shard_map/feed_forward/pallas_call | solution.py:424
  117.4 2.0 collective-permute-done.25
  119.4 1.2 fusion.8
  121.1 1.2 collective-permute-start.27
  122.3 24.3 %feed_forward_back.1 = (bf16[192,768]{1,0:T(8,128)(2,1)}, f32[192,768]{1,0:T(8,128)}, f32[1,3072]{1,0:T(1,128)S(1)}, f32[1,768]{1,0:T(1,128)S(1)}, f32[1,768]{1,...) custom-call(s32[2]{0:T(128)S(1)} %pad_add_fusion.place_ref, ...), custom_call_target="tpu_custom_call" | custom-call | flops 14300000256 | bytes 46800000 | tf_op jit(solution)/shard_map/feed_forward_back/pallas_call | solution.py:424
  147.4 2.5 collective-permute-start.29
  149.9 3.2 %collective-permute-start.30 = (bf16[192,192]{1,0:T(8,128)(2,1)S(1)}, bf16[192,192]{1,0:T(8,128)(2,1)S(1)}, u32[]{:S(2)}, u32[]{:S(2)}) collective-permute-start(bf16[192,192]{1,0:T(8,128)(2,1)S(1)} %get-tuple-element.115), channel_id=1, source_target_pairs={{0,2},{1,3},{2,0},{3,1},{4,6},{5,7},{6,4},{7,5},{8,10},{9,11},{10,... | collective-permute-start | bytes 221192 | tf_op jit(solution)/shard_map/ppermute | solution.py:320
  153.2 1.1 collective-permute-done.32
  157.5 1.7 collective-permute-start.33
  159.9 1.0 slice_bitcast_fusion
  161.4 13.7 %attend_back.1 = (bf16[4,96,576]{2,1,0:T(8,128)(2,1)S(1)}, bf16[4,96,576]{2,1,0:T(8,128)(2,1)}, f32[3,1536]{1,0:T(4,128)S(1)}, f32[768,3]{1,0:T(8,128)S(1)}, f32...) custom-call(s32[2]{0:T(128)S(1)} %pad_add_fusion.place_ref, bf16[192,192]{1,0:T(8,128)(2,1)S(1)} %get-tuple-element.113.refs_0_, ...), custom_call_target="tpu_custom_call" | custom-call | flops 13200000000 | bytes 43200000 | tf_op jit(solution)/shard_map/attend_back/pallas_call | solution.py:424
  175.2 2.0 slice_bitcast_fusion.3
  177.3 1.5 fusion.9
  180.0 2.3 fusion.7
  182.4 1.1 collective-permute-start.36
  183.5 1.7 collective-permute-start.37
  185.2 1.1 add_convert_fusion.2
  187.3 1.1 collective-permute-start.39
  188.3 1.3 collective-permute-start.40
  189.7 1.1 collective-permute-start.41
  190.8 4.2 %collective-permute-done.36 = bf16[48,3840]{1,0:T(8,128)(2,1)S(1)} collective-permute-done((bf16[48,3840]{1,0:T(8,128)(2,1)S(1)}, bf16[48,3840]{1,0:T(8,128)(2,1)S(1)}, u32[]{:S(2)}, u32[]{:S(2)}) %collective-permute-start.36) | collective-permute-done | bytes 368672 | tf_op jit(solution)/shard_map/ppermute | solution.py:315
  195.2 1.2 pad_maximum_fusion.2
  196.5 2.3 collective-permute-done.39
  198.7 1.3 collective-permute-done.40
  200.0 1.7 collective-permute-start.42
  203.1 1.4 reshape.195
  204.6 1.3 pad.11
  205.9 1.4 convert_element_type.303
  207.3 1.1 dynamic-slice_bitcast_fusion
  208.4 2.2 collective-permute-start.44
  211.2 1.2 collective-permute-start.46
  212.3 1.0 fusion.32
  213.4 7.3 %collective-permute-done.44 = bf16[96,768]{1,0:T(8,128)(2,1)S(1)} collective-permute-done((bf16[96,768]{1,0:T(8,128)(2,1)S(1)}, bf16[96,768]{1,0:T(8,128)(2,1)S(1)}, u32[]{:S(2)}, u32[]{:S(2)}) %collective-permute-start.44) | collective-permute-done | bytes 147488 | tf_op jit(solution)/shard_map/ppermute | solution.py:320
  221.5 1.7 fusion.22
  223.2 1.6 fusion.5
  225.6 3.6 %collective-permute-start.47 = (bf16[26,4416]{1,0:T(8,128)(2,1)S(1)}, bf16[26,4416]{1,0:T(8,128)(2,1)S(1)}, u32[]{:S(2)}, u32[]{:S(2)}) collective-permute-start(bf16[26,4416]{1,0:T(8,128)(2,1)S(1)} %get-tuple-element.158), channel_id=1, source_target_pairs={{0,1},{1,2},{2,3},{3,0},{4,5},{5,6},{6,7},{7,4},{8,9},{9,10},{10,1... | collective-permute-start | bytes 688904 | tf_op jit(solution)/shard_map/ppermute | solution.py:320
  230.0 1.0 fusion.20
  231.0 14.1 %collective-permute-done.48 = bf16[26,4416]{1,0:T(8,128)(2,1)S(1)} collective-permute-done((bf16[26,4416]{1,0:T(8,128)(2,1)S(1)}, bf16[26,4416]{1,0:T(8,128)(2,1)S(1)}, u32[]{:S(2)}, u32[]{:S(2)}) %collective-permute-start.48) | collective-permute-done | bytes 229664 | tf_op jit(solution)/shard_map/ppermute | solution.py:320
  245.1 8.1 %collective-permute-done.47 = bf16[26,4416]{1,0:T(8,128)(2,1)S(1)} collective-permute-done((bf16[26,4416]{1,0:T(8,128)(2,1)S(1)}, bf16[26,4416]{1,0:T(8,128)(2,1)S(1)}, u32[]{:S(2)}, u32[]{:S(2)}) %collective-permute-start.47) | collective-permute-done | bytes 229664 | tf_op jit(solution)/shard_map/ppermute | solution.py:320
  (238 shorter events, 29.9 us)
Async XLA Ops:
  7.2 67.8 %copy-start = (f32[513,12]{0,1:T(8,128)S(1)}, f32[513,12]{0,1:T(8,128)}, u32[]{:S(2)}) copy-start(f32[513,12]{0,1:T(8,128)} %param.26) | copy-start | bytes 73876
  7.2 67.0 %all-gather.2.cloned.1.call-start = ((), (), s32[]{:S(2)}) async-start(), calls=%async_computation.1 | async-start | bytes 1474560 | tf_op jit(solution)/shard_map/all_gather | solution.py:774
  9.7 17.5 %collective-permute-start = (bf16[24,4416]{1,0:T(8,128)(2,1)S(1)}, bf16[24,4416]{1,0:T(8,128)(2,1)S(1)}, u32[]{:S(2)}, u32[]{:S(2)}) collective-permute-start(bf16[24,4416]{1,0:T(8,128)(2,1)S(1)} %get-tuple-element.161), channel_id=1, source_target_pairs={{0,1},{1,2},{2,3},{3,0},{4,5},{5,6},{6,7},{7,4},{8,9},{9,10},{10,1... | collective-permute-start | bytes 635912 | tf_op jit(solution)/shard_map/ppermute | solution.py:320
  11.3 15.8 %collective-permute-start.1 = (bf16[24,4416]{1,0:T(8,128)(2,1)S(1)}, bf16[24,4416]{1,0:T(8,128)(2,1)S(1)}, u32[]{:S(2)}, u32[]{:S(2)}) collective-permute-start(bf16[24,4416]{1,0:T(8,128)(2,1)S(1)} %get-tuple-element.162), channel_id=1, source_target_pairs={{0,2},{1,3},{2,0},{3,1},{4,6},{5,7},{6,4},{7,5},{8,10},{9,11},{10,... | collective-permute-start | bytes 635912 | tf_op jit(solution)/shard_map/ppermute | solution.py:320
  11.6 17.8 %collective-permute-start.2 = (bf16[24,4416]{1,0:T(8,128)(2,1)S(1)}, bf16[24,4416]{1,0:T(8,128)(2,1)S(1)}, u32[]{:S(2)}, u32[]{:S(2)}) collective-permute-start(bf16[24,4416]{1,0:T(8,128)(2,1)S(1)} %get-tuple-element.163), channel_id=1, source_target_pairs={{0,3},{1,0},{2,1},{3,2},{4,7},{5,4},{6,5},{7,6},{8,11},{9,8},{10,9... | collective-permute-start | bytes 635912 | tf_op jit(solution)/shard_map/ppermute | solution.py:320
  29.9 44.3 %copy-start.15 = (bf16[96,4416]{1,0:T(8,128)(2,1)}, bf16[96,4416]{1,0:T(8,128)(2,1)S(1)}, u32[]{:S(2)}) copy-start(bf16[96,4416]{1,0:T(8,128)(2,1)S(1)} %pad_maximum_fusion.refs_0_.refs_9_.refs_14_) | copy-start | bytes 2543620
  29.9 26.1 %collective-permute-start.3 = (bf16[96,4416]{1,0:T(8,128)(2,1)S(1)}, bf16[96,4416]{1,0:T(8,128)(2,1)}, u32[]{:S(2)}, u32[]{:S(2)}) collective-permute-start(bf16[96,4416]{1,0:T(8,128)(2,1)S(1)} %pad_maximum_fusion.refs_0_.refs_9_.refs_14_), channel_id=1, source_target_pairs={{0,8},{4,12},{8,0},{12,4},{16,24},{20,28},{24,16},{28,20},{1,9},{5... | collective-permute-start | bytes 2543624 | tf_op jit(solution)/shard_map/ppermute | solution.py:315
  30.5 25.5 %collective-permute-start.4 = (bf16[96,4416]{1,0:T(8,128)(2,1)S(1)}, bf16[96,4416]{1,0:T(8,128)(2,1)}, u32[]{:S(2)}, u32[]{:S(2)}) collective-permute-start(bf16[96,4416]{1,0:T(8,128)(2,1)S(1)} %pad_maximum_fusion.refs_0_.refs_9_.refs_14_), channel_id=1, source_target_pairs={{0,16},{4,20},{8,24},{12,28},{16,0},{20,4},{24,8},{28,12},{1,17},{... | collective-permute-start | bytes 2543624 | tf_op jit(solution)/shard_map/ppermute | solution.py:315
  32.0 42.2 %copy-start.39 = (s32[1,4]{1,0:T(1,128)S(1)}, s32[1,4]{1,0:T(1,128)}, u32[]{:S(2)}) copy-start(s32[1,4]{1,0:T(1,128)} %param.15) | copy-start | bytes 52
  32.1 42.6 %copy-start.28 = (s32[2049]{0:T(1024)S(1)}, s32[2049]{0:T(1024)}, u32[]{:S(2)}) copy-start(s32[2049]{0:T(1024)} %param.16) | copy-start | bytes 24592
  32.1 192.9 %reduce-scatter.2.cloned.1.call-start = ((), (), s32[]{:S(2)}) async-start(), calls=%async_computation.2 | async-start | bytes 1474560 | tf_op jit(solution)/shard_map/reduce_scatter | solution.py:939
  32.1 8.9 %collective-permute-start.5 = (bf16[96,768]{1,0:T(8,128)(2,1)S(1)}, bf16[96,768]{1,0:T(8,128)(2,1)S(1)}, u32[]{:S(2)}, u32[]{:S(2)}) collective-permute-start(bf16[96,768]{1,0:T(8,128)(2,1)S(1)} %copy-done.21), channel_id=1, source_target_pairs={{0,1},{1,2},{2,3},{3,0},{4,5},{5,6},{6,7},{7,4},{8,9},{9,10},{10,1... | collective-permute-start | bytes 442376 | tf_op jit(solution)/shard_map/ppermute | solution.py:320
  34.8 10.6 %collective-permute-start.6 = (bf16[96,768]{1,0:T(8,128)(2,1)S(1)}, bf16[96,768]{1,0:T(8,128)(2,1)S(1)}, u32[]{:S(2)}, u32[]{:S(2)}) collective-permute-start(bf16[96,768]{1,0:T(8,128)(2,1)S(1)} %copy-done.21), channel_id=1, source_target_pairs={{0,2},{1,3},{2,0},{3,1},{4,6},{5,7},{6,4},{7,5},{8,10},{9,11},{10,... | collective-permute-start | bytes 442376 | tf_op jit(solution)/shard_map/ppermute | solution.py:320
  36.1 19.9 %collective-permute-start.7 = (bf16[96,768]{1,0:T(8,128)(2,1)S(1)}, bf16[96,768]{1,0:T(8,128)(2,1)S(1)}, u32[]{:S(2)}, u32[]{:S(2)}) collective-permute-start(bf16[96,768]{1,0:T(8,128)(2,1)S(1)} %copy-done.21), channel_id=1, source_target_pairs={{0,3},{1,0},{2,1},{3,2},{4,7},{5,4},{6,5},{7,6},{8,11},{9,8},{10,9... | collective-permute-start | bytes 442376 | tf_op jit(solution)/shard_map/ppermute | solution.py:320
  57.0 17.7 %copy-start.31 = (f32[12]{0:T(128)S(1)}, f32[12]{0:T(128)}, u32[]{:S(2)}) copy-start(f32[12]{0:T(128)} %param.25) | copy-start | bytes 148
  57.1 17.8 %copy-start.26 = (f32[768]{0:T(1024)S(1)}, f32[768]{0:T(1024)}, u32[]{:S(2)}) copy-start(f32[768]{0:T(1024)} %param.21) | copy-start | bytes 9220
  57.1 11.7 %collective-permute-start.8 = (bf16[48,4416]{1,0:T(8,128)(2,1)S(1)}, bf16[48,4416]{1,0:T(8,128)(2,1)S(1)}, u32[]{:S(2)}, u32[]{:S(2)}) collective-permute-start(bf16[48,4416]{1,0:T(8,128)(2,1)S(1)} %slice.234), channel_id=1, source_target_pairs={{0,8},{4,12},{8,0},{12,4},{16,24},{20,28},{24,16},{28,20},{1,9},{5... | collective-permute-start | bytes 1271816 | tf_op jit(solution)/shard_map/ppermute | solution.py:315
  61.0 15.7 %collective-permute-start.11 = (bf16[96,4416]{1,0:T(8,128)(2,1)}, bf16[96,4416]{1,0:T(8,128)(2,1)}, u32[]{:S(2)}, u32[]{:S(2)}) collective-permute-start(bf16[96,4416]{1,0:T(8,128)(2,1)} %collective-permute-done.3.refs_1_.refs_10_.refs_15_), channel_id=1, source_target_pairs={{0,4},{4,0},{8,12},{12,8},{16,20},{20,16},{24,28},{28,24},{1,5},{5... | collective-permute-start | bytes 2543624 | tf_op jit(solution)/shard_map/ppermute | solution.py:315
  61.1 15.7 %collective-permute-start.12 = (bf16[96,4416]{1,0:T(8,128)(2,1)}, bf16[96,4416]{1,0:T(8,128)(2,1)}, u32[]{:S(2)}, u32[]{:S(2)}) collective-permute-start(bf16[96,4416]{1,0:T(8,128)(2,1)} %collective-permute-done.4.refs_2_.refs_11_.refs_16_), channel_id=1, source_target_pairs={{0,4},{4,0},{8,12},{12,8},{16,20},{20,16},{24,28},{28,24},{1,5},{5... | collective-permute-start | bytes 2543624 | tf_op jit(solution)/shard_map/ppermute | solution.py:315
  61.5 11.9 %collective-permute-start.9 = (bf16[48,4416]{1,0:T(8,128)(2,1)S(1)}, bf16[48,4416]{1,0:T(8,128)(2,1)S(1)}, u32[]{:S(2)}, u32[]{:S(2)}) collective-permute-start(bf16[48,4416]{1,0:T(8,128)(2,1)S(1)} %slice.235), channel_id=1, source_target_pairs={{0,16},{4,20},{8,24},{12,28},{16,0},{20,4},{24,8},{28,12},{1,17},{... | collective-permute-start | bytes 1271816 | tf_op jit(solution)/shard_map/ppermute | solution.py:315
  61.6 14.8 %collective-permute-start.10 = (bf16[96,4416]{1,0:T(8,128)(2,1)S(1)}, bf16[96,4416]{1,0:T(8,128)(2,1)}, u32[]{:S(2)}, u32[]{:S(2)}) collective-permute-start(bf16[96,4416]{1,0:T(8,128)(2,1)S(1)} %pad_maximum_fusion.refs_0_.refs_9_.refs_14_), channel_id=1, source_target_pairs={{0,4},{4,0},{8,12},{12,8},{16,20},{20,16},{24,28},{28,24},{1,5},{5... | collective-permute-start | bytes 2543624 | tf_op jit(solution)/shard_map/ppermute | solution.py:315
  74.2 2.7 %collective-permute-start.13 = (bf16[96,4416]{1,0:T(8,128)(2,1)}, bf16[96,4416]{1,0:T(8,128)(2,1)}, u32[]{:S(2)}, u32[]{:S(2)}) collective-permute-start(bf16[96,4416]{1,0:T(8,128)(2,1)} %constant_dynamic-update-slice_fusion.refs_3_.refs_12_.refs_17_), channel_id=1, source_target_pairs={{0,4},{4,0},{8,12},{12,8},{16,20},{20,16},{24,28},{28,24},{1,5},{5... | collective-permute-start | bytes 2543624 | tf_op jit(solution)/shard_map/ppermute | solution.py:315
  76.3 28.0 %copy-start.16 = (bf16[384,768]{1,0:T(8,128)(2,1)}, bf16[384,768]{1,0:T(8,128)(2,1)S(1)}, u32[]{:S(2)}) copy-start(bf16[384,768]{1,0:T(8,128)(2,1)S(1)} %pad_maximum_fusion.4.refs_22_) | copy-start | bytes 1769476
  76.3 15.8 %collective-permute-start.14 = (bf16[384,768]{1,0:T(8,128)(2,1)S(1)}, bf16[384,768]{1,0:T(8,128)(2,1)S(1)}, u32[]{:S(2)}, u32[]{:S(2)}) collective-permute-start(bf16[384,768]{1,0:T(8,128)(2,1)S(1)} %pad_maximum_fusion.4.refs_22_), channel_id=1, source_target_pairs={{0,8},{4,12},{8,0},{12,4},{16,24},{20,28},{24,16},{28,20},{1,9},{5... | collective-permute-start | bytes 1769480 | tf_op jit(solution)/shard_map/ppermute | solution.py:315
  76.4 15.8 %collective-permute-start.15 = (bf16[384,768]{1,0:T(8,128)(2,1)S(1)}, bf16[384,768]{1,0:T(8,128)(2,1)S(1)}, u32[]{:S(2)}, u32[]{:S(2)}) collective-permute-start(bf16[384,768]{1,0:T(8,128)(2,1)S(1)} %pad_maximum_fusion.4.refs_22_), channel_id=1, source_target_pairs={{0,16},{4,20},{8,24},{12,28},{16,0},{20,4},{24,8},{28,12},{1,17},{... | collective-permute-start | bytes 1769480 | tf_op jit(solution)/shard_map/ppermute | solution.py:315
  92.1 23.5 %copy-start.22 = (bf16[384,768]{1,0:T(8,128)(2,1)}, bf16[384,768]{1,0:T(8,128)(2,1)S(1)}, u32[]{:S(2)}) copy-start(bf16[384,768]{1,0:T(8,128)(2,1)S(1)} %collective-permute-done.14.refs_23_) | copy-start | bytes 1769476
  92.2 23.4 %copy-start.23 = (bf16[384,768]{1,0:T(8,128)(2,1)}, bf16[384,768]{1,0:T(8,128)(2,1)S(1)}, u32[]{:S(2)}) copy-start(bf16[384,768]{1,0:T(8,128)(2,1)S(1)} %collective-permute-done.15.refs_24_) | copy-start | bytes 1769476
  92.2 8.7 %collective-permute-start.16 = (bf16[192,768]{1,0:T(8,128)(2,1)S(1)}, bf16[192,768]{1,0:T(8,128)(2,1)S(1)}, u32[]{:S(2)}, u32[]{:S(2)}) collective-permute-start(bf16[192,768]{1,0:T(8,128)(2,1)S(1)} %slice.236), channel_id=1, source_target_pairs={{0,8},{4,12},{8,0},{12,4},{16,24},{20,28},{24,16},{28,20},{1,9},{5... | collective-permute-start | bytes 884744 | tf_op jit(solution)/shard_map/ppermute | solution.py:315
  93.9 8.1 %collective-permute-start.17 = (bf16[192,768]{1,0:T(8,128)(2,1)S(1)}, bf16[192,768]{1,0:T(8,128)(2,1)S(1)}, u32[]{:S(2)}, u32[]{:S(2)}) collective-permute-start(bf16[192,768]{1,0:T(8,128)(2,1)S(1)} %slice.237), channel_id=1, source_target_pairs={{0,16},{4,20},{8,24},{12,28},{16,0},{20,4},{24,8},{28,12},{1,17},{... | collective-permute-start | bytes 884744 | tf_op jit(solution)/shard_map/ppermute | solution.py:315
  94.7 7.7 %collective-permute-start.18 = (bf16[192,192]{1,0:T(8,128)(2,1)S(1)}, bf16[192,192]{1,0:T(8,128)(2,1)S(1)}, u32[]{:S(2)}, u32[]{:S(2)}) collective-permute-start(bf16[192,192]{1,0:T(8,128)(2,1)S(1)} %get-tuple-element.180), channel_id=1, source_target_pairs={{0,1},{1,2},{2,3},{3,0},{4,5},{5,6},{6,7},{7,4},{8,9},{9,10},{10,1... | collective-permute-start | bytes 221192 | tf_op jit(solution)/shard_map/ppermute | solution.py:320
  95.1 9.0 %collective-permute-start.19 = (bf16[192,192]{1,0:T(8,128)(2,1)S(1)}, bf16[192,192]{1,0:T(8,128)(2,1)S(1)}, u32[]{:S(2)}, u32[]{:S(2)}) collective-permute-start(bf16[192,192]{1,0:T(8,128)(2,1)S(1)} %get-tuple-element.179), channel_id=1, source_target_pairs={{0,2},{1,3},{2,0},{3,1},{4,6},{5,7},{6,4},{7,5},{8,10},{9,11},{10,... | collective-permute-start | bytes 221192 | tf_op jit(solution)/shard_map/ppermute | solution.py:320
  98.9 5.3 %collective-permute-start.20 = (bf16[192,192]{1,0:T(8,128)(2,1)S(1)}, bf16[192,192]{1,0:T(8,128)(2,1)S(1)}, u32[]{:S(2)}, u32[]{:S(2)}) collective-permute-start(bf16[192,192]{1,0:T(8,128)(2,1)S(1)} %get-tuple-element.178), channel_id=1, source_target_pairs={{0,3},{1,0},{2,1},{3,2},{4,7},{5,4},{6,5},{7,6},{8,11},{9,8},{10,9... | collective-permute-start | bytes 221192 | tf_op jit(solution)/shard_map/ppermute | solution.py:320
  104.3 11.4 %collective-permute-start.21 = (bf16[384,768]{1,0:T(8,128)(2,1)S(1)}, bf16[384,768]{1,0:T(8,128)(2,1)S(1)}, u32[]{:S(2)}, u32[]{:S(2)}) collective-permute-start(bf16[384,768]{1,0:T(8,128)(2,1)S(1)} %pad_maximum_fusion.4.refs_22_), channel_id=1, source_target_pairs={{0,4},{4,0},{8,12},{12,8},{16,20},{20,16},{24,28},{28,24},{1,5},{5... | collective-permute-start | bytes 1769480 | tf_op jit(solution)/shard_map/ppermute | solution.py:315
  104.3 11.4 %collective-permute-start.22 = (bf16[384,768]{1,0:T(8,128)(2,1)S(1)}, bf16[384,768]{1,0:T(8,128)(2,1)S(1)}, u32[]{:S(2)}, u32[]{:S(2)}) collective-permute-start(bf16[384,768]{1,0:T(8,128)(2,1)S(1)} %collective-permute-done.14.refs_23_), channel_id=1, source_target_pairs={{0,4},{4,0},{8,12},{12,8},{16,20},{20,16},{24,28},{28,24},{1,5},{5... | collective-permute-start | bytes 1769480 | tf_op jit(solution)/shard_map/ppermute | solution.py:315
  104.8 10.9 %collective-permute-start.23 = (bf16[384,768]{1,0:T(8,128)(2,1)S(1)}, bf16[384,768]{1,0:T(8,128)(2,1)S(1)}, u32[]{:S(2)}, u32[]{:S(2)}) collective-permute-start(bf16[384,768]{1,0:T(8,128)(2,1)S(1)} %collective-permute-done.15.refs_24_), channel_id=1, source_target_pairs={{0,4},{4,0},{8,12},{12,8},{16,20},{20,16},{24,28},{28,24},{1,5},{5... | collective-permute-start | bytes 1769480 | tf_op jit(solution)/shard_map/ppermute | solution.py:315
  104.8 10.9 %collective-permute-start.24 = (bf16[384,768]{1,0:T(8,128)(2,1)S(1)}, bf16[384,768]{1,0:T(8,128)(2,1)S(1)}, u32[]{:S(2)}, u32[]{:S(2)}) collective-permute-start(bf16[384,768]{1,0:T(8,128)(2,1)S(1)} %constant_dynamic-update-slice_fusion.2.refs_25_), channel_id=1, source_target_pairs={{0,4},{4,0},{8,12},{12,8},{16,20},{20,16},{24,28},{28,24},{1,5},{5... | collective-permute-start | bytes 1769480 | tf_op jit(solution)/shard_map/ppermute | solution.py:315
  117.1 2.2 collective-permute-start.25
  120.6 26.0 %collective-permute-start.26 = (bf16[192,768]{1,0:T(8,128)(2,1)S(1)}, bf16[192,768]{1,0:T(8,128)(2,1)S(1)}, u32[]{:S(2)}, u32[]{:S(2)}) collective-permute-start(bf16[192,768]{1,0:T(8,128)(2,1)S(1)} %get-tuple-element.170), channel_id=1, source_target_pairs={{0,8},{4,12},{8,0},{12,4},{16,24},{20,28},{24,16},{28,20},{1,9},{5... | collective-permute-start | bytes 884744 | tf_op jit(solution)/shard_map/ppermute | solution.py:315
  121.1 25.5 %collective-permute-start.27 = (bf16[192,768]{1,0:T(8,128)(2,1)S(1)}, bf16[192,768]{1,0:T(8,128)(2,1)S(1)}, u32[]{:S(2)}, u32[]{:S(2)}) collective-permute-start(bf16[192,768]{1,0:T(8,128)(2,1)S(1)} %get-tuple-element.169), channel_id=1, source_target_pairs={{0,16},{4,20},{8,24},{12,28},{16,0},{20,4},{24,8},{28,12},{1,17},{... | collective-permute-start | bytes 884744 | tf_op jit(solution)/shard_map/ppermute | solution.py:315
  122.3 24.4 %copy-start.34 = (bf16[3,384,768]{2,1,0:T(8,128)(2,1)S(1)}, bf16[3,384,768]{2,1,0:T(8,128)(2,1)}, u32[]{:S(2)}) copy-start(bf16[3,384,768]{2,1,0:T(8,128)(2,1)} %get-tuple-element.124) | copy-start | bytes 5308420
  122.3 32.0 %copy-start.11 = (bf16[4,384,768]{2,1,0:T(8,128)(2,1)S(1)}, bf16[4,384,768]{2,1,0:T(8,128)(2,1)}, u32[]{:S(2)}) copy-start(bf16[4,384,768]{2,1,0:T(8,128)(2,1)} %get-tuple-element.87) | copy-start | bytes 7077892
  146.6 10.9 %collective-permute-start.28 = (bf16[4,96,3840]{2,1,0:T(8,128)(2,1)}, bf16[4,96,3840]{2,1,0:T(8,128)(2,1)S(1)}, u32[]{:S(2)}, u32[]{:S(2)}) collective-permute-start(bf16[4,96,3840]{2,1,0:T(8,128)(2,1)} %get-tuple-element.112), channel_id=1, source_target_pairs={{0,4},{4,0},{8,12},{12,8},{16,20},{20,16},{24,28},{28,24},{1,5},{5... | collective-permute-start | bytes 8847368 | tf_op jit(solution)/shard_map/ppermute | solution.py:315
  146.7 7.5 %collective-permute-start.32 = (bf16[3,384,768]{2,1,0:T(8,128)(2,1)S(1)}, bf16[3,384,768]{2,1,0:T(8,128)(2,1)S(1)}, u32[]{:S(2)}, u32[]{:S(2)}) collective-permute-start(bf16[3,384,768]{2,1,0:T(8,128)(2,1)S(1)} %copy-done.34), channel_id=1, source_target_pairs={{0,4},{4,0},{8,12},{12,8},{16,20},{20,16},{24,28},{28,24},{1,5},{5... | collective-permute-start | bytes 5308424 | tf_op jit(solution)/shard_map/ppermute | solution.py:315
  147.4 13.5 %collective-permute-start.29 = (bf16[192,192]{1,0:T(8,128)(2,1)S(1)}, bf16[192,192]{1,0:T(8,128)(2,1)S(1)}, u32[]{:S(2)}, u32[]{:S(2)}) collective-permute-start(bf16[192,192]{1,0:T(8,128)(2,1)S(1)} %get-tuple-element.114), channel_id=1, source_target_pairs={{0,3},{1,0},{2,1},{3,2},{4,7},{5,4},{6,5},{7,6},{8,11},{9,8},{10,9... | collective-permute-start | bytes 221192 | tf_op jit(solution)/shard_map/ppermute | solution.py:320
  149.9 11.0 %collective-permute-start.30 = (bf16[192,192]{1,0:T(8,128)(2,1)S(1)}, bf16[192,192]{1,0:T(8,128)(2,1)S(1)}, u32[]{:S(2)}, u32[]{:S(2)}) collective-permute-start(bf16[192,192]{1,0:T(8,128)(2,1)S(1)} %get-tuple-element.115), channel_id=1, source_target_pairs={{0,2},{1,3},{2,0},{3,1},{4,6},{5,7},{6,4},{7,5},{8,10},{9,11},{10,... | collective-permute-start | bytes 221192 | tf_op jit(solution)/shard_map/ppermute | solution.py:320
  153.2 8.3 %collective-permute-start.31 = (bf16[192,192]{1,0:T(8,128)(2,1)S(1)}, bf16[192,192]{1,0:T(8,128)(2,1)S(1)}, u32[]{:S(2)}, u32[]{:S(2)}) collective-permute-start(bf16[192,192]{1,0:T(8,128)(2,1)S(1)} %get-tuple-element.116), channel_id=1, source_target_pairs={{0,1},{1,2},{2,3},{3,0},{4,5},{5,6},{6,7},{7,4},{8,9},{9,10},{10,1... | collective-permute-start | bytes 221192 | tf_op jit(solution)/shard_map/ppermute | solution.py:320
  155.8 21.5 %collective-permute-start.34 = (bf16[384,768]{1,0:T(8,128)(2,1)}, bf16[384,768]{1,0:T(8,128)(2,1)}, u32[]{:S(2)}, u32[]{:S(2)}) collective-permute-start(bf16[384,768]{1,0:T(8,128)(2,1)} %pad_maximum_fusion.6), channel_id=1, source_target_pairs={{0,16},{4,20},{8,24},{12,28},{16,0},{20,4},{24,8},{28,12},{1,17},{... | collective-permute-start | bytes 1769480 | tf_op jit(solution)/shard_map/ppermute | solution.py:315
  157.5 19.7 %collective-permute-start.33 = (bf16[384,768]{1,0:T(8,128)(2,1)}, bf16[384,768]{1,0:T(8,128)(2,1)}, u32[]{:S(2)}, u32[]{:S(2)}) collective-permute-start(bf16[384,768]{1,0:T(8,128)(2,1)} %pad_maximum_fusion.5), channel_id=1, source_target_pairs={{0,8},{4,12},{8,0},{12,4},{16,24},{20,28},{24,16},{28,20},{1,9},{5... | collective-permute-start | bytes 1769480 | tf_op jit(solution)/shard_map/ppermute | solution.py:315
  177.2 5.1 %collective-permute-start.35 = (bf16[4,96,576]{2,1,0:T(8,128)(2,1)S(1)}, bf16[4,96,576]{2,1,0:T(8,128)(2,1)}, u32[]{:S(2)}, u32[]{:S(2)}) collective-permute-start(bf16[4,96,576]{2,1,0:T(8,128)(2,1)S(1)} %get-tuple-element.127), channel_id=1, source_target_pairs={{0,4},{4,0},{8,12},{12,8},{16,20},{20,16},{24,28},{28,24},{1,5},{5... | collective-permute-start | bytes 1327112 | tf_op jit(solution)/shard_map/ppermute | solution.py:315
  179.5 2.9 %collective-permute-start.38 = (bf16[13,576]{1,0:T(8,128)(2,1)S(1)}, bf16[13,576]{1,0:T(8,128)(2,1)S(1)}, u32[]{:S(2)}, u32[]{:S(2)}) collective-permute-start(bf16[13,576]{1,0:T(8,128)(2,1)S(1)} %convert_element_type.286), channel_id=1, source_target_pairs={{0,4},{4,0},{8,12},{12,8},{16,20},{20,16},{24,28},{28,24},{1,5},{5... | collective-permute-start | bytes 44936 | tf_op jit(solution)/shard_map/ppermute | solution.py:315
  182.4 12.6 %collective-permute-start.36 = (bf16[48,3840]{1,0:T(8,128)(2,1)S(1)}, bf16[48,3840]{1,0:T(8,128)(2,1)S(1)}, u32[]{:S(2)}, u32[]{:S(2)}) collective-permute-start(bf16[48,3840]{1,0:T(8,128)(2,1)S(1)} %get-tuple-element.165), channel_id=1, source_target_pairs={{0,16},{4,20},{8,24},{12,28},{16,0},{20,4},{24,8},{28,12},{1,17},{... | collective-permute-start | bytes 1105928 | tf_op jit(solution)/shard_map/ppermute | solution.py:315
  183.5 11.5 %collective-permute-start.37 = (bf16[48,3840]{1,0:T(8,128)(2,1)S(1)}, bf16[48,3840]{1,0:T(8,128)(2,1)S(1)}, u32[]{:S(2)}, u32[]{:S(2)}) collective-permute-start(bf16[48,3840]{1,0:T(8,128)(2,1)S(1)} %get-tuple-element.164), channel_id=1, source_target_pairs={{0,8},{4,12},{8,0},{12,4},{16,24},{20,28},{24,16},{28,20},{1,9},{5... | collective-permute-start | bytes 1105928 | tf_op jit(solution)/shard_map/ppermute | solution.py:315
  187.3 11.5 %collective-permute-start.39 = (bf16[109,576]{1,0:T(8,128)(2,1)S(1)}, bf16[109,576]{1,0:T(8,128)(2,1)S(1)}, u32[]{:S(2)}, u32[]{:S(2)}) collective-permute-start(bf16[109,576]{1,0:T(8,128)(2,1)S(1)} %get-tuple-element.191), channel_id=1, source_target_pairs={{0,24},{4,28},{8,16},{12,20},{16,8},{20,12},{24,0},{28,4},{1,25},{... | collective-permute-start | bytes 376712 | tf_op jit(solution)/shard_map/ppermute | solution.py:315
  188.3 11.7 %collective-permute-start.40 = (bf16[109,576]{1,0:T(8,128)(2,1)S(1)}, bf16[109,576]{1,0:T(8,128)(2,1)S(1)}, u32[]{:S(2)}, u32[]{:S(2)}) collective-permute-start(bf16[109,576]{1,0:T(8,128)(2,1)S(1)} %get-tuple-element.189), channel_id=1, source_target_pairs={{0,8},{4,12},{8,0},{12,4},{16,24},{20,28},{24,16},{28,20},{1,9},{5... | collective-permute-start | bytes 376712 | tf_op jit(solution)/shard_map/ppermute | solution.py:315
  189.7 10.3 %collective-permute-start.41 = (bf16[109,576]{1,0:T(8,128)(2,1)S(1)}, bf16[109,576]{1,0:T(8,128)(2,1)S(1)}, u32[]{:S(2)}, u32[]{:S(2)}) collective-permute-start(bf16[109,576]{1,0:T(8,128)(2,1)S(1)} %get-tuple-element.190), channel_id=1, source_target_pairs={{0,16},{4,20},{8,24},{12,28},{16,0},{20,4},{24,8},{28,12},{1,17},{... | collective-permute-start | bytes 376712 | tf_op jit(solution)/shard_map/ppermute | solution.py:315
  200.0 23.3 %collective-permute-start.42 = (bf16[96,3840]{1,0:T(8,128)(2,1)}, bf16[96,3840]{1,0:T(8,128)(2,1)}, u32[]{:S(2)}, u32[]{:S(2)}) collective-permute-start(bf16[96,3840]{1,0:T(8,128)(2,1)} %get-tuple-element.136), channel_id=1, source_target_pairs={{0,8},{4,12},{8,0},{12,4},{16,24},{20,28},{24,16},{28,20},{1,9},{5... | collective-permute-start | bytes 2211848 | tf_op jit(solution)/shard_map/ppermute | solution.py:315
  201.6 21.6 %collective-permute-start.43 = (bf16[96,3840]{1,0:T(8,128)(2,1)}, bf16[96,3840]{1,0:T(8,128)(2,1)}, u32[]{:S(2)}, u32[]{:S(2)}) collective-permute-start(bf16[96,3840]{1,0:T(8,128)(2,1)} %get-tuple-element.137), channel_id=1, source_target_pairs={{0,16},{4,20},{8,24},{12,28},{16,0},{20,4},{24,8},{28,12},{1,17},{... | collective-permute-start | bytes 2211848 | tf_op jit(solution)/shard_map/ppermute | solution.py:315
  208.4 12.2 %collective-permute-start.44 = (bf16[96,768]{1,0:T(8,128)(2,1)S(1)}, bf16[96,768]{1,0:T(8,128)(2,1)S(1)}, u32[]{:S(2)}, u32[]{:S(2)}) collective-permute-start(bf16[96,768]{1,0:T(8,128)(2,1)S(1)} %get-tuple-element.168), channel_id=1, source_target_pairs={{0,1},{1,2},{2,3},{3,0},{4,5},{5,6},{6,7},{7,4},{8,9},{9,10},{10,1... | collective-permute-start | bytes 442376 | tf_op jit(solution)/shard_map/ppermute | solution.py:320
  210.6 10.1 %collective-permute-start.45 = (bf16[96,768]{1,0:T(8,128)(2,1)S(1)}, bf16[96,768]{1,0:T(8,128)(2,1)S(1)}, u32[]{:S(2)}, u32[]{:S(2)}) collective-permute-start(bf16[96,768]{1,0:T(8,128)(2,1)S(1)} %get-tuple-element.167), channel_id=1, source_target_pairs={{0,2},{1,3},{2,0},{3,1},{4,6},{5,7},{6,4},{7,5},{8,10},{9,11},{10,... | collective-permute-start | bytes 442376 | tf_op jit(solution)/shard_map/ppermute | solution.py:320
  211.2 10.4 %collective-permute-start.46 = (bf16[96,768]{1,0:T(8,128)(2,1)S(1)}, bf16[96,768]{1,0:T(8,128)(2,1)S(1)}, u32[]{:S(2)}, u32[]{:S(2)}) collective-permute-start(bf16[96,768]{1,0:T(8,128)(2,1)S(1)} %get-tuple-element.166), channel_id=1, source_target_pairs={{0,3},{1,0},{2,1},{3,2},{4,7},{5,4},{6,5},{7,6},{8,11},{9,8},{10,9... | collective-permute-start | bytes 442376 | tf_op jit(solution)/shard_map/ppermute | solution.py:320
  225.2 19.9 %collective-permute-start.48 = (bf16[26,4416]{1,0:T(8,128)(2,1)S(1)}, bf16[26,4416]{1,0:T(8,128)(2,1)S(1)}, u32[]{:S(2)}, u32[]{:S(2)}) collective-permute-start(bf16[26,4416]{1,0:T(8,128)(2,1)S(1)} %get-tuple-element.159), channel_id=1, source_target_pairs={{0,2},{1,3},{2,0},{3,1},{4,6},{5,7},{6,4},{7,5},{8,10},{9,11},{10,... | collective-permute-start | bytes 688904 | tf_op jit(solution)/shard_map/ppermute | solution.py:320
  225.6 27.7 %collective-permute-start.47 = (bf16[26,4416]{1,0:T(8,128)(2,1)S(1)}, bf16[26,4416]{1,0:T(8,128)(2,1)S(1)}, u32[]{:S(2)}, u32[]{:S(2)}) collective-permute-start(bf16[26,4416]{1,0:T(8,128)(2,1)S(1)} %get-tuple-element.158), channel_id=1, source_target_pairs={{0,1},{1,2},{2,3},{3,0},{4,5},{5,6},{6,7},{7,4},{8,9},{9,10},{10,1... | collective-permute-start | bytes 688904 | tf_op jit(solution)/shard_map/ppermute | solution.py:320
  229.2 24.2 %collective-permute-start.49 = (bf16[26,4416]{1,0:T(8,128)(2,1)S(1)}, bf16[26,4416]{1,0:T(8,128)(2,1)S(1)}, u32[]{:S(2)}, u32[]{:S(2)}) collective-permute-start(bf16[26,4416]{1,0:T(8,128)(2,1)S(1)} %get-tuple-element.160), channel_id=1, source_target_pairs={{0,3},{1,0},{2,1},{3,2},{4,7},{5,4},{6,5},{7,6},{8,11},{9,8},{10,9... | collective-permute-start | bytes 688904 | tf_op jit(solution)/shard_map/ppermute | solution.py:320
  229.3 26.5 %copy-start.33 = (f32[12]{0:T(128)S(1)}, f32[12]{0:T(128)}, u32[]{:S(2)}) copy-start(f32[12]{0:T(128)} %param.25) | copy-start | bytes 148
  (28 other events, 190.5 us)
Sparse Core Ops, SparseCore 0:
  32.2 34.3 all-gather.1
  175.3 29.8 reduce-scatter.1

commit v4 on v3

--- a/solution.py
+++ b/solution.py
@@ -488,14 +488,24 @@
     return lax.rem(place_ref[1] - steps + size, size)
 
 
+def bias_kernel(heads, place_ref, diagonal_ref, bias_ref, semaphores):
+    for head in range(heads):
+        for step in range(diagonal_ref.shape[1] // lanes - 1):
+            window = diagonal_ref[head : head + 1, step * lanes : (step + 2) * lanes]
+            window = jnp.broadcast_to(window, (lanes, 2 * lanes))
+            window = pltpu.roll(window, 0, 1, stride=1, stride_axis=0)
+            bias_ref[head, :, step * lanes : (step + 1) * lanes] = window[:, lanes:]
+
+
 def attend_kernel(
-    heads, head_size, place_ref, gain_ref, diagonal_ref, doc_col_ref, doc_row_ref, scale_ref, tokens_ref, *refs
+    heads, head_size, place_ref, gain_ref, doc_col_ref, doc_row_ref, scale_ref, tokens_ref, *refs
 ):
     parts, refs = refs[:8], refs[8:]
-    w_ref, qkv_ref, normed_ref, attention_ref, scaled_ref, probs_out, bias, probs_ref, semaphores = refs
+    bias_in, w_ref, qkv_ref, normed_ref, attention_ref, scaled_ref, probs_out, bias, probs_ref, semaphores = refs
     copies = Copies(semaphores)
     last = parts[0].shape[1]
     arriving = fill_planes(copies, place_ref, parts, slice(last - w_ref.shape[1], last), w_ref)
+    bias_here = copies.start(bias_in, bias)
     leaving = []
     length = tokens_ref.shape[0]
     blocks = length // lanes
@@ -505,15 +515,11 @@
         normed, _ = normalize(tokens_ref[rows, :].astype(jnp.float32))
         normed_ref[rows, :] = (normed * gain_ref[...]).astype(jnp.bfloat16)
     wait_all(arriving)
+    bias_here.wait()
     projected = contract(normed_ref[...], w_ref[...], 1, 0)
     qkv_ref[:, :width] = (projected[:, :width] * query_scale).astype(jnp.bfloat16)
     qkv_ref[:, width:] = projected[:, width:].astype(jnp.bfloat16)
     for head in range(heads):
-        for step in range(2 * blocks - 1):
-            window = diagonal_ref[head : head + 1, step * lanes : (step + 2) * lanes]
-            window = jnp.broadcast_to(window, (lanes, 2 * lanes))
-            window = pltpu.roll(window, 0, 1, stride=1, stride_axis=0)
-            bias[:, step * lanes : (step + 1) * lanes] = window[:, lanes:]
         low = head * head_size
         keys = qkv_ref[:, width + low : width + low + head_size]
         values = qkv_ref[:, 2 * width + low : 2 * width + low + head_size]
@@ -521,7 +527,7 @@
         for block in range(blocks):
             rows = slice(block * lanes, (block + 1) * lanes)
             first = (blocks - 1 - block) * lanes
-            scores = all_scores[rows, :] + bias[:, first : first + length]
+            scores = all_scores[rows, :] + bias[head, :, first : first + length]
             same = doc_col_ref[rows, :] == doc_row_ref[...]
             scores = jnp.where(same, scores, masked_score)
             weights = jnp.exp(scores - jnp.max(scores, axis=1, keepdims=True))
@@ -711,8 +717,10 @@
         out_ref[:, 2 * width + low : 2 * width + low + head_size] = d_values.T.astype(jnp.bfloat16)
         row_ids = lax.broadcasted_iota(jnp.int32, (lanes, lanes), 0)
         col_ids = lax.broadcasted_iota(jnp.int32, (lanes, lanes), 1)
-        reverse = (row_ids + col_ids == lanes - 1).astype(jnp.float32)
-        flipped = jnp.dot(reverse, sums[...], precision=highest)
+        reverse = (row_ids + col_ids == lanes - 1).astype(jnp.bfloat16)
+        high = sums[...].astype(jnp.bfloat16)
+        rest = (sums[...] - high.astype(jnp.float32)).astype(jnp.bfloat16)
+        flipped = contract(reverse, high, 1, 0) + contract(reverse, rest, 1, 0)
         for step in range(2 * blocks - 1):
             window = flipped[:, step * lanes : (step + 1) * lanes]
             window = jnp.concatenate([window, jnp.zeros_like(window)], axis=1)
@@ -762,21 +770,9 @@
     bucket_count = bias_table.shape[0]
     shard_rows = w_qkv.shape[0]
 
-    hidden_width = w_fc1.shape[1]
-    summed = hidden_width + width
-    by_head = w_qkv.reshape(shard_rows, 3, line_size, part).transpose(2, 0, 1, 3)
-    by_head = by_head.reshape(line_size, shard_rows, 3 * part)
-    shared = jnp.broadcast_to(
-        jnp.concatenate([w_fc1, w_out], axis=1)[None], (line_size, shard_rows, summed)
-    )
-    first_pieces = deal_line(jnp.concatenate([shared, by_head], axis=2))
-    first_line = in_line(first_pieces)
-    row_tokens = lax.all_gather(after(tokens[0], first_line), "blk", axis=0, tiled=True)
-    second_pieces = turns(after(w_fc2, first_line))
-    first_planes = across_plane(all_after(beside(first_line), *second_pieces[1:]))
-    first_others = swap_cores(first_planes[:3] + [after(first_planes[3], row_tokens)])
-    second_near = beside(after(in_line(second_pieces), *first_planes))
-
+    low, wide = jnp.bfloat16, jnp.float32
+    planes = lax.axis_size("dp")
+    place_here = jnp.stack([lax.axis_index("dp"), here]).astype(jnp.int32)
     ends = jnp.cumsum(lengths[0])
     positions = jnp.arange(row_len, dtype=jnp.int32)
     documents = jnp.sum((positions[:, None] >= ends[None, :]).astype(jnp.int32), axis=1)
@@ -790,16 +786,39 @@
     scale_cols = jnp.repeat(head_scale, head_size)
     head_cols = lax.dynamic_slice_in_dim(scale_cols, here * part, part, 0)[None, :]
 
-    low, wide = jnp.bfloat16, jnp.float32
-    planes = lax.axis_size("dp")
-    place_here = jnp.stack([lax.axis_index("dp"), here]).astype(jnp.int32)
+    (bias,) = run_kernel(
+        functools.partial(bias_kernel, heads),
+        "relative_bias",
+        2,
+        place_here,
+        (diagonals,),
+        (),
+        [((heads, lanes, 2 * row_len - lanes), wide)],
+        (),
+    )
+
+    hidden_width = w_fc1.shape[1]
+    summed = hidden_width + width
+    by_head = w_qkv.reshape(shard_rows, 3, line_size, part).transpose(2, 0, 1, 3)
+    by_head = by_head.reshape(line_size, shard_rows, 3 * part)
+    shared = jnp.broadcast_to(
+        jnp.concatenate([w_fc1, w_out], axis=1)[None], (line_size, shard_rows, summed)
+    )
+    first_pieces = deal_line(jnp.concatenate([shared, by_head], axis=2))
+    first_line = after(in_line(first_pieces), bias)
+    row_tokens = lax.all_gather(after(tokens[0], first_line), "blk", axis=0, tiled=True)
+    second_pieces = turns(after(w_fc2, first_line))
+    first_planes = across_plane(all_after(beside(first_line), *second_pieces[1:]))
+    first_others = swap_cores(first_planes[:3] + [after(first_planes[3], row_tokens)])
+    second_near = beside(after(in_line(second_pieces), *first_planes))
+
     wqkv_part, qkv, normed_row, attention, scaled_part, probs = run_kernel(
         functools.partial(attend_kernel, heads, head_size),
         "attend",
         13,
         place_here,
-        (gain_in[None], diagonals, documents[:, None], documents[None, :], head_cols, row_tokens),
-        (*first_planes, *first_others),
+        (gain_in[None], documents[:, None], documents[None, :], head_cols, row_tokens),
+        (*first_planes, *first_others, bias),
         [
             ((width, 3 * part), low),
             ((row_len, 3 * part), low),
@@ -808,8 +827,8 @@
             ((row_len, part), low),
         ],
         [((heads, row_len, row_len), low)],
-        [((lanes, 2 * row_len - lanes), wide), ((heads, row_len, row_len), low)],
-        8 + heads,
+        [((heads, lanes, 2 * row_len - lanes), wide), ((heads, row_len, row_len), low)],
+        9 + heads,
     )
 
     dealt = deal_line(scaled_part.reshape(line_size, rows_here, part))
@@ -906,7 +925,7 @@
     ]
     got_first = swap(after(send_first, *halves), core_bit)
     first = add_low(keep_first, got_first)
-    grad_pieces[0] = after(grad_pieces[0], got_first)
+    grad_pieces[0] = after(grad_pieces[0], first)
     second_x, second_y = add_across(halves, second_rest[0], second_rest[1])
     second_got = [swap(second_x, x_bit), swap(second_y, y_bit)]
     send_qkv, keep_qkv, diagonal_sums_here, deltas, gain_sums, d_normed = run_kernel(
@@ -954,28 +973,32 @@
     terms = flat.astype(low)
     got = swap(send_qkv, core_bit)
     halves = halves_across(after(first[0], second_line, got))
-    first_x, first_y = add_across(halves, first[1], first[2])
     last = add_low(keep_qkv, got)
     terms = add_low(terms, swap(terms, core_bit))
     last_got = [
         swap(jnp.concatenate([last[slot], terms], axis=0), bits) for slot, bits in enumerate(far_first[:3])
     ]
+    arrived = all_after([*halves, *last_got])
+    halves, last_got = arrived[:2], arrived[2:]
+    first_x, first_y = add_across(halves, first[1], first[2])
+    first_got = [swap(first_x, x_bit), swap(first_y, y_bit)]
     last_line = sum_parts([last[3]] + [piece[:block_rows] for piece in last_got]).astype(low)
     plane_sums = [piece[block_rows:].astype(wide) for piece in last_got]
     flat = (terms.astype(wide) + plane_sums[1]) + (plane_sums[2] + plane_sums[0])
     flat = flat.reshape(-1)
-    flat = jnp.pad(flat, (0, -flat.shape[0] % (2 * pack_cols))).reshape(-1, pack_cols).astype(low)
-    first_x, first_y = all_after([first_x, first_y], *last_got)
-    first_got = [swap(first_x, x_bit), swap(first_y, y_bit)]
-    first_line = sum_parts([first[3], *first_got]).astype(low)
-    second_line = after(second_line, *last_got, *halves)
-    second_dealt = deal_line(second_line.reshape((line_size, -1, width)))
-    grad_fc2 = sum_parts(second_dealt)
-    both_lines = after(jnp.concatenate([first_line, last_line], axis=1), d_normed_low, *second_dealt[1:])
-    both_lines = both_lines.reshape(line_size, shard_rows, pack_cols)
+    flat = jnp.pad(flat, (0, -flat.shape[0] % (2 * width))).reshape(-1, width).astype(low)
+
+    second_rows = hidden_rows // line_size
     spread = jnp.broadcast_to(flat[None], (line_size,) + flat.shape)
-    dealt_back = deal_line(jnp.concatenate([both_lines, spread], axis=1))
-    flats = [piece[shard_rows:].astype(wide).reshape(-1) for piece in dealt_back]
+    second_stack = jnp.concatenate([second_line.reshape(line_size, second_rows, width), spread], axis=1)
+    second_dealt = deal_line(after(second_stack, d_normed_low, *last_got))
+    first_line = sum_parts([first[3], *all_after(first_got, *second_dealt[1:])]).astype(low)
+    both_lines = after(jnp.concatenate([first_line, last_line], axis=1), *second_dealt[1:])
+    dealt_back = deal_line(both_lines.reshape(line_size, shard_rows, pack_cols))
+    grad_fc2 = sum_parts([piece[:second_rows] for piece in second_dealt])
+    flats = [
+        piece[second_rows:].astype(wide).reshape(-1) for piece in all_after(second_dealt, dealt_back[1])
+    ]
     common = sum(sizes)
     totals = [flat[:common] for flat in flats]
     while len(totals) > 1:
@@ -985,7 +1008,7 @@
     by_owner = in_line([flat[None, common:owned] for flat in flats])
     grad_scale = by_owner[:, :heads].reshape(-1)
     d_bias = by_owner[:, heads:].reshape(all_heads, bucket_count)
-    dealt_back = [piece[:shard_rows] for piece in dealt_back]
+
     grad_fc1 = sum_parts([piece[:, :hidden_width] for piece in dealt_back])
     grad_out = sum_parts([piece[:, hidden_width:summed] for piece in dealt_back])
     grad_qkv = in_line([piece[:, summed:].astype(jnp.float32) for piece in dealt_back])

time: 272 us -> 264 us (0.971)
  waiting for transfers between devices: 95.4 us -> 88.3 us
  other arithmetic: 21.3 us -> 27.3 us
  local copies, waits for them, and re-layouts: 20.9 us -> 15.7 us
    ppermute x18, waiting for transfers between devices: 69.2 us -> 49.6 us  [turn(): lax.ppermute(value, 'blk', [(i, (i + steps) % size) for i in range(size)])]
    ppermute x32, waiting for transfers between devices: 26.1 us -> 37.5 us  [swap(): return lax.ppermute(value, 'dp', [(i, i ^ bit) for i in range(size)])]
    pallas_call x4 -> x5, Pallas kernels: 61.4 us -> 62.4 us  [run_kernel(): pl.pallas_call(kernel, out_shape=[jax.ShapeDtypeStruct(shape, dtype) for...]
  transfers between devices with their start and end apart: 52 -> 52, of which waited for: 25 -> 27; matrix products, arithmetic and copies ran while one was open for 12% -> 13% of each run, Pallas kernels for 23% -> 24%
where the time goes in v4:
time: 264 us; the launch traced here: 260 us
  waiting for transfers between devices  88.3 us (33%)
  Pallas kernels  62.4 us (24%)
  starting transfers between devices  48.3 us (18%)
  other arithmetic  27.3 us (10%)
  local copies, waits for them, and re-layouts  15.7 us (6%)
  between operations  15.2 us (6%)
  matrix products  2.64 us (1%)
    pallas_call x5, Pallas kernels, run_kernel(): pl.pallas_call(kernel, out_shape=[jax.ShapeDtypeStruct(shape, dtype) for...  62.4 us
    ppermute x18, waiting for transfers between devices, turn(): lax.ppermute(value, 'blk', [(i, (i + steps) % size) for i in range(size)])  49.6 us
    ppermute x32, waiting for transfers between devices, swap(): return lax.ppermute(value, 'dp', [(i, i ^ bit) for i in range(size)])  37.5 us
    ppermute x18, starting transfers between devices, turn(): lax.ppermute(value, 'blk', [(i, (i + steps) % size) for i in range(size)])  26.6 us
    ppermute x32, starting transfers between devices, swap(): return lax.ppermute(value, 'dp', [(i, i ^ bit) for i in range(size)])  21.6 us
    convert_element_type x7, other arithmetic, add_low(): (left.astype(jnp.float32) + right.astype(jnp.float32)).astype(jnp.bfloat16)  5.9 us
  transfers between devices with their start and end apart: 52, of which 27 were waited for; matrix products, arithmetic and copies ran while one was open for 13% of the time, Pallas kernels for 24%

profile of v4, /device:TPU:18, one launch (start us, length us, event | category | flops | bytes accessed | tf_op | source)
XLA Modules:
  0.0 259.7 jit_solution(6217991655878881224)
XLA Ops:
  7.3 1.1 reshape.189
  9.7 1.6 collective-permute-start
  11.7 1.3 collective-permute-start.2
  13.0 1.1 fusion.1.diagonal_ref
  14.2 3.1 %relative_bias.1.refs_8_ = f32[3,128,1408]{2,1,0:T(8,128)} custom-call(s32[2]{0:T(128)S(1)} %pad_add_fusion.place_ref, f32[3,1536]{1,0:T(4,128)S(1)} %fusion.1.diagonal_ref), custom_call_target="tpu_custom_call" | custom-call | flops 2200000000 | bytes 7200000 | tf_op jit(solution)/shard_map/relative_bias/pallas_call | solution.py:424
  17.4 9.8 %collective-permute-done = bf16[24,4416]{1,0:T(8,128)(2,1)S(1)} collective-permute-done((bf16[24,4416]{1,0:T(8,128)(2,1)S(1)}, bf16[24,4416]{1,0:T(8,128)(2,1)S(1)}, u32[]{:S(2)}, u32[]{:S(2)}) %collective-permute-start) | collective-permute-done | bytes 212000 | tf_op jit(solution)/shard_map/ppermute | solution.py:320
  27.1 2.3 collective-permute-done.2
  30.5 1.5 collective-permute-start.4
  32.1 2.7 %collective-permute-start.5 = (bf16[96,768]{1,0:T(8,128)(2,1)S(1)}, bf16[96,768]{1,0:T(8,128)(2,1)S(1)}, u32[]{:S(2)}, u32[]{:S(2)}) collective-permute-start(bf16[96,768]{1,0:T(8,128)(2,1)S(1)} %copy-done.21), channel_id=1, source_target_pairs={{0,1},{1,2},{2,3},{3,0},{4,5},{5,6},{6,7},{7,4},{8,9},{9,10},{10,1... | collective-permute-start | bytes 442376 | tf_op jit(solution)/shard_map/ppermute | solution.py:320
  34.8 1.3 collective-permute-start.6
  36.3 4.6 %collective-permute-done.5 = bf16[96,768]{1,0:T(8,128)(2,1)S(1)} collective-permute-done((bf16[96,768]{1,0:T(8,128)(2,1)S(1)}, bf16[96,768]{1,0:T(8,128)(2,1)S(1)}, u32[]{:S(2)}, u32[]{:S(2)}) %collective-permute-start.5) | collective-permute-done | bytes 147488 | tf_op jit(solution)/shard_map/ppermute | solution.py:320
  41.0 4.5 %collective-permute-done.6 = bf16[96,768]{1,0:T(8,128)(2,1)S(1)} collective-permute-done((bf16[96,768]{1,0:T(8,128)(2,1)S(1)}, bf16[96,768]{1,0:T(8,128)(2,1)S(1)}, u32[]{:S(2)}, u32[]{:S(2)}) %collective-permute-start.6) | collective-permute-done | bytes 147488 | tf_op jit(solution)/shard_map/ppermute | solution.py:320
  45.4 10.6 %collective-permute-done.7 = bf16[96,768]{1,0:T(8,128)(2,1)S(1)} collective-permute-done((bf16[96,768]{1,0:T(8,128)(2,1)S(1)}, bf16[96,768]{1,0:T(8,128)(2,1)S(1)}, u32[]{:S(2)}, u32[]{:S(2)}) %collective-permute-start.7) | collective-permute-done | bytes 147488 | tf_op jit(solution)/shard_map/ppermute | solution.py:320
  56.0 1.0 slice.244
  57.1 2.9 %collective-permute-start.8 = (bf16[48,4416]{1,0:T(8,128)(2,1)S(1)}, bf16[48,4416]{1,0:T(8,128)(2,1)S(1)}, u32[]{:S(2)}, u32[]{:S(2)}) collective-permute-start(bf16[48,4416]{1,0:T(8,128)(2,1)S(1)} %slice.244), channel_id=1, source_target_pairs={{0,8},{4,12},{8,0},{12,4},{16,24},{20,28},{24,16},{28,20},{1,9},{5... | collective-permute-start | bytes 1271816 | tf_op jit(solution)/shard_map/ppermute | solution.py:315
  59.9 1.0 slice.245
  61.6 7.2 %collective-permute-done.8 = bf16[48,4416]{1,0:T(8,128)(2,1)S(1)} collective-permute-done((bf16[48,4416]{1,0:T(8,128)(2,1)S(1)}, bf16[48,4416]{1,0:T(8,128)(2,1)S(1)}, u32[]{:S(2)}, u32[]{:S(2)}) %collective-permute-start.8) | collective-permute-done | bytes 423968 | tf_op jit(solution)/shard_map/ppermute | solution.py:315
  69.6 3.8 %collective-permute-done.9 = bf16[48,4416]{1,0:T(8,128)(2,1)S(1)} collective-permute-done((bf16[48,4416]{1,0:T(8,128)(2,1)S(1)}, bf16[48,4416]{1,0:T(8,128)(2,1)S(1)}, u32[]{:S(2)}, u32[]{:S(2)}) %collective-permute-start.9) | collective-permute-done | bytes 423968 | tf_op jit(solution)/shard_map/ppermute | solution.py:315
  75.5 1.5 collective-permute-done.13.refs_7_.refs_16_.refs_21_
  77.0 11.6 %attend.1 = (bf16[768,576]{1,0:T(8,128)(2,1)}, bf16[768,576]{1,0:T(8,128)(2,1)}, bf16[768,768]{1,0:T(8,128)(2,1)}, f32[768,192]{1,0:T(8,128)S(1)}, bf16[768,192]...) custom-call(s32[2]{0:T(128)S(1)} %pad_add_fusion.place_ref, f32[1,768]{1,0:T(1,128)S(1)} %broadcast_in_dim.65.gain_ref, ...), custom_call_target="tpu_custom_call" | custom-call | flops 14300000256 | bytes 46800000 | tf_op jit(solution)/shard_map/attend/pallas_call | solution.py:424
  89.4 1.4 collective-permute-done.14.refs_23_
  91.0 1.7 collective-permute-start.16
  93.8 3.6 %collective-permute-start.19 = (bf16[192,192]{1,0:T(8,128)(2,1)S(1)}, bf16[192,192]{1,0:T(8,128)(2,1)S(1)}, u32[]{:S(2)}, u32[]{:S(2)}) collective-permute-start(bf16[192,192]{1,0:T(8,128)(2,1)S(1)} %get-tuple-element.203), channel_id=1, source_target_pairs={{0,2},{1,3},{2,0},{3,1},{4,6},{5,7},{6,4},{7,5},{8,10},{9,11},{10,... | collective-permute-start | bytes 221192 | tf_op jit(solution)/shard_map/ppermute | solution.py:320
  97.6 2.0 collective-permute-done.16
  99.7 1.1 collective-permute-done.17
  100.9 1.3 collective-permute-done.19.refs_2_
  103.3 10.3 %feed_forward.1 = (f32[192,768]{1,0:T(8,128)}, f32[192,768]{1,0:T(8,128)}, bf16[192,768]{1,0:T(8,128)(2,1)S(1)}, f32[192,1]{1,0:T(8,128)S(1)}, f32[192,1]{1,0:T(...) custom-call(s32[2]{0:T(128)S(1)} %pad_add_fusion.place_ref, ...), custom_call_target="tpu_custom_call" | custom-call | flops 9900000256 | bytes 32400000 | tf_op jit(solution)/shard_map/feed_forward/pallas_call | solution.py:424
  115.4 2.0 collective-permute-done.25
  117.3 1.2 fusion.8
  119.4 1.7 collective-permute-start.27
  121.1 24.3 %feed_forward_back.1 = (bf16[192,768]{1,0:T(8,128)(2,1)}, f32[192,768]{1,0:T(8,128)}, f32[1,3072]{1,0:T(1,128)S(1)}, f32[1,768]{1,0:T(1,128)S(1)}, f32[1,768]{1,...) custom-call(s32[2]{0:T(128)S(1)} %pad_add_fusion.place_ref, ...), custom_call_target="tpu_custom_call" | custom-call | flops 14300000256 | bytes 46800000 | tf_op jit(solution)/shard_map/feed_forward_back/pallas_call | solution.py:424
  146.2 2.5 collective-permute-start.29
  148.7 3.2 %collective-permute-start.30 = (bf16[192,192]{1,0:T(8,128)(2,1)S(1)}, bf16[192,192]{1,0:T(8,128)(2,1)S(1)}, u32[]{:S(2)}, u32[]{:S(2)}) collective-permute-start(bf16[192,192]{1,0:T(8,128)(2,1)S(1)} %get-tuple-element.127), channel_id=1, source_target_pairs={{0,2},{1,3},{2,0},{3,1},{4,6},{5,7},{6,4},{7,5},{8,10},{9,11},{10,... | collective-permute-start | bytes 221192 | tf_op jit(solution)/shard_map/ppermute | solution.py:320
  152.0 1.1 collective-permute-done.32
  155.8 1.4 collective-permute-start.33
  157.2 2.3 add_convert_fusion
  160.2 13.1 %attend_back.1 = (bf16[4,96,576]{2,1,0:T(8,128)(2,1)S(1)}, bf16[4,96,576]{2,1,0:T(8,128)(2,1)}, f32[3,1536]{1,0:T(4,128)S(1)}, f32[768,3]{1,0:T(8,128)S(1)}, f32...) custom-call(s32[2]{0:T(128)S(1)} %pad_add_fusion.place_ref, bf16[192,192]{1,0:T(8,128)(2,1)S(1)} %get-tuple-element.125.refs_0_, ...), custom_call_target="tpu_custom_call" | custom-call | flops 13200000000 | bytes 43200000 | tf_op jit(solution)/shard_map/attend_back/pallas_call | solution.py:424
  173.3 1.5 fusion.9
  176.0 1.2 slice_bitcast_fusion
  177.3 2.3 fusion.7
  179.9 1.2 collective-permute-start.39
  181.1 1.4 collective-permute-start.40
  182.5 1.0 collective-permute-start.41
  183.5 1.4 collective-permute-start.36
  186.2 1.3 collective-permute-done.39
  187.5 2.6 %collective-permute-done.40 = bf16[109,576]{1,0:T(8,128)(2,1)S(1)} collective-permute-done((bf16[109,576]{1,0:T(8,128)(2,1)S(1)}, bf16[109,576]{1,0:T(8,128)(2,1)S(1)}, u32[]{:S(2)}, u32[]{:S(2)}) %collective-permute-start.40) | collective-permute-done | bytes 125600 | tf_op jit(solution)/shard_map/ppermute | solution.py:315
  190.1 7.1 %collective-permute-done.36 = bf16[48,3840]{1,0:T(8,128)(2,1)} collective-permute-done((bf16[48,3840]{1,0:T(8,128)(2,1)S(1)}, bf16[48,3840]{1,0:T(8,128)(2,1)}, u32[]{:S(2)}, u32[]{:S(2)}) %collective-permute-start.36) | collective-permute-done | bytes 368672 | tf_op jit(solution)/shard_map/ppermute | solution.py:315
  197.9 1.6 fusion.10
  200.4 1.0 collective-permute-start.43
  205.2 1.1 reduce-scatter.2.cloned.1.call-done
  206.3 1.3 dynamic-slice_bitcast_fusion.4
  207.6 2.0 collective-permute-start.44
  210.2 2.2 collective-permute-start.46
  212.4 1.3 fusion.15
  214.0 1.0 fusion.20
  215.0 4.1 %collective-permute-done.43 = bf16[96,3840]{1,0:T(8,128)(2,1)} collective-permute-done((bf16[96,3840]{1,0:T(8,128)(2,1)}, bf16[96,3840]{1,0:T(8,128)(2,1)}, u32[]{:S(2)}, u32[]{:S(2)}) %collective-permute-start.43) | collective-permute-done | bytes 737312 | tf_op jit(solution)/shard_map/ppermute | solution.py:315
  219.1 1.7 collective-permute-done.42
  220.8 1.5 collective-permute-done.44
  222.3 2.0 collective-permute-done.46
  224.3 1.7 fusion.5
  226.2 2.2 collective-permute-start.47
  228.4 1.8 collective-permute-start.48
  230.2 1.7 fusion.22
  231.9 12.2 %collective-permute-done.47 = bf16[24,4416]{1,0:T(8,128)(2,1)S(1)} collective-permute-done((bf16[24,4416]{1,0:T(8,128)(2,1)S(1)}, bf16[24,4416]{1,0:T(8,128)(2,1)S(1)}, u32[]{:S(2)}, u32[]{:S(2)}) %collective-permute-start.47) | collective-permute-done | bytes 212000 | tf_op jit(solution)/shard_map/ppermute | solution.py:320
  (250 shorter events, 34.3 us)
Async XLA Ops:
  7.2 67.0 %all-gather.2.cloned.1.call-start = ((), (), s32[]{:S(2)}) async-start(), calls=%async_computation.1 | async-start | bytes 1474560 | tf_op jit(solution)/shard_map/all_gather | solution.py:809
  9.7 17.5 %collective-permute-start = (bf16[24,4416]{1,0:T(8,128)(2,1)S(1)}, bf16[24,4416]{1,0:T(8,128)(2,1)S(1)}, u32[]{:S(2)}, u32[]{:S(2)}) collective-permute-start(bf16[24,4416]{1,0:T(8,128)(2,1)S(1)} %get-tuple-element.184), channel_id=1, source_target_pairs={{0,1},{1,2},{2,3},{3,0},{4,5},{5,6},{6,7},{7,4},{8,9},{9,10},{10,1... | collective-permute-start | bytes 635912 | tf_op jit(solution)/shard_map/ppermute | solution.py:320
  11.3 15.8 %collective-permute-start.1 = (bf16[24,4416]{1,0:T(8,128)(2,1)S(1)}, bf16[24,4416]{1,0:T(8,128)(2,1)S(1)}, u32[]{:S(2)}, u32[]{:S(2)}) collective-permute-start(bf16[24,4416]{1,0:T(8,128)(2,1)S(1)} %get-tuple-element.185), channel_id=1, source_target_pairs={{0,2},{1,3},{2,0},{3,1},{4,6},{5,7},{6,4},{7,5},{8,10},{9,11},{10,... | collective-permute-start | bytes 635912 | tf_op jit(solution)/shard_map/ppermute | solution.py:320
  11.7 17.8 %collective-permute-start.2 = (bf16[24,4416]{1,0:T(8,128)(2,1)S(1)}, bf16[24,4416]{1,0:T(8,128)(2,1)S(1)}, u32[]{:S(2)}, u32[]{:S(2)}) collective-permute-start(bf16[24,4416]{1,0:T(8,128)(2,1)S(1)} %get-tuple-element.186), channel_id=1, source_target_pairs={{0,3},{1,0},{2,1},{3,2},{4,7},{5,4},{6,5},{7,6},{8,11},{9,8},{10,9... | collective-permute-start | bytes 635912 | tf_op jit(solution)/shard_map/ppermute | solution.py:320
  29.9 44.3 %copy-start.14 = (bf16[96,4416]{1,0:T(8,128)(2,1)}, bf16[96,4416]{1,0:T(8,128)(2,1)S(1)}, u32[]{:S(2)}) copy-start(bf16[96,4416]{1,0:T(8,128)(2,1)S(1)} %pad_maximum_fusion.refs_0_.refs_9_.refs_14_) | copy-start | bytes 2543620
  29.9 26.1 %collective-permute-start.3 = (bf16[96,4416]{1,0:T(8,128)(2,1)S(1)}, bf16[96,4416]{1,0:T(8,128)(2,1)}, u32[]{:S(2)}, u32[]{:S(2)}) collective-permute-start(bf16[96,4416]{1,0:T(8,128)(2,1)S(1)} %pad_maximum_fusion.refs_0_.refs_9_.refs_14_), channel_id=1, source_target_pairs={{0,8},{4,12},{8,0},{12,4},{16,24},{20,28},{24,16},{28,20},{1,9},{5... | collective-permute-start | bytes 2543624 | tf_op jit(solution)/shard_map/ppermute | solution.py:315
  30.5 25.5 %collective-permute-start.4 = (bf16[96,4416]{1,0:T(8,128)(2,1)S(1)}, bf16[96,4416]{1,0:T(8,128)(2,1)}, u32[]{:S(2)}, u32[]{:S(2)}) collective-permute-start(bf16[96,4416]{1,0:T(8,128)(2,1)S(1)} %pad_maximum_fusion.refs_0_.refs_9_.refs_14_), channel_id=1, source_target_pairs={{0,16},{4,20},{8,24},{12,28},{16,0},{20,4},{24,8},{28,12},{1,17},{... | collective-permute-start | bytes 2543624 | tf_op jit(solution)/shard_map/ppermute | solution.py:315
  32.1 42.2 %copy-start.43 = (s32[1,4]{1,0:T(1,128)S(1)}, s32[1,4]{1,0:T(1,128)}, u32[]{:S(2)}) copy-start(s32[1,4]{1,0:T(1,128)} %param.15) | copy-start | bytes 52
  32.1 42.6 %copy-start.36 = (f32[12]{0:T(128)S(1)}, f32[12]{0:T(128)}, u32[]{:S(2)}) copy-start(f32[12]{0:T(128)} %param.25) | copy-start | bytes 148
  32.1 174.2 %reduce-scatter.2.cloned.1.call-start = ((), (), s32[]{:S(2)}) async-start(), calls=%async_computation.2 | async-start | bytes 1474560 | tf_op jit(solution)/shard_map/reduce_scatter | solution.py:958
  32.1 8.9 %collective-permute-start.5 = (bf16[96,768]{1,0:T(8,128)(2,1)S(1)}, bf16[96,768]{1,0:T(8,128)(2,1)S(1)}, u32[]{:S(2)}, u32[]{:S(2)}) collective-permute-start(bf16[96,768]{1,0:T(8,128)(2,1)S(1)} %copy-done.21), channel_id=1, source_target_pairs={{0,1},{1,2},{2,3},{3,0},{4,5},{5,6},{6,7},{7,4},{8,9},{9,10},{10,1... | collective-permute-start | bytes 442376 | tf_op jit(solution)/shard_map/ppermute | solution.py:320
  34.8 10.6 %collective-permute-start.6 = (bf16[96,768]{1,0:T(8,128)(2,1)S(1)}, bf16[96,768]{1,0:T(8,128)(2,1)S(1)}, u32[]{:S(2)}, u32[]{:S(2)}) collective-permute-start(bf16[96,768]{1,0:T(8,128)(2,1)S(1)} %copy-done.21), channel_id=1, source_target_pairs={{0,2},{1,3},{2,0},{3,1},{4,6},{5,7},{6,4},{7,5},{8,10},{9,11},{10,... | collective-permute-start | bytes 442376 | tf_op jit(solution)/shard_map/ppermute | solution.py:320
  36.1 19.9 %collective-permute-start.7 = (bf16[96,768]{1,0:T(8,128)(2,1)S(1)}, bf16[96,768]{1,0:T(8,128)(2,1)S(1)}, u32[]{:S(2)}, u32[]{:S(2)}) collective-permute-start(bf16[96,768]{1,0:T(8,128)(2,1)S(1)} %copy-done.21), channel_id=1, source_target_pairs={{0,3},{1,0},{2,1},{3,2},{4,7},{5,4},{6,5},{7,6},{8,11},{9,8},{10,9... | collective-permute-start | bytes 442376 | tf_op jit(solution)/shard_map/ppermute | solution.py:320
  57.1 17.8 %copy-start.29 = (f32[768]{0:T(1024)S(1)}, f32[768]{0:T(1024)}, u32[]{:S(2)}) copy-start(f32[768]{0:T(1024)} %param.21) | copy-start | bytes 9220
  57.1 11.7 %collective-permute-start.8 = (bf16[48,4416]{1,0:T(8,128)(2,1)S(1)}, bf16[48,4416]{1,0:T(8,128)(2,1)S(1)}, u32[]{:S(2)}, u32[]{:S(2)}) collective-permute-start(bf16[48,4416]{1,0:T(8,128)(2,1)S(1)} %slice.244), channel_id=1, source_target_pairs={{0,8},{4,12},{8,0},{12,4},{16,24},{20,28},{24,16},{28,20},{1,9},{5... | collective-permute-start | bytes 1271816 | tf_op jit(solution)/shard_map/ppermute | solution.py:315
  61.0 14.5 %collective-permute-start.11 = (bf16[96,4416]{1,0:T(8,128)(2,1)}, bf16[96,4416]{1,0:T(8,128)(2,1)}, u32[]{:S(2)}, u32[]{:S(2)}) collective-permute-start(bf16[96,4416]{1,0:T(8,128)(2,1)} %collective-permute-done.3.refs_1_.refs_10_.refs_15_), channel_id=1, source_target_pairs={{0,4},{4,0},{8,12},{12,8},{16,20},{20,16},{24,28},{28,24},{1,5},{5... | collective-permute-start | bytes 2543624 | tf_op jit(solution)/shard_map/ppermute | solution.py:315
  61.1 14.4 %collective-permute-start.12 = (bf16[96,4416]{1,0:T(8,128)(2,1)}, bf16[96,4416]{1,0:T(8,128)(2,1)}, u32[]{:S(2)}, u32[]{:S(2)}) collective-permute-start(bf16[96,4416]{1,0:T(8,128)(2,1)} %collective-permute-done.4.refs_2_.refs_11_.refs_16_), channel_id=1, source_target_pairs={{0,4},{4,0},{8,12},{12,8},{16,20},{20,16},{24,28},{28,24},{1,5},{5... | collective-permute-start | bytes 2543624 | tf_op jit(solution)/shard_map/ppermute | solution.py:315
  61.6 11.9 %collective-permute-start.9 = (bf16[48,4416]{1,0:T(8,128)(2,1)S(1)}, bf16[48,4416]{1,0:T(8,128)(2,1)S(1)}, u32[]{:S(2)}, u32[]{:S(2)}) collective-permute-start(bf16[48,4416]{1,0:T(8,128)(2,1)S(1)} %slice.245), channel_id=1, source_target_pairs={{0,16},{4,20},{8,24},{12,28},{16,0},{20,4},{24,8},{28,12},{1,17},{... | collective-permute-start | bytes 1271816 | tf_op jit(solution)/shard_map/ppermute | solution.py:315
  61.6 13.6 %collective-permute-start.10 = (bf16[96,4416]{1,0:T(8,128)(2,1)S(1)}, bf16[96,4416]{1,0:T(8,128)(2,1)}, u32[]{:S(2)}, u32[]{:S(2)}) collective-permute-start(bf16[96,4416]{1,0:T(8,128)(2,1)S(1)} %pad_maximum_fusion.refs_0_.refs_9_.refs_14_), channel_id=1, source_target_pairs={{0,4},{4,0},{8,12},{12,8},{16,20},{20,16},{24,28},{28,24},{1,5},{5... | collective-permute-start | bytes 2543624 | tf_op jit(solution)/shard_map/ppermute | solution.py:315
  74.2 2.7 %collective-permute-start.13 = (bf16[96,4416]{1,0:T(8,128)(2,1)}, bf16[96,4416]{1,0:T(8,128)(2,1)}, u32[]{:S(2)}, u32[]{:S(2)}) collective-permute-start(bf16[96,4416]{1,0:T(8,128)(2,1)} %constant_dynamic-update-slice_fusion.refs_3_.refs_12_.refs_17_), channel_id=1, source_target_pairs={{0,4},{4,0},{8,12},{12,8},{16,20},{20,16},{24,28},{28,24},{1,5},{5... | collective-permute-start | bytes 2543624 | tf_op jit(solution)/shard_map/ppermute | solution.py:315
  75.0 27.2 %copy-start.15 = (bf16[384,768]{1,0:T(8,128)(2,1)}, bf16[384,768]{1,0:T(8,128)(2,1)S(1)}, u32[]{:S(2)}) copy-start(bf16[384,768]{1,0:T(8,128)(2,1)S(1)} %pad_maximum_fusion.5.refs_22_) | copy-start | bytes 1769476
  75.0 15.8 %collective-permute-start.14 = (bf16[384,768]{1,0:T(8,128)(2,1)S(1)}, bf16[384,768]{1,0:T(8,128)(2,1)S(1)}, u32[]{:S(2)}, u32[]{:S(2)}) collective-permute-start(bf16[384,768]{1,0:T(8,128)(2,1)S(1)} %pad_maximum_fusion.5.refs_22_), channel_id=1, source_target_pairs={{0,8},{4,12},{8,0},{12,4},{16,24},{20,28},{24,16},{28,20},{1,9},{5... | collective-permute-start | bytes 1769480 | tf_op jit(solution)/shard_map/ppermute | solution.py:315
  75.1 15.8 %collective-permute-start.15 = (bf16[384,768]{1,0:T(8,128)(2,1)S(1)}, bf16[384,768]{1,0:T(8,128)(2,1)S(1)}, u32[]{:S(2)}, u32[]{:S(2)}) collective-permute-start(bf16[384,768]{1,0:T(8,128)(2,1)S(1)} %pad_maximum_fusion.5.refs_22_), channel_id=1, source_target_pairs={{0,16},{4,20},{8,24},{12,28},{16,0},{20,4},{24,8},{28,12},{1,17},{... | collective-permute-start | bytes 1769480 | tf_op jit(solution)/shard_map/ppermute | solution.py:315
  77.0 16.1 %copy-start.34 = (f32[768]{0:T(1024)S(1)}, f32[768]{0:T(1024)}, u32[]{:S(2)}) copy-start(f32[768]{0:T(1024)} %param.22) | copy-start | bytes 9220
  77.0 16.1 %copy-start.35 = (f32[768]{0:T(1024)S(1)}, f32[768]{0:T(1024)}, u32[]{:S(2)}) copy-start(f32[768]{0:T(1024)} %param.23) | copy-start | bytes 9220
  90.8 22.7 %copy-start.22 = (bf16[384,768]{1,0:T(8,128)(2,1)}, bf16[384,768]{1,0:T(8,128)(2,1)S(1)}, u32[]{:S(2)}) copy-start(bf16[384,768]{1,0:T(8,128)(2,1)S(1)} %collective-permute-done.14.refs_23_) | copy-start | bytes 1769476
  90.9 22.6 %copy-start.23 = (bf16[384,768]{1,0:T(8,128)(2,1)}, bf16[384,768]{1,0:T(8,128)(2,1)S(1)}, u32[]{:S(2)}) copy-start(bf16[384,768]{1,0:T(8,128)(2,1)S(1)} %collective-permute-done.15.refs_24_) | copy-start | bytes 1769476
  91.0 8.7 %collective-permute-start.16 = (bf16[192,768]{1,0:T(8,128)(2,1)S(1)}, bf16[192,768]{1,0:T(8,128)(2,1)S(1)}, u32[]{:S(2)}, u32[]{:S(2)}) collective-permute-start(bf16[192,768]{1,0:T(8,128)(2,1)S(1)} %slice.246), channel_id=1, source_target_pairs={{0,8},{4,12},{8,0},{12,4},{16,24},{20,28},{24,16},{28,20},{1,9},{5... | collective-permute-start | bytes 884744 | tf_op jit(solution)/shard_map/ppermute | solution.py:315
  92.7 8.1 %collective-permute-start.17 = (bf16[192,768]{1,0:T(8,128)(2,1)S(1)}, bf16[192,768]{1,0:T(8,128)(2,1)S(1)}, u32[]{:S(2)}, u32[]{:S(2)}) collective-permute-start(bf16[192,768]{1,0:T(8,128)(2,1)S(1)} %slice.247), channel_id=1, source_target_pairs={{0,16},{4,20},{8,24},{12,28},{16,0},{20,4},{24,8},{28,12},{1,17},{... | collective-permute-start | bytes 884744 | tf_op jit(solution)/shard_map/ppermute | solution.py:315
  93.1 7.7 %collective-permute-start.18 = (bf16[192,192]{1,0:T(8,128)(2,1)S(1)}, bf16[192,192]{1,0:T(8,128)(2,1)S(1)}, u32[]{:S(2)}, u32[]{:S(2)}) collective-permute-start(bf16[192,192]{1,0:T(8,128)(2,1)S(1)} %get-tuple-element.204), channel_id=1, source_target_pairs={{0,1},{1,2},{2,3},{3,0},{4,5},{5,6},{6,7},{7,4},{8,9},{9,10},{10,1... | collective-permute-start | bytes 221192 | tf_op jit(solution)/shard_map/ppermute | solution.py:320
  93.8 8.3 %collective-permute-start.19 = (bf16[192,192]{1,0:T(8,128)(2,1)S(1)}, bf16[192,192]{1,0:T(8,128)(2,1)S(1)}, u32[]{:S(2)}, u32[]{:S(2)}) collective-permute-start(bf16[192,192]{1,0:T(8,128)(2,1)S(1)} %get-tuple-element.203), channel_id=1, source_target_pairs={{0,2},{1,3},{2,0},{3,1},{4,6},{5,7},{6,4},{7,5},{8,10},{9,11},{10,... | collective-permute-start | bytes 221192 | tf_op jit(solution)/shard_map/ppermute | solution.py:320
  97.4 4.9 %collective-permute-start.20 = (bf16[192,192]{1,0:T(8,128)(2,1)S(1)}, bf16[192,192]{1,0:T(8,128)(2,1)S(1)}, u32[]{:S(2)}, u32[]{:S(2)}) collective-permute-start(bf16[192,192]{1,0:T(8,128)(2,1)S(1)} %get-tuple-element.202), channel_id=1, source_target_pairs={{0,3},{1,0},{2,1},{3,2},{4,7},{5,4},{6,5},{7,6},{8,11},{9,8},{10,9... | collective-permute-start | bytes 221192 | tf_op jit(solution)/shard_map/ppermute | solution.py:320
  102.2 11.3 %collective-permute-start.21 = (bf16[384,768]{1,0:T(8,128)(2,1)S(1)}, bf16[384,768]{1,0:T(8,128)(2,1)S(1)}, u32[]{:S(2)}, u32[]{:S(2)}) collective-permute-start(bf16[384,768]{1,0:T(8,128)(2,1)S(1)} %pad_maximum_fusion.5.refs_22_), channel_id=1, source_target_pairs={{0,4},{4,0},{8,12},{12,8},{16,20},{20,16},{24,28},{28,24},{1,5},{5... | collective-permute-start | bytes 1769480 | tf_op jit(solution)/shard_map/ppermute | solution.py:315
  102.2 11.4 %collective-permute-start.22 = (bf16[384,768]{1,0:T(8,128)(2,1)S(1)}, bf16[384,768]{1,0:T(8,128)(2,1)S(1)}, u32[]{:S(2)}, u32[]{:S(2)}) collective-permute-start(bf16[384,768]{1,0:T(8,128)(2,1)S(1)} %collective-permute-done.14.refs_23_), channel_id=1, source_target_pairs={{0,4},{4,0},{8,12},{12,8},{16,20},{20,16},{24,28},{28,24},{1,5},{5... | collective-permute-start | bytes 1769480 | tf_op jit(solution)/shard_map/ppermute | solution.py:315
  102.7 10.9 %collective-permute-start.23 = (bf16[384,768]{1,0:T(8,128)(2,1)S(1)}, bf16[384,768]{1,0:T(8,128)(2,1)S(1)}, u32[]{:S(2)}, u32[]{:S(2)}) collective-permute-start(bf16[384,768]{1,0:T(8,128)(2,1)S(1)} %collective-permute-done.15.refs_24_), channel_id=1, source_target_pairs={{0,4},{4,0},{8,12},{12,8},{16,20},{20,16},{24,28},{28,24},{1,5},{5... | collective-permute-start | bytes 1769480 | tf_op jit(solution)/shard_map/ppermute | solution.py:315
  102.8 10.9 %collective-permute-start.24 = (bf16[384,768]{1,0:T(8,128)(2,1)S(1)}, bf16[384,768]{1,0:T(8,128)(2,1)S(1)}, u32[]{:S(2)}, u32[]{:S(2)}) collective-permute-start(bf16[384,768]{1,0:T(8,128)(2,1)S(1)} %constant_dynamic-update-slice_fusion.2.refs_25_), channel_id=1, source_target_pairs={{0,4},{4,0},{8,12},{12,8},{16,20},{20,16},{24,28},{28,24},{1,5},{5... | collective-permute-start | bytes 1769480 | tf_op jit(solution)/shard_map/ppermute | solution.py:315
  115.1 2.2 collective-permute-start.25
  118.6 26.8 %collective-permute-start.26 = (bf16[192,768]{1,0:T(8,128)(2,1)S(1)}, bf16[192,768]{1,0:T(8,128)(2,1)S(1)}, u32[]{:S(2)}, u32[]{:S(2)}) collective-permute-start(bf16[192,768]{1,0:T(8,128)(2,1)S(1)} %get-tuple-element.194), channel_id=1, source_target_pairs={{0,8},{4,12},{8,0},{12,4},{16,24},{20,28},{24,16},{28,20},{1,9},{5... | collective-permute-start | bytes 884744 | tf_op jit(solution)/shard_map/ppermute | solution.py:315
  119.4 26.1 %collective-permute-start.27 = (bf16[192,768]{1,0:T(8,128)(2,1)S(1)}, bf16[192,768]{1,0:T(8,128)(2,1)S(1)}, u32[]{:S(2)}, u32[]{:S(2)}) collective-permute-start(bf16[192,768]{1,0:T(8,128)(2,1)S(1)} %get-tuple-element.193), channel_id=1, source_target_pairs={{0,16},{4,20},{8,24},{12,28},{16,0},{20,4},{24,8},{28,12},{1,17},{... | collective-permute-start | bytes 884744 | tf_op jit(solution)/shard_map/ppermute | solution.py:315
  121.1 24.5 %copy-start.38 = (bf16[3,384,768]{2,1,0:T(8,128)(2,1)S(1)}, bf16[3,384,768]{2,1,0:T(8,128)(2,1)}, u32[]{:S(2)}) copy-start(bf16[3,384,768]{2,1,0:T(8,128)(2,1)} %get-tuple-element.135) | copy-start | bytes 5308420
  121.1 32.0 %copy-start.9 = (bf16[4,384,768]{2,1,0:T(8,128)(2,1)S(1)}, bf16[4,384,768]{2,1,0:T(8,128)(2,1)}, u32[]{:S(2)}) copy-start(bf16[4,384,768]{2,1,0:T(8,128)(2,1)} %get-tuple-element.98) | copy-start | bytes 7077892
  145.4 10.4 %collective-permute-start.28 = (bf16[4,96,3840]{2,1,0:T(8,128)(2,1)}, bf16[4,96,3840]{2,1,0:T(8,128)(2,1)S(1)}, u32[]{:S(2)}, u32[]{:S(2)}) collective-permute-start(bf16[4,96,3840]{2,1,0:T(8,128)(2,1)} %get-tuple-element.124), channel_id=1, source_target_pairs={{0,4},{4,0},{8,12},{12,8},{16,20},{20,16},{24,28},{28,24},{1,5},{5... | collective-permute-start | bytes 8847368 | tf_op jit(solution)/shard_map/ppermute | solution.py:315
  145.5 7.5 %collective-permute-start.32 = (bf16[3,384,768]{2,1,0:T(8,128)(2,1)S(1)}, bf16[3,384,768]{2,1,0:T(8,128)(2,1)S(1)}, u32[]{:S(2)}, u32[]{:S(2)}) collective-permute-start(bf16[3,384,768]{2,1,0:T(8,128)(2,1)S(1)} %copy-done.38), channel_id=1, source_target_pairs={{0,4},{4,0},{8,12},{12,8},{16,20},{20,16},{24,28},{28,24},{1,5},{5... | collective-permute-start | bytes 5308424 | tf_op jit(solution)/shard_map/ppermute | solution.py:315
  146.2 13.3 %collective-permute-start.29 = (bf16[192,192]{1,0:T(8,128)(2,1)S(1)}, bf16[192,192]{1,0:T(8,128)(2,1)S(1)}, u32[]{:S(2)}, u32[]{:S(2)}) collective-permute-start(bf16[192,192]{1,0:T(8,128)(2,1)S(1)} %get-tuple-element.126), channel_id=1, source_target_pairs={{0,3},{1,0},{2,1},{3,2},{4,7},{5,4},{6,5},{7,6},{8,11},{9,8},{10,9... | collective-permute-start | bytes 221192 | tf_op jit(solution)/shard_map/ppermute | solution.py:320
  148.7 10.8 %collective-permute-start.30 = (bf16[192,192]{1,0:T(8,128)(2,1)S(1)}, bf16[192,192]{1,0:T(8,128)(2,1)S(1)}, u32[]{:S(2)}, u32[]{:S(2)}) collective-permute-start(bf16[192,192]{1,0:T(8,128)(2,1)S(1)} %get-tuple-element.127), channel_id=1, source_target_pairs={{0,2},{1,3},{2,0},{3,1},{4,6},{5,7},{6,4},{7,5},{8,10},{9,11},{10,... | collective-permute-start | bytes 221192 | tf_op jit(solution)/shard_map/ppermute | solution.py:320
  152.0 8.3 %collective-permute-start.31 = (bf16[192,192]{1,0:T(8,128)(2,1)S(1)}, bf16[192,192]{1,0:T(8,128)(2,1)S(1)}, u32[]{:S(2)}, u32[]{:S(2)}) collective-permute-start(bf16[192,192]{1,0:T(8,128)(2,1)S(1)} %get-tuple-element.128), channel_id=1, source_target_pairs={{0,1},{1,2},{2,3},{3,0},{4,5},{5,6},{6,7},{7,4},{8,9},{9,10},{10,1... | collective-permute-start | bytes 221192 | tf_op jit(solution)/shard_map/ppermute | solution.py:320
  154.6 22.7 %collective-permute-start.34 = (bf16[384,768]{1,0:T(8,128)(2,1)}, bf16[384,768]{1,0:T(8,128)(2,1)}, u32[]{:S(2)}, u32[]{:S(2)}) collective-permute-start(bf16[384,768]{1,0:T(8,128)(2,1)} %pad_maximum_fusion.7), channel_id=1, source_target_pairs={{0,16},{4,20},{8,24},{12,28},{16,0},{20,4},{24,8},{28,12},{1,17},{... | collective-permute-start | bytes 1769480 | tf_op jit(solution)/shard_map/ppermute | solution.py:315
  155.8 21.5 %collective-permute-start.33 = (bf16[384,768]{1,0:T(8,128)(2,1)}, bf16[384,768]{1,0:T(8,128)(2,1)}, u32[]{:S(2)}, u32[]{:S(2)}) collective-permute-start(bf16[384,768]{1,0:T(8,128)(2,1)} %pad_maximum_fusion.6), channel_id=1, source_target_pairs={{0,8},{4,12},{8,0},{12,4},{16,24},{20,28},{24,16},{28,20},{1,9},{5... | collective-permute-start | bytes 1769480 | tf_op jit(solution)/shard_map/ppermute | solution.py:315
  175.4 4.2 %collective-permute-start.38 = (bf16[13,576]{1,0:T(8,128)(2,1)S(1)}, bf16[13,576]{1,0:T(8,128)(2,1)S(1)}, u32[]{:S(2)}, u32[]{:S(2)}) collective-permute-start(bf16[13,576]{1,0:T(8,128)(2,1)S(1)} %convert_element_type.282), channel_id=1, source_target_pairs={{0,4},{4,0},{8,12},{12,8},{16,20},{20,16},{24,28},{28,24},{1,5},{5... | collective-permute-start | bytes 44936 | tf_op jit(solution)/shard_map/ppermute | solution.py:315
  175.5 4.1 %collective-permute-start.35 = (bf16[4,96,576]{2,1,0:T(8,128)(2,1)S(1)}, bf16[4,96,576]{2,1,0:T(8,128)(2,1)S(1)}, u32[]{:S(2)}, u32[]{:S(2)}) collective-permute-start(bf16[4,96,576]{2,1,0:T(8,128)(2,1)S(1)} %get-tuple-element.138), channel_id=1, source_target_pairs={{0,4},{4,0},{8,12},{12,8},{16,20},{20,16},{24,28},{28,24},{1,5},{5... | collective-permute-start | bytes 1327112 | tf_op jit(solution)/shard_map/ppermute | solution.py:315
  179.9 7.6 %collective-permute-start.39 = (bf16[109,576]{1,0:T(8,128)(2,1)S(1)}, bf16[109,576]{1,0:T(8,128)(2,1)S(1)}, u32[]{:S(2)}, u32[]{:S(2)}) collective-permute-start(bf16[109,576]{1,0:T(8,128)(2,1)S(1)} %get-tuple-element.212), channel_id=1, source_target_pairs={{0,24},{4,28},{8,16},{12,20},{16,8},{20,12},{24,0},{28,4},{1,25},{... | collective-permute-start | bytes 376712 | tf_op jit(solution)/shard_map/ppermute | solution.py:315
  181.1 9.1 %collective-permute-start.40 = (bf16[109,576]{1,0:T(8,128)(2,1)S(1)}, bf16[109,576]{1,0:T(8,128)(2,1)S(1)}, u32[]{:S(2)}, u32[]{:S(2)}) collective-permute-start(bf16[109,576]{1,0:T(8,128)(2,1)S(1)} %get-tuple-element.211), channel_id=1, source_target_pairs={{0,8},{4,12},{8,0},{12,4},{16,24},{20,28},{24,16},{28,20},{1,9},{5... | collective-permute-start | bytes 376712 | tf_op jit(solution)/shard_map/ppermute | solution.py:315
  182.5 7.7 %collective-permute-start.41 = (bf16[109,576]{1,0:T(8,128)(2,1)S(1)}, bf16[109,576]{1,0:T(8,128)(2,1)S(1)}, u32[]{:S(2)}, u32[]{:S(2)}) collective-permute-start(bf16[109,576]{1,0:T(8,128)(2,1)S(1)} %get-tuple-element.210), channel_id=1, source_target_pairs={{0,16},{4,20},{8,24},{12,28},{16,0},{20,4},{24,8},{28,12},{1,17},{... | collective-permute-start | bytes 376712 | tf_op jit(solution)/shard_map/ppermute | solution.py:315
  183.5 13.7 %collective-permute-start.36 = (bf16[48,3840]{1,0:T(8,128)(2,1)S(1)}, bf16[48,3840]{1,0:T(8,128)(2,1)}, u32[]{:S(2)}, u32[]{:S(2)}) collective-permute-start(bf16[48,3840]{1,0:T(8,128)(2,1)S(1)} %get-tuple-element.188), channel_id=1, source_target_pairs={{0,8},{4,12},{8,0},{12,4},{16,24},{20,28},{24,16},{28,20},{1,9},{5... | collective-permute-start | bytes 1105928 | tf_op jit(solution)/shard_map/ppermute | solution.py:315
  184.9 12.8 %collective-permute-start.37 = (bf16[48,3840]{1,0:T(8,128)(2,1)S(1)}, bf16[48,3840]{1,0:T(8,128)(2,1)}, u32[]{:S(2)}, u32[]{:S(2)}) collective-permute-start(bf16[48,3840]{1,0:T(8,128)(2,1)S(1)} %get-tuple-element.187), channel_id=1, source_target_pairs={{0,16},{4,20},{8,24},{12,28},{16,0},{20,4},{24,8},{28,12},{1,17},{... | collective-permute-start | bytes 1105928 | tf_op jit(solution)/shard_map/ppermute | solution.py:315
  200.4 18.7 %collective-permute-start.43 = (bf16[96,3840]{1,0:T(8,128)(2,1)}, bf16[96,3840]{1,0:T(8,128)(2,1)}, u32[]{:S(2)}, u32[]{:S(2)}) collective-permute-start(bf16[96,3840]{1,0:T(8,128)(2,1)} %pad_maximum_fusion.3), channel_id=1, source_target_pairs={{0,16},{4,20},{8,24},{12,28},{16,0},{20,4},{24,8},{28,12},{1,17},{... | collective-permute-start | bytes 2211848 | tf_op jit(solution)/shard_map/ppermute | solution.py:315
  202.4 18.4 %collective-permute-start.42 = (bf16[96,3840]{1,0:T(8,128)(2,1)}, bf16[96,3840]{1,0:T(8,128)(2,1)}, u32[]{:S(2)}, u32[]{:S(2)}) collective-permute-start(bf16[96,3840]{1,0:T(8,128)(2,1)} %pad_maximum_fusion.2), channel_id=1, source_target_pairs={{0,8},{4,12},{8,0},{12,4},{16,24},{20,28},{24,16},{28,20},{1,9},{5... | collective-permute-start | bytes 2211848 | tf_op jit(solution)/shard_map/ppermute | solution.py:315
  207.6 14.7 %collective-permute-start.44 = (bf16[106,768]{1,0:T(8,128)(2,1)S(1)}, bf16[106,768]{1,0:T(8,128)(2,1)S(1)}, u32[]{:S(2)}, u32[]{:S(2)}) collective-permute-start(bf16[106,768]{1,0:T(8,128)(2,1)S(1)} %get-tuple-element.192), channel_id=1, source_target_pairs={{0,1},{1,2},{2,3},{3,0},{4,5},{5,6},{6,7},{7,4},{8,9},{9,10},{10,1... | collective-permute-start | bytes 488456 | tf_op jit(solution)/shard_map/ppermute | solution.py:320
  209.6 12.7 %collective-permute-start.45 = (bf16[106,768]{1,0:T(8,128)(2,1)S(1)}, bf16[106,768]{1,0:T(8,128)(2,1)S(1)}, u32[]{:S(2)}, u32[]{:S(2)}) collective-permute-start(bf16[106,768]{1,0:T(8,128)(2,1)S(1)} %get-tuple-element.191), channel_id=1, source_target_pairs={{0,2},{1,3},{2,0},{3,1},{4,6},{5,7},{6,4},{7,5},{8,10},{9,11},{10,... | collective-permute-start | bytes 488456 | tf_op jit(solution)/shard_map/ppermute | solution.py:320
  210.2 14.1 %collective-permute-start.46 = (bf16[106,768]{1,0:T(8,128)(2,1)S(1)}, bf16[106,768]{1,0:T(8,128)(2,1)S(1)}, u32[]{:S(2)}, u32[]{:S(2)}) collective-permute-start(bf16[106,768]{1,0:T(8,128)(2,1)S(1)} %get-tuple-element.190), channel_id=1, source_target_pairs={{0,3},{1,0},{2,1},{3,2},{4,7},{5,4},{6,5},{7,6},{8,11},{9,8},{10,9... | collective-permute-start | bytes 488456 | tf_op jit(solution)/shard_map/ppermute | solution.py:320
  226.1 21.4 %copy-start.37 = (f32[12]{0:T(128)S(1)}, f32[12]{0:T(128)}, u32[]{:S(2)}) copy-start(f32[12]{0:T(128)} %param.25) | copy-start | bytes 148
  226.2 18.0 %collective-permute-start.47 = (bf16[24,4416]{1,0:T(8,128)(2,1)S(1)}, bf16[24,4416]{1,0:T(8,128)(2,1)S(1)}, u32[]{:S(2)}, u32[]{:S(2)}) collective-permute-start(bf16[24,4416]{1,0:T(8,128)(2,1)S(1)} %get-tuple-element.183), channel_id=1, source_target_pairs={{0,1},{1,2},{2,3},{3,0},{4,5},{5,6},{6,7},{7,4},{8,9},{9,10},{10,1... | collective-permute-start | bytes 635912 | tf_op jit(solution)/shard_map/ppermute | solution.py:320
  228.4 21.5 %collective-permute-start.48 = (bf16[24,4416]{1,0:T(8,128)(2,1)S(1)}, bf16[24,4416]{1,0:T(8,128)(2,1)S(1)}, u32[]{:S(2)}, u32[]{:S(2)}) collective-permute-start(bf16[24,4416]{1,0:T(8,128)(2,1)S(1)} %get-tuple-element.182), channel_id=1, source_target_pairs={{0,2},{1,3},{2,0},{3,1},{4,6},{5,7},{6,4},{7,5},{8,10},{9,11},{10,... | collective-permute-start | bytes 635912 | tf_op jit(solution)/shard_map/ppermute | solution.py:320
  230.2 19.6 %collective-permute-start.49 = (bf16[24,4416]{1,0:T(8,128)(2,1)S(1)}, bf16[24,4416]{1,0:T(8,128)(2,1)S(1)}, u32[]{:S(2)}, u32[]{:S(2)}) collective-permute-start(bf16[24,4416]{1,0:T(8,128)(2,1)S(1)} %get-tuple-element.181), channel_id=1, source_target_pairs={{0,3},{1,0},{2,1},{3,2},{4,7},{5,4},{6,5},{7,6},{8,11},{9,8},{10,9... | collective-permute-start | bytes 635912 | tf_op jit(solution)/shard_map/ppermute | solution.py:320
  (32 other events, 190.6 us)
Sparse Core Ops, SparseCore 0:
  32.2 34.3 all-gather.1
  176.2 30.1 reduce-scatter.1

commit v5 on v4

--- a/solution.py
+++ b/solution.py
@@ -415,7 +415,7 @@
     )
 
 
-tile_cols = 512
+tile_cols = 256
 far_first = (x_bit | y_bit, x_bit, y_bit, 0)
 
 
@@ -545,7 +545,7 @@
     tokens_ref, gain_attn_ref, gain_mid_ref, gain_hidden_ref, cotangent_ref, *refs = refs
     blocks, refs = refs[:8], refs[8:]
     (attn_ref, middle_ref, normed_ref, mean_ref, scale_ref, activated_ref,
-     hidden_out, below_out, across_out, send_out, keep_out,
+     hidden_out, across_out, send_out, keep_out,
      wout_ref, fc1_ref, hidden_ref, below_ref, grads_ref, semaphores) = refs
     copies = Copies(semaphores)
     part = pieces[0].shape[1]
@@ -574,7 +574,6 @@
         hidden_ref[:, cols] = hidden
         below_ref[:, cols] = below
         leaving.append(copies.start(hidden_ref.at[:, cols], hidden_out.at[:, cols]))
-        leaving.append(copies.start(below_ref.at[:, cols], below_out.at[:, cols]))
         total = total + jnp.sum(hidden * below, axis=1, keepdims=True)
     mean = total / hidden_width
     total = jnp.zeros(mean_ref.shape, jnp.float32)
@@ -602,7 +601,7 @@
     (cotangent_ref, attn_ref, middle_ref, normed_ref, mean_ref, scale_ref, gain_attn_ref, gain_mid_ref,
      gain_hidden_ref, head_scale_ref, *refs) = refs
     first_blocks, second_blocks, refs = refs[:8], refs[8:16], refs[16:]
-    hidden_in, below_in, activated_in, *refs = refs
+    hidden_in, activated_in, *refs = refs
     mixed_ref, d_middle_ref, d_hidden_gain_ref, d_mid_gain_ref, d_attn_gain_ref, *refs = refs
     grads, refs = refs[:line], refs[line:]
     (send_out, keep_out, wout_ref, fc1_ref, fc2_ref, hidden_ref, below_ref, activated_ref, inner_ref, fc1_grad,
@@ -610,8 +609,12 @@
     copies = Copies(semaphores)
     part = pieces[0].shape[1]
     hidden_width, width = fc1_ref.shape[1], wout_ref.shape[1]
-    hidden_here = [copies.start(hidden_in, hidden_ref), copies.start(below_in, below_ref)]
-    fc2_here = fill_planes(copies, place_ref, second_blocks, slice(0, width), fc2_ref)
+    fc2_here, hidden_here = [], []
+    for bit, block in zip(near_first + tuple(bit | core_bit for bit in near_first), second_blocks):
+        size = block.shape[0]
+        part_here = pl.ds(pl.multiple_of((place_ref[0] ^ bit) * size, lanes), size)
+        fc2_here.append(copies.start(block, fc2_ref.at[part_here, :]))
+        hidden_here.append(copies.start(hidden_in.at[:, part_here], hidden_ref.at[:, part_here]))
     fc1_here = fill_planes(copies, place_ref, first_blocks, slice(0, hidden_width), fc1_ref)
     activated_here = copies.start(activated_in, activated_ref)
     wout_here = fill_planes(
@@ -620,12 +623,18 @@
     grad_in = cotangent_ref[...]
     mean, scale = mean_ref[...], scale_ref[...]
     tiles = [slice(begin, begin + tile_cols) for begin in range(0, hidden_width, tile_cols)]
-    wait_all(hidden_here + fc2_here)
+    size = hidden_width // len(fc2_here)
+    bits = near_first + tuple(bit | core_bit for bit in near_first)
     total = jnp.zeros(mean.shape, jnp.float32)
     along = jnp.zeros(mean.shape, jnp.float32)
-    for cols in tiles:
+    for bit, arriving in zip(bits, zip(fc2_here, hidden_here)):
+        wait_all(arriving)
+        cols = pl.ds(pl.multiple_of((place_ref[0] ^ bit) * size, lanes), size)
         d_activated = contract(grad_in, fc2_ref[cols, :], 1, 1)
-        normed = (hidden_ref[:, cols] * below_ref[:, cols] - mean) * scale
+        hidden = hidden_ref[:, cols]
+        below = 0.5 * (1.0 + lax.erf(hidden * (0.5**0.5)))
+        below_ref[:, cols] = below
+        normed = (hidden * below - mean) * scale
         d_hidden_gain_ref[:, cols] = jnp.sum(d_activated * normed, axis=0, keepdims=True)
         inner = d_activated * gain_hidden_ref[:, cols]
         inner_ref[:, cols] = inner
@@ -677,7 +686,7 @@
     pieces, refs = refs[:line], refs[line:]
     (qkv_ref, attention_ref, probs_in, normed_in, w_in,
      send_ref, keep_ref, diagonal_ref, delta_ref, gain_ref, d_normed_out,
-     grad_ref, out_ref, w_grad, sums, probs_ref, normed_ref, w_ref, d_normed_ref, semaphores) = refs
+     grad_ref, out_ref, w_grad, sums, probs_ref, normed_ref, w_ref, d_normed_ref, scores_ref, semaphores) = refs
     copies = Copies(semaphores)
     probs_here = [copies.start(probs_in.at[head], probs_ref.at[head]) for head in range(heads)]
     rest_here = [copies.start(w_in, w_ref), copies.start(normed_in, normed_ref)]
@@ -695,24 +704,23 @@
         low = head * head_size
         keys = qkv_ref[:, width + low : width + low + head_size]
         values = qkv_ref[:, 2 * width + low : 2 * width + low + head_size]
-        d_keys = jnp.zeros((head_size, length), jnp.float32)
-        d_values = jnp.zeros((head_size, length), jnp.float32)
+        queries = qkv_ref[:, low : low + head_size]
+        grad = grad_ref[:, low : low + head_size]
+        product = grad.astype(jnp.float32) * attention_ref[:, low : low + head_size]
+        delta = jnp.sum(product, axis=1, keepdims=True)
+        delta_ref[:, head : head + 1] = delta
+        d_probs = contract(grad, values, 1, 1)
         for block in range(blocks):
             rows = slice(block * lanes, (block + 1) * lanes)
             first = (blocks - 1 - block) * lanes
-            queries = qkv_ref[rows, low : low + head_size]
-            grad = grad_ref[rows, low : low + head_size]
-            probs = probs_ref[head, rows, :]
-            product = grad.astype(jnp.float32) * attention_ref[rows, low : low + head_size]
-            delta = jnp.sum(product, axis=1, keepdims=True)
-            delta_ref[rows, head : head + 1] = delta
-            d_scores = probs.astype(jnp.float32) * (contract(grad, values, 1, 1) - delta)
+            d_scores = probs_ref[head, rows, :].astype(jnp.float32) * (d_probs[rows, :] - delta[rows, :])
             sums[:, first : first + length] += d_scores
-            d_scores = d_scores.astype(jnp.bfloat16)
-            d_query = contract(d_scores, keys, 1, 0).astype(jnp.bfloat16)
-            out_ref[rows, low : low + head_size] = d_query * jnp.asarray(query_scale, jnp.bfloat16)
-            d_keys = d_keys + contract(queries, d_scores, 0, 0)
-            d_values = d_values + contract(grad, probs, 0, 0)
+            scores_ref[rows, :] = d_scores.astype(jnp.bfloat16)
+        d_scores = scores_ref[...]
+        d_query = contract(d_scores, keys, 1, 0).astype(jnp.bfloat16)
+        out_ref[:, low : low + head_size] = d_query * jnp.asarray(query_scale, jnp.bfloat16)
+        d_keys = contract(queries, d_scores, 0, 0)
+        d_values = contract(grad, probs_ref[head], 0, 0)
         out_ref[:, width + low : width + low + head_size] = d_keys.T.astype(jnp.bfloat16)
         out_ref[:, 2 * width + low : 2 * width + low + head_size] = d_values.T.astype(jnp.bfloat16)
         row_ids = lax.broadcasted_iota(jnp.int32, (lanes, lanes), 0)
@@ -839,7 +847,7 @@
     grad_in = cotangent[0]
     gains = (gain_attn[None], gain_ffn_in[None], gain_hidden[None])
     block_rows, hidden_rows = width // planes, hidden_width // planes
-    *kept, activated, hidden, below, across_fc2, send_fc2, keep_fc2 = run_kernel(
+    *kept, activated, hidden, across_fc2, send_fc2, keep_fc2 = run_kernel(
         functools.partial(forward_kernel, line_size),
         "feed_forward",
         9,
@@ -856,7 +864,6 @@
         ],
         [
             ((rows_here, hidden_width), wide),
-            ((rows_here, hidden_width), wide),
             ((hidden_rows, width), low),
             ((3, hidden_rows, width), low),
             ((4, hidden_rows, width), low),
@@ -868,7 +875,7 @@
             ((rows_here, hidden_width), wide),
             ((8, hidden_rows, width), low),
         ],
-        24 + 2 * (hidden_width // tile_cols),
+        24 + hidden_width // tile_cols,
     )
     across_fc2, send_fc2 = all_after([across_fc2, send_fc2], *second_others)
     second_across = add_low(keep_fc2[0], swap(across_fc2, core_bit))
@@ -895,7 +902,7 @@
             *gains,
             scale_cols.reshape(line_size, part),
         ),
-        (*first_planes, *first_others, *second_planes, *second_others, hidden, below, activated),
+        (*first_planes, *first_others, *second_planes, *second_others, hidden, activated),
         [
             ((rows_here, width), low),
             ((rows_here, width), wide),
@@ -916,7 +923,7 @@
             ((width, hidden_width), low),
             ((width, width), low),
         ],
-        3 + 24 + 16,
+        1 + 32 + 16,
     )
 
     grad_pieces = all_after(grad_pieces, *halves)
@@ -924,8 +931,8 @@
         turn(piece, line_size - steps) for steps, piece in enumerate(grad_pieces[1:], 1)
     ]
     got_first = swap(after(send_first, *halves), core_bit)
-    first = add_low(keep_first, got_first)
-    grad_pieces[0] = after(grad_pieces[0], first)
+    first_across = add_low(keep_first[0], got_first[0])
+    grad_pieces[0] = after(grad_pieces[0], got_first)
     second_x, second_y = add_across(halves, second_rest[0], second_rest[1])
     second_got = [swap(second_x, x_bit), swap(second_y, y_bit)]
     send_qkv, keep_qkv, diagonal_sums_here, deltas, gain_sums, d_normed = run_kernel(
@@ -952,6 +959,7 @@
             ((row_len, width), low),
             ((width, 3 * part), low),
             ((row_len, width), low),
+            ((row_len, row_len), low),
         ],
         heads + 3,
     )
@@ -959,7 +967,6 @@
     d_normed_here = d_normed_low.astype(jnp.float32)
 
     second_got = all_after(second_got, d_normed)
-    second_line = sum_parts([second_rest[2], *second_got]).astype(low)
     grad_gain_in = gain_sums[:, 0] / gain_in
     d_table = lax.dot_general(
         diagonal_sums_here, selector, (((1,), (1,)), ((), ())), precision=highest
@@ -972,7 +979,9 @@
     flat = jnp.pad(flat, (0, -flat.shape[0] % tail_cols)).reshape(-1, tail_cols)
     terms = flat.astype(low)
     got = swap(send_qkv, core_bit)
-    halves = halves_across(after(first[0], second_line, got))
+    halves = halves_across(after(first_across, *second_got))
+    second_line = sum_parts([second_rest[2], *all_after(second_got, got)]).astype(low)
+    first_rest = add_low(keep_first[1:], after(got_first[1:], got))
     last = add_low(keep_qkv, got)
     terms = add_low(terms, swap(terms, core_bit))
     last_got = [
@@ -980,7 +989,7 @@
     ]
     arrived = all_after([*halves, *last_got])
     halves, last_got = arrived[:2], arrived[2:]
-    first_x, first_y = add_across(halves, first[1], first[2])
+    first_x, first_y = add_across(halves, first_rest[0], first_rest[1])
     first_got = [swap(first_x, x_bit), swap(first_y, y_bit)]
     last_line = sum_parts([last[3]] + [piece[:block_rows] for piece in last_got]).astype(low)
     plane_sums = [piece[block_rows:].astype(wide) for piece in last_got]
@@ -992,7 +1001,7 @@
     spread = jnp.broadcast_to(flat[None], (line_size,) + flat.shape)
     second_stack = jnp.concatenate([second_line.reshape(line_size, second_rows, width), spread], axis=1)
     second_dealt = deal_line(after(second_stack, d_normed_low, *last_got))
-    first_line = sum_parts([first[3], *all_after(first_got, *second_dealt[1:])]).astype(low)
+    first_line = sum_parts([first_rest[2], *all_after(first_got, *second_dealt[1:])]).astype(low)
     both_lines = after(jnp.concatenate([first_line, last_line], axis=1), *second_dealt[1:])
     dealt_back = deal_line(both_lines.reshape(line_size, shard_rows, pack_cols))
     grad_fc2 = sum_parts([piece[:second_rows] for piece in second_dealt])

time: 264 us -> 255 us (0.966)
  the two profiles are of different devices: /device:TPU:18 before, /device:TPU:24 now
where the time goes in v5:
time: 255 us; the launch traced here: 251 us
  waiting for transfers between devices  88.6 us (35%)
  Pallas kernels  61.6 us (24%)
  starting transfers between devices  45.3 us (18%)
  other arithmetic  22.7 us (9%)
  local copies, waits for them, and re-layouts  15.4 us (6%)
  between operations  15.3 us (6%)
  matrix products  2.64 us (1%)
    pallas_call x5, Pallas kernels, run_kernel(): pl.pallas_call(kernel, out_shape=[jax.ShapeDtypeStruct(shape, dtype) for...  61.6 us
    ppermute x18, waiting for transfers between devices, turn(): lax.ppermute(value, 'blk', [(i, (i + steps) % size) for i in range(size)])  50.7 us
    ppermute x32, waiting for transfers between devices, swap(): return lax.ppermute(value, 'dp', [(i, i ^ bit) for i in range(size)])  37.8 us
    ppermute x32, starting transfers between devices, swap(): return lax.ppermute(value, 'dp', [(i, i ^ bit) for i in range(size)])  23.3 us
    ppermute x18, starting transfers between devices, turn(): lax.ppermute(value, 'blk', [(i, (i + steps) % size) for i in range(size)])  21.9 us
    unnamed x90, local copies, waits for them, and re-layouts  6.1 us
    convert_element_type x8, other arithmetic, add_low(): (left.astype(jnp.float32) + right.astype(jnp.float32)).astype(jnp.bfloat16)  5.36 us
  transfers between devices with their start and end apart: 52, of which 25 were waited for; matrix products, arithmetic and copies ran while one was open for 11% of the time, Pallas kernels for 24%

profile of v5, /device:TPU:24, one launch (start us, length us, event | category | flops | bytes accessed | tf_op | source)
XLA Modules:
  0.0 251.4 jit_solution(18226198822401672228)
XLA Ops:
  7.3 1.1 reshape.193
  8.6 0.9 pad_maximum_fusion.12
  9.8 1.9 collective-permute-start.1
  12.1 1.1 fusion.1.diagonal_ref
  13.3 3.1 %relative_bias.1.refs_8_ = f32[3,128,1408]{2,1,0:T(8,128)} custom-call(s32[2]{0:T(128)S(1)} %pad_add_fusion.place_ref, f32[3,1536]{1,0:T(4,128)S(1)} %fusion.1.diagonal_ref), custom_call_target="tpu_custom_call" | custom-call | flops 2200000000 | bytes 7200000 | tf_op jit(solution)/shard_map/relative_bias/pallas_call | solution.py:424
  17.2 13.3 %collective-permute-done.1 = bf16[24,4416]{1,0:T(8,128)(2,1)S(1)} collective-permute-done((bf16[24,4416]{1,0:T(8,128)(2,1)S(1)}, bf16[24,4416]{1,0:T(8,128)(2,1)S(1)}, u32[]{:S(2)}, u32[]{:S(2)}) %collective-permute-start.1) | collective-permute-done | bytes 212000 | tf_op jit(solution)/shard_map/ppermute | solution.py:320
  30.9 1.6 collective-permute-start.3
  32.5 1.5 collective-permute-start.4
  34.2 1.4 collective-permute-start.6
  35.6 1.9 collective-permute-start.7
  37.5 2.6 %collective-permute-done.5 = bf16[96,768]{1,0:T(8,128)(2,1)S(1)} collective-permute-done((bf16[96,768]{1,0:T(8,128)(2,1)S(1)}, bf16[96,768]{1,0:T(8,128)(2,1)S(1)}, u32[]{:S(2)}, u32[]{:S(2)}) %collective-permute-start.5) | collective-permute-done | bytes 147488 | tf_op jit(solution)/shard_map/ppermute | solution.py:320
  40.1 17.0 %collective-permute-done.6 = bf16[96,768]{1,0:T(8,128)(2,1)S(1)} collective-permute-done((bf16[96,768]{1,0:T(8,128)(2,1)S(1)}, bf16[96,768]{1,0:T(8,128)(2,1)S(1)}, u32[]{:S(2)}, u32[]{:S(2)}) %collective-permute-start.6) | collective-permute-done | bytes 147488 | tf_op jit(solution)/shard_map/ppermute | solution.py:320
  57.1 1.0 slice.253
  58.8 1.0 slice.254
  60.9 5.5 %collective-permute-done.8 = bf16[48,4416]{1,0:T(8,128)(2,1)S(1)} collective-permute-done((bf16[48,4416]{1,0:T(8,128)(2,1)S(1)}, bf16[48,4416]{1,0:T(8,128)(2,1)S(1)}, u32[]{:S(2)}, u32[]{:S(2)}) %collective-permute-start.8) | collective-permute-done | bytes 423968 | tf_op jit(solution)/shard_map/ppermute | solution.py:315
  67.2 5.1 %collective-permute-done.9 = bf16[48,4416]{1,0:T(8,128)(2,1)S(1)} collective-permute-done((bf16[48,4416]{1,0:T(8,128)(2,1)S(1)}, bf16[48,4416]{1,0:T(8,128)(2,1)S(1)}, u32[]{:S(2)}, u32[]{:S(2)}) %collective-permute-start.9) | collective-permute-done | bytes 423968 | tf_op jit(solution)/shard_map/ppermute | solution.py:315
  73.9 1.6 collective-permute-start.14
  76.0 11.5 %attend.1 = (bf16[768,576]{1,0:T(8,128)(2,1)}, bf16[768,576]{1,0:T(8,128)(2,1)}, bf16[768,768]{1,0:T(8,128)(2,1)}, f32[768,192]{1,0:T(8,128)S(1)}, bf16[768,192]...) custom-call(s32[2]{0:T(128)S(1)} %pad_add_fusion.place_ref, f32[1,768]{1,0:T(1,128)S(1)} %broadcast_in_dim.65.gain_ref, ...), custom_call_target="tpu_custom_call" | custom-call | flops 14300000256 | bytes 46800000 | tf_op jit(solution)/shard_map/attend/pallas_call | solution.py:424
  87.5 0.9 copy-done.5
  88.4 1.3 collective-permute-done.14.refs_23_
  89.7 1.2 collective-permute-done.15.refs_24_
  92.3 3.4 %collective-permute-start.19 = (bf16[192,192]{1,0:T(8,128)(2,1)S(1)}, bf16[192,192]{1,0:T(8,128)(2,1)S(1)}, u32[]{:S(2)}, u32[]{:S(2)}) collective-permute-start(bf16[192,192]{1,0:T(8,128)(2,1)S(1)} %get-tuple-element.207), channel_id=1, source_target_pairs={{0,2},{1,3},{2,0},{3,1},{4,6},{5,7},{6,4},{7,5},{8,10},{9,11},{10,... | collective-permute-start | bytes 221192 | tf_op jit(solution)/shard_map/ppermute | solution.py:320
  95.7 2.2 collective-permute-start.20
  97.9 1.4 collective-permute-done.16
  99.8 4.3 %collective-permute-done.19.refs_2_ = bf16[192,192]{1,0:T(8,128)(2,1)S(1)} collective-permute-done((bf16[192,192]{1,0:T(8,128)(2,1)S(1)}, bf16[192,192]{1,0:T(8,128)(2,1)S(1)}, u32[]{:S(2)}, u32[]{:S(2)}) %collective-permute-start.19) | collective-permute-done | bytes 73760 | tf_op jit(solution)/shard_map/ppermute | solution.py:320
  105.2 10.1 %feed_forward.1 = (f32[192,768]{1,0:T(8,128)}, f32[192,768]{1,0:T(8,128)}, bf16[192,768]{1,0:T(8,128)(2,1)S(1)}, f32[192,1]{1,0:T(8,128)S(1)}, f32[192,1]{1,0:T(...) custom-call(s32[2]{0:T(128)S(1)} %pad_add_fusion.place_ref, ...), custom_call_target="tpu_custom_call" | custom-call | flops 9900000256 | bytes 32400000 | tf_op jit(solution)/shard_map/feed_forward/pallas_call | solution.py:424
  117.0 1.9 collective-permute-done.25
  119.0 1.2 fusion.8
  120.2 1.4 collective-permute-start.26
  121.6 1.7 collective-permute-start.27
  123.4 24.6 %feed_forward_back.1 = (bf16[192,768]{1,0:T(8,128)(2,1)}, f32[192,768]{1,0:T(8,128)}, f32[1,3072]{1,0:T(1,128)S(1)}, f32[1,768]{1,0:T(1,128)S(1)}, f32[1,768]{1,...) custom-call(s32[2]{0:T(128)S(1)} %pad_add_fusion.place_ref, ...), custom_call_target="tpu_custom_call" | custom-call | flops 14300000256 | bytes 46800000 | tf_op jit(solution)/shard_map/feed_forward_back/pallas_call | solution.py:424
  148.9 1.0 collective-permute-start.30
  149.9 2.8 %collective-permute-start.31 = (bf16[192,192]{1,0:T(8,128)(2,1)S(1)}, bf16[192,192]{1,0:T(8,128)(2,1)S(1)}, u32[]{:S(2)}, u32[]{:S(2)}) collective-permute-start(bf16[192,192]{1,0:T(8,128)(2,1)S(1)} %get-tuple-element.128), channel_id=1, source_target_pairs={{0,1},{1,2},{2,3},{3,0},{4,5},{5,6},{6,7},{7,4},{8,9},{9,10},{10,1... | collective-permute-start | bytes 221192 | tf_op jit(solution)/shard_map/ppermute | solution.py:320
  152.7 2.9 %collective-permute-done.33 = bf16[3,384,768]{2,1,0:T(8,128)(2,1)S(1)} collective-permute-done((bf16[3,384,768]{2,1,0:T(8,128)(2,1)S(1)}, bf16[3,384,768]{2,1,0:T(8,128)(2,1)S(1)}, u32[]{:S(2)}, u32[]{:S(2)}) %collective-permute-start.33) | collective-permute-done | bytes 1769504 | tf_op jit(solution)/shard_map/ppermute | solution.py:315
  156.4 0.9 copy-done.7
  158.5 1.2 collective-permute-done.30.refs_2_
  159.7 12.2 %attend_back.1 = (bf16[4,96,576]{2,1,0:T(8,128)(2,1)S(1)}, bf16[4,96,576]{2,1,0:T(8,128)(2,1)}, f32[3,1536]{1,0:T(4,128)S(1)}, f32[768,3]{1,0:T(8,128)S(1)}, f32...) custom-call(s32[2]{0:T(128)S(1)} %pad_add_fusion.place_ref, bf16[192,192]{1,0:T(8,128)(2,1)S(1)} %get-tuple-element.125.refs_0_, ...), custom_call_target="tpu_custom_call" | custom-call | flops 13200000000 | bytes 43200000 | tf_op jit(solution)/shard_map/attend_back/pallas_call | solution.py:424
  171.9 1.0 collective-permute-done.35
  173.2 1.5 fusion.9
  175.9 1.5 fusion.10
  178.2 1.7 collective-permute-start.37
  180.2 1.8 collective-permute-start.39
  182.7 1.0 collective-permute-start.41
  184.4 1.0 copy-done.17
  185.4 2.3 fusion.7
  187.7 1.4 collective-permute-done.36
  189.1 3.3 %collective-permute-done.37 = bf16[48,3840]{1,0:T(8,128)(2,1)} collective-permute-done((bf16[48,3840]{1,0:T(8,128)(2,1)S(1)}, bf16[48,3840]{1,0:T(8,128)(2,1)}, u32[]{:S(2)}, u32[]{:S(2)}) %collective-permute-start.37) | collective-permute-done | bytes 368672 | tf_op jit(solution)/shard_map/ppermute | solution.py:315
  193.3 0.9 collective-permute-done.40
  195.7 1.3 fusion.11
  197.0 0.9 pad_maximum_fusion.3
  198.0 1.7 collective-permute-start.43
  199.7 0.9 pad_maximum_fusion.2
  200.6 1.1 collective-permute-start.42
  201.8 1.0 fusion.26
  203.8 1.9 collective-permute-start.46
  205.8 1.3 fusion.16
  207.4 1.0 fusion.21
  208.4 7.6 %collective-permute-done.43 = bf16[96,3840]{1,0:T(8,128)(2,1)} collective-permute-done((bf16[96,3840]{1,0:T(8,128)(2,1)}, bf16[96,3840]{1,0:T(8,128)(2,1)}, u32[]{:S(2)}, u32[]{:S(2)}) %collective-permute-start.43) | collective-permute-done | bytes 737312 | tf_op jit(solution)/shard_map/ppermute | solution.py:315
  216.0 2.4 collective-permute-done.42
  218.4 1.8 fusion.5
  220.8 1.4 collective-permute-start.48
  222.3 1.9 collective-permute-start.49
  225.0 1.2 collective-permute-done.47
  231.2 10.3 %collective-permute-done.48 = bf16[24,4416]{1,0:T(8,128)(2,1)S(1)} collective-permute-done((bf16[24,4416]{1,0:T(8,128)(2,1)S(1)}, bf16[24,4416]{1,0:T(8,128)(2,1)S(1)}, u32[]{:S(2)}, u32[]{:S(2)}) %collective-permute-start.48) | collective-permute-done | bytes 212000 | tf_op jit(solution)/shard_map/ppermute | solution.py:320
  (252 shorter events, 30.7 us)
Async XLA Ops:
  7.2 65.9 %all-gather.2.cloned.1.call-start = ((), (), s32[]{:S(2)}) async-start(), calls=%async_computation.1 | async-start | bytes 1474560 | tf_op jit(solution)/shard_map/all_gather | solution.py:817
  9.7 7.5 %collective-permute-start = (bf16[24,4416]{1,0:T(8,128)(2,1)S(1)}, bf16[24,4416]{1,0:T(8,128)(2,1)S(1)}, u32[]{:S(2)}, u32[]{:S(2)}) collective-permute-start(bf16[24,4416]{1,0:T(8,128)(2,1)S(1)} %get-tuple-element.188), channel_id=1, source_target_pairs={{0,1},{1,2},{2,3},{3,0},{4,5},{5,6},{6,7},{7,4},{8,9},{9,10},{10,1... | collective-permute-start | bytes 635912 | tf_op jit(solution)/shard_map/ppermute | solution.py:320
  9.8 20.7 %collective-permute-start.1 = (bf16[24,4416]{1,0:T(8,128)(2,1)S(1)}, bf16[24,4416]{1,0:T(8,128)(2,1)S(1)}, u32[]{:S(2)}, u32[]{:S(2)}) collective-permute-start(bf16[24,4416]{1,0:T(8,128)(2,1)S(1)} %get-tuple-element.189), channel_id=1, source_target_pairs={{0,2},{1,3},{2,0},{3,1},{4,6},{5,7},{6,4},{7,5},{8,10},{9,11},{10,... | collective-permute-start | bytes 635912 | tf_op jit(solution)/shard_map/ppermute | solution.py:320
  11.7 18.8 %collective-permute-start.2 = (bf16[24,4416]{1,0:T(8,128)(2,1)S(1)}, bf16[24,4416]{1,0:T(8,128)(2,1)S(1)}, u32[]{:S(2)}, u32[]{:S(2)}) collective-permute-start(bf16[24,4416]{1,0:T(8,128)(2,1)S(1)} %get-tuple-element.190), channel_id=1, source_target_pairs={{0,3},{1,0},{2,1},{3,2},{4,7},{5,4},{6,5},{7,6},{8,11},{9,8},{10,9... | collective-permute-start | bytes 635912 | tf_op jit(solution)/shard_map/ppermute | solution.py:320
  30.9 42.1 %copy-start.13 = (bf16[96,4416]{1,0:T(8,128)(2,1)}, bf16[96,4416]{1,0:T(8,128)(2,1)S(1)}, u32[]{:S(2)}) copy-start(bf16[96,4416]{1,0:T(8,128)(2,1)S(1)} %pad_maximum_fusion.refs_0_.refs_9_.refs_14_) | copy-start | bytes 2543620
  30.9 26.2 %collective-permute-start.3 = (bf16[96,4416]{1,0:T(8,128)(2,1)S(1)}, bf16[96,4416]{1,0:T(8,128)(2,1)}, u32[]{:S(2)}, u32[]{:S(2)}) collective-permute-start(bf16[96,4416]{1,0:T(8,128)(2,1)S(1)} %pad_maximum_fusion.refs_0_.refs_9_.refs_14_), channel_id=1, source_target_pairs={{0,8},{4,12},{8,0},{12,4},{16,24},{20,28},{24,16},{28,20},{1,9},{5... | collective-permute-start | bytes 2543624 | tf_op jit(solution)/shard_map/ppermute | solution.py:315
  32.5 24.6 %collective-permute-start.4 = (bf16[96,4416]{1,0:T(8,128)(2,1)S(1)}, bf16[96,4416]{1,0:T(8,128)(2,1)}, u32[]{:S(2)}, u32[]{:S(2)}) collective-permute-start(bf16[96,4416]{1,0:T(8,128)(2,1)S(1)} %pad_maximum_fusion.refs_0_.refs_9_.refs_14_), channel_id=1, source_target_pairs={{0,16},{4,20},{8,24},{12,28},{16,0},{20,4},{24,8},{28,12},{1,17},{... | collective-permute-start | bytes 2543624 | tf_op jit(solution)/shard_map/ppermute | solution.py:315
  34.0 39.0 %copy-start.43 = (s32[1,4]{1,0:T(1,128)S(1)}, s32[1,4]{1,0:T(1,128)}, u32[]{:S(2)}) copy-start(s32[1,4]{1,0:T(1,128)} %param.15) | copy-start | bytes 52
  34.1 39.5 %copy-start.36 = (f32[12]{0:T(128)S(1)}, f32[12]{0:T(128)}, u32[]{:S(2)}) copy-start(f32[12]{0:T(128)} %param.25) | copy-start | bytes 148
  34.1 168.7 %reduce-scatter.2.cloned.1.call-start = ((), (), s32[]{:S(2)}) async-start(), calls=%async_computation.2 | async-start | bytes 1474560 | tf_op jit(solution)/shard_map/reduce_scatter | solution.py:966
  34.1 6.0 %collective-permute-start.5 = (bf16[96,768]{1,0:T(8,128)(2,1)S(1)}, bf16[96,768]{1,0:T(8,128)(2,1)S(1)}, u32[]{:S(2)}, u32[]{:S(2)}) collective-permute-start(bf16[96,768]{1,0:T(8,128)(2,1)S(1)} %copy-done.21), channel_id=1, source_target_pairs={{0,1},{1,2},{2,3},{3,0},{4,5},{5,6},{6,7},{7,4},{8,9},{9,10},{10,1... | collective-permute-start | bytes 442376 | tf_op jit(solution)/shard_map/ppermute | solution.py:320
  34.2 22.9 %collective-permute-start.6 = (bf16[96,768]{1,0:T(8,128)(2,1)S(1)}, bf16[96,768]{1,0:T(8,128)(2,1)S(1)}, u32[]{:S(2)}, u32[]{:S(2)}) collective-permute-start(bf16[96,768]{1,0:T(8,128)(2,1)S(1)} %copy-done.21), channel_id=1, source_target_pairs={{0,2},{1,3},{2,0},{3,1},{4,6},{5,7},{6,4},{7,5},{8,10},{9,11},{10,... | collective-permute-start | bytes 442376 | tf_op jit(solution)/shard_map/ppermute | solution.py:320
  35.6 21.5 %collective-permute-start.7 = (bf16[96,768]{1,0:T(8,128)(2,1)S(1)}, bf16[96,768]{1,0:T(8,128)(2,1)S(1)}, u32[]{:S(2)}, u32[]{:S(2)}) collective-permute-start(bf16[96,768]{1,0:T(8,128)(2,1)S(1)} %copy-done.21), channel_id=1, source_target_pairs={{0,3},{1,0},{2,1},{3,2},{4,7},{5,4},{6,5},{7,6},{8,11},{9,8},{10,9... | collective-permute-start | bytes 442376 | tf_op jit(solution)/shard_map/ppermute | solution.py:320
  58.2 8.2 %collective-permute-start.8 = (bf16[48,4416]{1,0:T(8,128)(2,1)S(1)}, bf16[48,4416]{1,0:T(8,128)(2,1)S(1)}, u32[]{:S(2)}, u32[]{:S(2)}) collective-permute-start(bf16[48,4416]{1,0:T(8,128)(2,1)S(1)} %slice.253), channel_id=1, source_target_pairs={{0,8},{4,12},{8,0},{12,4},{16,24},{20,28},{24,16},{28,20},{1,9},{5... | collective-permute-start | bytes 1271816 | tf_op jit(solution)/shard_map/ppermute | solution.py:315
  59.8 16.2 %collective-permute-start.11 = (bf16[96,4416]{1,0:T(8,128)(2,1)}, bf16[96,4416]{1,0:T(8,128)(2,1)}, u32[]{:S(2)}, u32[]{:S(2)}) collective-permute-start(bf16[96,4416]{1,0:T(8,128)(2,1)} %collective-permute-done.3.refs_1_.refs_10_.refs_15_), channel_id=1, source_target_pairs={{0,4},{4,0},{8,12},{12,8},{16,20},{20,16},{24,28},{28,24},{1,5},{5... | collective-permute-start | bytes 2543624 | tf_op jit(solution)/shard_map/ppermute | solution.py:315
  59.9 16.1 %collective-permute-start.12 = (bf16[96,4416]{1,0:T(8,128)(2,1)}, bf16[96,4416]{1,0:T(8,128)(2,1)}, u32[]{:S(2)}, u32[]{:S(2)}) collective-permute-start(bf16[96,4416]{1,0:T(8,128)(2,1)} %collective-permute-done.4.refs_2_.refs_11_.refs_16_), channel_id=1, source_target_pairs={{0,4},{4,0},{8,12},{12,8},{16,20},{20,16},{24,28},{28,24},{1,5},{5... | collective-permute-start | bytes 2543624 | tf_op jit(solution)/shard_map/ppermute | solution.py:315
  60.4 11.9 %collective-permute-start.9 = (bf16[48,4416]{1,0:T(8,128)(2,1)S(1)}, bf16[48,4416]{1,0:T(8,128)(2,1)S(1)}, u32[]{:S(2)}, u32[]{:S(2)}) collective-permute-start(bf16[48,4416]{1,0:T(8,128)(2,1)S(1)} %slice.254), channel_id=1, source_target_pairs={{0,16},{4,20},{8,24},{12,28},{16,0},{20,4},{24,8},{28,12},{1,17},{... | collective-permute-start | bytes 1271816 | tf_op jit(solution)/shard_map/ppermute | solution.py:315
  60.9 14.5 %collective-permute-start.10 = (bf16[96,4416]{1,0:T(8,128)(2,1)S(1)}, bf16[96,4416]{1,0:T(8,128)(2,1)}, u32[]{:S(2)}, u32[]{:S(2)}) collective-permute-start(bf16[96,4416]{1,0:T(8,128)(2,1)S(1)} %pad_maximum_fusion.refs_0_.refs_9_.refs_14_), channel_id=1, source_target_pairs={{0,4},{4,0},{8,12},{12,8},{16,20},{20,16},{24,28},{28,24},{1,5},{5... | collective-permute-start | bytes 2543624 | tf_op jit(solution)/shard_map/ppermute | solution.py:315
  73.1 2.9 %collective-permute-start.13 = (bf16[96,4416]{1,0:T(8,128)(2,1)}, bf16[96,4416]{1,0:T(8,128)(2,1)}, u32[]{:S(2)}, u32[]{:S(2)}) collective-permute-start(bf16[96,4416]{1,0:T(8,128)(2,1)} %constant_dynamic-update-slice_fusion.refs_3_.refs_12_.refs_17_), channel_id=1, source_target_pairs={{0,4},{4,0},{8,12},{12,8},{16,20},{20,16},{24,28},{28,24},{1,5},{5... | collective-permute-start | bytes 2543624 | tf_op jit(solution)/shard_map/ppermute | solution.py:315
  73.9 30.2 %copy-start.14 = (bf16[384,768]{1,0:T(8,128)(2,1)}, bf16[384,768]{1,0:T(8,128)(2,1)S(1)}, u32[]{:S(2)}) copy-start(bf16[384,768]{1,0:T(8,128)(2,1)S(1)} %pad_maximum_fusion.5.refs_22_) | copy-start | bytes 1769476
  73.9 15.8 %collective-permute-start.14 = (bf16[384,768]{1,0:T(8,128)(2,1)S(1)}, bf16[384,768]{1,0:T(8,128)(2,1)S(1)}, u32[]{:S(2)}, u32[]{:S(2)}) collective-permute-start(bf16[384,768]{1,0:T(8,128)(2,1)S(1)} %pad_maximum_fusion.5.refs_22_), channel_id=1, source_target_pairs={{0,8},{4,12},{8,0},{12,4},{16,24},{20,28},{24,16},{28,20},{1,9},{5... | collective-permute-start | bytes 1769480 | tf_op jit(solution)/shard_map/ppermute | solution.py:315
  75.5 15.5 %collective-permute-start.15 = (bf16[384,768]{1,0:T(8,128)(2,1)S(1)}, bf16[384,768]{1,0:T(8,128)(2,1)S(1)}, u32[]{:S(2)}, u32[]{:S(2)}) collective-permute-start(bf16[384,768]{1,0:T(8,128)(2,1)S(1)} %pad_maximum_fusion.5.refs_22_), channel_id=1, source_target_pairs={{0,16},{4,20},{8,24},{12,28},{16,0},{20,4},{24,8},{28,12},{1,17},{... | collective-permute-start | bytes 1769480 | tf_op jit(solution)/shard_map/ppermute | solution.py:315
  76.0 16.2 %copy-start.34 = (f32[768]{0:T(1024)S(1)}, f32[768]{0:T(1024)}, u32[]{:S(2)}) copy-start(f32[768]{0:T(1024)} %param.22) | copy-start | bytes 9220
  88.4 16.7 %copy-start.2 = (bf16[1,192,768]{2,1,0:T(8,128)(2,1)S(1)}, bf16[1,192,768]{2,1,0:T(8,128)(2,1)}, u32[]{:S(2)}) copy-start(bf16[1,192,768]{2,1,0:T(8,128)(2,1)} %param.14) | copy-start | bytes 884740
  88.4 16.7 %copy-start.3 = (bf16[1,192,768]{2,1,0:T(8,128)(2,1)S(1)}, bf16[1,192,768]{2,1,0:T(8,128)(2,1)}, u32[]{:S(2)}) copy-start(bf16[1,192,768]{2,1,0:T(8,128)(2,1)} %param.27) | copy-start | bytes 884740
  88.4 16.7 %copy-start.4 = (f32[3072]{0:T(1024)S(1)}, f32[3072]{0:T(1024)}, u32[]{:S(2)}) copy-start(f32[3072]{0:T(1024)} %param.24) | copy-start | bytes 36868
  89.7 25.6 %copy-start.22 = (bf16[384,768]{1,0:T(8,128)(2,1)}, bf16[384,768]{1,0:T(8,128)(2,1)S(1)}, u32[]{:S(2)}) copy-start(bf16[384,768]{1,0:T(8,128)(2,1)S(1)} %collective-permute-done.14.refs_23_) | copy-start | bytes 1769476
  90.9 24.4 %copy-start.23 = (bf16[384,768]{1,0:T(8,128)(2,1)}, bf16[384,768]{1,0:T(8,128)(2,1)S(1)}, u32[]{:S(2)}) copy-start(bf16[384,768]{1,0:T(8,128)(2,1)S(1)} %collective-permute-done.15.refs_24_) | copy-start | bytes 1769476
  90.9 8.4 %collective-permute-start.16 = (bf16[192,768]{1,0:T(8,128)(2,1)S(1)}, bf16[192,768]{1,0:T(8,128)(2,1)S(1)}, u32[]{:S(2)}, u32[]{:S(2)}) collective-permute-start(bf16[192,768]{1,0:T(8,128)(2,1)S(1)} %slice.255), channel_id=1, source_target_pairs={{0,8},{4,12},{8,0},{12,4},{16,24},{20,28},{24,16},{28,20},{1,9},{5... | collective-permute-start | bytes 884744 | tf_op jit(solution)/shard_map/ppermute | solution.py:315
  91.6 8.2 %collective-permute-start.17 = (bf16[192,768]{1,0:T(8,128)(2,1)S(1)}, bf16[192,768]{1,0:T(8,128)(2,1)S(1)}, u32[]{:S(2)}, u32[]{:S(2)}) collective-permute-start(bf16[192,768]{1,0:T(8,128)(2,1)S(1)} %slice.256), channel_id=1, source_target_pairs={{0,16},{4,20},{8,24},{12,28},{16,0},{20,4},{24,8},{28,12},{1,17},{... | collective-permute-start | bytes 884744 | tf_op jit(solution)/shard_map/ppermute | solution.py:315
  92.3 7.5 %collective-permute-start.18 = (bf16[192,192]{1,0:T(8,128)(2,1)S(1)}, bf16[192,192]{1,0:T(8,128)(2,1)S(1)}, u32[]{:S(2)}, u32[]{:S(2)}) collective-permute-start(bf16[192,192]{1,0:T(8,128)(2,1)S(1)} %get-tuple-element.208), channel_id=1, source_target_pairs={{0,1},{1,2},{2,3},{3,0},{4,5},{5,6},{6,7},{7,4},{8,9},{9,10},{10,1... | collective-permute-start | bytes 221192 | tf_op jit(solution)/shard_map/ppermute | solution.py:320
  92.3 11.8 %collective-permute-start.19 = (bf16[192,192]{1,0:T(8,128)(2,1)S(1)}, bf16[192,192]{1,0:T(8,128)(2,1)S(1)}, u32[]{:S(2)}, u32[]{:S(2)}) collective-permute-start(bf16[192,192]{1,0:T(8,128)(2,1)S(1)} %get-tuple-element.207), channel_id=1, source_target_pairs={{0,2},{1,3},{2,0},{3,1},{4,6},{5,7},{6,4},{7,5},{8,10},{9,11},{10,... | collective-permute-start | bytes 221192 | tf_op jit(solution)/shard_map/ppermute | solution.py:320
  95.7 8.4 %collective-permute-start.20 = (bf16[192,192]{1,0:T(8,128)(2,1)S(1)}, bf16[192,192]{1,0:T(8,128)(2,1)S(1)}, u32[]{:S(2)}, u32[]{:S(2)}) collective-permute-start(bf16[192,192]{1,0:T(8,128)(2,1)S(1)} %get-tuple-element.206), channel_id=1, source_target_pairs={{0,3},{1,0},{2,1},{3,2},{4,7},{5,4},{6,5},{7,6},{8,11},{9,8},{10,9... | collective-permute-start | bytes 221192 | tf_op jit(solution)/shard_map/ppermute | solution.py:320
  104.1 11.2 %collective-permute-start.21 = (bf16[384,768]{1,0:T(8,128)(2,1)S(1)}, bf16[384,768]{1,0:T(8,128)(2,1)S(1)}, u32[]{:S(2)}, u32[]{:S(2)}) collective-permute-start(bf16[384,768]{1,0:T(8,128)(2,1)S(1)} %pad_maximum_fusion.5.refs_22_), channel_id=1, source_target_pairs={{0,4},{4,0},{8,12},{12,8},{16,20},{20,16},{24,28},{28,24},{1,5},{5... | collective-permute-start | bytes 1769480 | tf_op jit(solution)/shard_map/ppermute | solution.py:315
  104.1 11.2 %collective-permute-start.22 = (bf16[384,768]{1,0:T(8,128)(2,1)S(1)}, bf16[384,768]{1,0:T(8,128)(2,1)S(1)}, u32[]{:S(2)}, u32[]{:S(2)}) collective-permute-start(bf16[384,768]{1,0:T(8,128)(2,1)S(1)} %collective-permute-done.14.refs_23_), channel_id=1, source_target_pairs={{0,4},{4,0},{8,12},{12,8},{16,20},{20,16},{24,28},{28,24},{1,5},{5... | collective-permute-start | bytes 1769480 | tf_op jit(solution)/shard_map/ppermute | solution.py:315
  104.6 10.7 %collective-permute-start.23 = (bf16[384,768]{1,0:T(8,128)(2,1)S(1)}, bf16[384,768]{1,0:T(8,128)(2,1)S(1)}, u32[]{:S(2)}, u32[]{:S(2)}) collective-permute-start(bf16[384,768]{1,0:T(8,128)(2,1)S(1)} %collective-permute-done.15.refs_24_), channel_id=1, source_target_pairs={{0,4},{4,0},{8,12},{12,8},{16,20},{20,16},{24,28},{28,24},{1,5},{5... | collective-permute-start | bytes 1769480 | tf_op jit(solution)/shard_map/ppermute | solution.py:315
  104.7 10.7 %collective-permute-start.24 = (bf16[384,768]{1,0:T(8,128)(2,1)S(1)}, bf16[384,768]{1,0:T(8,128)(2,1)S(1)}, u32[]{:S(2)}, u32[]{:S(2)}) collective-permute-start(bf16[384,768]{1,0:T(8,128)(2,1)S(1)} %constant_dynamic-update-slice_fusion.2.refs_25_), channel_id=1, source_target_pairs={{0,4},{4,0},{8,12},{12,8},{16,20},{20,16},{24,28},{28,24},{1,5},{5... | collective-permute-start | bytes 1769480 | tf_op jit(solution)/shard_map/ppermute | solution.py:315
  116.7 2.2 collective-permute-start.25
  120.2 27.7 %collective-permute-start.26 = (bf16[192,768]{1,0:T(8,128)(2,1)S(1)}, bf16[192,768]{1,0:T(8,128)(2,1)S(1)}, u32[]{:S(2)}, u32[]{:S(2)}) collective-permute-start(bf16[192,768]{1,0:T(8,128)(2,1)S(1)} %get-tuple-element.198), channel_id=1, source_target_pairs={{0,8},{4,12},{8,0},{12,4},{16,24},{20,28},{24,16},{28,20},{1,9},{5... | collective-permute-start | bytes 884744 | tf_op jit(solution)/shard_map/ppermute | solution.py:315
  121.6 26.4 %collective-permute-start.27 = (bf16[192,768]{1,0:T(8,128)(2,1)S(1)}, bf16[192,768]{1,0:T(8,128)(2,1)S(1)}, u32[]{:S(2)}, u32[]{:S(2)}) collective-permute-start(bf16[192,768]{1,0:T(8,128)(2,1)S(1)} %get-tuple-element.197), channel_id=1, source_target_pairs={{0,16},{4,20},{8,24},{12,28},{16,0},{20,4},{24,8},{28,12},{1,17},{... | collective-permute-start | bytes 884744 | tf_op jit(solution)/shard_map/ppermute | solution.py:315
  123.4 24.7 %copy-start.38 = (bf16[3,384,768]{2,1,0:T(8,128)(2,1)S(1)}, bf16[3,384,768]{2,1,0:T(8,128)(2,1)}, u32[]{:S(2)}) copy-start(bf16[3,384,768]{2,1,0:T(8,128)(2,1)} %get-tuple-element.138) | copy-start | bytes 5308420
  123.4 32.3 %copy-start.10 = (bf16[4,384,768]{2,1,0:T(8,128)(2,1)S(1)}, bf16[4,384,768]{2,1,0:T(8,128)(2,1)}, u32[]{:S(2)}) copy-start(bf16[4,384,768]{2,1,0:T(8,128)(2,1)} %get-tuple-element.100) | copy-start | bytes 7077892
  148.0 9.7 %collective-permute-start.28 = (bf16[4,96,3840]{2,1,0:T(8,128)(2,1)}, bf16[4,96,3840]{2,1,0:T(8,128)(2,1)S(1)}, u32[]{:S(2)}, u32[]{:S(2)}) collective-permute-start(bf16[4,96,3840]{2,1,0:T(8,128)(2,1)} %get-tuple-element.124), channel_id=1, source_target_pairs={{0,4},{4,0},{8,12},{12,8},{16,20},{20,16},{24,28},{28,24},{1,5},{5... | collective-permute-start | bytes 8847368 | tf_op jit(solution)/shard_map/ppermute | solution.py:315
  148.1 7.5 %collective-permute-start.33 = (bf16[3,384,768]{2,1,0:T(8,128)(2,1)S(1)}, bf16[3,384,768]{2,1,0:T(8,128)(2,1)S(1)}, u32[]{:S(2)}, u32[]{:S(2)}) collective-permute-start(bf16[3,384,768]{2,1,0:T(8,128)(2,1)S(1)} %copy-done.38), channel_id=1, source_target_pairs={{0,4},{4,0},{8,12},{12,8},{16,20},{20,16},{24,28},{28,24},{1,5},{5... | collective-permute-start | bytes 5308424 | tf_op jit(solution)/shard_map/ppermute | solution.py:315
  148.8 9.7 %collective-permute-start.29 = (bf16[192,192]{1,0:T(8,128)(2,1)S(1)}, bf16[192,192]{1,0:T(8,128)(2,1)S(1)}, u32[]{:S(2)}, u32[]{:S(2)}) collective-permute-start(bf16[192,192]{1,0:T(8,128)(2,1)S(1)} %get-tuple-element.126), channel_id=1, source_target_pairs={{0,3},{1,0},{2,1},{3,2},{4,7},{5,4},{6,5},{7,6},{8,11},{9,8},{10,9... | collective-permute-start | bytes 221192 | tf_op jit(solution)/shard_map/ppermute | solution.py:320
  148.9 10.8 %collective-permute-start.30 = (bf16[192,192]{1,0:T(8,128)(2,1)S(1)}, bf16[192,192]{1,0:T(8,128)(2,1)S(1)}, u32[]{:S(2)}, u32[]{:S(2)}) collective-permute-start(bf16[192,192]{1,0:T(8,128)(2,1)S(1)} %get-tuple-element.127), channel_id=1, source_target_pairs={{0,2},{1,3},{2,0},{3,1},{4,6},{5,7},{6,4},{7,5},{8,10},{9,11},{10,... | collective-permute-start | bytes 221192 | tf_op jit(solution)/shard_map/ppermute | solution.py:320
  149.9 9.8 %collective-permute-start.31 = (bf16[192,192]{1,0:T(8,128)(2,1)S(1)}, bf16[192,192]{1,0:T(8,128)(2,1)S(1)}, u32[]{:S(2)}, u32[]{:S(2)}) collective-permute-start(bf16[192,192]{1,0:T(8,128)(2,1)S(1)} %get-tuple-element.128), channel_id=1, source_target_pairs={{0,1},{1,2},{2,3},{3,0},{4,5},{5,6},{6,7},{7,4},{8,9},{9,10},{10,1... | collective-permute-start | bytes 221192 | tf_op jit(solution)/shard_map/ppermute | solution.py:320
  157.3 15.6 %collective-permute-start.35 = (bf16[384,768]{1,0:T(8,128)(2,1)S(1)}, bf16[384,768]{1,0:T(8,128)(2,1)S(1)}, u32[]{:S(2)}, u32[]{:S(2)}) collective-permute-start(bf16[384,768]{1,0:T(8,128)(2,1)S(1)} %pad_maximum_fusion.7), channel_id=1, source_target_pairs={{0,16},{4,20},{8,24},{12,28},{16,0},{20,4},{24,8},{28,12},{1,17},{... | collective-permute-start | bytes 1769480 | tf_op jit(solution)/shard_map/ppermute | solution.py:315
  157.7 15.5 %collective-permute-start.34 = (bf16[384,768]{1,0:T(8,128)(2,1)S(1)}, bf16[384,768]{1,0:T(8,128)(2,1)}, u32[]{:S(2)}, u32[]{:S(2)}) collective-permute-start(bf16[384,768]{1,0:T(8,128)(2,1)S(1)} %pad_maximum_fusion.6), channel_id=1, source_target_pairs={{0,8},{4,12},{8,0},{12,4},{16,24},{20,28},{24,16},{28,20},{1,9},{5... | collective-permute-start | bytes 1769480 | tf_op jit(solution)/shard_map/ppermute | solution.py:315
  173.2 6.8 %collective-permute-start.32 = (bf16[4,96,576]{2,1,0:T(8,128)(2,1)S(1)}, bf16[4,96,576]{2,1,0:T(8,128)(2,1)S(1)}, u32[]{:S(2)}, u32[]{:S(2)}) collective-permute-start(bf16[4,96,576]{2,1,0:T(8,128)(2,1)S(1)} %get-tuple-element.136), channel_id=1, source_target_pairs={{0,4},{4,0},{8,12},{12,8},{16,20},{20,16},{24,28},{28,24},{1,5},{5... | collective-permute-start | bytes 1327112 | tf_op jit(solution)/shard_map/ppermute | solution.py:315
  175.3 4.6 %collective-permute-start.38 = (bf16[13,576]{1,0:T(8,128)(2,1)S(1)}, bf16[13,576]{1,0:T(8,128)(2,1)S(1)}, u32[]{:S(2)}, u32[]{:S(2)}) collective-permute-start(bf16[13,576]{1,0:T(8,128)(2,1)S(1)} %convert_element_type.295), channel_id=1, source_target_pairs={{0,4},{4,0},{8,12},{12,8},{16,20},{20,16},{24,28},{28,24},{1,5},{5... | collective-permute-start | bytes 44936 | tf_op jit(solution)/shard_map/ppermute | solution.py:315
  177.5 11.6 %collective-permute-start.36 = (bf16[48,3840]{1,0:T(8,128)(2,1)S(1)}, bf16[48,3840]{1,0:T(8,128)(2,1)}, u32[]{:S(2)}, u32[]{:S(2)}) collective-permute-start(bf16[48,3840]{1,0:T(8,128)(2,1)S(1)} %get-tuple-element.192), channel_id=1, source_target_pairs={{0,8},{4,12},{8,0},{12,4},{16,24},{20,28},{24,16},{28,20},{1,9},{5... | collective-permute-start | bytes 1105928 | tf_op jit(solution)/shard_map/ppermute | solution.py:315
  178.2 14.2 %collective-permute-start.37 = (bf16[48,3840]{1,0:T(8,128)(2,1)S(1)}, bf16[48,3840]{1,0:T(8,128)(2,1)}, u32[]{:S(2)}, u32[]{:S(2)}) collective-permute-start(bf16[48,3840]{1,0:T(8,128)(2,1)S(1)} %get-tuple-element.191), channel_id=1, source_target_pairs={{0,16},{4,20},{8,24},{12,28},{16,0},{20,4},{24,8},{28,12},{1,17},{... | collective-permute-start | bytes 1105928 | tf_op jit(solution)/shard_map/ppermute | solution.py:315
  180.2 13.1 %collective-permute-start.39 = (bf16[109,576]{1,0:T(8,128)(2,1)S(1)}, bf16[109,576]{1,0:T(8,128)(2,1)S(1)}, u32[]{:S(2)}, u32[]{:S(2)}) collective-permute-start(bf16[109,576]{1,0:T(8,128)(2,1)S(1)} %get-tuple-element.216), channel_id=1, source_target_pairs={{0,24},{4,28},{8,16},{12,20},{16,8},{20,12},{24,0},{28,4},{1,25},{... | collective-permute-start | bytes 376712 | tf_op jit(solution)/shard_map/ppermute | solution.py:315
  182.1 12.2 %collective-permute-start.40 = (bf16[109,576]{1,0:T(8,128)(2,1)S(1)}, bf16[109,576]{1,0:T(8,128)(2,1)S(1)}, u32[]{:S(2)}, u32[]{:S(2)}) collective-permute-start(bf16[109,576]{1,0:T(8,128)(2,1)S(1)} %get-tuple-element.215), channel_id=1, source_target_pairs={{0,8},{4,12},{8,0},{12,4},{16,24},{20,28},{24,16},{28,20},{1,9},{5... | collective-permute-start | bytes 376712 | tf_op jit(solution)/shard_map/ppermute | solution.py:315
  182.7 11.9 %collective-permute-start.41 = (bf16[109,576]{1,0:T(8,128)(2,1)S(1)}, bf16[109,576]{1,0:T(8,128)(2,1)S(1)}, u32[]{:S(2)}, u32[]{:S(2)}) collective-permute-start(bf16[109,576]{1,0:T(8,128)(2,1)S(1)} %get-tuple-element.214), channel_id=1, source_target_pairs={{0,16},{4,20},{8,24},{12,28},{16,0},{20,4},{24,8},{28,12},{1,17},{... | collective-permute-start | bytes 376712 | tf_op jit(solution)/shard_map/ppermute | solution.py:315
  198.0 18.0 %collective-permute-start.43 = (bf16[96,3840]{1,0:T(8,128)(2,1)}, bf16[96,3840]{1,0:T(8,128)(2,1)}, u32[]{:S(2)}, u32[]{:S(2)}) collective-permute-start(bf16[96,3840]{1,0:T(8,128)(2,1)} %pad_maximum_fusion.3), channel_id=1, source_target_pairs={{0,16},{4,20},{8,24},{12,28},{16,0},{20,4},{24,8},{28,12},{1,17},{... | collective-permute-start | bytes 2211848 | tf_op jit(solution)/shard_map/ppermute | solution.py:315
  200.6 17.7 %collective-permute-start.42 = (bf16[96,3840]{1,0:T(8,128)(2,1)}, bf16[96,3840]{1,0:T(8,128)(2,1)}, u32[]{:S(2)}, u32[]{:S(2)}) collective-permute-start(bf16[96,3840]{1,0:T(8,128)(2,1)} %pad_maximum_fusion.2), channel_id=1, source_target_pairs={{0,8},{4,12},{8,0},{12,4},{16,24},{20,28},{24,16},{28,20},{1,9},{5... | collective-permute-start | bytes 2211848 | tf_op jit(solution)/shard_map/ppermute | solution.py:315
  203.1 15.3 %collective-permute-start.44 = (bf16[106,768]{1,0:T(8,128)(2,1)S(1)}, bf16[106,768]{1,0:T(8,128)(2,1)S(1)}, u32[]{:S(2)}, u32[]{:S(2)}) collective-permute-start(bf16[106,768]{1,0:T(8,128)(2,1)S(1)} %get-tuple-element.196), channel_id=1, source_target_pairs={{0,1},{1,2},{2,3},{3,0},{4,5},{5,6},{6,7},{7,4},{8,9},{9,10},{10,1... | collective-permute-start | bytes 488456 | tf_op jit(solution)/shard_map/ppermute | solution.py:320
  203.6 14.8 %collective-permute-start.45 = (bf16[106,768]{1,0:T(8,128)(2,1)S(1)}, bf16[106,768]{1,0:T(8,128)(2,1)S(1)}, u32[]{:S(2)}, u32[]{:S(2)}) collective-permute-start(bf16[106,768]{1,0:T(8,128)(2,1)S(1)} %get-tuple-element.195), channel_id=1, source_target_pairs={{0,2},{1,3},{2,0},{3,1},{4,6},{5,7},{6,4},{7,5},{8,10},{9,11},{10,... | collective-permute-start | bytes 488456 | tf_op jit(solution)/shard_map/ppermute | solution.py:320
  203.8 14.5 %collective-permute-start.46 = (bf16[106,768]{1,0:T(8,128)(2,1)S(1)}, bf16[106,768]{1,0:T(8,128)(2,1)S(1)}, u32[]{:S(2)}, u32[]{:S(2)}) collective-permute-start(bf16[106,768]{1,0:T(8,128)(2,1)S(1)} %get-tuple-element.194), channel_id=1, source_target_pairs={{0,3},{1,0},{2,1},{3,2},{4,7},{5,4},{6,5},{7,6},{8,11},{9,8},{10,9... | collective-permute-start | bytes 488456 | tf_op jit(solution)/shard_map/ppermute | solution.py:320
  220.3 5.9 %collective-permute-start.47 = (bf16[24,4416]{1,0:T(8,128)(2,1)S(1)}, bf16[24,4416]{1,0:T(8,128)(2,1)S(1)}, u32[]{:S(2)}, u32[]{:S(2)}) collective-permute-start(bf16[24,4416]{1,0:T(8,128)(2,1)S(1)} %get-tuple-element.187), channel_id=1, source_target_pairs={{0,1},{1,2},{2,3},{3,0},{4,5},{5,6},{6,7},{7,4},{8,9},{9,10},{10,1... | collective-permute-start | bytes 635912 | tf_op jit(solution)/shard_map/ppermute | solution.py:320
  220.8 20.7 %collective-permute-start.48 = (bf16[24,4416]{1,0:T(8,128)(2,1)S(1)}, bf16[24,4416]{1,0:T(8,128)(2,1)S(1)}, u32[]{:S(2)}, u32[]{:S(2)}) collective-permute-start(bf16[24,4416]{1,0:T(8,128)(2,1)S(1)} %get-tuple-element.186), channel_id=1, source_target_pairs={{0,2},{1,3},{2,0},{3,1},{4,6},{5,7},{6,4},{7,5},{8,10},{9,11},{10,... | collective-permute-start | bytes 635912 | tf_op jit(solution)/shard_map/ppermute | solution.py:320
  222.3 19.2 %collective-permute-start.49 = (bf16[24,4416]{1,0:T(8,128)(2,1)S(1)}, bf16[24,4416]{1,0:T(8,128)(2,1)S(1)}, u32[]{:S(2)}, u32[]{:S(2)}) collective-permute-start(bf16[24,4416]{1,0:T(8,128)(2,1)S(1)} %get-tuple-element.185), channel_id=1, source_target_pairs={{0,3},{1,0},{2,1},{3,2},{4,7},{5,4},{6,5},{7,6},{8,11},{9,8},{10,9... | collective-permute-start | bytes 635912 | tf_op jit(solution)/shard_map/ppermute | solution.py:320
  (33 other events, 165.2 us)
Sparse Core Ops, SparseCore 0:
  34.2 33.6 all-gather.1
  172.1 26.7 reduce-scatter.1

commit v6 on v5

--- a/solution.py
+++ b/solution.py
@@ -932,7 +932,7 @@
     ]
     got_first = swap(after(send_first, *halves), core_bit)
     first_across = add_low(keep_first[0], got_first[0])
-    grad_pieces[0] = after(grad_pieces[0], got_first)
+    grad_pieces[0] = after(grad_pieces[0], got_first, first_across)
     second_x, second_y = add_across(halves, second_rest[0], second_rest[1])
     second_got = [swap(second_x, x_bit), swap(second_y, y_bit)]
     send_qkv, keep_qkv, diagonal_sums_here, deltas, gain_sums, d_normed = run_kernel(
@@ -1000,8 +1000,8 @@
     second_rows = hidden_rows // line_size
     spread = jnp.broadcast_to(flat[None], (line_size,) + flat.shape)
     second_stack = jnp.concatenate([second_line.reshape(line_size, second_rows, width), spread], axis=1)
-    second_dealt = deal_line(after(second_stack, d_normed_low, *last_got))
-    first_line = sum_parts([first_rest[2], *all_after(first_got, *second_dealt[1:])]).astype(low)
+    second_dealt = deal_line(after(second_stack, *last_got))
+    first_line = sum_parts([first_rest[2], *all_after(first_got, d_normed_low, *second_dealt[1:])]).astype(low)
     both_lines = after(jnp.concatenate([first_line, last_line], axis=1), *second_dealt[1:])
     dealt_back = deal_line(both_lines.reshape(line_size, shard_rows, pack_cols))
     grad_fc2 = sum_parts([piece[:second_rows] for piece in second_dealt])

time: 255 us -> 252 us (0.988)
  other arithmetic: 22.7 us -> 17.7 us
    ppermute x18, waiting for transfers between devices: 50.7 us -> 61.5 us  [turn(): lax.ppermute(value, 'blk', [(i, (i + steps) % size) for i in range(size)])]
    ppermute x32, waiting for transfers between devices: 37.8 us -> 28.7 us  [swap(): return lax.ppermute(value, 'dp', [(i, i ^ bit) for i in range(size)])]
    unnamed x90 -> x86, local copies, waits for them, and re-layouts: 6.1 us -> 5.12 us
  transfers between devices with their start and end apart: 52 -> 52, of which waited for: 25 -> 25; matrix products, arithmetic and copies ran while one was open for 11% -> 9% of each run, Pallas kernels for 24% -> 25%
where the time goes in v6:
time: 252 us; the launch traced here: 248 us
  waiting for transfers between devices  90.3 us (36%)
  Pallas kernels  61.4 us (24%)
  starting transfers between devices  45.9 us (18%)
  other arithmetic  17.7 us (7%)
  between operations  15.3 us (6%)
  local copies, waits for them, and re-layouts  14.9 us (6%)
  matrix products  2.64 us (1%)
    ppermute x18, waiting for transfers between devices, turn(): lax.ppermute(value, 'blk', [(i, (i + steps) % size) for i in range(size)])  61.5 us
    pallas_call x5, Pallas kernels, run_kernel(): pl.pallas_call(kernel, out_shape=[jax.ShapeDtypeStruct(shape, dtype) for...  61.4 us
    ppermute x32, waiting for transfers between devices, swap(): return lax.ppermute(value, 'dp', [(i, i ^ bit) for i in range(size)])  28.7 us
    ppermute x32, starting transfers between devices, swap(): return lax.ppermute(value, 'dp', [(i, i ^ bit) for i in range(size)])  23.4 us
    ppermute x18, starting transfers between devices, turn(): lax.ppermute(value, 'blk', [(i, (i + steps) % size) for i in range(size)])  22.4 us
    convert_element_type x8, other arithmetic, add_low(): (left.astype(jnp.float32) + right.astype(jnp.float32)).astype(jnp.bfloat16)  5.44 us
    unnamed x86, local copies, waits for them, and re-layouts  5.12 us
  transfers between devices with their start and end apart: 52, of which 25 were waited for; matrix products, arithmetic and copies ran while one was open for 9% of the time, Pallas kernels for 25%

profile of v6, /device:TPU:24, one launch (start us, length us, event | category | flops | bytes accessed | tf_op | source)
XLA Modules:
  0.0 248.3 jit_solution(1290676887090109767)
XLA Ops:
  7.3 1.1 reshape.193
  8.6 0.9 pad_maximum_fusion.12
  9.8 1.9 collective-permute-start.1
  12.1 1.1 fusion.1.diagonal_ref
  13.3 3.1 %relative_bias.1.refs_8_ = f32[3,128,1408]{2,1,0:T(8,128)} custom-call(s32[2]{0:T(128)S(1)} %pad_add_fusion.place_ref, f32[3,1536]{1,0:T(4,128)S(1)} %fusion.1.diagonal_ref), custom_call_target="tpu_custom_call" | custom-call | flops 2200000000 | bytes 7200000 | tf_op jit(solution)/shard_map/relative_bias/pallas_call | solution.py:424
  17.2 13.3 %collective-permute-done.1 = bf16[24,4416]{1,0:T(8,128)(2,1)S(1)} collective-permute-done((bf16[24,4416]{1,0:T(8,128)(2,1)S(1)}, bf16[24,4416]{1,0:T(8,128)(2,1)S(1)}, u32[]{:S(2)}, u32[]{:S(2)}) %collective-permute-start.1) | collective-permute-done | bytes 212000 | tf_op jit(solution)/shard_map/ppermute | solution.py:320
  30.9 1.6 collective-permute-start.3
  32.5 1.5 collective-permute-start.4
  34.2 1.4 collective-permute-start.6
  35.6 1.9 collective-permute-start.7
  37.5 2.6 %collective-permute-done.5 = bf16[96,768]{1,0:T(8,128)(2,1)S(1)} collective-permute-done((bf16[96,768]{1,0:T(8,128)(2,1)S(1)}, bf16[96,768]{1,0:T(8,128)(2,1)S(1)}, u32[]{:S(2)}, u32[]{:S(2)}) %collective-permute-start.5) | collective-permute-done | bytes 147488 | tf_op jit(solution)/shard_map/ppermute | solution.py:320
  40.1 17.0 %collective-permute-done.6 = bf16[96,768]{1,0:T(8,128)(2,1)S(1)} collective-permute-done((bf16[96,768]{1,0:T(8,128)(2,1)S(1)}, bf16[96,768]{1,0:T(8,128)(2,1)S(1)}, u32[]{:S(2)}, u32[]{:S(2)}) %collective-permute-start.6) | collective-permute-done | bytes 147488 | tf_op jit(solution)/shard_map/ppermute | solution.py:320
  57.1 1.0 slice.253
  58.8 1.0 slice.254
  60.9 5.5 %collective-permute-done.8 = bf16[48,4416]{1,0:T(8,128)(2,1)S(1)} collective-permute-done((bf16[48,4416]{1,0:T(8,128)(2,1)S(1)}, bf16[48,4416]{1,0:T(8,128)(2,1)S(1)}, u32[]{:S(2)}, u32[]{:S(2)}) %collective-permute-start.8) | collective-permute-done | bytes 423968 | tf_op jit(solution)/shard_map/ppermute | solution.py:315
  66.4 0.8 constant_dynamic-update-slice_fusion.1
  67.2 5.1 %collective-permute-done.9 = bf16[48,4416]{1,0:T(8,128)(2,1)S(1)} collective-permute-done((bf16[48,4416]{1,0:T(8,128)(2,1)S(1)}, bf16[48,4416]{1,0:T(8,128)(2,1)S(1)}, u32[]{:S(2)}, u32[]{:S(2)}) %collective-permute-start.9) | collective-permute-done | bytes 423968 | tf_op jit(solution)/shard_map/ppermute | solution.py:315
  72.3 0.8 constant_dynamic-update-slice_fusion.refs_3_.refs_12_.refs_17_
  73.9 1.6 collective-permute-start.14
  76.0 11.5 %attend.1 = (bf16[768,576]{1,0:T(8,128)(2,1)}, bf16[768,576]{1,0:T(8,128)(2,1)}, bf16[768,768]{1,0:T(8,128)(2,1)}, f32[768,192]{1,0:T(8,128)S(1)}, bf16[768,192]...) custom-call(s32[2]{0:T(128)S(1)} %pad_add_fusion.place_ref, f32[1,768]{1,0:T(1,128)S(1)} %broadcast_in_dim.65.gain_ref, ...), custom_call_target="tpu_custom_call" | custom-call | flops 14300000256 | bytes 46800000 | tf_op jit(solution)/shard_map/attend/pallas_call | solution.py:424
  87.6 0.9 copy-done.5
  88.5 1.3 collective-permute-done.14.refs_23_
  89.7 1.2 collective-permute-done.15.refs_24_
  92.3 3.4 %collective-permute-start.19 = (bf16[192,192]{1,0:T(8,128)(2,1)S(1)}, bf16[192,192]{1,0:T(8,128)(2,1)S(1)}, u32[]{:S(2)}, u32[]{:S(2)}) collective-permute-start(bf16[192,192]{1,0:T(8,128)(2,1)S(1)} %get-tuple-element.207), channel_id=1, source_target_pairs={{0,2},{1,3},{2,0},{3,1},{4,6},{5,7},{6,4},{7,5},{8,10},{9,11},{10,... | collective-permute-start | bytes 221192 | tf_op jit(solution)/shard_map/ppermute | solution.py:320
  95.7 2.2 collective-permute-start.20
  97.9 1.4 collective-permute-done.16
  99.8 4.3 %collective-permute-done.19.refs_2_ = bf16[192,192]{1,0:T(8,128)(2,1)S(1)} collective-permute-done((bf16[192,192]{1,0:T(8,128)(2,1)S(1)}, bf16[192,192]{1,0:T(8,128)(2,1)S(1)}, u32[]{:S(2)}, u32[]{:S(2)}) %collective-permute-start.19) | collective-permute-done | bytes 73760 | tf_op jit(solution)/shard_map/ppermute | solution.py:320
  105.2 10.1 %feed_forward.1 = (f32[192,768]{1,0:T(8,128)}, f32[192,768]{1,0:T(8,128)}, bf16[192,768]{1,0:T(8,128)(2,1)S(1)}, f32[192,1]{1,0:T(8,128)S(1)}, f32[192,1]{1,0:T(...) custom-call(s32[2]{0:T(128)S(1)} %pad_add_fusion.place_ref, ...), custom_call_target="tpu_custom_call" | custom-call | flops 9900000256 | bytes 32400000 | tf_op jit(solution)/shard_map/feed_forward/pallas_call | solution.py:424
  115.4 0.8 copy-done.38
  117.1 1.9 collective-permute-done.25
  119.0 1.2 fusion.8
  120.3 1.4 collective-permute-start.26
  121.7 1.7 collective-permute-start.27
  123.4 24.5 %feed_forward_back.1 = (bf16[192,768]{1,0:T(8,128)(2,1)}, f32[192,768]{1,0:T(8,128)}, f32[1,3072]{1,0:T(1,128)S(1)}, f32[1,768]{1,0:T(1,128)S(1)}, f32[1,768]{1,...) custom-call(s32[2]{0:T(128)S(1)} %pad_add_fusion.place_ref, ...), custom_call_target="tpu_custom_call" | custom-call | flops 14300000256 | bytes 46800000 | tf_op jit(solution)/shard_map/feed_forward_back/pallas_call | solution.py:424
  148.8 1.0 collective-permute-start.30
  149.8 2.8 %collective-permute-start.31 = (bf16[192,192]{1,0:T(8,128)(2,1)S(1)}, bf16[192,192]{1,0:T(8,128)(2,1)S(1)}, u32[]{:S(2)}, u32[]{:S(2)}) collective-permute-start(bf16[192,192]{1,0:T(8,128)(2,1)S(1)} %get-tuple-element.129), channel_id=1, source_target_pairs={{0,1},{1,2},{2,3},{3,0},{4,5},{5,6},{6,7},{7,4},{8,9},{9,10},{10,1... | collective-permute-start | bytes 221192 | tf_op jit(solution)/shard_map/ppermute | solution.py:320
  152.6 2.9 %collective-permute-done.33 = bf16[3,384,768]{2,1,0:T(8,128)(2,1)S(1)} collective-permute-done((bf16[3,384,768]{2,1,0:T(8,128)(2,1)S(1)}, bf16[3,384,768]{2,1,0:T(8,128)(2,1)S(1)}, u32[]{:S(2)}, u32[]{:S(2)}) %collective-permute-start.33) | collective-permute-done | bytes 1769504 | tf_op jit(solution)/shard_map/ppermute | solution.py:315
  156.3 0.9 copy-done.7
  158.4 1.5 fusion.10
  160.0 12.2 %attend_back.1 = (bf16[4,96,576]{2,1,0:T(8,128)(2,1)S(1)}, bf16[4,96,576]{2,1,0:T(8,128)(2,1)}, f32[3,1536]{1,0:T(4,128)S(1)}, f32[768,3]{1,0:T(8,128)S(1)}, f32...) custom-call(s32[2]{0:T(128)S(1)} %pad_add_fusion.place_ref, bf16[192,192]{1,0:T(8,128)(2,1)S(1)} %get-tuple-element.126.refs_0_, ...), custom_call_target="tpu_custom_call" | custom-call | flops 13200000000 | bytes 43200000 | tf_op jit(solution)/shard_map/attend_back/pallas_call | solution.py:424
  173.1 1.5 fusion.9
  176.6 1.7 collective-permute-start.37
  178.6 1.8 collective-permute-start.39
  181.1 1.0 collective-permute-start.41
  182.7 0.8 slice_bitcast_fusion.2
  183.5 1.6 fusion.7
  185.1 2.3 collective-permute-done.36
  187.5 3.4 %collective-permute-done.37 = bf16[48,3840]{1,0:T(8,128)(2,1)} collective-permute-done((bf16[48,3840]{1,0:T(8,128)(2,1)S(1)}, bf16[48,3840]{1,0:T(8,128)(2,1)}, u32[]{:S(2)}, u32[]{:S(2)}) %collective-permute-start.37) | collective-permute-done | bytes 368672 | tf_op jit(solution)/shard_map/ppermute | solution.py:315
  190.8 0.8 collective-permute-done.39
  191.6 1.0 collective-permute-done.40
  194.1 1.4 fusion.11
  195.5 1.8 collective-permute-start.43
  197.4 1.1 collective-permute-start.42
  199.6 1.9 collective-permute-start.46
  201.6 1.0 fusion.26
  202.5 2.3 collective-permute-done.44
  204.9 9.0 %collective-permute-done.45 = bf16[106,768]{1,0:T(8,128)(2,1)S(1)} collective-permute-done((bf16[106,768]{1,0:T(8,128)(2,1)S(1)}, bf16[106,768]{1,0:T(8,128)(2,1)S(1)}, u32[]{:S(2)}, u32[]{:S(2)}) %collective-permute-start.45) | collective-permute-done | bytes 162848 | tf_op jit(solution)/shard_map/ppermute | solution.py:320
  215.0 1.7 fusion.5
  217.4 1.7 collective-permute-start.48
  219.1 1.9 collective-permute-start.49
  221.7 1.0 fusion.21
  226.3 12.1 %collective-permute-done.48 = bf16[24,4416]{1,0:T(8,128)(2,1)S(1)} collective-permute-done((bf16[24,4416]{1,0:T(8,128)(2,1)S(1)}, bf16[24,4416]{1,0:T(8,128)(2,1)S(1)}, u32[]{:S(2)}, u32[]{:S(2)}) %collective-permute-start.48) | collective-permute-done | bytes 212000 | tf_op jit(solution)/shard_map/ppermute | solution.py:320
  238.9 0.9 reshape.201
  239.8 0.8 convert_add_fusion.8
  (248 shorter events, 25.8 us)
Async XLA Ops:
  7.2 65.9 %all-gather.2.cloned.1.call-start = ((), (), s32[]{:S(2)}) async-start(), calls=%async_computation.1 | async-start | bytes 1474560 | tf_op jit(solution)/shard_map/all_gather | solution.py:817
  9.7 7.5 %collective-permute-start = (bf16[24,4416]{1,0:T(8,128)(2,1)S(1)}, bf16[24,4416]{1,0:T(8,128)(2,1)S(1)}, u32[]{:S(2)}, u32[]{:S(2)}) collective-permute-start(bf16[24,4416]{1,0:T(8,128)(2,1)S(1)} %get-tuple-element.188), channel_id=1, source_target_pairs={{0,1},{1,2},{2,3},{3,0},{4,5},{5,6},{6,7},{7,4},{8,9},{9,10},{10,1... | collective-permute-start | bytes 635912 | tf_op jit(solution)/shard_map/ppermute | solution.py:320
  9.8 20.7 %collective-permute-start.1 = (bf16[24,4416]{1,0:T(8,128)(2,1)S(1)}, bf16[24,4416]{1,0:T(8,128)(2,1)S(1)}, u32[]{:S(2)}, u32[]{:S(2)}) collective-permute-start(bf16[24,4416]{1,0:T(8,128)(2,1)S(1)} %get-tuple-element.189), channel_id=1, source_target_pairs={{0,2},{1,3},{2,0},{3,1},{4,6},{5,7},{6,4},{7,5},{8,10},{9,11},{10,... | collective-permute-start | bytes 635912 | tf_op jit(solution)/shard_map/ppermute | solution.py:320
  11.7 18.8 %collective-permute-start.2 = (bf16[24,4416]{1,0:T(8,128)(2,1)S(1)}, bf16[24,4416]{1,0:T(8,128)(2,1)S(1)}, u32[]{:S(2)}, u32[]{:S(2)}) collective-permute-start(bf16[24,4416]{1,0:T(8,128)(2,1)S(1)} %get-tuple-element.190), channel_id=1, source_target_pairs={{0,3},{1,0},{2,1},{3,2},{4,7},{5,4},{6,5},{7,6},{8,11},{9,8},{10,9... | collective-permute-start | bytes 635912 | tf_op jit(solution)/shard_map/ppermute | solution.py:320
  30.9 42.1 %copy-start.13 = (bf16[96,4416]{1,0:T(8,128)(2,1)}, bf16[96,4416]{1,0:T(8,128)(2,1)S(1)}, u32[]{:S(2)}) copy-start(bf16[96,4416]{1,0:T(8,128)(2,1)S(1)} %pad_maximum_fusion.refs_0_.refs_9_.refs_14_) | copy-start | bytes 2543620
  30.9 26.2 %collective-permute-start.3 = (bf16[96,4416]{1,0:T(8,128)(2,1)S(1)}, bf16[96,4416]{1,0:T(8,128)(2,1)}, u32[]{:S(2)}, u32[]{:S(2)}) collective-permute-start(bf16[96,4416]{1,0:T(8,128)(2,1)S(1)} %pad_maximum_fusion.refs_0_.refs_9_.refs_14_), channel_id=1, source_target_pairs={{0,8},{4,12},{8,0},{12,4},{16,24},{20,28},{24,16},{28,20},{1,9},{5... | collective-permute-start | bytes 2543624 | tf_op jit(solution)/shard_map/ppermute | solution.py:315
  32.5 24.6 %collective-permute-start.4 = (bf16[96,4416]{1,0:T(8,128)(2,1)S(1)}, bf16[96,4416]{1,0:T(8,128)(2,1)}, u32[]{:S(2)}, u32[]{:S(2)}) collective-permute-start(bf16[96,4416]{1,0:T(8,128)(2,1)S(1)} %pad_maximum_fusion.refs_0_.refs_9_.refs_14_), channel_id=1, source_target_pairs={{0,16},{4,20},{8,24},{12,28},{16,0},{20,4},{24,8},{28,12},{1,17},{... | collective-permute-start | bytes 2543624 | tf_op jit(solution)/shard_map/ppermute | solution.py:315
  34.0 39.0 %copy-start.41 = (s32[1,4]{1,0:T(1,128)S(1)}, s32[1,4]{1,0:T(1,128)}, u32[]{:S(2)}) copy-start(s32[1,4]{1,0:T(1,128)} %param.15) | copy-start | bytes 52
  34.1 39.5 %copy-start.34 = (f32[12]{0:T(128)S(1)}, f32[12]{0:T(128)}, u32[]{:S(2)}) copy-start(f32[12]{0:T(128)} %param.25) | copy-start | bytes 148
  34.1 180.9 %reduce-scatter.2.cloned.1.call-start = ((), (), s32[]{:S(2)}) async-start(), calls=%async_computation.2 | async-start | bytes 1474560 | tf_op jit(solution)/shard_map/reduce_scatter | solution.py:966
  34.1 6.0 %collective-permute-start.5 = (bf16[96,768]{1,0:T(8,128)(2,1)S(1)}, bf16[96,768]{1,0:T(8,128)(2,1)S(1)}, u32[]{:S(2)}, u32[]{:S(2)}) collective-permute-start(bf16[96,768]{1,0:T(8,128)(2,1)S(1)} %copy-done.17), channel_id=1, source_target_pairs={{0,1},{1,2},{2,3},{3,0},{4,5},{5,6},{6,7},{7,4},{8,9},{9,10},{10,1... | collective-permute-start | bytes 442376 | tf_op jit(solution)/shard_map/ppermute | solution.py:320
  34.2 22.9 %collective-permute-start.6 = (bf16[96,768]{1,0:T(8,128)(2,1)S(1)}, bf16[96,768]{1,0:T(8,128)(2,1)S(1)}, u32[]{:S(2)}, u32[]{:S(2)}) collective-permute-start(bf16[96,768]{1,0:T(8,128)(2,1)S(1)} %copy-done.17), channel_id=1, source_target_pairs={{0,2},{1,3},{2,0},{3,1},{4,6},{5,7},{6,4},{7,5},{8,10},{9,11},{10,... | collective-permute-start | bytes 442376 | tf_op jit(solution)/shard_map/ppermute | solution.py:320
  35.6 21.5 %collective-permute-start.7 = (bf16[96,768]{1,0:T(8,128)(2,1)S(1)}, bf16[96,768]{1,0:T(8,128)(2,1)S(1)}, u32[]{:S(2)}, u32[]{:S(2)}) collective-permute-start(bf16[96,768]{1,0:T(8,128)(2,1)S(1)} %copy-done.17), channel_id=1, source_target_pairs={{0,3},{1,0},{2,1},{3,2},{4,7},{5,4},{6,5},{7,6},{8,11},{9,8},{10,9... | collective-permute-start | bytes 442376 | tf_op jit(solution)/shard_map/ppermute | solution.py:320
  58.2 8.2 %collective-permute-start.8 = (bf16[48,4416]{1,0:T(8,128)(2,1)S(1)}, bf16[48,4416]{1,0:T(8,128)(2,1)S(1)}, u32[]{:S(2)}, u32[]{:S(2)}) collective-permute-start(bf16[48,4416]{1,0:T(8,128)(2,1)S(1)} %slice.253), channel_id=1, source_target_pairs={{0,8},{4,12},{8,0},{12,4},{16,24},{20,28},{24,16},{28,20},{1,9},{5... | collective-permute-start | bytes 1271816 | tf_op jit(solution)/shard_map/ppermute | solution.py:315
  59.8 16.2 %collective-permute-start.11 = (bf16[96,4416]{1,0:T(8,128)(2,1)}, bf16[96,4416]{1,0:T(8,128)(2,1)}, u32[]{:S(2)}, u32[]{:S(2)}) collective-permute-start(bf16[96,4416]{1,0:T(8,128)(2,1)} %collective-permute-done.3.refs_1_.refs_10_.refs_15_), channel_id=1, source_target_pairs={{0,4},{4,0},{8,12},{12,8},{16,20},{20,16},{24,28},{28,24},{1,5},{5... | collective-permute-start | bytes 2543624 | tf_op jit(solution)/shard_map/ppermute | solution.py:315
  59.9 16.1 %collective-permute-start.12 = (bf16[96,4416]{1,0:T(8,128)(2,1)}, bf16[96,4416]{1,0:T(8,128)(2,1)}, u32[]{:S(2)}, u32[]{:S(2)}) collective-permute-start(bf16[96,4416]{1,0:T(8,128)(2,1)} %collective-permute-done.4.refs_2_.refs_11_.refs_16_), channel_id=1, source_target_pairs={{0,4},{4,0},{8,12},{12,8},{16,20},{20,16},{24,28},{28,24},{1,5},{5... | collective-permute-start | bytes 2543624 | tf_op jit(solution)/shard_map/ppermute | solution.py:315
  60.4 11.9 %collective-permute-start.9 = (bf16[48,4416]{1,0:T(8,128)(2,1)S(1)}, bf16[48,4416]{1,0:T(8,128)(2,1)S(1)}, u32[]{:S(2)}, u32[]{:S(2)}) collective-permute-start(bf16[48,4416]{1,0:T(8,128)(2,1)S(1)} %slice.254), channel_id=1, source_target_pairs={{0,16},{4,20},{8,24},{12,28},{16,0},{20,4},{24,8},{28,12},{1,17},{... | collective-permute-start | bytes 1271816 | tf_op jit(solution)/shard_map/ppermute | solution.py:315
  60.9 14.5 %collective-permute-start.10 = (bf16[96,4416]{1,0:T(8,128)(2,1)S(1)}, bf16[96,4416]{1,0:T(8,128)(2,1)}, u32[]{:S(2)}, u32[]{:S(2)}) collective-permute-start(bf16[96,4416]{1,0:T(8,128)(2,1)S(1)} %pad_maximum_fusion.refs_0_.refs_9_.refs_14_), channel_id=1, source_target_pairs={{0,4},{4,0},{8,12},{12,8},{16,20},{20,16},{24,28},{28,24},{1,5},{5... | collective-permute-start | bytes 2543624 | tf_op jit(solution)/shard_map/ppermute | solution.py:315
  73.1 2.9 %collective-permute-start.13 = (bf16[96,4416]{1,0:T(8,128)(2,1)}, bf16[96,4416]{1,0:T(8,128)(2,1)}, u32[]{:S(2)}, u32[]{:S(2)}) collective-permute-start(bf16[96,4416]{1,0:T(8,128)(2,1)} %constant_dynamic-update-slice_fusion.refs_3_.refs_12_.refs_17_), channel_id=1, source_target_pairs={{0,4},{4,0},{8,12},{12,8},{16,20},{20,16},{24,28},{28,24},{1,5},{5... | collective-permute-start | bytes 2543624 | tf_op jit(solution)/shard_map/ppermute | solution.py:315
  73.9 30.2 %copy-start.14 = (bf16[384,768]{1,0:T(8,128)(2,1)}, bf16[384,768]{1,0:T(8,128)(2,1)S(1)}, u32[]{:S(2)}) copy-start(bf16[384,768]{1,0:T(8,128)(2,1)S(1)} %pad_maximum_fusion.5.refs_22_) | copy-start | bytes 1769476
  73.9 15.8 %collective-permute-start.14 = (bf16[384,768]{1,0:T(8,128)(2,1)S(1)}, bf16[384,768]{1,0:T(8,128)(2,1)S(1)}, u32[]{:S(2)}, u32[]{:S(2)}) collective-permute-start(bf16[384,768]{1,0:T(8,128)(2,1)S(1)} %pad_maximum_fusion.5.refs_22_), channel_id=1, source_target_pairs={{0,8},{4,12},{8,0},{12,4},{16,24},{20,28},{24,16},{28,20},{1,9},{5... | collective-permute-start | bytes 1769480 | tf_op jit(solution)/shard_map/ppermute | solution.py:315
  75.5 15.5 %collective-permute-start.15 = (bf16[384,768]{1,0:T(8,128)(2,1)S(1)}, bf16[384,768]{1,0:T(8,128)(2,1)S(1)}, u32[]{:S(2)}, u32[]{:S(2)}) collective-permute-start(bf16[384,768]{1,0:T(8,128)(2,1)S(1)} %pad_maximum_fusion.5.refs_22_), channel_id=1, source_target_pairs={{0,16},{4,20},{8,24},{12,28},{16,0},{20,4},{24,8},{28,12},{1,17},{... | collective-permute-start | bytes 1769480 | tf_op jit(solution)/shard_map/ppermute | solution.py:315
  76.0 16.2 %copy-start.32 = (f32[768]{0:T(1024)S(1)}, f32[768]{0:T(1024)}, u32[]{:S(2)}) copy-start(f32[768]{0:T(1024)} %param.22) | copy-start | bytes 9220
  88.4 16.7 %copy-start.2 = (bf16[1,192,768]{2,1,0:T(8,128)(2,1)S(1)}, bf16[1,192,768]{2,1,0:T(8,128)(2,1)}, u32[]{:S(2)}) copy-start(bf16[1,192,768]{2,1,0:T(8,128)(2,1)} %param.14) | copy-start | bytes 884740
  88.5 16.7 %copy-start.3 = (bf16[1,192,768]{2,1,0:T(8,128)(2,1)S(1)}, bf16[1,192,768]{2,1,0:T(8,128)(2,1)}, u32[]{:S(2)}) copy-start(bf16[1,192,768]{2,1,0:T(8,128)(2,1)} %param.27) | copy-start | bytes 884740
  88.5 16.7 %copy-start.4 = (f32[3072]{0:T(1024)S(1)}, f32[3072]{0:T(1024)}, u32[]{:S(2)}) copy-start(f32[3072]{0:T(1024)} %param.24) | copy-start | bytes 36868
  89.7 25.6 %copy-start.18 = (bf16[384,768]{1,0:T(8,128)(2,1)}, bf16[384,768]{1,0:T(8,128)(2,1)S(1)}, u32[]{:S(2)}) copy-start(bf16[384,768]{1,0:T(8,128)(2,1)S(1)} %collective-permute-done.14.refs_23_) | copy-start | bytes 1769476
  90.9 24.4 %copy-start.19 = (bf16[384,768]{1,0:T(8,128)(2,1)}, bf16[384,768]{1,0:T(8,128)(2,1)S(1)}, u32[]{:S(2)}) copy-start(bf16[384,768]{1,0:T(8,128)(2,1)S(1)} %collective-permute-done.15.refs_24_) | copy-start | bytes 1769476
  91.0 8.4 %collective-permute-start.16 = (bf16[192,768]{1,0:T(8,128)(2,1)S(1)}, bf16[192,768]{1,0:T(8,128)(2,1)S(1)}, u32[]{:S(2)}, u32[]{:S(2)}) collective-permute-start(bf16[192,768]{1,0:T(8,128)(2,1)S(1)} %slice.255), channel_id=1, source_target_pairs={{0,8},{4,12},{8,0},{12,4},{16,24},{20,28},{24,16},{28,20},{1,9},{5... | collective-permute-start | bytes 884744 | tf_op jit(solution)/shard_map/ppermute | solution.py:315
  91.6 8.2 %collective-permute-start.17 = (bf16[192,768]{1,0:T(8,128)(2,1)S(1)}, bf16[192,768]{1,0:T(8,128)(2,1)S(1)}, u32[]{:S(2)}, u32[]{:S(2)}) collective-permute-start(bf16[192,768]{1,0:T(8,128)(2,1)S(1)} %slice.256), channel_id=1, source_target_pairs={{0,16},{4,20},{8,24},{12,28},{16,0},{20,4},{24,8},{28,12},{1,17},{... | collective-permute-start | bytes 884744 | tf_op jit(solution)/shard_map/ppermute | solution.py:315
  92.3 7.5 %collective-permute-start.18 = (bf16[192,192]{1,0:T(8,128)(2,1)S(1)}, bf16[192,192]{1,0:T(8,128)(2,1)S(1)}, u32[]{:S(2)}, u32[]{:S(2)}) collective-permute-start(bf16[192,192]{1,0:T(8,128)(2,1)S(1)} %get-tuple-element.208), channel_id=1, source_target_pairs={{0,1},{1,2},{2,3},{3,0},{4,5},{5,6},{6,7},{7,4},{8,9},{9,10},{10,1... | collective-permute-start | bytes 221192 | tf_op jit(solution)/shard_map/ppermute | solution.py:320
  92.3 11.8 %collective-permute-start.19 = (bf16[192,192]{1,0:T(8,128)(2,1)S(1)}, bf16[192,192]{1,0:T(8,128)(2,1)S(1)}, u32[]{:S(2)}, u32[]{:S(2)}) collective-permute-start(bf16[192,192]{1,0:T(8,128)(2,1)S(1)} %get-tuple-element.207), channel_id=1, source_target_pairs={{0,2},{1,3},{2,0},{3,1},{4,6},{5,7},{6,4},{7,5},{8,10},{9,11},{10,... | collective-permute-start | bytes 221192 | tf_op jit(solution)/shard_map/ppermute | solution.py:320
  95.7 8.4 %collective-permute-start.20 = (bf16[192,192]{1,0:T(8,128)(2,1)S(1)}, bf16[192,192]{1,0:T(8,128)(2,1)S(1)}, u32[]{:S(2)}, u32[]{:S(2)}) collective-permute-start(bf16[192,192]{1,0:T(8,128)(2,1)S(1)} %get-tuple-element.206), channel_id=1, source_target_pairs={{0,3},{1,0},{2,1},{3,2},{4,7},{5,4},{6,5},{7,6},{8,11},{9,8},{10,9... | collective-permute-start | bytes 221192 | tf_op jit(solution)/shard_map/ppermute | solution.py:320
  104.1 11.2 %collective-permute-start.21 = (bf16[384,768]{1,0:T(8,128)(2,1)S(1)}, bf16[384,768]{1,0:T(8,128)(2,1)S(1)}, u32[]{:S(2)}, u32[]{:S(2)}) collective-permute-start(bf16[384,768]{1,0:T(8,128)(2,1)S(1)} %pad_maximum_fusion.5.refs_22_), channel_id=1, source_target_pairs={{0,4},{4,0},{8,12},{12,8},{16,20},{20,16},{24,28},{28,24},{1,5},{5... | collective-permute-start | bytes 1769480 | tf_op jit(solution)/shard_map/ppermute | solution.py:315
  104.1 11.2 %collective-permute-start.22 = (bf16[384,768]{1,0:T(8,128)(2,1)S(1)}, bf16[384,768]{1,0:T(8,128)(2,1)S(1)}, u32[]{:S(2)}, u32[]{:S(2)}) collective-permute-start(bf16[384,768]{1,0:T(8,128)(2,1)S(1)} %collective-permute-done.14.refs_23_), channel_id=1, source_target_pairs={{0,4},{4,0},{8,12},{12,8},{16,20},{20,16},{24,28},{28,24},{1,5},{5... | collective-permute-start | bytes 1769480 | tf_op jit(solution)/shard_map/ppermute | solution.py:315
  104.6 10.7 %collective-permute-start.23 = (bf16[384,768]{1,0:T(8,128)(2,1)S(1)}, bf16[384,768]{1,0:T(8,128)(2,1)S(1)}, u32[]{:S(2)}, u32[]{:S(2)}) collective-permute-start(bf16[384,768]{1,0:T(8,128)(2,1)S(1)} %collective-permute-done.15.refs_24_), channel_id=1, source_target_pairs={{0,4},{4,0},{8,12},{12,8},{16,20},{20,16},{24,28},{28,24},{1,5},{5... | collective-permute-start | bytes 1769480 | tf_op jit(solution)/shard_map/ppermute | solution.py:315
  104.7 10.7 %collective-permute-start.24 = (bf16[384,768]{1,0:T(8,128)(2,1)S(1)}, bf16[384,768]{1,0:T(8,128)(2,1)S(1)}, u32[]{:S(2)}, u32[]{:S(2)}) collective-permute-start(bf16[384,768]{1,0:T(8,128)(2,1)S(1)} %constant_dynamic-update-slice_fusion.2.refs_25_), channel_id=1, source_target_pairs={{0,4},{4,0},{8,12},{12,8},{16,20},{20,16},{24,28},{28,24},{1,5},{5... | collective-permute-start | bytes 1769480 | tf_op jit(solution)/shard_map/ppermute | solution.py:315
  116.8 2.2 collective-permute-start.25
  120.3 27.6 %collective-permute-start.26 = (bf16[192,768]{1,0:T(8,128)(2,1)S(1)}, bf16[192,768]{1,0:T(8,128)(2,1)S(1)}, u32[]{:S(2)}, u32[]{:S(2)}) collective-permute-start(bf16[192,768]{1,0:T(8,128)(2,1)S(1)} %get-tuple-element.198), channel_id=1, source_target_pairs={{0,8},{4,12},{8,0},{12,4},{16,24},{20,28},{24,16},{28,20},{1,9},{5... | collective-permute-start | bytes 884744 | tf_op jit(solution)/shard_map/ppermute | solution.py:315
  121.7 26.2 %collective-permute-start.27 = (bf16[192,768]{1,0:T(8,128)(2,1)S(1)}, bf16[192,768]{1,0:T(8,128)(2,1)S(1)}, u32[]{:S(2)}, u32[]{:S(2)}) collective-permute-start(bf16[192,768]{1,0:T(8,128)(2,1)S(1)} %get-tuple-element.197), channel_id=1, source_target_pairs={{0,16},{4,20},{8,24},{12,28},{16,0},{20,4},{24,8},{28,12},{1,17},{... | collective-permute-start | bytes 884744 | tf_op jit(solution)/shard_map/ppermute | solution.py:315
  123.4 24.6 %copy-start.36 = (bf16[3,384,768]{2,1,0:T(8,128)(2,1)S(1)}, bf16[3,384,768]{2,1,0:T(8,128)(2,1)}, u32[]{:S(2)}) copy-start(bf16[3,384,768]{2,1,0:T(8,128)(2,1)} %get-tuple-element.138) | copy-start | bytes 5308420
  123.4 32.1 %copy-start.10 = (bf16[4,384,768]{2,1,0:T(8,128)(2,1)S(1)}, bf16[4,384,768]{2,1,0:T(8,128)(2,1)}, u32[]{:S(2)}) copy-start(bf16[4,384,768]{2,1,0:T(8,128)(2,1)} %get-tuple-element.100) | copy-start | bytes 7077892
  147.9 9.7 %collective-permute-start.28 = (bf16[4,96,3840]{2,1,0:T(8,128)(2,1)}, bf16[4,96,3840]{2,1,0:T(8,128)(2,1)S(1)}, u32[]{:S(2)}, u32[]{:S(2)}) collective-permute-start(bf16[4,96,3840]{2,1,0:T(8,128)(2,1)} %get-tuple-element.124), channel_id=1, source_target_pairs={{0,4},{4,0},{8,12},{12,8},{16,20},{20,16},{24,28},{28,24},{1,5},{5... | collective-permute-start | bytes 8847368 | tf_op jit(solution)/shard_map/ppermute | solution.py:315
  148.0 7.5 %collective-permute-start.33 = (bf16[3,384,768]{2,1,0:T(8,128)(2,1)S(1)}, bf16[3,384,768]{2,1,0:T(8,128)(2,1)S(1)}, u32[]{:S(2)}, u32[]{:S(2)}) collective-permute-start(bf16[3,384,768]{2,1,0:T(8,128)(2,1)S(1)} %copy-done.36), channel_id=1, source_target_pairs={{0,4},{4,0},{8,12},{12,8},{16,20},{20,16},{24,28},{28,24},{1,5},{5... | collective-permute-start | bytes 5308424 | tf_op jit(solution)/shard_map/ppermute | solution.py:315
  148.7 11.2 %collective-permute-start.29 = (bf16[192,192]{1,0:T(8,128)(2,1)S(1)}, bf16[192,192]{1,0:T(8,128)(2,1)S(1)}, u32[]{:S(2)}, u32[]{:S(2)}) collective-permute-start(bf16[192,192]{1,0:T(8,128)(2,1)S(1)} %get-tuple-element.127), channel_id=1, source_target_pairs={{0,3},{1,0},{2,1},{3,2},{4,7},{5,4},{6,5},{7,6},{8,11},{9,8},{10,9... | collective-permute-start | bytes 221192 | tf_op jit(solution)/shard_map/ppermute | solution.py:320
  148.8 11.2 %collective-permute-start.30 = (bf16[192,192]{1,0:T(8,128)(2,1)S(1)}, bf16[192,192]{1,0:T(8,128)(2,1)S(1)}, u32[]{:S(2)}, u32[]{:S(2)}) collective-permute-start(bf16[192,192]{1,0:T(8,128)(2,1)S(1)} %get-tuple-element.128), channel_id=1, source_target_pairs={{0,2},{1,3},{2,0},{3,1},{4,6},{5,7},{6,4},{7,5},{8,10},{9,11},{10,... | collective-permute-start | bytes 221192 | tf_op jit(solution)/shard_map/ppermute | solution.py:320
  149.8 10.2 %collective-permute-start.31 = (bf16[192,192]{1,0:T(8,128)(2,1)S(1)}, bf16[192,192]{1,0:T(8,128)(2,1)S(1)}, u32[]{:S(2)}, u32[]{:S(2)}) collective-permute-start(bf16[192,192]{1,0:T(8,128)(2,1)S(1)} %get-tuple-element.129), channel_id=1, source_target_pairs={{0,1},{1,2},{2,3},{3,0},{4,5},{5,6},{6,7},{7,4},{8,9},{9,10},{10,1... | collective-permute-start | bytes 221192 | tf_op jit(solution)/shard_map/ppermute | solution.py:320
  157.2 15.7 %collective-permute-start.35 = (bf16[384,768]{1,0:T(8,128)(2,1)S(1)}, bf16[384,768]{1,0:T(8,128)(2,1)}, u32[]{:S(2)}, u32[]{:S(2)}) collective-permute-start(bf16[384,768]{1,0:T(8,128)(2,1)S(1)} %pad_maximum_fusion.7), channel_id=1, source_target_pairs={{0,16},{4,20},{8,24},{12,28},{16,0},{20,4},{24,8},{28,12},{1,17},{... | collective-permute-start | bytes 1769480 | tf_op jit(solution)/shard_map/ppermute | solution.py:315
  157.6 15.5 %collective-permute-start.34 = (bf16[384,768]{1,0:T(8,128)(2,1)S(1)}, bf16[384,768]{1,0:T(8,128)(2,1)}, u32[]{:S(2)}, u32[]{:S(2)}) collective-permute-start(bf16[384,768]{1,0:T(8,128)(2,1)S(1)} %pad_maximum_fusion.6), channel_id=1, source_target_pairs={{0,8},{4,12},{8,0},{12,4},{16,24},{20,28},{24,16},{28,20},{1,9},{5... | collective-permute-start | bytes 1769480 | tf_op jit(solution)/shard_map/ppermute | solution.py:315
  173.1 5.3 %collective-permute-start.32 = (bf16[4,96,576]{2,1,0:T(8,128)(2,1)S(1)}, bf16[4,96,576]{2,1,0:T(8,128)(2,1)S(1)}, u32[]{:S(2)}, u32[]{:S(2)}) collective-permute-start(bf16[4,96,576]{2,1,0:T(8,128)(2,1)S(1)} %get-tuple-element.136), channel_id=1, source_target_pairs={{0,4},{4,0},{8,12},{12,8},{16,20},{20,16},{24,28},{28,24},{1,5},{5... | collective-permute-start | bytes 1327112 | tf_op jit(solution)/shard_map/ppermute | solution.py:315
  175.2 3.1 %collective-permute-start.38 = (bf16[13,576]{1,0:T(8,128)(2,1)S(1)}, bf16[13,576]{1,0:T(8,128)(2,1)S(1)}, u32[]{:S(2)}, u32[]{:S(2)}) collective-permute-start(bf16[13,576]{1,0:T(8,128)(2,1)S(1)} %convert_element_type.295), channel_id=1, source_target_pairs={{0,4},{4,0},{8,12},{12,8},{16,20},{20,16},{24,28},{28,24},{1,5},{5... | collective-permute-start | bytes 44936 | tf_op jit(solution)/shard_map/ppermute | solution.py:315
  175.8 11.6 %collective-permute-start.36 = (bf16[48,3840]{1,0:T(8,128)(2,1)S(1)}, bf16[48,3840]{1,0:T(8,128)(2,1)}, u32[]{:S(2)}, u32[]{:S(2)}) collective-permute-start(bf16[48,3840]{1,0:T(8,128)(2,1)S(1)} %get-tuple-element.192), channel_id=1, source_target_pairs={{0,8},{4,12},{8,0},{12,4},{16,24},{20,28},{24,16},{28,20},{1,9},{5... | collective-permute-start | bytes 1105928 | tf_op jit(solution)/shard_map/ppermute | solution.py:315
  176.6 14.2 %collective-permute-start.37 = (bf16[48,3840]{1,0:T(8,128)(2,1)S(1)}, bf16[48,3840]{1,0:T(8,128)(2,1)}, u32[]{:S(2)}, u32[]{:S(2)}) collective-permute-start(bf16[48,3840]{1,0:T(8,128)(2,1)S(1)} %get-tuple-element.191), channel_id=1, source_target_pairs={{0,16},{4,20},{8,24},{12,28},{16,0},{20,4},{24,8},{28,12},{1,17},{... | collective-permute-start | bytes 1105928 | tf_op jit(solution)/shard_map/ppermute | solution.py:315
  178.6 13.1 %collective-permute-start.39 = (bf16[109,576]{1,0:T(8,128)(2,1)S(1)}, bf16[109,576]{1,0:T(8,128)(2,1)S(1)}, u32[]{:S(2)}, u32[]{:S(2)}) collective-permute-start(bf16[109,576]{1,0:T(8,128)(2,1)S(1)} %get-tuple-element.216), channel_id=1, source_target_pairs={{0,24},{4,28},{8,16},{12,20},{16,8},{20,12},{24,0},{28,4},{1,25},{... | collective-permute-start | bytes 376712 | tf_op jit(solution)/shard_map/ppermute | solution.py:315
  180.4 12.2 %collective-permute-start.40 = (bf16[109,576]{1,0:T(8,128)(2,1)S(1)}, bf16[109,576]{1,0:T(8,128)(2,1)S(1)}, u32[]{:S(2)}, u32[]{:S(2)}) collective-permute-start(bf16[109,576]{1,0:T(8,128)(2,1)S(1)} %get-tuple-element.215), channel_id=1, source_target_pairs={{0,8},{4,12},{8,0},{12,4},{16,24},{20,28},{24,16},{28,20},{1,9},{5... | collective-permute-start | bytes 376712 | tf_op jit(solution)/shard_map/ppermute | solution.py:315
  181.1 11.9 %collective-permute-start.41 = (bf16[109,576]{1,0:T(8,128)(2,1)S(1)}, bf16[109,576]{1,0:T(8,128)(2,1)S(1)}, u32[]{:S(2)}, u32[]{:S(2)}) collective-permute-start(bf16[109,576]{1,0:T(8,128)(2,1)S(1)} %get-tuple-element.214), channel_id=1, source_target_pairs={{0,16},{4,20},{8,24},{12,28},{16,0},{20,4},{24,8},{28,12},{1,17},{... | collective-permute-start | bytes 376712 | tf_op jit(solution)/shard_map/ppermute | solution.py:315
  195.5 19.2 %collective-permute-start.43 = (bf16[96,3840]{1,0:T(8,128)(2,1)S(1)}, bf16[96,3840]{1,0:T(8,128)(2,1)}, u32[]{:S(2)}, u32[]{:S(2)}) collective-permute-start(bf16[96,3840]{1,0:T(8,128)(2,1)S(1)} %pad_maximum_fusion.3), channel_id=1, source_target_pairs={{0,16},{4,20},{8,24},{12,28},{16,0},{20,4},{24,8},{28,12},{1,17},{... | collective-permute-start | bytes 2211848 | tf_op jit(solution)/shard_map/ppermute | solution.py:315
  197.4 17.6 %collective-permute-start.42 = (bf16[96,3840]{1,0:T(8,128)(2,1)S(1)}, bf16[96,3840]{1,0:T(8,128)(2,1)}, u32[]{:S(2)}, u32[]{:S(2)}) collective-permute-start(bf16[96,3840]{1,0:T(8,128)(2,1)S(1)} %pad_maximum_fusion.2), channel_id=1, source_target_pairs={{0,8},{4,12},{8,0},{12,4},{16,24},{20,28},{24,16},{28,20},{1,9},{5... | collective-permute-start | bytes 2211848 | tf_op jit(solution)/shard_map/ppermute | solution.py:315
  198.7 6.2 %collective-permute-start.44 = (bf16[106,768]{1,0:T(8,128)(2,1)S(1)}, bf16[106,768]{1,0:T(8,128)(2,1)S(1)}, u32[]{:S(2)}, u32[]{:S(2)}) collective-permute-start(bf16[106,768]{1,0:T(8,128)(2,1)S(1)} %get-tuple-element.196), channel_id=1, source_target_pairs={{0,1},{1,2},{2,3},{3,0},{4,5},{5,6},{6,7},{7,4},{8,9},{9,10},{10,1... | collective-permute-start | bytes 488456 | tf_op jit(solution)/shard_map/ppermute | solution.py:320
  199.4 14.5 %collective-permute-start.45 = (bf16[106,768]{1,0:T(8,128)(2,1)S(1)}, bf16[106,768]{1,0:T(8,128)(2,1)S(1)}, u32[]{:S(2)}, u32[]{:S(2)}) collective-permute-start(bf16[106,768]{1,0:T(8,128)(2,1)S(1)} %get-tuple-element.195), channel_id=1, source_target_pairs={{0,2},{1,3},{2,0},{3,1},{4,6},{5,7},{6,4},{7,5},{8,10},{9,11},{10,... | collective-permute-start | bytes 488456 | tf_op jit(solution)/shard_map/ppermute | solution.py:320
  199.6 14.3 %collective-permute-start.46 = (bf16[106,768]{1,0:T(8,128)(2,1)S(1)}, bf16[106,768]{1,0:T(8,128)(2,1)S(1)}, u32[]{:S(2)}, u32[]{:S(2)}) collective-permute-start(bf16[106,768]{1,0:T(8,128)(2,1)S(1)} %get-tuple-element.194), channel_id=1, source_target_pairs={{0,3},{1,0},{2,1},{3,2},{4,7},{5,4},{6,5},{7,6},{8,11},{9,8},{10,9... | collective-permute-start | bytes 488456 | tf_op jit(solution)/shard_map/ppermute | solution.py:320
  216.8 6.0 %collective-permute-start.47 = (bf16[24,4416]{1,0:T(8,128)(2,1)S(1)}, bf16[24,4416]{1,0:T(8,128)(2,1)S(1)}, u32[]{:S(2)}, u32[]{:S(2)}) collective-permute-start(bf16[24,4416]{1,0:T(8,128)(2,1)S(1)} %get-tuple-element.187), channel_id=1, source_target_pairs={{0,1},{1,2},{2,3},{3,0},{4,5},{5,6},{6,7},{7,4},{8,9},{9,10},{10,1... | collective-permute-start | bytes 635912 | tf_op jit(solution)/shard_map/ppermute | solution.py:320
  217.4 21.1 %collective-permute-start.48 = (bf16[24,4416]{1,0:T(8,128)(2,1)S(1)}, bf16[24,4416]{1,0:T(8,128)(2,1)S(1)}, u32[]{:S(2)}, u32[]{:S(2)}) collective-permute-start(bf16[24,4416]{1,0:T(8,128)(2,1)S(1)} %get-tuple-element.186), channel_id=1, source_target_pairs={{0,2},{1,3},{2,0},{3,1},{4,6},{5,7},{6,4},{7,5},{8,10},{9,11},{10,... | collective-permute-start | bytes 635912 | tf_op jit(solution)/shard_map/ppermute | solution.py:320
  219.1 19.3 %collective-permute-start.49 = (bf16[24,4416]{1,0:T(8,128)(2,1)S(1)}, bf16[24,4416]{1,0:T(8,128)(2,1)S(1)}, u32[]{:S(2)}, u32[]{:S(2)}) collective-permute-start(bf16[24,4416]{1,0:T(8,128)(2,1)S(1)} %get-tuple-element.185), channel_id=1, source_target_pairs={{0,3},{1,0},{2,1},{3,2},{4,7},{5,4},{6,5},{7,6},{8,11},{9,8},{10,9... | collective-permute-start | bytes 635912 | tf_op jit(solution)/shard_map/ppermute | solution.py:320
  (31 other events, 145.7 us)
Sparse Core Ops, SparseCore 0:
  34.2 33.6 all-gather.1
  172.3 27.7 reduce-scatter.1
